TPU v7x, 256 devices: a whole 4x4x8 slice. The times are simulated.
256 devices in a mesh: dp: 64 (over z, x_lo, y), block: 4 (over x_hi, core).
Axes of the slice: x: 4 (x_hi: 2, x_lo: 2; x = x_hi * 2 + x_lo), y: 4, z: 8, core: 2. Of those that a mesh axis runs over, the one named last changes fastest.
Arguments:
- acts: bfloat16 [49152, 4096], P('dp', 'block'), as said below
- grads_out: bfloat16 [49152, 4096], P('dp', 'block'), as said below
- gradient: float32 [4, 1024, 4096], P('block', 'dp'), may hold values from -96 to 96
Outputs:
- precond: bfloat16 [4, 1024, 4096], P('block', 'dp')
Inputs may be any that keep to these rules, and one draw needn't show every extreme that they name: `acts`: activations of order one with feature scales spread over a factor of about ten. `grads_out`: output gradients of order one with feature scales spread over a factor of about ten.
All inputs are finite; a program needn't handle non-finite values.
Results may differ from a plain program's by a relative error of at most 0.0022.
The roundings to bfloat16 on the way count: a program that leaves them out, or rounds other values in their place, can miss the bound.
Values may be sent and summed in bfloat16 or wider, within the bound.
No kernel may reach another device: no remote copies, remote signals or barrier semaphores. Data moves between devices by JAX's collectives and lax.ppermute only.
A program may use at most 128 MiB of HBM per device.

v0:
```python
import jax
import jax.numpy as jnp
from jax import lax
from jax.sharding import PartitionSpec as P

ITERS = 3


damping = 0.05


def local(acts, grads_out, gradient):
    dp_count = lax.axis_size("dp")
    block_count = lax.axis_size("block")
    tok_local, order = acts.shape
    all_tokens = tok_local * dp_count
    slab_rows = order // dp_count
    first_row = lax.axis_index("dp") * slab_rows
    act_term = lax.dot_general(
        acts, acts, (((0,), (0,)), ((), ())), preferred_element_type=jnp.float32
    )
    out_term = lax.dot_general(
        grads_out, grads_out, (((0,), (0,)), ((), ())), preferred_element_type=jnp.float32
    )
    share = lax.psum_scatter(
        jnp.stack((act_term, out_term), axis=1), "dp", scatter_dimension=0, tiled=True
    )
    row_ids = jnp.arange(slab_rows, dtype=jnp.int32)[:, None] + first_row
    eye_rows = (row_ids == jnp.arange(order, dtype=jnp.int32)[None, :]).astype(jnp.float32)[
        :, None, :
    ]
    damped = share / all_tokens + damping * eye_rows
    squares = lax.psum(jnp.sum(damped * damped, axis=(0, 2)), "dp")
    frob_norm = jnp.sqrt(squares)[None, :, None]
    scaled_rows = (damped / frob_norm).astype(jnp.bfloat16)
    scaled_full = lax.all_gather(scaled_rows, "dp", axis=0, tiled=True)
    eye_full = jnp.eye(order, dtype=jnp.float32)[:, None, :]
    iterate = 1.5 * eye_rows - 0.5 * scaled_rows.astype(jnp.float32)
    iterate_full = (1.5 * eye_full - 0.5 * scaled_full.astype(jnp.float32)).astype(jnp.bfloat16)
    for sweep in range(ITERS - 1):
        if sweep > 0:
            iterate_full = lax.all_gather(iterate.astype(jnp.bfloat16), "dp", axis=0, tiled=True)
        iterate_b = iterate.astype(jnp.bfloat16)
        square_b = jnp.einsum(
            "rbk,kbc->rbc", iterate_b, iterate_full, preferred_element_type=jnp.float32
        ).astype(jnp.bfloat16)
        cubic_b = jnp.einsum(
            "rbk,kbc->rbc", square_b, scaled_full, preferred_element_type=jnp.float32
        ).astype(jnp.bfloat16)
        iterate = 1.5 * iterate - 0.5 * jnp.einsum(
            "rbk,kbc->rbc", cubic_b, iterate_full, preferred_element_type=jnp.float32
        )
    root_rows = (iterate / jnp.sqrt(frob_norm)).astype(jnp.bfloat16)
    roots = lax.all_gather(root_rows, "dp", axis=0, tiled=True)
    act_root = roots[:, 0, :]
    out_root = roots[:, 1, :]
    grad_b = gradient[0].astype(jnp.bfloat16)
    out_width = grad_b.shape[1]
    all_roots = lax.all_gather(out_root[None], "block", axis=0, tiled=True)
    right_done = jnp.einsum(
        "rkc,kcd->rkd",
        grad_b.reshape(slab_rows, block_count, order),
        all_roots,
        preferred_element_type=jnp.float32,
    )
    right_done = right_done.astype(jnp.bfloat16).reshape(slab_rows, out_width)
    across = lax.all_to_all(right_done, "dp", split_axis=1, concat_axis=0, tiled=True)
    result = jnp.dot(act_root, across, preferred_element_type=jnp.float32).astype(jnp.bfloat16)
    returned = lax.all_to_all(result, "dp", split_axis=0, concat_axis=1, tiled=True)
    return returned[None]


def solution(mesh):
    in_specs = (P("dp", "block"), P("dp", "block"), P("block", "dp", None))
    out_specs = P("block", "dp", None)
    return jax.shard_map(local, mesh=mesh, in_specs=in_specs, out_specs=out_specs, check_vma=False)
```

profile of v0, /device:TPU:2, one launch (start us, length us, event | category | flops | bytes accessed | tf_op | source)
XLA Modules:
  0.0 1549.8 jit_solution(5102950518260662609)
XLA Ops:
  6.5 1.4 copy-done
  7.9 1.9 convolution_bitcast_fusion
  9.8 1.8 convolution_bitcast_fusion.1
  11.7 4.1 pad_maximum_fusion
  15.8 0.1 fusion.23
  15.9 327.5 %reduce-scatter.2.cloned.1.call-done = f32[16,2,1024]{2,0,1:T(8,128)} async-done(((f32[1024,2,1024]{2,0,1:T(8,128)}), f32[16,2,1024]{2,0,1:T(8,128)}) %reduce-scatter.2.cloned.1.call-update) | async-done | bytes 131088 | tf_op jit(solution)/shard_map/reduce_scatter | solution.py:25
  343.4 1.0 multiply_reduce_fusion
  344.4 153.4 %psum.7 = f32[2]{0:T(128)S(1)} all-reduce(f32[2]{0:T(128)S(1)} %multiply_reduce_fusion), channel_id=1, replica_groups=mesh['dp'=64,'block'=4] {'dp'}, use_global_device_ids=true, to_apply=%region_2.0 | all-reduce | flops 2 | bytes 16 | tf_op jit(solution)/shard_map/psum | solution.py:33
  497.8 1.6 divide_convert_fusion
  499.5 2.5 fusion
  502.0 303.3 %all-gather.6.cloned.1.call-done = bf16[1024,2,1024]{2,0,1:T(8,128)(2,1)} async-done(((bf16[16,2,1024]{2,0,1:T(8,128)(2,1)}), bf16[1024,2,1024]{2,0,1:T(8,128)(2,1)}) %all-gather.6.cloned.1.call-update) | async-done | bytes 4194320 | tf_op jit(solution)/shard_map/all_gather | solution.py:36
  805.3 6.3 fusion.11
  811.6 5.2 fusion.27
  816.9 301.5 %all-gather.8.cloned.1.call-done = bf16[1024,2,1024]{2,0,1:T(8,128)(2,1)} async-done(((bf16[16,2,1024]{2,0,1:T(8,128)(2,1)}), bf16[1024,2,1024]{2,0,1:T(8,128)(2,1)}) %all-gather.8.cloned.1.call-update) | async-done | bytes 4194320 | tf_op jit(solution)/shard_map/all_gather | solution.py:42
  1118.4 4.7 fusion.13
  1123.1 3.5 fusion.9
  1126.7 301.5 %all-gather.10.cloned.1.call-done = bf16[1024,2,1024]{2,0,1:T(8,128)(2,1)} async-done(((bf16[16,2,1024]{2,0,1:T(8,128)(2,1)}), bf16[1024,2,1024]{2,0,1:T(8,128)(2,1)}) %all-gather.10.cloned.1.call-update) | async-done | bytes 4194320 | tf_op jit(solution)/shard_map/all_gather | solution.py:54
  1428.2 3.1 slice.9
  1431.4 65.1 %all-gather.12.cloned.1.call-done = bf16[4096,1,1024]{2,0,1:T(8,128)(2,1)} async-done(((bf16[1024,1,1024]{2,0,1:T(8,128)(2,1)}), bf16[4096,1,1024]{2,0,1:T(8,128)(2,1)}) %all-gather.12.cloned.1.call-update) | async-done | bytes 8388624 | tf_op jit(solution)/shard_map/all_gather | solution.py:59
  1496.5 4.6 fusion.3
  1501.1 0.1 copy.16
  1501.2 0.2 all_to_all.26
  1501.4 0.2 copy.23
  1501.6 0.2 reshape.66
  1501.8 22.2 %all_to_all.35 = bf16[64,2,512]{2,1,0:T(2,128)(2,1)S(1)} all-to-all(bf16[64,2,512]{2,1,0:T(2,128)(2,1)S(1)} %reshape.66), channel_id=1, replica_groups=mesh['dp'=64,'block'=4] {'dp'}, dimensions={0} | all-to-all | bytes 262144 | tf_op jit(solution)/shard_map/all_to_all | solution.py:67
  1524.0 0.2 reshape.67
  1524.3 2.4 fusion.2
  1526.6 0.2 copy.18
  1526.8 0.2 reshape.68
  1527.0 15.0 all_to_all.36
  1542.0 0.2 reshape.69
  1542.3 0.9 broadcast_in_dim.2
  (22 shorter events, 0.4 us)
Async XLA Ops:
  6.5 1.4 copy-start
  6.5 3.3 copy-start.3
  6.5 336.9 %reduce-scatter.2.cloned.1.call-start = ((), (), s32[]{:S(2)}) async-start(), calls=%async_computation.3 | async-start | bytes 8519680 | tf_op jit(solution)/shard_map/reduce_scatter | solution.py:25
  15.8 789.6 %all-gather.6.cloned.1.call-start = ((), (), s32[]{:S(2)}) async-start(), calls=%async_computation.4 | async-start | bytes 4259840 | tf_op jit(solution)/shard_map/all_gather | solution.py:36
  499.5 305.9 %copy-start.1 = (bf16[16,2,1024]{2,0,1:T(8,128)(2,1)S(1)}, bf16[16,2,1024]{2,0,1:T(8,128)(2,1)}, u32[]{:S(2)}) copy-start(bf16[16,2,1024]{2,0,1:T(8,128)(2,1)} %divide_convert_fusion) | copy-start | bytes 196612
  499.5 618.9 %all-gather.8.cloned.1.call-start = ((), (), s32[]{:S(2)}) async-start(), calls=%async_computation.5 | async-start | bytes 4259840 | tf_op jit(solution)/shard_map/all_gather | solution.py:42
  816.8 611.3 %all-gather.10.cloned.1.call-start = ((), (), s32[]{:S(2)}) async-start(), calls=%async_computation.6 | async-start | bytes 4259840 | tf_op jit(solution)/shard_map/all_gather | solution.py:54
  1126.6 304.7 %copy-start.2 = (f32[1,16,4096]{2,1,0:T(8,128)S(1)}, f32[1,16,4096]{2,1,0:T(8,128)}, u32[]{:S(2)}) copy-start(f32[1,16,4096]{2,1,0:T(8,128)} %param.5) | copy-start | bytes 786436
  1126.6 369.9 %all-gather.12.cloned.1.call-start = ((), (), s32[]{:S(2)}) async-start(), calls=%async_computation.7 | async-start | bytes 10485760 | tf_op jit(solution)/shard_map/all_gather | solution.py:59
Sparse Core Ops, SparseCore 0:
  15.9 327.4 reduce-scatter.1
  499.6 305.6 all-gather.5
  817.0 301.4 all-gather.7
  1126.7 301.4 all-gather.9
  1431.4 65.0 all-gather.11
where the time goes:
time: 1550 us
  waiting for transfers between devices  1300 us (84%)
  blocking collectives  191 us (12%)
  matrix products  30.3 us (2%)
    reduce_scatter x1, waiting for transfers between devices, local(): lax.psum_scatter(jnp.stack((act_term, out_term), axis=1), 'dp', scatter_d...  327 us
    all_gather x1, waiting for transfers between devices, local(): scaled_full = lax.all_gather(scaled_rows, 'dp', axis=0, tiled=True)  303 us
    all_gather x1, waiting for transfers between devices, local(): lax.all_gather(iterate.astype(jnp.bfloat16), 'dp', axis=0, tiled=True)  302 us
    all_gather x1, waiting for transfers between devices, local(): roots = lax.all_gather(root_rows, 'dp', axis=0, tiled=True)  302 us
    psum x1, blocking collectives, local(): squares = lax.psum(jnp.sum(damped * damped, axis=(0, 2)), 'dp')  153 us
    all_gather x1, waiting for transfers between devices, local(): all_roots = lax.all_gather(out_root[None], 'block', axis=0, tiled=True)  65.1 us
  transfers between devices with their start and end apart: 5, of which 5 were waited for; matrix products, arithmetic and copies ran while one was open for 0% of the time, Pallas kernels for 0%

commit v1 on v0

v1 whole, which is shorter than its diff:
```python
import jax
import jax.numpy as jnp
import numpy as np
from jax import lax
from jax.sharding import Mesh, PartitionSpec as P

ITERS = 3
DAMPING = 0.05
TILE = 128

AXES = ("z", "xl", "y", "xh", "c")
SIZES = (8, 2, 4, 2, 2)
NZ, NXL, NY, NXH, NC = SIZES

ORDER = 1024
GRID = ORDER // TILE
PAIRS = [(r, c) for r in range(GRID) for c in range(r, GRID)]
PER_Y = len(PAIRS) // NY
PIECE = PER_Y * TILE


def pack_upper(term):
    blocks = [term[r * TILE:(r + 1) * TILE, c * TILE:(c + 1) * TILE] for r, c in PAIRS]
    return jnp.concatenate(blocks, axis=0).astype(jnp.bfloat16)


def unpack_upper(packed):
    where = {pair: n for n, pair in enumerate(PAIRS)}
    rows = []
    for r in range(GRID):
        row = []
        for c in range(GRID):
            n = where[(min(r, c), max(r, c))]
            block = packed[n * TILE:(n + 1) * TILE]
            row.append(block if r <= c else block.T)
        rows.append(jnp.concatenate(row, axis=1))
    return jnp.concatenate(rows, axis=0)


def gram(columns):
    return lax.dot_general(
        columns, columns, (((0,), (0,)), ((), ())), preferred_element_type=jnp.float32
    )


def local(acts, grads_out, gradient):
    all_tokens = acts.shape[0] * NZ * NXL * NY
    y = lax.axis_index("y")
    z = lax.axis_index("z")

    grad_b = gradient[0].astype(jnp.bfloat16)
    rows = grad_b.shape[0]
    by_block = grad_b.reshape(rows, NY, ORDER).transpose(1, 0, 2)
    slab = lax.all_to_all(by_block, "y", 0, 0, tiled=True).reshape(1, NY * rows, ORDER)
    half = lax.all_to_all(
        jnp.broadcast_to(slab, (NZ, NY * rows, ORDER)), "z", 0, 0, tiled=True
    )
    other = lax.ppermute(half, "xl", [(1, 0)])
    grad_block = jnp.stack((half, other), axis=1).reshape(ORDER, ORDER)

    packed = jnp.concatenate((pack_upper(gram(acts)), pack_upper(gram(grads_out))), axis=0)
    packed = packed.reshape(NXL * NY, PIECE, TILE)
    got = lax.all_to_all(packed, ("xl", "y"), 0, 0, tiled=True)
    piece = jnp.sum(got.astype(jnp.float32), axis=0)
    got = lax.all_to_all(piece.reshape(NZ, PIECE // NZ, TILE), "z", 0, 0, tiled=True)
    part = jnp.sum(got, axis=0)
    piece = lax.all_to_all(
        jnp.broadcast_to(part[None], (NZ,) + part.shape), "z", 0, 0, tiled=True
    ).reshape(PER_Y, TILE, TILE)

    on_diag = np.array([float(r == c) for r, c in PAIRS], np.float32).reshape(NY, PER_Y)
    diag = jnp.asarray(on_diag)[y][:, None, None]
    damped = piece / all_tokens + DAMPING * diag * jnp.eye(TILE, dtype=jnp.float32)[None]
    squares = jnp.sum((2.0 - diag) * damped * damped)
    squares = jnp.full((8, TILE), squares, jnp.float32)
    total = squares
    for shift in range(1, NY):
        total = total + lax.ppermute(
            squares, "y", [(n, (n + shift) % NY) for n in range(NY)]
        )
    frob_norm = jnp.sqrt(total[0, 0])
    scaled_piece = (damped / frob_norm).astype(jnp.bfloat16).reshape(1, PIECE, TILE)
    scaled = unpack_upper(
        lax.all_to_all(
            jnp.broadcast_to(scaled_piece, (NY, PIECE, TILE)), "y", 0, 0, tiled=True
        ).reshape(NY * PIECE, TILE)
    )

    iterate = 1.5 * jnp.eye(ORDER, dtype=jnp.float32) - 0.5 * scaled.astype(jnp.float32)
    for sweep in range(ITERS - 1):
        iterate_b = iterate.astype(jnp.bfloat16)
        square_b = jnp.dot(iterate_b, iterate_b, preferred_element_type=jnp.float32).astype(jnp.bfloat16)
        cubic_b = jnp.dot(square_b, scaled, preferred_element_type=jnp.float32).astype(jnp.bfloat16)
        iterate = 1.5 * iterate - 0.5 * jnp.dot(cubic_b, iterate_b, preferred_element_type=jnp.float32)
    root = (iterate / jnp.sqrt(frob_norm)).astype(jnp.bfloat16)

    columns = lax.dynamic_slice_in_dim(root, z * TILE, TILE, axis=1)
    pairs = []
    for i in range(NXH * NC):
        for k in range(NXH * NC):
            source = (NY + i) * NXH * NC + k
            target = k * NXH * NC + i
            pairs.append((source, target))
    columns = lax.ppermute(columns, ("xl", "y", "xh", "c"), pairs)
    right_done = jnp.dot(grad_block, columns, preferred_element_type=jnp.float32).astype(jnp.bfloat16)
    result = jnp.dot(root, right_done, preferred_element_type=jnp.float32).astype(jnp.bfloat16)
    result = result.reshape(NZ * NXL * NY, rows, TILE)
    returned = lax.all_to_all(result, ("z", "xl", "y"), 0, 0, tiled=True)
    returned = returned.reshape(NZ, NXL, NY, rows, TILE)[:, 0]
    return returned.transpose(2, 1, 0, 3).reshape(1, rows, NY * NZ * TILE)


def solution(mesh):
    split = Mesh(mesh.devices.reshape(SIZES), AXES)
    dp, block = ("z", "xl", "y"), ("xh", "c")
    in_specs = (P(dp, block), P(dp, block), P(block, dp, None))
    out_specs = P(block, dp, None)
    return jax.shard_map(local, mesh=split, in_specs=in_specs, out_specs=out_specs, check_vma=False)
```

time: 1550 us -> 272 us (0.18)
  waiting for transfers between devices: 1300 us -> 49.1 us
  blocking collectives: 191 us -> 72.4 us
  local copies, waits for them, and re-layouts: 7.09 us -> 67.3 us
  starting transfers between devices: 0.17 us -> 30.1 us
    all_gather x4 -> x0, waiting for transfers between devices: 971 us -> none  [the longest x1 303 us: local(): scaled_full = lax.all_gather(scaled_rows, 'dp', axis=0, tiled=True)]
    reduce_scatter x1 -> x0, waiting for transfers between devices: 327 us -> none  [local(): lax.psum_scatter(jnp.stack((act_term, out_term), axis=1), 'dp', scatter_d...]
    psum x1 -> x0, blocking collectives: 153 us -> none  [local(): squares = lax.psum(jnp.sum(damped * damped, axis=(0, 2)), 'dp')]
    unnamed x12 -> x187, local copies, waits for them, and re-layouts: 2.22 us -> 48.4 us
    all_to_all x0 -> x4, waiting for transfers between devices: none -> 43.1 us  [the longest x1 16.3 us: local(): lax.all_to_all(piece.reshape(NZ, PIECE // NZ, TILE), 'z', 0, 0, tiled=True)]
    all_to_all x2 -> x3, blocking collectives: 37.2 us -> 72.4 us  [the longest x1 34.3 us: local(): got = lax.all_to_all(packed, ('xl', 'y'), 0, 0, tiled=True)]
    all_to_all x0 -> x4, starting transfers between devices: none -> 18.9 us  [the longest x1 8.46 us: local(): lax.all_to_all(piece.reshape(NZ, PIECE // NZ, TILE), 'z', 0, 0, tiled=True)]
    dot_general x8 -> x7, matrix products: 30.3 us -> 42.4 us  [the longest x2 21.1 us: local(): jnp.dot(cubic_b, iterate_b, preferred_element_type=jnp.float32)]
  transfers between devices with their start and end apart: 5 -> 9, of which waited for: 5 -> 8; matrix products, arithmetic and copies ran while one was open for 0% -> 37% of each run, Pallas kernels for 0% -> 0%
where the time goes in v1:
time: 272 us; the launch traced here: 269 us
  blocking collectives  72.4 us (27%)
  local copies, waits for them, and re-layouts  67.3 us (25%)
  waiting for transfers between devices  49.1 us (18%)
  matrix products  42.4 us (16%)
  starting transfers between devices  30.1 us (11%)
  other arithmetic  6.54 us (2%)
    unnamed x187, local copies, waits for them, and re-layouts  48.4 us
    all_to_all x1, blocking collectives, local(): got = lax.all_to_all(packed, ('xl', 'y'), 0, 0, tiled=True)  34.3 us
    dot_general x2, matrix products, local(): jnp.dot(cubic_b, iterate_b, preferred_element_type=jnp.float32)  21.1 us
    all_to_all x1, blocking collectives, local(): returned = lax.all_to_all(result, ('z', 'xl', 'y'), 0, 0, tiled=True)  20.3 us
    all_to_all x1, blocking collectives, local(): lax.all_to_all(jnp.broadcast_to(part[None], (NZ,) + part.shape), 'z', 0,...  17.8 us
    all_to_all x1, waiting for transfers between devices, local(): lax.all_to_all(piece.reshape(NZ, PIECE // NZ, TILE), 'z', 0, 0, tiled=True)  16.3 us
    dot_general x2, matrix products, local(): jnp.dot(iterate_b, iterate_b, preferred_element_type=jnp.float32)  13.2 us
    all_to_all x1, waiting for transfers between devices, local(): lax.all_to_all(jnp.broadcast_to(slab, (NZ, NY * rows, ORDER)), 'z', 0, 0,...  12.4 us
  transfers between devices with their start and end apart: 9, of which 8 were waited for; matrix products, arithmetic and copies ran while one was open for 37% of the time, Pallas kernels for 0%

profile of v1, /device:TPU:2, one launch (start us, length us, event | category | flops | bytes accessed | tf_op | source)
XLA Modules:
  0.0 269.4 jit_solution(4183509920513405583)
XLA Ops:
  0.0 1.4 copy-done
  1.4 1.8 convolution_convert_fusion.1
  4.7 1.8 convolution_convert_fusion
  7.4 34.3 %all_to_all.35 = bf16[8,1152,128]{2,1,0:T(8,128)(2,1)S(1)} all-to-all(bf16[8,1152,128]{2,1,0:T(8,128)(2,1)S(1)} %bitcast.136), channel_id=1, replica_groups=mesh['z'=8,'xl'=2,'y'=4,'xh'=2,'c'=2] {'xl','y'}, dimensions={0} | all-to-all | bytes 4718592 | tf_op jit(solution)/shard_map/all_to_all | solution.py:63
  42.8 8.5 %all-to-all-start.1 = ((f32[8,144,128]{2,1,0:T(8,128)}), f32[8,144,128]{2,1,0:T(8,128)S(1)}, u32[]{:S(2)}, u32[]{:S(2)}) async-start(f32[8,144,128]{2,1,0:T(8,128)} %bitcast.1), calls=%async_computation.1 | async-start | bytes 1179648 | tf_op jit(solution)/shard_map/all_to_all | solution.py:65
  52.1 16.3 %all-to-all-done.1 = f32[8,144,128]{2,1,0:T(8,128)S(1)} async-done(((f32[8,144,128]{2,1,0:T(8,128)}), f32[8,144,128]{2,1,0:T(8,128)S(1)}, u32[]{:S(2)}, u32[]{:S(2)}) %all-to-all-start.1) | async-done | bytes 589856 | tf_op jit(solution)/shard_map/all_to_all | solution.py:65
  68.4 3.3 %all-to-all-start.4 = ((bf16[4,16,1024]{2,1,0:T(8,128)(2,1)}), bf16[4,16,1024]{2,1,0:T(8,128)(2,1)S(1)}, u32[]{:S(2)}, u32[]{:S(2)}) async-start(bf16[4,16,1024]{2,1,0:T(8,128)(2,1)} %copy.169), calls=%async_computation.4 | async-start | bytes 262144 | tf_op jit(solution)/shard_map/all_to_all | solution.py:54
  71.8 5.9 %all-to-all-done.4 = bf16[4,16,1024]{2,1,0:T(8,128)(2,1)S(1)} async-done(((bf16[4,16,1024]{2,1,0:T(8,128)(2,1)}), bf16[4,16,1024]{2,1,0:T(8,128)(2,1)S(1)}, u32[]{:S(2)}, u32[]{:S(2)}) %all-to-all-start.4) | async-done | bytes 131104 | tf_op jit(solution)/shard_map/all_to_all | solution.py:54
  77.7 17.8 %all_to_all.36 = f32[8,144,128]{2,1,0:T(8,128)S(1)} all-to-all(f32[8,144,128]{2,1,0:T(8,128)S(1)} %broadcast_in_dim.10), channel_id=1, replica_groups=mesh['z'=8,'xl'=2,'y'=4,'xh'=2,'c'=2] {'z'}, dimensions={0} | all-to-all | bytes 1179648 | tf_op jit(solution)/shard_map/all_to_all | solution.py:67
  96.6 3.6 %all-to-all-start.5 = ((bf16[8,64,1024]{2,1,0:T(8,128)(2,1)}), bf16[8,64,1024]{2,1,0:T(8,128)(2,1)S(1)}, u32[]{:S(2)}, u32[]{:S(2)}) async-start(bf16[8,64,1024]{2,1,0:T(8,128)(2,1)} %broadcast_in_dim.26), calls=%async_computation.5 | async-start | bytes 2097152 | tf_op jit(solution)/shard_map/all_to_all | solution.py:55
  103.6 2.1 collective-permute-start.1
  111.3 12.4 %all-to-all-done.5 = bf16[8,64,1024]{2,1,0:T(8,128)(2,1)S(1)} async-done(((bf16[8,64,1024]{2,1,0:T(8,128)(2,1)}), bf16[8,64,1024]{2,1,0:T(8,128)(2,1)S(1)}, u32[]{:S(2)}, u32[]{:S(2)}) %all-to-all-start.5) | async-done | bytes 1048608 | tf_op jit(solution)/shard_map/all_to_all | solution.py:55
  123.8 1.3 broadcast_in_dim.24
  125.1 3.5 %all-to-all-start.3 = ((bf16[4,1152,128]{2,1,0:T(8,128)(2,1)}), bf16[4,1152,128]{2,1,0:T(8,128)(2,1)S(1)}, u32[]{:S(2)}, u32[]{:S(2)}) async-start(bf16[4,1152,128]{2,1,0:T(8,128)(2,1)} %broadcast_in_dim.24), calls=%async_computation.3 | async-start | bytes 2359296 | tf_op jit(solution)/shard_map/all_to_all | solution.py:84
  128.7 4.3 %collective-permute-start.3 = (bf16[8,64,1024]{2,1,0:T(8,128)(2,1)}, bf16[8,64,1024]{2,1,0:T(8,128)(2,1)}, u32[]{:S(2)}, u32[]{:S(2)}) collective-permute-start(bf16[8,64,1024]{2,1,0:T(8,128)(2,1)} %copy-done.1), channel_id=1, source_target_pairs={{16,0},{17,1},{18,2},{19,3},{20,4},{21,5},{22,6},{23,7},{24,8},{25... | collective-permute-start | bytes 3145736 | tf_op jit(solution)/shard_map/ppermute | solution.py:58
  133.1 8.4 %all-to-all-done.3 = bf16[4,1152,128]{2,1,0:T(8,128)(2,1)S(1)} async-done(((bf16[4,1152,128]{2,1,0:T(8,128)(2,1)}), bf16[4,1152,128]{2,1,0:T(8,128)(2,1)S(1)}, u32[]{:S(2)}, u32[]{:S(2)}) %all-to-all-start.3) | async-done | bytes 1179680 | tf_op jit(solution)/shard_map/all_to_all | solution.py:84
  164.8 1.5 copy.145
  167.0 1.5 constant_dynamic-update-slice_fusion.99
  168.5 1.4 constant_dynamic-update-slice_fusion.136
  173.5 1.5 copy.152
  175.7 1.4 constant_dynamic-update-slice_fusion.97
  177.1 1.4 constant_dynamic-update-slice_fusion.131
  180.0 1.4 constant_dynamic-update-slice_fusion.129
  199.1 6.0 %fusion.8 = bf16[1024,1024]{1,0:T(8,128)(2,1)} fusion(bf16[1024,1024]{1,0:T(8,128)(2,1)} %constant_dynamic-update-slice_fusion.109), kind=kOutput, calls=%fused_computation.13 | convolution fusion | flops 2153775104 | bytes 4194304 | tf_op jit(solution)/shard_map/dot_general | solution.py:92
  205.1 10.2 %multiply_subtract_fusion = f32[1024,1024]{1,0:T(8,128)} fusion(bf16[1024,1024]{1,0:T(8,128)(2,1)} %constant_dynamic-update-slice_fusion.109, bf16[1024,1024]{1,0:T(8,128)(2,1)} %fusion.8), kind=kOutput, calls=%fused_computation.2 | convolution fusion | flops 4310695936 | bytes 8388608 | tf_op jit(solution)/shard_map/dot_general | solution.py:94
  215.3 7.2 %fusion.23 = bf16[1024,1024]{1,0:T(8,128)(2,1)} fusion(f32[1024,1024]{1,0:T(8,128)} %multiply_subtract_fusion), kind=kOutput, calls=%fused_computation.23 | convolution fusion | flops 2148532224 | bytes 6291456 | tf_op jit(solution)/shard_map/dot_general | solution.py:92
  222.5 10.9 %divide_convert_fusion = bf16[1024,1024]{1,0:T(8,128)(2,1)} fusion(f32[1024,1024]{1,0:T(8,128)} %multiply_subtract_fusion, f32[]{:T(128)S(6)} %sqrt.11, bf16[1024,1024]{1,0:T(8,128)(2,1)} %constant_dynamic-update-slice_fusion.109, bf16[1024,1024]{1,0:T(8,128)(2,1)} %fusion.23), kind=kOutput, calls=%fused_computation.1 | convolution fusion | flops 4302307328 | bytes 10485764 | tf_op jit(solution)/shard_map/dot_general | solution.py:94
  234.4 3.3 %collective-permute-start.4 = (bf16[1024,128]{1,0:T(8,128)(2,1)S(1)}, bf16[1024,128]{1,0:T(8,128)(2,1)S(1)}, u32[]{:S(2)}, u32[]{:S(2)}) collective-permute-start(bf16[1024,128]{1,0:T(8,128)(2,1)S(1)} %constant_dynamic-slice_fusion), channel_id=1, source_target_pairs={{16,0},{17,4},{18,8},{19,12},{20,1},{21,5},{22,9},{23,13},{24,2},{... | collective-permute-start | bytes 786440 | tf_op jit(solution)/shard_map/ppermute | solution.py:104
  237.8 2.8 %pad_maximum_fusion = bf16[8,2,64,1024]{3,2,1,0:T(8,128)(2,1)} fusion(bf16[8,1,64,1024]{3,2,1,0:T(8,128)(2,1)} %bitcast.42, bf16[8,1,64,1024]{3,2,1,0:T(8,128)(2,1)S(1)} %bitcast.135), kind=kLoop, calls=%fused_computation.6 | loop fusion | flops 1048576 | bytes 4194304 | tf_op jit(solution)/shard_map/stack | solution.py:59
  240.5 3.3 %collective-permute-done.4 = bf16[1024,128]{1,0:T(8,128)(2,1)S(1)} collective-permute-done((bf16[1024,128]{1,0:T(8,128)(2,1)S(1)}, bf16[1024,128]{1,0:T(8,128)(2,1)S(1)}, u32[]{:S(2)}, u32[]{:S(2)}) %collective-permute-start.4) | collective-permute-done | bytes 262176 | tf_op jit(solution)/shard_map/ppermute | solution.py:104
  243.8 4.4 %convolution_convert_fusion.2 = bf16[1024,128]{1,0:T(8,128)(2,1)S(1)} fusion(bf16[1024,1024]{1,0:T(8,128)(2,1)} %divide_convert_fusion, bf16[1024,1024]{1,0:T(8,128)(2,1)} %bitcast.138, bf16[1024,128]{1,0:T(8,128)(2,1)S(1)} %collective-permute-done.4), kind=kOutput, calls=%fused_computation.20 | convolution fusion | flops 537133056 | bytes 4718592 | tf_op jit(solution)/shard_map/dot_general | solution.py:106
  248.3 20.3 %all_to_all.37 = bf16[64,16,128]{2,1,0:T(8,128)(2,1)S(1)} all-to-all(bf16[64,16,128]{2,1,0:T(8,128)(2,1)S(1)} %bitcast.143), channel_id=1, replica_groups=mesh['z'=8,'xl'=2,'y'=4,'xh'=2,'c'=2] {'z','xl','y'}, dimensions={0} | all-to-all | bytes 524288 | tf_op jit(solution)/shard_map/all_to_all | solution.py:108
  (228 shorter events, 62.6 us)
Async XLA Ops:
  0.0 1.4 copy-start
  3.2 1.4 copy-start.21
  41.7 9.6 %copy-start.18 = (f32[1,16,4096]{2,1,0:T(8,128)S(1)}, f32[1,16,4096]{2,1,0:T(8,128)}, u32[]{:S(2)}) copy-start(f32[1,16,4096]{2,1,0:T(8,128)} %param.6) | copy-start | bytes 786436
  42.8 25.6 %all-to-all-start.1 = ((f32[8,144,128]{2,1,0:T(8,128)}), f32[8,144,128]{2,1,0:T(8,128)S(1)}, u32[]{:S(2)}, u32[]{:S(2)}) async-start(f32[8,144,128]{2,1,0:T(8,128)} %bitcast.1), calls=%async_computation.1 | async-start | bytes 1179648 | tf_op jit(solution)/shard_map/all_to_all | solution.py:65
  68.4 9.3 %all-to-all-start.4 = ((bf16[4,16,1024]{2,1,0:T(8,128)(2,1)}), bf16[4,16,1024]{2,1,0:T(8,128)(2,1)S(1)}, u32[]{:S(2)}, u32[]{:S(2)}) async-start(bf16[4,16,1024]{2,1,0:T(8,128)(2,1)} %copy.169), calls=%async_computation.4 | async-start | bytes 262144 | tf_op jit(solution)/shard_map/all_to_all | solution.py:54
  96.6 27.1 %all-to-all-start.5 = ((bf16[8,64,1024]{2,1,0:T(8,128)(2,1)}), bf16[8,64,1024]{2,1,0:T(8,128)(2,1)S(1)}, u32[]{:S(2)}, u32[]{:S(2)}) async-start(bf16[8,64,1024]{2,1,0:T(8,128)(2,1)} %broadcast_in_dim.26), calls=%async_computation.5 | async-start | bytes 2097152 | tf_op jit(solution)/shard_map/all_to_all | solution.py:55
  102.9 4.9 %collective-permute-start = (f32[8,128]{1,0:T(8,128)S(1)}, f32[8,128]{1,0:T(8,128)S(1)}, u32[]{:S(2)}, u32[]{:S(2)}) collective-permute-start(f32[8,128]{1,0:T(8,128)S(1)} %broadcast_in_dim.11), channel_id=1, source_target_pairs={{0,4},{4,8},{8,12},{12,0},{1,5},{5,9},{9,13},{13,1},{2,6},{6,10},{... | collective-permute-start | bytes 12296 | tf_op jit(solution)/shard_map/ppermute | solution.py:78
  103.6 5.1 %collective-permute-start.1 = (f32[8,128]{1,0:T(8,128)S(1)}, f32[8,128]{1,0:T(8,128)S(1)}, u32[]{:S(2)}, u32[]{:S(2)}) collective-permute-start(f32[8,128]{1,0:T(8,128)S(1)} %broadcast_in_dim.11), channel_id=1, source_target_pairs={{0,8},{4,12},{8,0},{12,4},{1,9},{5,13},{9,1},{13,5},{2,10},{6,14},... | collective-permute-start | bytes 12296 | tf_op jit(solution)/shard_map/ppermute | solution.py:78
  105.6 3.6 %collective-permute-start.2 = (f32[8,128]{1,0:T(8,128)S(1)}, f32[8,128]{1,0:T(8,128)S(1)}, u32[]{:S(2)}, u32[]{:S(2)}) collective-permute-start(f32[8,128]{1,0:T(8,128)S(1)} %broadcast_in_dim.11), channel_id=1, source_target_pairs={{0,12},{4,0},{8,4},{12,8},{1,13},{5,1},{9,5},{13,9},{2,14},{6,2},{... | collective-permute-start | bytes 12296 | tf_op jit(solution)/shard_map/ppermute | solution.py:78
  123.8 1.4 copy-start.1
  125.1 16.3 %all-to-all-start.3 = ((bf16[4,1152,128]{2,1,0:T(8,128)(2,1)}), bf16[4,1152,128]{2,1,0:T(8,128)(2,1)S(1)}, u32[]{:S(2)}, u32[]{:S(2)}) async-start(bf16[4,1152,128]{2,1,0:T(8,128)(2,1)} %broadcast_in_dim.24), calls=%async_computation.3 | async-start | bytes 2359296 | tf_op jit(solution)/shard_map/all_to_all | solution.py:84
  128.7 109.1 %collective-permute-start.3 = (bf16[8,64,1024]{2,1,0:T(8,128)(2,1)}, bf16[8,64,1024]{2,1,0:T(8,128)(2,1)}, u32[]{:S(2)}, u32[]{:S(2)}) collective-permute-start(bf16[8,64,1024]{2,1,0:T(8,128)(2,1)} %copy-done.1), channel_id=1, source_target_pairs={{16,0},{17,1},{18,2},{19,3},{20,4},{21,5},{22,6},{23,7},{24,8},{25... | collective-permute-start | bytes 3145736 | tf_op jit(solution)/shard_map/ppermute | solution.py:58
  143.2 5.2 %copy-start.5 = (bf16[128,128]{0,1:T(8,128)(2,1)}, bf16[128,128]{0,1:T(8,128)(2,1)S(1)}, u32[]{:S(2)}) copy-start(bf16[128,128]{0,1:T(8,128)(2,1)S(1)} %copy.185) | copy-start | bytes 98308
  147.7 0.7 copy-start.3
  151.2 3.3 %copy-start.13 = (bf16[128,128]{0,1:T(8,128)(2,1)}, bf16[128,128]{0,1:T(8,128)(2,1)S(1)}, u32[]{:S(2)}) copy-start(bf16[128,128]{0,1:T(8,128)(2,1)S(1)} %copy.180) | copy-start | bytes 98308
  153.0 1.6 copy-start.9
  153.8 0.7 copy-start.7
  155.6 7.5 %copy-start.17 = (bf16[128,128]{0,1:T(8,128)(2,1)}, bf16[128,128]{0,1:T(8,128)(2,1)S(1)}, u32[]{:S(2)}) copy-start(bf16[128,128]{0,1:T(8,128)(2,1)S(1)} %copy.173) | copy-start | bytes 98308
  157.4 5.7 %copy-start.16 = (bf16[128,128]{0,1:T(8,128)(2,1)}, bf16[128,128]{0,1:T(8,128)(2,1)S(1)}, u32[]{:S(2)}) copy-start(bf16[128,128]{0,1:T(8,128)(2,1)S(1)} %copy.175) | copy-start | bytes 98308
  159.1 3.9 %copy-start.14 = (bf16[128,128]{0,1:T(8,128)(2,1)}, bf16[128,128]{0,1:T(8,128)(2,1)S(1)}, u32[]{:S(2)}) copy-start(bf16[128,128]{0,1:T(8,128)(2,1)S(1)} %copy.177) | copy-start | bytes 98308
  160.0 3.1 %copy-start.11 = (bf16[128,128]{0,1:T(8,128)(2,1)}, bf16[128,128]{0,1:T(8,128)(2,1)S(1)}, u32[]{:S(2)}) copy-start(bf16[128,128]{0,1:T(8,128)(2,1)S(1)} %copy.178) | copy-start | bytes 98308
  167.0 19.1 %copy-start.15 = (bf16[128,128]{0,1:T(8,128)(2,1)S(1)}, bf16[128,128]{0,1:T(8,128)(2,1)}, u32[]{:S(2)}) copy-start(bf16[128,128]{0,1:T(8,128)(2,1)} %copy-done.14) | copy-start | bytes 98308
  167.0 21.2 %copy-start.10 = (bf16[128,128]{0,1:T(8,128)(2,1)S(1)}, bf16[128,128]{0,1:T(8,128)(2,1)}, u32[]{:S(2)}) copy-start(bf16[128,128]{0,1:T(8,128)(2,1)} %copy-done.9) | copy-start | bytes 98308
  167.0 23.3 %copy-start.6 = (bf16[128,128]{0,1:T(8,128)(2,1)S(1)}, bf16[128,128]{0,1:T(8,128)(2,1)}, u32[]{:S(2)}) copy-start(bf16[128,128]{0,1:T(8,128)(2,1)} %copy-done.5) | copy-start | bytes 98308
  167.0 26.6 %copy-start.12 = (bf16[128,128]{0,1:T(8,128)(2,1)S(1)}, bf16[128,128]{0,1:T(8,128)(2,1)}, u32[]{:S(2)}) copy-start(bf16[128,128]{0,1:T(8,128)(2,1)} %copy-done.11) | copy-start | bytes 98308
  167.0 28.7 %copy-start.8 = (bf16[128,128]{0,1:T(8,128)(2,1)S(1)}, bf16[128,128]{0,1:T(8,128)(2,1)}, u32[]{:S(2)}) copy-start(bf16[128,128]{0,1:T(8,128)(2,1)} %copy-done.7) | copy-start | bytes 98308
  167.0 29.4 %copy-start.20 = (bf16[128,128]{0,1:T(8,128)(2,1)S(1)}, bf16[128,128]{0,1:T(8,128)(2,1)}, u32[]{:S(2)}) copy-start(bf16[128,128]{0,1:T(8,128)(2,1)} %get-tuple-element.14) | copy-start | bytes 98308
  167.0 30.1 %copy-start.4 = (bf16[128,128]{0,1:T(8,128)(2,1)S(1)}, bf16[128,128]{0,1:T(8,128)(2,1)}, u32[]{:S(2)}) copy-start(bf16[128,128]{0,1:T(8,128)(2,1)} %copy-done.3) | copy-start | bytes 98308
  167.0 30.7 %copy-start.19 = (bf16[128,128]{0,1:T(8,128)(2,1)S(1)}, bf16[128,128]{0,1:T(8,128)(2,1)}, u32[]{:S(2)}) copy-start(bf16[128,128]{0,1:T(8,128)(2,1)} %get-tuple-element.5) | copy-start | bytes 98308
  222.5 15.2 %copy-start.2 = (bf16[8,64,1024]{2,1,0:T(8,128)(2,1)S(1)}, bf16[8,64,1024]{2,1,0:T(8,128)(2,1)}, u32[]{:S(2)}) copy-start(bf16[8,64,1024]{2,1,0:T(8,128)(2,1)} %copy-done.1) | copy-start | bytes 3145732
  234.4 9.4 %collective-permute-start.4 = (bf16[1024,128]{1,0:T(8,128)(2,1)S(1)}, bf16[1024,128]{1,0:T(8,128)(2,1)S(1)}, u32[]{:S(2)}, u32[]{:S(2)}) collective-permute-start(bf16[1024,128]{1,0:T(8,128)(2,1)S(1)} %constant_dynamic-slice_fusion), channel_id=1, source_target_pairs={{16,0},{17,4},{18,8},{19,12},{20,1},{21,5},{22,9},{23,13},{24,2},{... | collective-permute-start | bytes 786440 | tf_op jit(solution)/shard_map/ppermute | solution.py:104

commit v2 on v0

v2 whole, which is shorter than its diff:
```python
import functools

import jax
import jax.numpy as jnp
import numpy as np
from jax import lax
from jax.experimental import pallas as pl
from jax.experimental.pallas import tpu as pltpu
from jax.sharding import Mesh, PartitionSpec as P

F32, BF16 = jnp.float32, jnp.bfloat16
SWEEPS = 2
DAMPING = 0.05
TILE = 128
VMEM_BYTES = 48 << 20

AXES = ("zh", "zl", "xl", "y", "xh", "c")
SIZES = (4, 2, 2, 4, 2, 2)
NZH, NZL, NXL, NY, NXH, NC = SIZES
NZ, NBLOCK = NZH * NZL, NXH * NC
DP = ("zh", "zl", "xl", "y")

ORDER = 1024
GRID = ORDER // TILE
PAIRS = [(r, c) for r in range(GRID) for c in range(r, GRID)]
WHERE = {pair: n for n, pair in enumerate(PAIRS)}
PIECE = len(PAIRS) * TILE // (NZL * NY)
SHARE = PIECE // NZH
HALF = len(PAIRS) // NZL
ON_DIAG = np.repeat(np.array([float(r == c) for r, c in PAIRS], np.float32), TILE)
ROWS = 16


def call(kernel, name, out_shape, args, specs=None, scratch=(), flops=0):
    extra = {} if specs is None else {"in_specs": specs}
    return pl.pallas_call(
        kernel,
        out_shape=out_shape,
        scratch_shapes=list(scratch),
        compiler_params=pltpu.CompilerParams(vmem_limit_bytes=VMEM_BYTES),
        cost_estimate=pl.CostEstimate(flops=flops, bytes_accessed=4 << 20, transcendentals=0),
        name=name,
        **extra,
    )(*args)


SMEM = pl.BlockSpec(memory_space=pltpu.SMEM)
VMEM = pl.BlockSpec(memory_space=pltpu.VMEM)


def gram_kernel(y_ref, acts_ref, grads_ref, gradient_ref, out_ref, *turn_refs):
    y = y_ref[0]
    for shift, ref in enumerate(turn_refs):
        start = pl.multiple_of(lax.rem(y + shift, NY) * ORDER, ORDER)
        ref[...] = gradient_ref[0, :, pl.ds(start, ORDER)].astype(BF16)
    width = 2 * TILE
    for which, ref in enumerate((acts_ref, grads_ref)):
        for first in range(0, ORDER, width):
            slab = lax.dot_general(
                ref[:, first:first + width],
                ref[:, first:],
                (((0,), (0,)), ((), ())),
                preferred_element_type=F32,
            )
            for r in range(first // TILE, (first + width) // TILE):
                for c in range(r, GRID):
                    n = WHERE[(r, c)]
                    n = ((n // HALF) * NXL + which) * HALF + n % HALF
                    out_ref[n * TILE:(n + 1) * TILE, :] = slab[
                        r * TILE - first:(r + 1) * TILE - first,
                        c * TILE - first:(c + 1) * TILE - first,
                    ].astype(BF16)


def root_kernel(z_ref, packed_ref, frob_ref, root_ref, cols_ref, scaled, iterate, iterate_b, square_b, cubic_b):
    for (r, c), n in WHERE.items():
        block = packed_ref[n * TILE:(n + 1) * TILE, :]
        scaled[r * TILE:(r + 1) * TILE, c * TILE:(c + 1) * TILE] = block
        if r != c:
            scaled[c * TILE:(c + 1) * TILE, r * TILE:(r + 1) * TILE] = block.T
    width = 2 * TILE
    tiles = [slice(n, n + width) for n in range(0, ORDER, width)]
    for s in tiles:
        row = lax.broadcasted_iota(jnp.int32, (ORDER, width), 0)
        col = lax.broadcasted_iota(jnp.int32, (ORDER, width), 1) + s.start
        first = 1.5 * (row == col).astype(F32) - 0.5 * scaled[:, s].astype(F32)
        iterate[:, s] = first
        iterate_b[:, s] = first.astype(BF16)
    root_frob = jnp.sqrt(frob_ref[0:1, 0:1])
    for sweep in range(SWEEPS):
        for s in tiles:
            square_b[:, s] = jnp.dot(
                iterate_b[...], iterate_b[:, s], preferred_element_type=F32
            ).astype(BF16)
        for s in tiles:
            cubic_b[:, s] = jnp.dot(
                square_b[...], scaled[:, s], preferred_element_type=F32
            ).astype(BF16)
        for s in tiles:
            new = 1.5 * iterate[:, s] - 0.5 * jnp.dot(
                cubic_b[...], iterate_b[:, s], preferred_element_type=F32
            )
            if sweep < SWEEPS - 1:
                iterate[:, s] = new
            else:
                root_ref[:, s] = (new / root_frob).astype(BF16)
        if sweep < SWEEPS - 1:
            for s in tiles:
                iterate_b[:, s] = iterate[:, s].astype(BF16)
    cols_ref[...] = root_ref[:, pl.ds(pl.multiple_of(z_ref[0] * TILE, TILE), TILE)]


def finish_kernel(zy_ref, cols_ref, root_ref, *refs):
    slabs, out_ref, right = refs[:2 * NZ], refs[2 * NZ], refs[2 * NZ + 1]
    z, y = zy_ref[0], zy_ref[1]
    for back in range(NZ):
        first = lax.rem(z + NZ - back, NZ) * (NXL * NY * ROWS)
        for half in range(NXL):
            done = jnp.dot(
                slabs[half * NZ + back][...], cols_ref[...], preferred_element_type=F32
            ).astype(BF16)
            for turn in range(NY):
                at = first + half * (NY * ROWS) + lax.rem(y + NY - turn, NY) * ROWS
                right[pl.ds(pl.multiple_of(at, ROWS), ROWS), :] = done[turn * ROWS:(turn + 1) * ROWS]
    out_ref[...] = jnp.dot(root_ref[...], right[...], preferred_element_type=F32).astype(BF16)


def turned(x, axes, size, shift):
    return lax.ppermute(x, axes, [(n, (n + shift) % size) for n in range(size)])


def local(acts, grads_out, gradient):
    all_tokens = acts.shape[0] * NZ * NXL * NY
    y = lax.axis_index("y")
    z = lax.axis_index(("zh", "zl"))
    piece_id = lax.axis_index(("zl", "y"))
    part_id = piece_id * NZH + lax.axis_index("zh")

    packed, *turns = call(
        gram_kernel,
        "gram",
        [jax.ShapeDtypeStruct((NXL * len(PAIRS) * TILE, TILE), BF16)]
        + [jax.ShapeDtypeStruct((ROWS, ORDER), BF16)] * NY,
        (y[None], acts, grads_out, gradient),
        specs=[SMEM, VMEM, VMEM, VMEM],
        flops=4 * acts.shape[0] * ORDER * ORDER,
    )

    slab = jnp.concatenate(
        [turns[0]] + [turned(turns[shift], "y", NY, shift) for shift in range(1, NY)], axis=0
    )
    slabs = [slab] + [turned(slab, ("zh", "zl"), NZ, shift) for shift in range(1, NZ)]
    slabs = slabs + [lax.ppermute(slab, "xl", [(1, 0)]) for slab in slabs]

    got = lax.all_to_all(
        packed.reshape(NZL * NXL * NY, PIECE, TILE), ("zl", "xl", "y"), 0, 0, tiled=True
    )
    piece = jnp.sum(got.astype(F32), axis=0)
    got = lax.all_to_all(piece.reshape(NZH, SHARE, TILE), "zh", 0, 0, tiled=True)
    part = jnp.sum(got, axis=0)

    diag = jnp.asarray(ON_DIAG.reshape(-1, SHARE, 1))[part_id]
    inner = lax.rem(part_id * SHARE + lax.broadcasted_iota(jnp.int32, (SHARE, TILE), 0), TILE)
    eye = (inner == lax.broadcasted_iota(jnp.int32, (SHARE, TILE), 1)).astype(F32)
    damped = part / all_tokens + DAMPING * diag * eye
    squares = jnp.full((8, TILE), jnp.sum((2.0 - diag) * damped * damped), F32)
    piece = lax.all_to_all(
        jnp.broadcast_to(damped[None], (NZH, SHARE, TILE)), "zh", 0, 0, tiled=True
    ).reshape(PIECE, TILE)
    squares = sum([turned(squares, ("zl", "y"), NZL * NY, s) for s in range(1, NZL * NY)], squares)
    squares = sum([turned(squares, "zh", NZH, s) for s in range(1, NZH)], squares)
    frob_norm = jnp.sqrt(squares)
    scaled_piece = (piece / frob_norm[0, 0]).astype(BF16)
    packed = lax.all_to_all(
        jnp.broadcast_to(scaled_piece[None], (NZL * NY, PIECE, TILE)), ("zl", "y"), 0, 0, tiled=True
    ).reshape(len(PAIRS) * TILE, TILE)

    square = jax.ShapeDtypeStruct((ORDER, ORDER), BF16)
    root, columns = call(
        root_kernel,
        "root",
        [square, jax.ShapeDtypeStruct((ORDER, TILE), BF16)],
        (z[None], packed, frob_norm),
        specs=[SMEM, VMEM, VMEM],
        scratch=[
            pltpu.VMEM((ORDER, ORDER), BF16),
            pltpu.VMEM((ORDER, ORDER), F32),
            pltpu.VMEM((ORDER, ORDER), BF16),
            pltpu.VMEM((ORDER, ORDER), BF16),
            pltpu.VMEM((ORDER, ORDER), BF16),
        ],
        flops=6 * SWEEPS * ORDER**3,
    )

    pairs = [
        ((NY + i) * NBLOCK + k, k * NBLOCK + i) for i in range(NBLOCK) for k in range(NBLOCK)
    ]
    columns = lax.ppermute(columns, ("xl", "y", "xh", "c"), pairs)
    result = call(
        finish_kernel,
        "finish",
        jax.ShapeDtypeStruct((ORDER, TILE), BF16),
        (jnp.stack((z, y)), columns, root, *slabs),
        specs=[SMEM] + [VMEM] * (2 + 2 * NZ),
        scratch=[pltpu.VMEM((ORDER, TILE), BF16)],
        flops=4 * ORDER * ORDER * TILE,
    )
    result = result.reshape(NZ * NXL * NY, ROWS, TILE)
    returned = lax.all_to_all(result, DP, 0, 0, tiled=True)
    returned = returned.reshape(NZ, NXL, NY, ROWS, TILE)[:, 0]
    return returned.transpose(2, 1, 0, 3).reshape(1, ROWS, NY * NZ * TILE)


def solution(mesh):
    split = Mesh(mesh.devices.reshape(SIZES), AXES)
    block = ("xh", "c")
    in_specs = (P(DP, block), P(DP, block), P(block, DP, None))
    out_specs = P(block, DP, None)
    return jax.shard_map(local, mesh=split, in_specs=in_specs, out_specs=out_specs, check_vma=False)
```

time: 1550 us -> 190 us (0.12)
  waiting for transfers between devices: 1300 us -> 34 us
  blocking collectives: 191 us -> 56.4 us
  starting transfers between devices: 0.17 us -> 66.7 us
  matrix products: 30.3 us -> 0 us
  Pallas kernels: 0 us -> 17.7 us
    all_gather x4 -> x0, waiting for transfers between devices: 971 us -> none  [the longest x1 303 us: local(): scaled_full = lax.all_gather(scaled_rows, 'dp', axis=0, tiled=True)]
    reduce_scatter x1 -> x0, waiting for transfers between devices: 327 us -> none  [local(): lax.psum_scatter(jnp.stack((act_term, out_term), axis=1), 'dp', scatter_d...]
    psum x1 -> x0, blocking collectives: 153 us -> none  [local(): squares = lax.psum(jnp.sum(damped * damped, axis=(0, 2)), 'dp')]
    ppermute x0 -> x29, starting transfers between devices: none -> 50.7 us  [the longest x20 36.8 us: turned(): return lax.ppermute(x, axes, [(n, (n + shift) % size) for n in range(size)])]
    dot_general x8 -> x0, matrix products: 30.3 us -> none  [the longest x2 11 us: local(): jnp.einsum('rbk,kbc->rbc', square_b, scaled_full, preferred_element_type=...]
    ppermute x0 -> x29, waiting for transfers between devices: none -> 24 us  [the longest x8 12.3 us: local(): slabs = slabs + [lax.ppermute(slab, 'xl', [(1, 0)]) for slab in slabs]]
    all_to_all x2, blocking collectives: 37.2 us -> 56.4 us  [the longest x1 36.4 us: local(): lax.all_to_all(packed.reshape(NZL * NXL * NY, PIECE, TILE), ('zl', 'xl',...]
    pallas_call x0 -> x3, Pallas kernels: none -> 17.7 us  [call(): pl.pallas_call(kernel, out_shape=out_shape, scratch_shapes=list(scratch),...]
  transfers between devices with their start and end apart: 5 -> 32, of which waited for: 5 -> 11; matrix products, arithmetic and copies ran while one was open for 0% -> 1% of each run, Pallas kernels for 0% -> 7%
where the time goes in v2:
time: 190 us; the launch traced here: 187 us
  starting transfers between devices  66.7 us (35%)
  blocking collectives  56.4 us (30%)
  waiting for transfers between devices  34 us (18%)
  Pallas kernels  17.7 us (9%)
  local copies, waits for them, and re-layouts  7.7 us (4%)
  other arithmetic  3.93 us (2%)
    ppermute x20, starting transfers between devices, turned(): return lax.ppermute(x, axes, [(n, (n + shift) % size) for n in range(size)])  36.8 us
    all_to_all x1, blocking collectives, local(): lax.all_to_all(packed.reshape(NZL * NXL * NY, PIECE, TILE), ('zl', 'xl',...  36.4 us
    all_to_all x1, blocking collectives, local(): returned = lax.all_to_all(result, DP, 0, 0, tiled=True)  20 us
    pallas_call x3, Pallas kernels, call(): pl.pallas_call(kernel, out_shape=out_shape, scratch_shapes=list(scratch),...  17.7 us
    ppermute x8, starting transfers between devices, local(): slabs = slabs + [lax.ppermute(slab, 'xl', [(1, 0)]) for slab in slabs]  12.7 us
    ppermute x8, waiting for transfers between devices, local(): slabs = slabs + [lax.ppermute(slab, 'xl', [(1, 0)]) for slab in slabs]  12.3 us
    ppermute x20, waiting for transfers between devices, turned(): return lax.ppermute(x, axes, [(n, (n + shift) % size) for n in range(size)])  11.7 us
    all_to_all x1, waiting for transfers between devices, local(): lax.all_to_all(piece.reshape(NZH, SHARE, TILE), 'zh', 0, 0, tiled=True)  10 us
  transfers between devices with their start and end apart: 32, of which 11 were waited for; matrix products, arithmetic and copies ran while one was open for 1% of the time, Pallas kernels for 7%

profile of v2, /device:TPU:2, one launch (start us, length us, event | category | flops | bytes accessed | tf_op | source)
XLA Modules:
  0.0 186.6 jit_solution(15467713258281039943)
XLA Ops:
  0.0 1.4 copy-done
  3.8 2.3 %gram.1 = (bf16[9216,128]{1,0:T(8,128)(2,1)S(1)}, bf16[16,1024]{1,0:T(8,128)(2,1)S(1)}, bf16[16,1024]{1,0:T(8,128)(2,1)S(1)}, bf16[16,1024]{1,0:T(8,128)(2,1)S(1)}, bf16[16,1024]{1,0:T(8,128)(2,1)S(1)}) custom-call(s32[1]{0:T(128)} %bitcast.1.y_ref, bf16[768,1024]{1,0:T(8,128)(2,1)S(1)} %copy-done, bf16[768,1024]{1,0:T(8,128)(2,1)S(1)} %copy-done.1, ...), custom_call_target="tpu_custom_call" | custom-call | flops 3221225472 | bytes 4194304 | tf_op jit(solution)/shard_map/gram/pallas_call | solution.py:36
  6.0 36.4 %all_to_all.25 = bf16[16,576,128]{2,1,0:T(8,128)(2,1)S(1)} all-to-all(bf16[16,576,128]{2,1,0:T(8,128)(2,1)S(1)} %bitcast.18), channel_id=1, replica_groups=mesh['zh'=4,'zl'=2,'xl'=2,'y'=4,'xh'=2,'c'=2] {'zl','xl','y'}, dimensions={0} | all-to-all | bytes 4718592 | tf_op jit(solution)/shard_map/all_to_all | solution.py:155
  43.5 7.6 %all-to-all-start.1 = ((f32[4,144,128]{2,1,0:T(8,128)}), f32[4,144,128]{2,1,0:T(8,128)S(1)}, u32[]{:S(2)}, u32[]{:S(2)}) async-start(f32[4,144,128]{2,1,0:T(8,128)} %bitcast.3), calls=%async_computation.1 | async-start | bytes 589824 | tf_op jit(solution)/shard_map/all_to_all | solution.py:159
  51.7 10.0 %all-to-all-done.1 = f32[4,144,128]{2,1,0:T(8,128)S(1)} async-done(((f32[4,144,128]{2,1,0:T(8,128)}), f32[4,144,128]{2,1,0:T(8,128)S(1)}, u32[]{:S(2)}, u32[]{:S(2)}) %all-to-all-start.1) | async-done | bytes 294944 | tf_op jit(solution)/shard_map/all_to_all | solution.py:159
  67.7 2.6 %collective-permute-start.2 = (f32[8,128]{1,0:T(8,128)S(1)}, f32[8,128]{1,0:T(8,128)S(1)}, u32[]{:S(2)}, u32[]{:S(2)}) collective-permute-start(f32[8,128]{1,0:T(8,128)S(1)} %broadcast_in_dim.7), channel_id=1, source_target_pairs={{0,12},{4,32},{8,36},{12,40},{32,44},{36,0},{40,4},{44,8},{1,13},{... | collective-permute-start | bytes 12296 | tf_op jit(solution)/shard_map/ppermute | solution.py:129
  70.3 1.5 collective-permute-start.1
  73.0 3.5 %all-to-all-start.2 = ((f32[4,144,128]{2,1,0:T(8,128)}), f32[4,144,128]{2,1,0:T(8,128)S(1)}, u32[]{:S(2)}, u32[]{:S(2)}) async-start(f32[4,144,128]{2,1,0:T(8,128)} %broadcast_in_dim.6), calls=%async_computation.2 | async-start | bytes 589824 | tf_op jit(solution)/shard_map/all_to_all | solution.py:167
  76.5 1.6 collective-permute-done
  78.7 2.6 %collective-permute-start.9 = (f32[8,128]{1,0:T(8,128)S(1)}, f32[8,128]{1,0:T(8,128)S(1)}, u32[]{:S(2)}, u32[]{:S(2)}) collective-permute-start(f32[8,128]{1,0:T(8,128)S(1)} %add_add_fusion), channel_id=1, source_target_pairs={{0,192},{64,0},{128,64},{192,128},{1,193},{65,1},{129,65},{193,129... | collective-permute-start | bytes 12296 | tf_op jit(solution)/shard_map/ppermute | solution.py:129
  81.3 2.4 %collective-permute-start.8 = (f32[8,128]{1,0:T(8,128)S(1)}, f32[8,128]{1,0:T(8,128)S(1)}, u32[]{:S(2)}, u32[]{:S(2)}) collective-permute-start(f32[8,128]{1,0:T(8,128)S(1)} %add_add_fusion), channel_id=1, source_target_pairs={{0,128},{64,192},{128,0},{192,64},{1,129},{65,193},{129,1},{193,65... | collective-permute-start | bytes 12296 | tf_op jit(solution)/shard_map/ppermute | solution.py:129
  83.7 2.4 %collective-permute-start.7 = (f32[8,128]{1,0:T(8,128)S(1)}, f32[8,128]{1,0:T(8,128)S(1)}, u32[]{:S(2)}, u32[]{:S(2)}) collective-permute-start(f32[8,128]{1,0:T(8,128)S(1)} %add_add_fusion), channel_id=1, source_target_pairs={{0,64},{64,128},{128,192},{192,0},{1,65},{65,129},{129,193},{193,1... | collective-permute-start | bytes 12296 | tf_op jit(solution)/shard_map/ppermute | solution.py:129
  86.0 2.8 %collective-permute-done.8 = f32[8,128]{1,0:T(8,128)S(1)} collective-permute-done((f32[8,128]{1,0:T(8,128)S(1)}, f32[8,128]{1,0:T(8,128)S(1)}, u32[]{:S(2)}, u32[]{:S(2)}) %collective-permute-start.8) | collective-permute-done | bytes 4128 | tf_op jit(solution)/shard_map/ppermute | solution.py:129
  91.8 4.9 %all-to-all-start.3 = ((bf16[8,576,128]{2,1,0:T(8,128)(2,1)}), bf16[8,576,128]{2,1,0:T(8,128)(2,1)S(1)}, u32[]{:S(2)}, u32[]{:S(2)}) async-start(bf16[8,576,128]{2,1,0:T(8,128)(2,1)} %broadcast_in_dim.8), calls=%async_computation.3 | async-start | bytes 2359296 | tf_op jit(solution)/shard_map/all_to_all | solution.py:174
  96.8 2.0 %collective-permute-start.11 = (bf16[16,1024]{1,0:T(8,128)(2,1)S(1)}, bf16[16,1024]{1,0:T(8,128)(2,1)S(1)}, u32[]{:S(2)}, u32[]{:S(2)}) collective-permute-start(bf16[16,1024]{1,0:T(8,128)(2,1)S(1)} %get-tuple-element.16), channel_id=1, source_target_pairs={{0,4},{4,8},{8,12},{12,0},{1,5},{5,9},{9,13},{13,1},{2,6},{6,10},{... | collective-permute-start | bytes 98312 | tf_op jit(solution)/shard_map/ppermute | solution.py:129
  98.8 2.7 %collective-permute-start.12 = (bf16[16,1024]{1,0:T(8,128)(2,1)S(1)}, bf16[16,1024]{1,0:T(8,128)(2,1)S(1)}, u32[]{:S(2)}, u32[]{:S(2)}) collective-permute-start(bf16[16,1024]{1,0:T(8,128)(2,1)S(1)} %get-tuple-element.17), channel_id=1, source_target_pairs={{0,8},{4,12},{8,0},{12,4},{1,9},{5,13},{9,1},{13,5},{2,10},{6,14},... | collective-permute-start | bytes 98312 | tf_op jit(solution)/shard_map/ppermute | solution.py:129
  101.5 1.5 collective-permute-start.13
  102.9 5.5 %collective-permute-done.11 = bf16[16,1024]{1,0:T(8,128)(2,1)S(1)} collective-permute-done((bf16[16,1024]{1,0:T(8,128)(2,1)S(1)}, bf16[16,1024]{1,0:T(8,128)(2,1)S(1)}, u32[]{:S(2)}, u32[]{:S(2)}) %collective-permute-start.11) | collective-permute-done | bytes 32800 | tf_op jit(solution)/shard_map/ppermute | solution.py:129
  109.2 2.0 %collective-permute-start.15 = (bf16[64,1024]{1,0:T(8,128)(2,1)S(1)}, bf16[64,1024]{1,0:T(8,128)(2,1)S(1)}, u32[]{:S(2)}, u32[]{:S(2)}) collective-permute-start(bf16[64,1024]{1,0:T(8,128)(2,1)S(1)} %constant_dynamic-update-slice_fusion.refs_0_), channel_id=1, source_target_pairs={{0,64},{32,96},{64,128},{96,160},{128,192},{160,224},{192,0},{224,... | collective-permute-start | bytes 393224 | tf_op jit(solution)/shard_map/ppermute | solution.py:129
  111.2 2.7 %collective-permute-start.16 = (bf16[64,1024]{1,0:T(8,128)(2,1)S(1)}, bf16[64,1024]{1,0:T(8,128)(2,1)S(1)}, u32[]{:S(2)}, u32[]{:S(2)}) collective-permute-start(bf16[64,1024]{1,0:T(8,128)(2,1)S(1)} %constant_dynamic-update-slice_fusion.refs_0_), channel_id=1, source_target_pairs={{0,96},{32,128},{64,160},{96,192},{128,224},{160,0},{192,32},{224,... | collective-permute-start | bytes 393224 | tf_op jit(solution)/shard_map/ppermute | solution.py:129
  113.9 2.9 %collective-permute-start.17 = (bf16[64,1024]{1,0:T(8,128)(2,1)S(1)}, bf16[64,1024]{1,0:T(8,128)(2,1)S(1)}, u32[]{:S(2)}, u32[]{:S(2)}) collective-permute-start(bf16[64,1024]{1,0:T(8,128)(2,1)S(1)} %constant_dynamic-update-slice_fusion.refs_0_), channel_id=1, source_target_pairs={{0,128},{32,160},{64,192},{96,224},{128,0},{160,32},{192,64},{224,... | collective-permute-start | bytes 393224 | tf_op jit(solution)/shard_map/ppermute | solution.py:129
  116.8 1.8 collective-permute-start.18
  118.6 4.1 %collective-permute-start.19 = (bf16[64,1024]{1,0:T(8,128)(2,1)S(1)}, bf16[64,1024]{1,0:T(8,128)(2,1)S(1)}, u32[]{:S(2)}, u32[]{:S(2)}) collective-permute-start(bf16[64,1024]{1,0:T(8,128)(2,1)S(1)} %constant_dynamic-update-slice_fusion.refs_0_), channel_id=1, source_target_pairs={{0,192},{32,224},{64,0},{96,32},{128,64},{160,96},{192,128},{224,1... | collective-permute-start | bytes 393224 | tf_op jit(solution)/shard_map/ppermute | solution.py:129
  123.9 13.5 %root.1 = (bf16[1024,1024]{1,0:T(8,128)(2,1)S(1)}, bf16[1024,128]{1,0:T(8,128)(2,1)S(1)}) custom-call(s32[1]{0:T(128)} %bitcast.z_ref, bf16[4608,128]{1,0:T(8,128)(2,1)S(1)} %bitcast.19, f32[8,128]{1,0:T(8,128)S(1)} %add_sqrt_fusion.frob_ref), custom_call_target="tpu_custom_call" | custom-call | flops 12884901888 | bytes 4194304 | tf_op jit(solution)/shard_map/root/pallas_call | solution.py:36
  137.4 3.0 %collective-permute-start.21 = (bf16[64,1024]{1,0:T(8,128)(2,1)S(1)}, bf16[64,1024]{1,0:T(8,128)(2,1)S(1)}, u32[]{:S(2)}, u32[]{:S(2)}) collective-permute-start(bf16[64,1024]{1,0:T(8,128)(2,1)S(1)} %constant_dynamic-update-slice_fusion.refs_0_), channel_id=1, source_target_pairs={{16,0},{17,1},{18,2},{19,3},{20,4},{21,5},{22,6},{23,7},{24,8},{25... | collective-permute-start | bytes 393224 | tf_op jit(solution)/shard_map/ppermute | solution.py:153
  145.8 1.6 collective-permute-start.25
  151.6 3.8 %collective-permute-done.25.refs_12_ = bf16[64,1024]{1,0:T(8,128)(2,1)S(1)} collective-permute-done((bf16[64,1024]{1,0:T(8,128)(2,1)S(1)}, bf16[64,1024]{1,0:T(8,128)(2,1)S(1)}, u32[]{:S(2)}, u32[]{:S(2)}) %collective-permute-start.25) | collective-permute-done | bytes 131104 | tf_op jit(solution)/shard_map/ppermute | solution.py:153
  155.4 2.8 %collective-permute-done.26.refs_13_ = bf16[64,1024]{1,0:T(8,128)(2,1)S(1)} collective-permute-done((bf16[64,1024]{1,0:T(8,128)(2,1)S(1)}, bf16[64,1024]{1,0:T(8,128)(2,1)S(1)}, u32[]{:S(2)}, u32[]{:S(2)}) %collective-permute-start.26) | collective-permute-done | bytes 131104 | tf_op jit(solution)/shard_map/ppermute | solution.py:153
  158.3 2.8 %collective-permute-done.27.refs_14_ = bf16[64,1024]{1,0:T(8,128)(2,1)S(1)} collective-permute-done((bf16[64,1024]{1,0:T(8,128)(2,1)S(1)}, bf16[64,1024]{1,0:T(8,128)(2,1)S(1)}, u32[]{:S(2)}, u32[]{:S(2)}) %collective-permute-start.27) | collective-permute-done | bytes 131104 | tf_op jit(solution)/shard_map/ppermute | solution.py:153
  161.1 2.8 %collective-permute-done.28.refs_15_ = bf16[64,1024]{1,0:T(8,128)(2,1)S(1)} collective-permute-done((bf16[64,1024]{1,0:T(8,128)(2,1)S(1)}, bf16[64,1024]{1,0:T(8,128)(2,1)S(1)}, u32[]{:S(2)}, u32[]{:S(2)}) %collective-permute-start.28) | collective-permute-done | bytes 131104 | tf_op jit(solution)/shard_map/ppermute | solution.py:153
  163.9 2.0 %finish.1 = bf16[1024,128]{1,0:T(8,128)(2,1)S(1)} custom-call(s32[2]{0:T(128)S(1)} %pad_add_fusion.zy_ref, bf16[1024,128]{1,0:T(8,128)(2,1)S(1)} %collective-permute-done.10.cols_ref, bf16[1024,1024]{1,0:T(8,128)(2,1)S(1)} %get-tuple-element.14.root_ref, bf16[64,1024]{1,0:T(8,128)(2,1)S(1)} %constant_dynamic-update-slice_fusion.refs_0_, ...), custom_call_target="tpu_custom_call" | custom-call | flops 536870912 | bytes 4194304 | tf_op jit(solution)/shard_map/finish/pallas_call | solution.py:36
  165.8 20.0 %all_to_all.26 = bf16[64,16,128]{2,1,0:T(8,128)(2,1)S(1)} all-to-all(bf16[64,16,128]{2,1,0:T(8,128)(2,1)S(1)} %bitcast.20), channel_id=1, replica_groups=mesh['zh'=4,'zl'=2,'xl'=2,'y'=4,'xh'=2,'c'=2] {'zh','zl','xl','y'}, dimensions={0} | all-to-all | bytes 524288 | tf_op jit(solution)/shard_map/all_to_all | solution.py:209
  (64 shorter events, 27.1 us)
Async XLA Ops:
  43.5 18.3 %all-to-all-start.1 = ((f32[4,144,128]{2,1,0:T(8,128)}), f32[4,144,128]{2,1,0:T(8,128)S(1)}, u32[]{:S(2)}, u32[]{:S(2)}) async-start(f32[4,144,128]{2,1,0:T(8,128)} %bitcast.3), calls=%async_computation.1 | async-start | bytes 589824 | tf_op jit(solution)/shard_map/all_to_all | solution.py:159
  63.2 7.1 %collective-permute-start.6 = (f32[8,128]{1,0:T(8,128)S(1)}, f32[8,128]{1,0:T(8,128)S(1)}, u32[]{:S(2)}, u32[]{:S(2)}) collective-permute-start(f32[8,128]{1,0:T(8,128)S(1)} %broadcast_in_dim.7), channel_id=1, source_target_pairs={{0,44},{4,0},{8,4},{12,8},{32,12},{36,32},{40,36},{44,40},{1,45},{... | collective-permute-start | bytes 12296 | tf_op jit(solution)/shard_map/ppermute | solution.py:129
  64.4 7.4 %collective-permute-start.5 = (f32[8,128]{1,0:T(8,128)S(1)}, f32[8,128]{1,0:T(8,128)S(1)}, u32[]{:S(2)}, u32[]{:S(2)}) collective-permute-start(f32[8,128]{1,0:T(8,128)S(1)} %broadcast_in_dim.7), channel_id=1, source_target_pairs={{0,40},{4,44},{8,0},{12,4},{32,8},{36,12},{40,32},{44,36},{1,41},{... | collective-permute-start | bytes 12296 | tf_op jit(solution)/shard_map/ppermute | solution.py:129
  65.8 10.7 %collective-permute-start.4 = (f32[8,128]{1,0:T(8,128)S(1)}, f32[8,128]{1,0:T(8,128)S(1)}, u32[]{:S(2)}, u32[]{:S(2)}) collective-permute-start(f32[8,128]{1,0:T(8,128)S(1)} %broadcast_in_dim.7), channel_id=1, source_target_pairs={{0,36},{4,40},{8,44},{12,0},{32,4},{36,8},{40,12},{44,32},{1,37},{... | collective-permute-start | bytes 12296 | tf_op jit(solution)/shard_map/ppermute | solution.py:129
  66.5 10.0 %collective-permute-start.3 = (f32[8,128]{1,0:T(8,128)S(1)}, f32[8,128]{1,0:T(8,128)S(1)}, u32[]{:S(2)}, u32[]{:S(2)}) collective-permute-start(f32[8,128]{1,0:T(8,128)S(1)} %broadcast_in_dim.7), channel_id=1, source_target_pairs={{0,32},{4,36},{8,40},{12,44},{32,0},{36,4},{40,8},{44,12},{1,33},{... | collective-permute-start | bytes 12296 | tf_op jit(solution)/shard_map/ppermute | solution.py:129
  67.7 8.8 %collective-permute-start.2 = (f32[8,128]{1,0:T(8,128)S(1)}, f32[8,128]{1,0:T(8,128)S(1)}, u32[]{:S(2)}, u32[]{:S(2)}) collective-permute-start(f32[8,128]{1,0:T(8,128)S(1)} %broadcast_in_dim.7), channel_id=1, source_target_pairs={{0,12},{4,32},{8,36},{12,40},{32,44},{36,0},{40,4},{44,8},{1,13},{... | collective-permute-start | bytes 12296 | tf_op jit(solution)/shard_map/ppermute | solution.py:129
  70.3 6.2 %collective-permute-start.1 = (f32[8,128]{1,0:T(8,128)S(1)}, f32[8,128]{1,0:T(8,128)S(1)}, u32[]{:S(2)}, u32[]{:S(2)}) collective-permute-start(f32[8,128]{1,0:T(8,128)S(1)} %broadcast_in_dim.7), channel_id=1, source_target_pairs={{0,8},{4,12},{8,32},{12,36},{32,40},{36,44},{40,0},{44,4},{1,9},{5... | collective-permute-start | bytes 12296 | tf_op jit(solution)/shard_map/ppermute | solution.py:129
  71.8 6.3 %collective-permute-start = (f32[8,128]{1,0:T(8,128)S(1)}, f32[8,128]{1,0:T(8,128)S(1)}, u32[]{:S(2)}, u32[]{:S(2)}) collective-permute-start(f32[8,128]{1,0:T(8,128)S(1)} %broadcast_in_dim.7), channel_id=1, source_target_pairs={{0,4},{4,8},{8,12},{12,32},{32,36},{36,40},{40,44},{44,0},{1,5},{5... | collective-permute-start | bytes 12296 | tf_op jit(solution)/shard_map/ppermute | solution.py:129
  73.0 17.0 %all-to-all-start.2 = ((f32[4,144,128]{2,1,0:T(8,128)}), f32[4,144,128]{2,1,0:T(8,128)S(1)}, u32[]{:S(2)}, u32[]{:S(2)}) async-start(f32[4,144,128]{2,1,0:T(8,128)} %broadcast_in_dim.6), calls=%async_computation.2 | async-start | bytes 589824 | tf_op jit(solution)/shard_map/all_to_all | solution.py:167
  78.7 7.3 %collective-permute-start.9 = (f32[8,128]{1,0:T(8,128)S(1)}, f32[8,128]{1,0:T(8,128)S(1)}, u32[]{:S(2)}, u32[]{:S(2)}) collective-permute-start(f32[8,128]{1,0:T(8,128)S(1)} %add_add_fusion), channel_id=1, source_target_pairs={{0,192},{64,0},{128,64},{192,128},{1,193},{65,1},{129,65},{193,129... | collective-permute-start | bytes 12296 | tf_op jit(solution)/shard_map/ppermute | solution.py:129
  81.3 7.5 %collective-permute-start.8 = (f32[8,128]{1,0:T(8,128)S(1)}, f32[8,128]{1,0:T(8,128)S(1)}, u32[]{:S(2)}, u32[]{:S(2)}) collective-permute-start(f32[8,128]{1,0:T(8,128)S(1)} %add_add_fusion), channel_id=1, source_target_pairs={{0,128},{64,192},{128,0},{192,64},{1,129},{65,193},{129,1},{193,65... | collective-permute-start | bytes 12296 | tf_op jit(solution)/shard_map/ppermute | solution.py:129
  83.7 5.7 %collective-permute-start.7 = (f32[8,128]{1,0:T(8,128)S(1)}, f32[8,128]{1,0:T(8,128)S(1)}, u32[]{:S(2)}, u32[]{:S(2)}) collective-permute-start(f32[8,128]{1,0:T(8,128)S(1)} %add_add_fusion), channel_id=1, source_target_pairs={{0,64},{64,128},{128,192},{192,0},{1,65},{65,129},{129,193},{193,1... | collective-permute-start | bytes 12296 | tf_op jit(solution)/shard_map/ppermute | solution.py:129
  91.8 32.1 %all-to-all-start.3 = ((bf16[8,576,128]{2,1,0:T(8,128)(2,1)}), bf16[8,576,128]{2,1,0:T(8,128)(2,1)S(1)}, u32[]{:S(2)}, u32[]{:S(2)}) async-start(bf16[8,576,128]{2,1,0:T(8,128)(2,1)} %broadcast_in_dim.8), calls=%async_computation.3 | async-start | bytes 2359296 | tf_op jit(solution)/shard_map/all_to_all | solution.py:174
  96.8 11.7 %collective-permute-start.11 = (bf16[16,1024]{1,0:T(8,128)(2,1)S(1)}, bf16[16,1024]{1,0:T(8,128)(2,1)S(1)}, u32[]{:S(2)}, u32[]{:S(2)}) collective-permute-start(bf16[16,1024]{1,0:T(8,128)(2,1)S(1)} %get-tuple-element.16), channel_id=1, source_target_pairs={{0,4},{4,8},{8,12},{12,0},{1,5},{5,9},{9,13},{13,1},{2,6},{6,10},{... | collective-permute-start | bytes 98312 | tf_op jit(solution)/shard_map/ppermute | solution.py:129
  98.8 10.3 %collective-permute-start.12 = (bf16[16,1024]{1,0:T(8,128)(2,1)S(1)}, bf16[16,1024]{1,0:T(8,128)(2,1)S(1)}, u32[]{:S(2)}, u32[]{:S(2)}) collective-permute-start(bf16[16,1024]{1,0:T(8,128)(2,1)S(1)} %get-tuple-element.17), channel_id=1, source_target_pairs={{0,8},{4,12},{8,0},{12,4},{1,9},{5,13},{9,1},{13,5},{2,10},{6,14},... | collective-permute-start | bytes 98312 | tf_op jit(solution)/shard_map/ppermute | solution.py:129
  101.5 7.7 %collective-permute-start.13 = (bf16[16,1024]{1,0:T(8,128)(2,1)S(1)}, bf16[16,1024]{1,0:T(8,128)(2,1)S(1)}, u32[]{:S(2)}, u32[]{:S(2)}) collective-permute-start(bf16[16,1024]{1,0:T(8,128)(2,1)S(1)} %get-tuple-element.18), channel_id=1, source_target_pairs={{0,12},{4,0},{8,4},{12,8},{1,13},{5,1},{9,5},{13,9},{2,14},{6,2},{... | collective-permute-start | bytes 98312 | tf_op jit(solution)/shard_map/ppermute | solution.py:129
  109.1 9.5 %collective-permute-start.14 = (bf16[64,1024]{1,0:T(8,128)(2,1)S(1)}, bf16[64,1024]{1,0:T(8,128)(2,1)S(1)}, u32[]{:S(2)}, u32[]{:S(2)}) collective-permute-start(bf16[64,1024]{1,0:T(8,128)(2,1)S(1)} %constant_dynamic-update-slice_fusion.refs_0_), channel_id=1, source_target_pairs={{0,32},{32,64},{64,96},{96,128},{128,160},{160,192},{192,224},{224... | collective-permute-start | bytes 393224 | tf_op jit(solution)/shard_map/ppermute | solution.py:129
  109.2 14.1 %collective-permute-start.15 = (bf16[64,1024]{1,0:T(8,128)(2,1)S(1)}, bf16[64,1024]{1,0:T(8,128)(2,1)S(1)}, u32[]{:S(2)}, u32[]{:S(2)}) collective-permute-start(bf16[64,1024]{1,0:T(8,128)(2,1)S(1)} %constant_dynamic-update-slice_fusion.refs_0_), channel_id=1, source_target_pairs={{0,64},{32,96},{64,128},{96,160},{128,192},{160,224},{192,0},{224,... | collective-permute-start | bytes 393224 | tf_op jit(solution)/shard_map/ppermute | solution.py:129
  111.2 26.2 %collective-permute-start.16 = (bf16[64,1024]{1,0:T(8,128)(2,1)S(1)}, bf16[64,1024]{1,0:T(8,128)(2,1)S(1)}, u32[]{:S(2)}, u32[]{:S(2)}) collective-permute-start(bf16[64,1024]{1,0:T(8,128)(2,1)S(1)} %constant_dynamic-update-slice_fusion.refs_0_), channel_id=1, source_target_pairs={{0,96},{32,128},{64,160},{96,192},{128,224},{160,0},{192,32},{224,... | collective-permute-start | bytes 393224 | tf_op jit(solution)/shard_map/ppermute | solution.py:129
  113.9 26.6 %collective-permute-start.17 = (bf16[64,1024]{1,0:T(8,128)(2,1)S(1)}, bf16[64,1024]{1,0:T(8,128)(2,1)S(1)}, u32[]{:S(2)}, u32[]{:S(2)}) collective-permute-start(bf16[64,1024]{1,0:T(8,128)(2,1)S(1)} %constant_dynamic-update-slice_fusion.refs_0_), channel_id=1, source_target_pairs={{0,128},{32,160},{64,192},{96,224},{128,0},{160,32},{192,64},{224,... | collective-permute-start | bytes 393224 | tf_op jit(solution)/shard_map/ppermute | solution.py:129
  116.8 25.0 %collective-permute-start.18 = (bf16[64,1024]{1,0:T(8,128)(2,1)S(1)}, bf16[64,1024]{1,0:T(8,128)(2,1)S(1)}, u32[]{:S(2)}, u32[]{:S(2)}) collective-permute-start(bf16[64,1024]{1,0:T(8,128)(2,1)S(1)} %constant_dynamic-update-slice_fusion.refs_0_), channel_id=1, source_target_pairs={{0,160},{32,192},{64,224},{96,0},{128,32},{160,64},{192,96},{224,1... | collective-permute-start | bytes 393224 | tf_op jit(solution)/shard_map/ppermute | solution.py:129
  118.6 24.5 %collective-permute-start.19 = (bf16[64,1024]{1,0:T(8,128)(2,1)S(1)}, bf16[64,1024]{1,0:T(8,128)(2,1)S(1)}, u32[]{:S(2)}, u32[]{:S(2)}) collective-permute-start(bf16[64,1024]{1,0:T(8,128)(2,1)S(1)} %constant_dynamic-update-slice_fusion.refs_0_), channel_id=1, source_target_pairs={{0,192},{32,224},{64,0},{96,32},{128,64},{160,96},{192,128},{224,1... | collective-permute-start | bytes 393224 | tf_op jit(solution)/shard_map/ppermute | solution.py:129
  123.3 21.1 %collective-permute-start.20 = (bf16[64,1024]{1,0:T(8,128)(2,1)S(1)}, bf16[64,1024]{1,0:T(8,128)(2,1)S(1)}, u32[]{:S(2)}, u32[]{:S(2)}) collective-permute-start(bf16[64,1024]{1,0:T(8,128)(2,1)S(1)} %constant_dynamic-update-slice_fusion.refs_0_), channel_id=1, source_target_pairs={{0,224},{32,0},{64,32},{96,64},{128,96},{160,128},{192,160},{224,1... | collective-permute-start | bytes 393224 | tf_op jit(solution)/shard_map/ppermute | solution.py:129
  137.4 8.3 %collective-permute-start.21 = (bf16[64,1024]{1,0:T(8,128)(2,1)S(1)}, bf16[64,1024]{1,0:T(8,128)(2,1)S(1)}, u32[]{:S(2)}, u32[]{:S(2)}) collective-permute-start(bf16[64,1024]{1,0:T(8,128)(2,1)S(1)} %constant_dynamic-update-slice_fusion.refs_0_), channel_id=1, source_target_pairs={{16,0},{17,1},{18,2},{19,3},{20,4},{21,5},{22,6},{23,7},{24,8},{25... | collective-permute-start | bytes 393224 | tf_op jit(solution)/shard_map/ppermute | solution.py:153
  140.5 6.8 %collective-permute-start.22 = (bf16[64,1024]{1,0:T(8,128)(2,1)S(1)}, bf16[64,1024]{1,0:T(8,128)(2,1)S(1)}, u32[]{:S(2)}, u32[]{:S(2)}) collective-permute-start(bf16[64,1024]{1,0:T(8,128)(2,1)S(1)} %collective-permute-done.14.refs_1_), channel_id=1, source_target_pairs={{16,0},{17,1},{18,2},{19,3},{20,4},{21,5},{22,6},{23,7},{24,8},{25... | collective-permute-start | bytes 393224 | tf_op jit(solution)/shard_map/ppermute | solution.py:153
  141.8 6.9 %collective-permute-start.23 = (bf16[64,1024]{1,0:T(8,128)(2,1)S(1)}, bf16[64,1024]{1,0:T(8,128)(2,1)S(1)}, u32[]{:S(2)}, u32[]{:S(2)}) collective-permute-start(bf16[64,1024]{1,0:T(8,128)(2,1)S(1)} %collective-permute-done.15.refs_2_), channel_id=1, source_target_pairs={{16,0},{17,1},{18,2},{19,3},{20,4},{21,5},{22,6},{23,7},{24,8},{25... | collective-permute-start | bytes 393224 | tf_op jit(solution)/shard_map/ppermute | solution.py:153
  143.1 7.0 %collective-permute-start.24 = (bf16[64,1024]{1,0:T(8,128)(2,1)S(1)}, bf16[64,1024]{1,0:T(8,128)(2,1)S(1)}, u32[]{:S(2)}, u32[]{:S(2)}) collective-permute-start(bf16[64,1024]{1,0:T(8,128)(2,1)S(1)} %collective-permute-done.16.refs_3_), channel_id=1, source_target_pairs={{16,0},{17,1},{18,2},{19,3},{20,4},{21,5},{22,6},{23,7},{24,8},{25... | collective-permute-start | bytes 393224 | tf_op jit(solution)/shard_map/ppermute | solution.py:153
  144.4 19.4 %collective-permute-start.10 = (bf16[1024,128]{1,0:T(8,128)(2,1)S(1)}, bf16[1024,128]{1,0:T(8,128)(2,1)S(1)}, u32[]{:S(2)}, u32[]{:S(2)}) collective-permute-start(bf16[1024,128]{1,0:T(8,128)(2,1)S(1)} %get-tuple-element.13), channel_id=1, source_target_pairs={{16,0},{17,4},{18,8},{19,12},{20,1},{21,5},{22,9},{23,13},{24,2},{... | collective-permute-start | bytes 786440 | tf_op jit(solution)/shard_map/ppermute | solution.py:198
  145.8 9.7 %collective-permute-start.25 = (bf16[64,1024]{1,0:T(8,128)(2,1)S(1)}, bf16[64,1024]{1,0:T(8,128)(2,1)S(1)}, u32[]{:S(2)}, u32[]{:S(2)}) collective-permute-start(bf16[64,1024]{1,0:T(8,128)(2,1)S(1)} %collective-permute-done.17.refs_4_), channel_id=1, source_target_pairs={{16,0},{17,1},{18,2},{19,3},{20,4},{21,5},{22,6},{23,7},{24,8},{25... | collective-permute-start | bytes 393224 | tf_op jit(solution)/shard_map/ppermute | solution.py:153
  147.3 10.9 %collective-permute-start.26 = (bf16[64,1024]{1,0:T(8,128)(2,1)S(1)}, bf16[64,1024]{1,0:T(8,128)(2,1)S(1)}, u32[]{:S(2)}, u32[]{:S(2)}) collective-permute-start(bf16[64,1024]{1,0:T(8,128)(2,1)S(1)} %collective-permute-done.18.refs_5_), channel_id=1, source_target_pairs={{16,0},{17,1},{18,2},{19,3},{20,4},{21,5},{22,6},{23,7},{24,8},{25... | collective-permute-start | bytes 393224 | tf_op jit(solution)/shard_map/ppermute | solution.py:153
  148.7 12.3 %collective-permute-start.27 = (bf16[64,1024]{1,0:T(8,128)(2,1)S(1)}, bf16[64,1024]{1,0:T(8,128)(2,1)S(1)}, u32[]{:S(2)}, u32[]{:S(2)}) collective-permute-start(bf16[64,1024]{1,0:T(8,128)(2,1)S(1)} %collective-permute-done.19.refs_6_), channel_id=1, source_target_pairs={{16,0},{17,1},{18,2},{19,3},{20,4},{21,5},{22,6},{23,7},{24,8},{25... | collective-permute-start | bytes 393224 | tf_op jit(solution)/shard_map/ppermute | solution.py:153
  150.1 13.7 %collective-permute-start.28 = (bf16[64,1024]{1,0:T(8,128)(2,1)S(1)}, bf16[64,1024]{1,0:T(8,128)(2,1)S(1)}, u32[]{:S(2)}, u32[]{:S(2)}) collective-permute-start(bf16[64,1024]{1,0:T(8,128)(2,1)S(1)} %collective-permute-done.20.refs_7_), channel_id=1, source_target_pairs={{16,0},{17,1},{18,2},{19,3},{20,4},{21,5},{22,6},{23,7},{24,8},{25... | collective-permute-start | bytes 393224 | tf_op jit(solution)/shard_map/ppermute | solution.py:153
  (3 other events, 3.8 us)

commit v3 on v2

v3 whole, which is shorter than its diff:
```python
import functools

import jax
import jax.numpy as jnp
from jax import lax
from jax.experimental import pallas as pl
from jax.experimental.pallas import tpu as pltpu
from jax.sharding import Mesh, PartitionSpec as P

F32, BF16 = jnp.float32, jnp.bfloat16
SWEEPS = 2
DAMPING = 0.05
TILE = 128
VMEM_BYTES = 48 << 20

AXES = ("zh", "zl", "xl", "y", "xh", "c")
SIZES = (4, 2, 2, 4, 2, 2)
NZH, NZL, NXL, NY, NXH, NC = SIZES
NZ, NBLOCK = NZH * NZL, NXH * NC
DP = ("zh", "zl", "xl", "y")

ORDER = 1024
GRID = ORDER // TILE
PAIRS = [(r, c) for r in range(GRID) for c in range(r, GRID)]
WHERE = {pair: n for n, pair in enumerate(PAIRS)}

HALF = TILE // 2
HALVES = 2 * len(PAIRS) // (NZL * NY)
PIECE = HALVES * HALF
REST = 16
ROWS = 16
LOADS = 4


def call(kernel, name, out_shape, args, specs=None, scratch=(), flops=0, vmem=VMEM_BYTES):
    extra = {} if specs is None else {"in_specs": specs}
    return pl.pallas_call(
        kernel,
        out_shape=out_shape,
        scratch_shapes=list(scratch),
        compiler_params=pltpu.CompilerParams(vmem_limit_bytes=vmem),
        cost_estimate=pl.CostEstimate(flops=flops, bytes_accessed=4 << 20, transcendentals=0),
        name=name,
        **extra,
    )(*args)


SMEM = pl.BlockSpec(memory_space=pltpu.SMEM)
VMEM = pl.BlockSpec(memory_space=pltpu.VMEM)


def gram_kernel(y_ref, acts_ref, grads_ref, gradient_ref, out_ref, *refs):
    turn_refs, (acts, grads, gradient, sems, gradient_sem) = refs[:NY], refs[NY:]
    rows = acts.shape[0] // LOADS
    loads = []
    for which, (far, near) in enumerate(((acts_ref, acts), (grads_ref, grads))):
        for n in range(LOADS):
            part = pl.ds(n * rows, rows)
            loads.append(pltpu.make_async_copy(far.at[part], near.at[part], sems.at[which, n]))
            loads[-1].start()
    gradient_load = pltpu.make_async_copy(gradient_ref, gradient, gradient_sem)
    gradient_load.start()
    width = 2 * TILE
    eye = lax.broadcasted_iota(jnp.int32, (TILE, TILE), 0) == lax.broadcasted_iota(
        jnp.int32, (TILE, TILE), 1
    )
    for which, ref in enumerate((acts, grads)):
        for load in loads[which * LOADS:(which + 1) * LOADS]:
            load.wait()
        rest = {}
        for first in range(0, ORDER, width):
            slab = lax.dot_general(
                ref[:, first:first + width],
                ref[:, first:],
                (((0,), (0,)), ((), ())),
                preferred_element_type=F32,
            )
            for r in range(first // TILE, (first + width) // TILE):
                for c in range(r, GRID):
                    block = slab[
                        r * TILE - first:(r + 1) * TILE - first,
                        c * TILE - first:(c + 1) * TILE - first,
                    ]
                    block_b = block.astype(BF16)
                    for half in range(2):
                        piece, at = divmod(2 * WHERE[(r, c)] + half, HALVES)
                        out_ref[target_of(which, piece), at * HALF:(at + 1) * HALF] = block_b[
                            half * HALF:(half + 1) * HALF
                        ]
                        if r == c:
                            rest[(piece, at)] = jnp.sum(
                                jnp.where(eye, block - block_b.astype(F32), 0.0), axis=0, keepdims=True
                            )
        for piece in range(NZL * NY):
            lines = [rest.get((piece, at), jnp.zeros((1, TILE), F32)) for at in range(HALVES)]
            put_rest(out_ref.at[target_of(which, piece)], lines)
    gradient_load.wait()
    for shift, ref in enumerate(turn_refs):
        start = pl.multiple_of(lax.rem(y_ref[0] + shift, NY) * ORDER, ORDER)
        ref[...] = gradient[0, :, pl.ds(start, ORDER)].astype(BF16)


def target_of(which, piece):
    return (piece // NY * NXL + which) * NY + piece % NY


def put_rest(ref, lines):
    lines = lines + [jnp.zeros((1, TILE), F32)] * (REST - len(lines))
    ref[PIECE:PIECE + REST] = jnp.concatenate(lines, axis=0).astype(BF16)


def eye_of(piece, at):
    row = lax.broadcasted_iota(jnp.int32, (HALF, TILE), 0)
    return row + lax.rem(piece * HALVES + at, 2) * HALF == lax.broadcasted_iota(
        jnp.int32, (HALF, TILE), 1
    )


def sum_halves(piece, got_ref):
    count = got_ref.shape[0]
    rest = sum([got_ref[n, PIECE:].astype(F32) for n in range(1, count)], got_ref[0, PIECE:].astype(F32))
    halves = []
    for at in range(HALVES):
        s = slice(at * HALF, (at + 1) * HALF)
        total = sum([got_ref[n, s].astype(F32) for n in range(1, count)], got_ref[0, s].astype(F32))
        halves.append(total + jnp.where(eye_of(piece, at), rest[at:at + 1], 0.0))
    return halves


def put_halves(piece, out_ref, halves):
    lines = []
    for at, half in enumerate(halves):
        half_b = half.astype(BF16)
        lines.append(
            jnp.sum(jnp.where(eye_of(piece, at), half - half_b.astype(F32), 0.0), axis=0, keepdims=True)
        )
        for n in range(out_ref.shape[0]):
            out_ref[n, at * HALF:(at + 1) * HALF] = half_b
    for n in range(out_ref.shape[0]):
        put_rest(out_ref.at[n], lines)


def sum_kernel(where_ref, got_ref, *refs):
    turn_refs, (out_ref, slab_ref) = refs[:NY], refs[NY:]
    for turn, ref in enumerate(turn_refs):
        at = lax.rem(where_ref[1] + NY - turn, NY) * ROWS
        slab_ref[pl.ds(pl.multiple_of(at, ROWS), ROWS), :] = ref[...]
    put_halves(where_ref[0], out_ref, sum_halves(where_ref[0], got_ref))


def damp_kernel(all_tokens, where_ref, got_ref, slab0_ref, slab1_ref, out_ref):
    piece = where_ref[0]
    halves = []
    for at, half in enumerate(sum_halves(piece, got_ref)):
        block = lax.div(piece * HALVES + at, 2)
        on_diag = functools.reduce(jnp.logical_or, [block == WHERE[(r, r)] for r in range(GRID)])
        damping = jnp.where(on_diag, DAMPING, 0.0)
        halves.append(half / all_tokens + jnp.where(eye_of(piece, at), damping, 0.0))
    put_halves(piece, out_ref, halves)


def root_kernel(packed_ref, slab0_ref, slab1_ref, root_ref, right_ref,
                scaled, iterate, iterate_b, square_b, cubic_b):
    def block_of(r, c):
        parts = []
        for half in range(2):
            piece, at = divmod(2 * WHERE[(r, c)] + half, HALVES)
            part = packed_ref[piece, at * HALF:(at + 1) * HALF].astype(F32)
            if r == c:
                rest = packed_ref[piece, PIECE:].astype(F32)[at:at + 1]
                part = part + jnp.where(eye_of(piece, at), rest, 0.0)
            parts.append(part)
        return jnp.concatenate(parts, axis=0)

    squares = {True: jnp.zeros((TILE, TILE), F32), False: jnp.zeros((TILE, TILE), F32)}
    for r, c in PAIRS:
        block = block_of(r, c)
        squares[r == c] = squares[r == c] + block * block
    total = jnp.sum(squares[True] + 2.0 * squares[False], axis=1, keepdims=True)
    frob = jnp.sqrt(jnp.sum(total, axis=0, keepdims=True))
    for r, c in PAIRS:
        block = (block_of(r, c) / frob).astype(BF16)
        scaled[r * TILE:(r + 1) * TILE, c * TILE:(c + 1) * TILE] = block
        if r != c:
            scaled[c * TILE:(c + 1) * TILE, r * TILE:(r + 1) * TILE] = block.T
    width = 2 * TILE
    tiles = [slice(n, n + width) for n in range(0, ORDER, width)]
    for s in tiles:
        row = lax.broadcasted_iota(jnp.int32, (ORDER, width), 0)
        col = lax.broadcasted_iota(jnp.int32, (ORDER, width), 1) + s.start
        first = 1.5 * (row == col).astype(F32) - 0.5 * scaled[:, s].astype(F32)
        iterate[:, s] = first
        iterate_b[:, s] = first.astype(BF16)
    root_frob = jnp.sqrt(frob)
    for sweep in range(SWEEPS):
        for s in tiles:
            square_b[:, s] = jnp.dot(
                iterate_b[...], iterate_b[:, s], preferred_element_type=F32
            ).astype(BF16)
        for s in tiles:
            cubic_b[:, s] = jnp.dot(
                square_b[...], scaled[:, s], preferred_element_type=F32
            ).astype(BF16)
        for s in tiles:
            new = 1.5 * iterate[:, s] - 0.5 * jnp.dot(
                cubic_b[...], iterate_b[:, s], preferred_element_type=F32
            )
            if sweep < SWEEPS - 1:
                iterate[:, s] = new
            else:
                new = (new / root_frob).astype(BF16)
                root_ref[:, s] = new
                for half, ref in enumerate((slab0_ref, slab1_ref)):
                    done = jnp.dot(ref[...], new, preferred_element_type=F32).astype(BF16)
                    for n in range(width // TILE):
                        right_ref[
                            s.start // TILE + n, half * NY * ROWS:(half + 1) * NY * ROWS
                        ] = done[:, n * TILE:(n + 1) * TILE]
        if sweep < SWEEPS - 1:
            for s in tiles:
                iterate_b[:, s] = iterate[:, s].astype(BF16)


def left_kernel(root_ref, right_ref, out_ref):
    out_ref[...] = jnp.dot(root_ref[...], right_ref[...], preferred_element_type=F32).astype(BF16)


def turned(x, axes, size, shift):
    return lax.ppermute(x, axes, [(n, (n + shift) % size) for n in range(size)])


def local(acts, grads_out, gradient):
    all_tokens = acts.shape[0] * NZ * NXL * NY
    y = lax.axis_index("y")
    where = jnp.stack((lax.axis_index(("zl", "y")), y))

    packed, *turns = call(
        gram_kernel,
        "gram",
        [jax.ShapeDtypeStruct((NZL * NXL * NY, PIECE + REST, TILE), BF16)]
        + [jax.ShapeDtypeStruct((ROWS, ORDER), BF16)] * NY,
        (y[None], acts, grads_out, gradient),
        specs=[SMEM] + [pl.BlockSpec(memory_space=pltpu.HBM)] * 3,
        scratch=[
            pltpu.VMEM(acts.shape, BF16),
            pltpu.VMEM(acts.shape, BF16),
            pltpu.VMEM(gradient.shape, F32),
            pltpu.SemaphoreType.DMA((2, LOADS)),
            pltpu.SemaphoreType.DMA(()),
        ],
        flops=4 * acts.shape[0] * ORDER * ORDER,
        vmem=60 << 20,
    )
    turns = [turns[0]] + [turned(turns[shift], "y", NY, shift) for shift in range(1, NY)]

    got = lax.all_to_all(packed, ("zl", "xl", "y"), 0, 0, tiled=True)
    pieces, slab = call(
        sum_kernel,
        "sum",
        [
            jax.ShapeDtypeStruct((NZH, PIECE + REST, TILE), BF16),
            jax.ShapeDtypeStruct((NY * ROWS, ORDER), BF16),
        ],
        (where, got, *turns),
        specs=[SMEM] + [VMEM] * (1 + NY),
    )
    cells = [(k, i) for k in range(NBLOCK) for i in range(NBLOCK)]
    slabs = [
        lax.ppermute(
            slab,
            ("xl", "y", "xh", "c"),
            [((xl * NY + k) * NBLOCK + i, (NY + i) * NBLOCK + k) for k, i in cells],
        )
        for xl in range(NXL)
    ]
    got = lax.all_to_all(pieces, "zh", 0, 0, tiled=True)
    pieces = call(
        functools.partial(damp_kernel, float(all_tokens)),
        "damp",
        jax.ShapeDtypeStruct((NZL * NY, PIECE + REST, TILE), BF16),
        (where, got, *slabs),
        specs=[SMEM, VMEM, pl.BlockSpec(memory_space=pl.ANY), pl.BlockSpec(memory_space=pl.ANY)],
    )
    packed = lax.all_to_all(pieces, ("zl", "y"), 0, 0, tiled=True)

    square_b = pltpu.VMEM((ORDER, ORDER), BF16)
    root, right_done = call(
        root_kernel,
        "root",
        [
            jax.ShapeDtypeStruct((ORDER, ORDER), BF16),
            jax.ShapeDtypeStruct((NZ, NXL * NY * ROWS, TILE), BF16),
        ],
        (packed, *slabs),
        scratch=[square_b, pltpu.VMEM((ORDER, ORDER), F32), square_b, square_b, square_b],
        flops=6 * SWEEPS * ORDER**3,
    )

    right_done = lax.all_to_all(right_done, ("zh", "zl"), 0, 0, tiled=True)
    right_done = lax.ppermute(
        right_done,
        ("xl", "y", "xh", "c"),
        [((NY + i) * NBLOCK + k, k * NBLOCK + i) for k, i in cells],
    )
    result = call(
        left_kernel,
        "left",
        jax.ShapeDtypeStruct((ORDER, TILE), BF16),
        (root, right_done.reshape(ORDER, TILE)),
        flops=2 * ORDER * ORDER * TILE,
    )
    result = result.reshape(NZ * NXL * NY, ROWS, TILE)
    returned = lax.all_to_all(result, DP, 0, 0, tiled=True)
    returned = returned.reshape(NZ, NXL, NY, ROWS, TILE)[:, 0]
    return returned.transpose(2, 1, 0, 3).reshape(1, ROWS, NY * NZ * TILE)


def solution(mesh):
    split = Mesh(mesh.devices.reshape(SIZES), AXES)
    block = ("xh", "c")
    in_specs = (P(DP, block), P(DP, block), P(block, DP, None))
    out_specs = P(block, DP, None)
    return jax.shard_map(local, mesh=split, in_specs=in_specs, out_specs=out_specs, check_vma=False)
```

time: 190 us -> 155 us (0.82); the launches traced: 187 us -> 155 us
  starting transfers between devices: 66.7 us -> 26 us
  waiting for transfers between devices: 34 us -> 45.6 us
  Pallas kernels: 17.7 us -> 25.9 us
  local copies, waits for them, and re-layouts: 7.7 us -> 0.83 us
  other arithmetic: 3.93 us -> 0.07 us
    ppermute x20 -> x3, starting transfers between devices: 36.8 us -> 5.68 us  [turned(): return lax.ppermute(x, axes, [(n, (n + shift) % size) for n in range(size)])]
    ppermute x20 -> x3, waiting for transfers between devices: 11.7 us -> 24.7 us  [turned(): return lax.ppermute(x, axes, [(n, (n + shift) % size) for n in range(size)])]
    ppermute x9 -> x3, starting transfers between devices: 14 us -> 5.36 us  [the longest x1 3.41 us: local(): lax.ppermute(right_done, ('xl', 'y', 'xh', 'c'), [((NY + i) * NBLOCK + k,...]
    pallas_call x3 -> x5, Pallas kernels: 17.7 us -> 25.9 us  [call(): pl.pallas_call(kernel, out_shape=out_shape, scratch_shapes=list(scratch),...]
    unnamed x10 -> x9, local copies, waits for them, and re-layouts: 3.86 us -> 0.11 us
    broadcast_in_dim x3 -> x0, local copies, waits for them, and re-layouts: 2.53 us -> none  [the longest x1 1.19 us: local(): jnp.broadcast_to(scaled_piece[None], (NZL * NY, PIECE, TILE))]
    all_to_all x3 -> x2, waiting for transfers between devices: 10 us -> 8.96 us  [the longest x1 8.95 us: local(): got = lax.all_to_all(pieces, 'zh', 0, 0, tiled=True)]
    all_to_all x3 -> x2, starting transfers between devices: 15.9 us -> 15 us  [the longest x1 7.53 us: local(): got = lax.all_to_all(pieces, 'zh', 0, 0, tiled=True)]
  transfers between devices with their start and end apart: 32 -> 8, of which waited for: 11 -> 5; matrix products, arithmetic and copies ran while one was open for 1% -> 0% of each run, Pallas kernels for 7% -> 0%
where the time goes in v3:
time: 155 us
  blocking collectives  56 us (36%)
  waiting for transfers between devices  45.6 us (29%)
  starting transfers between devices  26 us (17%)
  Pallas kernels  25.9 us (17%)
    pallas_call x5, Pallas kernels, call(): pl.pallas_call(kernel, out_shape=out_shape, scratch_shapes=list(scratch),...  25.9 us
    ppermute x3, waiting for transfers between devices, turned(): return lax.ppermute(x, axes, [(n, (n + shift) % size) for n in range(size)])  24.7 us
    all_to_all x1, blocking collectives, local(): returned = lax.all_to_all(result, DP, 0, 0, tiled=True)  20.3 us
    all_to_all x1, blocking collectives, local(): packed = lax.all_to_all(pieces, ('zl', 'y'), 0, 0, tiled=True)  19.7 us
    all_to_all x1, blocking collectives, local(): right_done = lax.all_to_all(right_done, ('zh', 'zl'), 0, 0, tiled=True)  16 us
    all_to_all x1, waiting for transfers between devices, local(): got = lax.all_to_all(pieces, 'zh', 0, 0, tiled=True)  8.95 us
    all_to_all x1, starting transfers between devices, local(): got = lax.all_to_all(pieces, 'zh', 0, 0, tiled=True)  7.53 us
    all_to_all x1, starting transfers between devices, local(): got = lax.all_to_all(packed, ('zl', 'xl', 'y'), 0, 0, tiled=True)  7.45 us
  transfers between devices with their start and end apart: 8, of which 5 were waited for; matrix products, arithmetic and copies ran while one was open for 0% of the time, Pallas kernels for 0%

profile of v3, /device:TPU:2, one launch (start us, length us, event | category | flops | bytes accessed | tf_op | source)
XLA Modules:
  0.0 154.5 jit_solution(10478973230147044759)
XLA Ops:
  0.0 5.4 %gram.1 = (bf16[16,592,128]{2,1,0:T(8,128)(2,1)}, bf16[16,1024]{1,0:T(8,128)(2,1)}, bf16[16,1024]{1,0:T(8,128)(2,1)}, bf16[16,1024]{1,0:T(8,128)(2,1)}, bf16[16,1024]{1,0:T(8,128)(2,1)}) custom-call(s32[1]{0:T(128)} %bitcast.1.y_ref, bf16[768,1024]{1,0:T(8,128)(2,1)} %acts_ref.1, bf16[768,1024]{1,0:T(8,128)(2,1)} %grads_ref.1, f32[1,16,4096]{2,1,0:T(8,128)} %gradient_ref.1), custom_call_target="tpu_custom_call" | custom-call | flops 3221225472 | bytes 4194304 | tf_op jit(solution)/shard_map/gram/pallas_call | solution.py:37
  5.4 0.0 copy-start.3
  5.4 0.0 copy-start.2
  5.4 0.0 copy-start.1
  5.4 0.0 copy-start
  5.4 7.5 %all-to-all-start = ((bf16[16,592,128]{2,1,0:T(8,128)(2,1)}), bf16[16,592,128]{2,1,0:T(8,128)(2,1)S(1)}, u32[]{:S(2)}, u32[]{:S(2)}) async-start(bf16[16,592,128]{2,1,0:T(8,128)(2,1)} %get-tuple-element.14), calls=%async_computation | async-start | bytes 4849664 | tf_op jit(solution)/shard_map/all_to_all | solution.py:256
  12.9 0.0 copy-done.3
  12.9 1.5 collective-permute-start
  14.4 2.7 %collective-permute-start.1 = (bf16[16,1024]{1,0:T(8,128)(2,1)S(1)}, bf16[16,1024]{1,0:T(8,128)(2,1)S(1)}, u32[]{:S(2)}, u32[]{:S(2)}) collective-permute-start(bf16[16,1024]{1,0:T(8,128)(2,1)S(1)} %copy-done.2), channel_id=1, source_target_pairs={{0,8},{4,12},{8,0},{12,4},{1,9},{5,13},{9,1},{13,5},{2,10},{6,14},... | collective-permute-start | bytes 98312 | tf_op jit(solution)/shard_map/ppermute | solution.py:229
  17.1 1.5 collective-permute-start.2
  18.6 0.1 pad_add_fusion.where_ref
  18.6 24.6 %collective-permute-done.refs_1_ = bf16[16,1024]{1,0:T(8,128)(2,1)S(1)} collective-permute-done((bf16[16,1024]{1,0:T(8,128)(2,1)S(1)}, bf16[16,1024]{1,0:T(8,128)(2,1)S(1)}, u32[]{:S(2)}, u32[]{:S(2)}) %collective-permute-start) | collective-permute-done | bytes 32800 | tf_op jit(solution)/shard_map/ppermute | solution.py:229
  43.3 0.0 collective-permute-done.1.refs_2_
  43.3 0.1 collective-permute-done.2.refs_3_
  43.4 0.0 all-to-all-done.got_ref
  43.4 1.8 %sum.1 = (bf16[4,592,128]{2,1,0:T(8,128)(2,1)}, bf16[64,1024]{1,0:T(8,128)(2,1)S(1)}) custom-call(s32[2]{0:T(128)S(1)} %pad_add_fusion.where_ref, bf16[16,592,128]{2,1,0:T(8,128)(2,1)S(1)} %all-to-all-done.got_ref, bf16[16,1024]{1,0:T(8,128)(2,1)S(1)} %copy-done, bf16[16,1024]{1,0:T(8,128)(2,1)S(1)} %collective-permute-done.refs_1_, ...), custom_call_target="tpu_custom_call" | custom-call | bytes 4194304 | tf_op jit(solution)/shard_map/sum/pallas_call | solution.py:37
  45.2 7.5 %all-to-all-start.1 = ((bf16[4,592,128]{2,1,0:T(8,128)(2,1)}), bf16[4,592,128]{2,1,0:T(8,128)(2,1)S(1)}, u32[]{:S(2)}, u32[]{:S(2)}) async-start(bf16[4,592,128]{2,1,0:T(8,128)(2,1)} %get-tuple-element.19), calls=%async_computation.1 | async-start | bytes 1212416 | tf_op jit(solution)/shard_map/all_to_all | solution.py:276
  52.7 0.7 collective-permute-start.4
  53.4 1.3 collective-permute-start.3
  54.7 0.0 collective-permute-done.4.slab1_ref
  54.7 5.9 %collective-permute-done.3.slab0_ref = bf16[64,1024]{1,0:T(8,128)(2,1)S(1)} collective-permute-done((bf16[64,1024]{1,0:T(8,128)(2,1)S(1)}, bf16[64,1024]{1,0:T(8,128)(2,1)S(1)}, u32[]{:S(2)}, u32[]{:S(2)}) %collective-permute-start.3) | collective-permute-done | bytes 131104 | tf_op jit(solution)/shard_map/ppermute | solution.py:269
  60.6 9.0 %all-to-all-done.1.got_ref = bf16[4,592,128]{2,1,0:T(8,128)(2,1)S(1)} async-done(((bf16[4,592,128]{2,1,0:T(8,128)(2,1)}), bf16[4,592,128]{2,1,0:T(8,128)(2,1)S(1)}, u32[]{:S(2)}, u32[]{:S(2)}) %all-to-all-start.1) | async-done | bytes 606240 | tf_op jit(solution)/shard_map/all_to_all | solution.py:276
  69.6 0.8 damp.1
  70.3 19.7 %all_to_all.25.packed_ref = bf16[8,592,128]{2,1,0:T(8,128)(2,1)S(1)} all-to-all(bf16[8,592,128]{2,1,0:T(8,128)(2,1)S(1)} %damp.1), channel_id=1, replica_groups=mesh['zh'=4,'zl'=2,'xl'=2,'y'=4,'xh'=2,'c'=2] {'zl','y'}, dimensions={0} | all-to-all | bytes 2424832 | tf_op jit(solution)/shard_map/all_to_all | solution.py:284
  90.0 17.3 %root.1 = (bf16[1024,1024]{1,0:T(8,128)(2,1)S(1)}, bf16[8,128,128]{2,1,0:T(8,128)(2,1)S(1)}) custom-call(bf16[8,592,128]{2,1,0:T(8,128)(2,1)S(1)} %all_to_all.25.packed_ref, bf16[64,1024]{1,0:T(8,128)(2,1)S(1)} %collective-permute-done.3.slab0_ref, bf16[64,1024]{1,0:T(8,128)(2,1)S(1)} %collective-permute-done.4.slab1_ref), custom_call_target="tpu_custom_call" | custom-call | flops 12884901888 | bytes 4194304 | tf_op jit(solution)/shard_map/root/pallas_call | solution.py:37
  107.3 16.0 %all_to_all.26 = bf16[8,128,128]{2,1,0:T(8,128)(2,1)S(1)} all-to-all(bf16[8,128,128]{2,1,0:T(8,128)(2,1)S(1)} %get-tuple-element.22), channel_id=1, replica_groups=mesh['zh'=4,'zl'=2,'xl'=2,'y'=4,'xh'=2,'c'=2] {'zh','zl'}, dimensions={0} | all-to-all | bytes 524288 | tf_op jit(solution)/shard_map/all_to_all | solution.py:299
  123.3 3.4 %collective-permute-start.5 = (bf16[8,128,128]{2,1,0:T(8,128)(2,1)S(1)}, bf16[8,128,128]{2,1,0:T(8,128)(2,1)S(1)}, u32[]{:S(2)}, u32[]{:S(2)}) collective-permute-start(bf16[8,128,128]{2,1,0:T(8,128)(2,1)S(1)} %all_to_all.26), channel_id=1, source_target_pairs={{16,0},{20,1},{24,2},{28,3},{17,4},{21,5},{25,6},{29,7},{18,8},{22... | collective-permute-start | bytes 786440 | tf_op jit(solution)/shard_map/ppermute | solution.py:300
  126.7 6.0 %collective-permute-done.5 = bf16[8,128,128]{2,1,0:T(8,128)(2,1)S(1)} collective-permute-done((bf16[8,128,128]{2,1,0:T(8,128)(2,1)S(1)}, bf16[8,128,128]{2,1,0:T(8,128)(2,1)S(1)}, u32[]{:S(2)}, u32[]{:S(2)}) %collective-permute-start.5) | collective-permute-done | bytes 262176 | tf_op jit(solution)/shard_map/ppermute | solution.py:300
  132.7 0.7 left.1
  133.4 20.3 %all_to_all.27 = bf16[64,16,128]{2,1,0:T(8,128)(2,1)S(1)} all-to-all(bf16[64,16,128]{2,1,0:T(8,128)(2,1)S(1)} %bitcast.12), channel_id=1, replica_groups=mesh['zh'=4,'zl'=2,'xl'=2,'y'=4,'xh'=2,'c'=2] {'zh','zl','xl','y'}, dimensions={0} | all-to-all | bytes 524288 | tf_op jit(solution)/shard_map/all_to_all | solution.py:313
  153.7 0.1 copy.7
  153.8 0.7 reshape.15
  (4 shorter events, 0.0 us)
Async XLA Ops:
  5.4 7.5 %copy-start.3 = (bf16[16,1024]{1,0:T(8,128)(2,1)S(1)}, bf16[16,1024]{1,0:T(8,128)(2,1)}, u32[]{:S(2)}) copy-start(bf16[16,1024]{1,0:T(8,128)(2,1)} %get-tuple-element.16) | copy-start | bytes 98308
  5.4 9.0 %copy-start.2 = (bf16[16,1024]{1,0:T(8,128)(2,1)S(1)}, bf16[16,1024]{1,0:T(8,128)(2,1)}, u32[]{:S(2)}) copy-start(bf16[16,1024]{1,0:T(8,128)(2,1)} %get-tuple-element.17) | copy-start | bytes 98308
  5.4 11.7 %copy-start.1 = (bf16[16,1024]{1,0:T(8,128)(2,1)S(1)}, bf16[16,1024]{1,0:T(8,128)(2,1)}, u32[]{:S(2)}) copy-start(bf16[16,1024]{1,0:T(8,128)(2,1)} %get-tuple-element.18) | copy-start | bytes 98308
  5.4 37.9 %copy-start = (bf16[16,1024]{1,0:T(8,128)(2,1)S(1)}, bf16[16,1024]{1,0:T(8,128)(2,1)}, u32[]{:S(2)}) copy-start(bf16[16,1024]{1,0:T(8,128)(2,1)} %get-tuple-element.15.refs_0_) | copy-start | bytes 98308
  5.4 37.9 %all-to-all-start = ((bf16[16,592,128]{2,1,0:T(8,128)(2,1)}), bf16[16,592,128]{2,1,0:T(8,128)(2,1)S(1)}, u32[]{:S(2)}, u32[]{:S(2)}) async-start(bf16[16,592,128]{2,1,0:T(8,128)(2,1)} %get-tuple-element.14), calls=%async_computation | async-start | bytes 4849664 | tf_op jit(solution)/shard_map/all_to_all | solution.py:256
  12.9 30.4 %collective-permute-start = (bf16[16,1024]{1,0:T(8,128)(2,1)S(1)}, bf16[16,1024]{1,0:T(8,128)(2,1)S(1)}, u32[]{:S(2)}, u32[]{:S(2)}) collective-permute-start(bf16[16,1024]{1,0:T(8,128)(2,1)S(1)} %copy-done.3), channel_id=1, source_target_pairs={{0,4},{4,8},{8,12},{12,0},{1,5},{5,9},{9,13},{13,1},{2,6},{6,10},{... | collective-permute-start | bytes 98312 | tf_op jit(solution)/shard_map/ppermute | solution.py:229
  14.4 28.8 %collective-permute-start.1 = (bf16[16,1024]{1,0:T(8,128)(2,1)S(1)}, bf16[16,1024]{1,0:T(8,128)(2,1)S(1)}, u32[]{:S(2)}, u32[]{:S(2)}) collective-permute-start(bf16[16,1024]{1,0:T(8,128)(2,1)S(1)} %copy-done.2), channel_id=1, source_target_pairs={{0,8},{4,12},{8,0},{12,4},{1,9},{5,13},{9,1},{13,5},{2,10},{6,14},... | collective-permute-start | bytes 98312 | tf_op jit(solution)/shard_map/ppermute | solution.py:229
  17.1 26.2 %collective-permute-start.2 = (bf16[16,1024]{1,0:T(8,128)(2,1)S(1)}, bf16[16,1024]{1,0:T(8,128)(2,1)S(1)}, u32[]{:S(2)}, u32[]{:S(2)}) collective-permute-start(bf16[16,1024]{1,0:T(8,128)(2,1)S(1)} %copy-done.1), channel_id=1, source_target_pairs={{0,12},{4,0},{8,4},{12,8},{1,13},{5,1},{9,5},{13,9},{2,14},{6,2},{... | collective-permute-start | bytes 98312 | tf_op jit(solution)/shard_map/ppermute | solution.py:229
  45.2 24.4 %all-to-all-start.1 = ((bf16[4,592,128]{2,1,0:T(8,128)(2,1)}), bf16[4,592,128]{2,1,0:T(8,128)(2,1)S(1)}, u32[]{:S(2)}, u32[]{:S(2)}) async-start(bf16[4,592,128]{2,1,0:T(8,128)(2,1)} %get-tuple-element.19), calls=%async_computation.1 | async-start | bytes 1212416 | tf_op jit(solution)/shard_map/all_to_all | solution.py:276
  52.7 2.0 %collective-permute-start.4 = (bf16[64,1024]{1,0:T(8,128)(2,1)S(1)}, bf16[64,1024]{1,0:T(8,128)(2,1)S(1)}, u32[]{:S(2)}, u32[]{:S(2)}) collective-permute-start(bf16[64,1024]{1,0:T(8,128)(2,1)S(1)} %get-tuple-element.20), channel_id=1, source_target_pairs={{16,16},{17,20},{18,24},{19,28},{20,17},{21,21},{22,25},{23,29},{2... | collective-permute-start | bytes 393224 | tf_op jit(solution)/shard_map/ppermute | solution.py:269
  53.4 7.3 %collective-permute-start.3 = (bf16[64,1024]{1,0:T(8,128)(2,1)S(1)}, bf16[64,1024]{1,0:T(8,128)(2,1)S(1)}, u32[]{:S(2)}, u32[]{:S(2)}) collective-permute-start(bf16[64,1024]{1,0:T(8,128)(2,1)S(1)} %get-tuple-element.20), channel_id=1, source_target_pairs={{0,16},{1,20},{2,24},{3,28},{4,17},{5,21},{6,25},{7,29},{8,18},{9,... | collective-permute-start | bytes 393224 | tf_op jit(solution)/shard_map/ppermute | solution.py:269
  123.3 9.4 %collective-permute-start.5 = (bf16[8,128,128]{2,1,0:T(8,128)(2,1)S(1)}, bf16[8,128,128]{2,1,0:T(8,128)(2,1)S(1)}, u32[]{:S(2)}, u32[]{:S(2)}) collective-permute-start(bf16[8,128,128]{2,1,0:T(8,128)(2,1)S(1)} %all_to_all.26), channel_id=1, source_target_pairs={{16,0},{20,1},{24,2},{28,3},{17,4},{21,5},{25,6},{29,7},{18,8},{22... | collective-permute-start | bytes 786440 | tf_op jit(solution)/shard_map/ppermute | solution.py:300

commit v4 on v3

--- a/solution.py
+++ b/solution.py
@@ -29,7 +29,9 @@
 PIECE = HALVES * HALF
 REST = 16
 ROWS = 16
+TERMS = 3
 LOADS = 4
+ZROWS = NZL * NXL * NY * ROWS
 
 
 def call(kernel, name, out_shape, args, specs=None, scratch=(), flops=0, vmem=VMEM_BYTES):
@@ -127,7 +129,7 @@
     return halves
 
 
-def put_halves(piece, out_ref, halves):
+def put_halves(piece, out_ref, halves, more=()):
     lines = []
     for at, half in enumerate(halves):
         half_b = half.astype(BF16)
@@ -137,7 +139,7 @@
         for n in range(out_ref.shape[0]):
             out_ref[n, at * HALF:(at + 1) * HALF] = half_b
     for n in range(out_ref.shape[0]):
-        put_rest(out_ref.at[n], lines)
+        put_rest(out_ref.at[n], lines + list(more))
 
 
 def sum_kernel(where_ref, got_ref, *refs):
@@ -148,20 +150,36 @@
     put_halves(where_ref[0], out_ref, sum_halves(where_ref[0], got_ref))
 
 
-def damp_kernel(all_tokens, where_ref, got_ref, slab0_ref, slab1_ref, out_ref):
+def damp_kernel(all_tokens, where_ref, got_ref, *refs):
+    out_ref = refs[-1]
     piece = where_ref[0]
     halves = []
+    squares = jnp.zeros((HALF, TILE), F32)
     for at, half in enumerate(sum_halves(piece, got_ref)):
         block = lax.div(piece * HALVES + at, 2)
         on_diag = functools.reduce(jnp.logical_or, [block == WHERE[(r, r)] for r in range(GRID)])
         damping = jnp.where(on_diag, DAMPING, 0.0)
-        halves.append(half / all_tokens + jnp.where(eye_of(piece, at), damping, 0.0))
-    put_halves(piece, out_ref, halves)
-
-
-def root_kernel(packed_ref, slab0_ref, slab1_ref, root_ref, right_ref,
-                scaled, iterate, iterate_b, square_b, cubic_b):
-    def block_of(r, c):
+        half = half / all_tokens + jnp.where(eye_of(piece, at), damping, 0.0)
+        squares = squares + jnp.where(on_diag, 1.0, 2.0) * half * half
+        halves.append(half)
+    left = jnp.sum(jnp.sum(squares, axis=0, keepdims=True), axis=1, keepdims=True)
+    left = jnp.broadcast_to(left, (1, TILE))
+    terms = []
+    for _ in range(TERMS):
+        terms.append(left.astype(BF16).astype(F32))
+        left = left - terms[-1]
+    put_halves(piece, out_ref, halves, terms)
+
+
+def root_kernel(where_ref, packed_ref, *refs):
+    slab_refs, refs = refs[:NZL * NXL], refs[NZL * NXL:]
+    root_ref, right_refs, refs = refs[0], refs[1:1 + NZH], refs[1 + NZH:]
+    scaled, iterate, iterate_b, square_b, cubic_b, right = refs
+    terms = sum([packed_ref[n, PIECE:].astype(F32) for n in range(NZL * NY)])[HALVES:HALVES + TERMS]
+    frob = jnp.sqrt(jnp.sum(terms, axis=0, keepdims=True)[:, 0:1])
+    over_frob = 1.0 / frob
+    over_root = 1.0 / jnp.sqrt(frob)
+    for r, c in PAIRS:
         parts = []
         for half in range(2):
             piece, at = divmod(2 * WHERE[(r, c)] + half, HALVES)
@@ -170,16 +188,7 @@
                 rest = packed_ref[piece, PIECE:].astype(F32)[at:at + 1]
                 part = part + jnp.where(eye_of(piece, at), rest, 0.0)
             parts.append(part)
-        return jnp.concatenate(parts, axis=0)
-
-    squares = {True: jnp.zeros((TILE, TILE), F32), False: jnp.zeros((TILE, TILE), F32)}
-    for r, c in PAIRS:
-        block = block_of(r, c)
-        squares[r == c] = squares[r == c] + block * block
-    total = jnp.sum(squares[True] + 2.0 * squares[False], axis=1, keepdims=True)
-    frob = jnp.sqrt(jnp.sum(total, axis=0, keepdims=True))
-    for r, c in PAIRS:
-        block = (block_of(r, c) / frob).astype(BF16)
+        block = (jnp.concatenate(parts, axis=0) * over_frob).astype(BF16)
         scaled[r * TILE:(r + 1) * TILE, c * TILE:(c + 1) * TILE] = block
         if r != c:
             scaled[c * TILE:(c + 1) * TILE, r * TILE:(r + 1) * TILE] = block.T
@@ -191,7 +200,6 @@
         first = 1.5 * (row == col).astype(F32) - 0.5 * scaled[:, s].astype(F32)
         iterate[:, s] = first
         iterate_b[:, s] = first.astype(BF16)
-    root_frob = jnp.sqrt(frob)
     for sweep in range(SWEEPS):
         for s in tiles:
             square_b[:, s] = jnp.dot(
@@ -208,21 +216,33 @@
             if sweep < SWEEPS - 1:
                 iterate[:, s] = new
             else:
-                new = (new / root_frob).astype(BF16)
-                root_ref[:, s] = new
-                for half, ref in enumerate((slab0_ref, slab1_ref)):
-                    done = jnp.dot(ref[...], new, preferred_element_type=F32).astype(BF16)
-                    for n in range(width // TILE):
-                        right_ref[
-                            s.start // TILE + n, half * NY * ROWS:(half + 1) * NY * ROWS
-                        ] = done[:, n * TILE:(n + 1) * TILE]
+                root_ref[:, s] = (new * over_root).astype(BF16)
         if sweep < SWEEPS - 1:
             for s in tiles:
                 iterate_b[:, s] = iterate[:, s].astype(BF16)
-
-
-def left_kernel(root_ref, right_ref, out_ref):
-    out_ref[...] = jnp.dot(root_ref[...], right_ref[...], preferred_element_type=F32).astype(BF16)
+    zh, zl = where_ref[0], where_ref[1]
+    cols = root_ref[:, pl.ds(pl.multiple_of(zl * (NZH * TILE), NZH * TILE), NZH * TILE)]
+    for turn, ref in enumerate(slab_refs):
+        from_zl = lax.rem(zl + turn // NXL, NZL)
+        at = (from_zl * NXL + turn % NXL) * (NY * ROWS)
+        right[pl.ds(pl.multiple_of(at, NY * ROWS), NY * ROWS), :] = jnp.dot(
+            ref[...], cols, preferred_element_type=F32
+        ).astype(BF16)
+    for shift, ref in enumerate(right_refs):
+        at = lax.rem(zh + shift, NZH) * TILE
+        ref[...] = right[:, pl.ds(pl.multiple_of(at, TILE), TILE)]
+
+
+def left_kernel(where_ref, root_ref, *refs):
+    right_refs, (out_ref, right) = refs[:NZH], refs[NZH:]
+    for shift, ref in enumerate(right_refs):
+        at = lax.rem(where_ref[0] + NZH - shift, NZH) * ZROWS
+        right[pl.ds(pl.multiple_of(at, ZROWS), ZROWS), :] = ref[...]
+    out_ref[...] = jnp.dot(root_ref[...], right[...], preferred_element_type=F32).astype(BF16)
+
+
+def place(zl, xl, y, block):
+    return ((zl * NXL + xl) * NY + y) * NBLOCK + block
 
 
 def turned(x, axes, size, shift):
@@ -265,12 +285,18 @@
         specs=[SMEM] + [VMEM] * (1 + NY),
     )
     cells = [(k, i) for k in range(NBLOCK) for i in range(NBLOCK)]
+    count = NZL * NXL * NY * NBLOCK
     slabs = [
         lax.ppermute(
             slab,
-            ("xl", "y", "xh", "c"),
-            [((xl * NY + k) * NBLOCK + i, (NY + i) * NBLOCK + k) for k, i in cells],
+            ("zl", "xl", "y", "xh", "c"),
+            [
+                (place((zl + turn) % NZL, xl, k, i), place(zl, 1, i, k))
+                for zl in range(NZL)
+                for k, i in cells
+            ],
         )
+        for turn in range(NZL)
         for xl in range(NXL)
     ]
     got = lax.all_to_all(pieces, "zh", 0, 0, tiled=True)
@@ -279,40 +305,50 @@
         "damp",
         jax.ShapeDtypeStruct((NZL * NY, PIECE + REST, TILE), BF16),
         (where, got, *slabs),
-        specs=[SMEM, VMEM, pl.BlockSpec(memory_space=pl.ANY), pl.BlockSpec(memory_space=pl.ANY)],
+        specs=[SMEM, VMEM] + [pl.BlockSpec(memory_space=pl.ANY)] * len(slabs),
     )
     packed = lax.all_to_all(pieces, ("zl", "y"), 0, 0, tiled=True)
 
     square_b = pltpu.VMEM((ORDER, ORDER), BF16)
-    root, right_done = call(
+    z_where = jnp.stack((lax.axis_index("zh"), lax.axis_index("zl")))
+    right_done = jax.ShapeDtypeStruct((ZROWS, TILE), BF16)
+    root, *right_done = call(
         root_kernel,
         "root",
-        [
-            jax.ShapeDtypeStruct((ORDER, ORDER), BF16),
-            jax.ShapeDtypeStruct((NZ, NXL * NY * ROWS, TILE), BF16),
-        ],
-        (packed, *slabs),
-        scratch=[square_b, pltpu.VMEM((ORDER, ORDER), F32), square_b, square_b, square_b],
+        [jax.ShapeDtypeStruct((ORDER, ORDER), BF16)] + [right_done] * NZH,
+        (z_where, packed, *slabs),
+        specs=[SMEM] + [VMEM] * (1 + len(slabs)),
+        scratch=[square_b, pltpu.VMEM((ORDER, ORDER), F32), square_b, square_b, square_b,
+                 pltpu.VMEM((ZROWS, NZH * TILE), BF16)],
         flops=6 * SWEEPS * ORDER**3,
     )
 
-    right_done = lax.all_to_all(right_done, ("zh", "zl"), 0, 0, tiled=True)
-    right_done = lax.ppermute(
-        right_done,
-        ("xl", "y", "xh", "c"),
-        [((NY + i) * NBLOCK + k, k * NBLOCK + i) for k, i in cells],
-    )
+    right_done = [
+        lax.ppermute(
+            right_done[shift],
+            ("zh", "zl", "xl", "y", "xh", "c"),
+            [
+                (zh * count + place(zl, 1, i, k), (zh + shift) % NZH * count + place(zl, 0, k, i))
+                for zh in range(NZH)
+                for zl in range(NZL)
+                for k, i in cells
+            ],
+        )
+        for shift in range(NZH)
+    ]
     result = call(
         left_kernel,
         "left",
         jax.ShapeDtypeStruct((ORDER, TILE), BF16),
-        (root, right_done.reshape(ORDER, TILE)),
+        (z_where, root, *right_done),
+        specs=[SMEM] + [VMEM] * (1 + NZH),
+        scratch=[pltpu.VMEM((ORDER, TILE), BF16)],
         flops=2 * ORDER * ORDER * TILE,
     )
     result = result.reshape(NZ * NXL * NY, ROWS, TILE)
     returned = lax.all_to_all(result, DP, 0, 0, tiled=True)
-    returned = returned.reshape(NZ, NXL, NY, ROWS, TILE)[:, 0]
-    return returned.transpose(2, 1, 0, 3).reshape(1, ROWS, NY * NZ * TILE)
+    returned = returned.reshape(NZH, NZL, NXL, NY, ROWS, TILE)[:, :, 0]
+    return returned.transpose(3, 2, 1, 0, 4).reshape(1, ROWS, NY * NZ * TILE)
 
 
 def solution(mesh):

time: 155 us -> 157 us (1.013)
  blocking collectives: 56 us -> 23.5 us
  starting transfers between devices: 26 us -> 48.2 us
  waiting for transfers between devices: 45.6 us -> 58.4 us
    all_to_all x2 -> x0, blocking collectives: 35.7 us -> none  [the longest x1 19.7 us: local(): packed = lax.all_to_all(pieces, ('zl', 'y'), 0, 0, tiled=True)]
    all_to_all x0 -> x1, waiting for transfers between devices: none -> 15.9 us  [local(): packed = lax.all_to_all(pieces, ('zl', 'y'), 0, 0, tiled=True)]
    ppermute x3 -> x8, starting transfers between devices: 5.36 us -> 16.5 us  [the longest x4 8.32 us: local(): lax.ppermute(right_done[shift], ('zh', 'zl', 'xl', 'y', 'xh', 'c'), [(zh...]
    all_to_all x0 -> x1, starting transfers between devices: none -> 11.1 us  [local(): packed = lax.all_to_all(pieces, ('zl', 'y'), 0, 0, tiled=True)]
    all_to_all x1, waiting for transfers between devices: 8.95 us -> 2.73 us  [local(): got = lax.all_to_all(pieces, 'zh', 0, 0, tiled=True)]
    all_to_all x1, blocking collectives: 20.3 us -> 23.5 us  [local(): returned = lax.all_to_all(result, DP, 0, 0, tiled=True)]
    ppermute x3 -> x8, waiting for transfers between devices: 11.9 us -> 15 us  [the longest x4 9.02 us: local(): lax.ppermute(slab, ('zl', 'xl', 'y', 'xh', 'c'), [(place((zl + turn) % NZ...]
  transfers between devices with their start and end apart: 8 -> 14, of which waited for: 5 -> 7; matrix products, arithmetic and copies ran while one was open for 0% -> 0% of each run, Pallas kernels for 0% -> 0%
where the time goes in v4:
time: 157 us
  waiting for transfers between devices  58.4 us (37%)
  starting transfers between devices  48.2 us (31%)
  Pallas kernels  25.6 us (16%)
  blocking collectives  23.5 us (15%)
    pallas_call x5, Pallas kernels, call(): pl.pallas_call(kernel, out_shape=out_shape, scratch_shapes=list(scratch),...  25.6 us
    ppermute x3, waiting for transfers between devices, turned(): return lax.ppermute(x, axes, [(n, (n + shift) % size) for n in range(size)])  24.7 us
    all_to_all x1, blocking collectives, local(): returned = lax.all_to_all(result, DP, 0, 0, tiled=True)  23.5 us
    all_to_all x1, waiting for transfers between devices, local(): packed = lax.all_to_all(pieces, ('zl', 'y'), 0, 0, tiled=True)  15.9 us
    all_to_all x1, starting transfers between devices, local(): packed = lax.all_to_all(pieces, ('zl', 'y'), 0, 0, tiled=True)  11.1 us
    ppermute x4, waiting for transfers between devices, local(): lax.ppermute(slab, ('zl', 'xl', 'y', 'xh', 'c'), [(place((zl + turn) % NZ...  9.02 us
    ppermute x4, starting transfers between devices, local(): lax.ppermute(right_done[shift], ('zh', 'zl', 'xl', 'y', 'xh', 'c'), [(zh...  8.32 us
    ppermute x4, starting transfers between devices, local(): lax.ppermute(slab, ('zl', 'xl', 'y', 'xh', 'c'), [(place((zl + turn) % NZ...  8.17 us
  transfers between devices with their start and end apart: 14, of which 7 were waited for; matrix products, arithmetic and copies ran while one was open for 0% of the time, Pallas kernels for 0%

profile of v4, /device:TPU:2, one launch (start us, length us, event | category | flops | bytes accessed | tf_op | source)
XLA Modules:
  0.0 156.8 jit_solution(3483924732592344908)
XLA Ops:
  0.0 5.4 %gram.1 = (bf16[16,592,128]{2,1,0:T(8,128)(2,1)}, bf16[16,1024]{1,0:T(8,128)(2,1)}, bf16[16,1024]{1,0:T(8,128)(2,1)}, bf16[16,1024]{1,0:T(8,128)(2,1)}, bf16[16,1024]{1,0:T(8,128)(2,1)}) custom-call(s32[1]{0:T(128)} %bitcast.3.y_ref, bf16[768,1024]{1,0:T(8,128)(2,1)} %acts_ref.1, bf16[768,1024]{1,0:T(8,128)(2,1)} %grads_ref.1, f32[1,16,4096]{2,1,0:T(8,128)} %gradient_ref.1), custom_call_target="tpu_custom_call" | custom-call | flops 3221225472 | bytes 4194304 | tf_op jit(solution)/shard_map/gram/pallas_call | solution.py:39
  5.4 0.0 copy-start
  5.4 7.5 %all-to-all-start = ((bf16[16,592,128]{2,1,0:T(8,128)(2,1)}), bf16[16,592,128]{2,1,0:T(8,128)(2,1)S(1)}, u32[]{:S(2)}, u32[]{:S(2)}) async-start(bf16[16,592,128]{2,1,0:T(8,128)(2,1)} %get-tuple-element.17), calls=%async_computation | async-start | bytes 4849664 | tf_op jit(solution)/shard_map/all_to_all | solution.py:276
  12.9 1.5 collective-permute-start
  14.5 2.7 %collective-permute-start.1 = (bf16[16,1024]{1,0:T(8,128)(2,1)S(1)}, bf16[16,1024]{1,0:T(8,128)(2,1)S(1)}, u32[]{:S(2)}, u32[]{:S(2)}) collective-permute-start(bf16[16,1024]{1,0:T(8,128)(2,1)S(1)} %copy-done.2), channel_id=1, source_target_pairs={{0,8},{4,12},{8,0},{12,4},{1,9},{5,13},{9,1},{13,5},{2,10},{6,14},... | collective-permute-start | bytes 98312 | tf_op jit(solution)/shard_map/ppermute | solution.py:249
  17.1 1.5 collective-permute-start.2
  18.6 0.1 pad_add_fusion.1.where_ref
  18.7 24.6 %collective-permute-done.refs_1_ = bf16[16,1024]{1,0:T(8,128)(2,1)S(1)} collective-permute-done((bf16[16,1024]{1,0:T(8,128)(2,1)S(1)}, bf16[16,1024]{1,0:T(8,128)(2,1)S(1)}, u32[]{:S(2)}, u32[]{:S(2)}) %collective-permute-start) | collective-permute-done | bytes 32800 | tf_op jit(solution)/shard_map/ppermute | solution.py:249
  43.3 0.1 collective-permute-done.2.refs_3_
  43.4 1.8 %sum.1 = (bf16[4,592,128]{2,1,0:T(8,128)(2,1)}, bf16[64,1024]{1,0:T(8,128)(2,1)S(1)}) custom-call(s32[2]{0:T(128)S(1)} %pad_add_fusion.1.where_ref, bf16[16,592,128]{2,1,0:T(8,128)(2,1)S(1)} %all-to-all-done.got_ref, bf16[16,1024]{1,0:T(8,128)(2,1)S(1)} %copy-done, bf16[16,1024]{1,0:T(8,128)(2,1)S(1)} %collective-permute-done.refs_1_, ...), custom_call_target="tpu_custom_call" | custom-call | bytes 4194304 | tf_op jit(solution)/shard_map/sum/pallas_call | solution.py:39
  45.2 7.5 %all-to-all-start.1 = ((bf16[4,592,128]{2,1,0:T(8,128)(2,1)}), bf16[4,592,128]{2,1,0:T(8,128)(2,1)S(1)}, u32[]{:S(2)}, u32[]{:S(2)}) async-start(bf16[4,592,128]{2,1,0:T(8,128)(2,1)} %get-tuple-element.22), calls=%async_computation.1 | async-start | bytes 1212416 | tf_op jit(solution)/shard_map/all_to_all | solution.py:302
  52.7 4.9 %collective-permute-start.6 = (bf16[64,1024]{1,0:T(8,128)(2,1)S(1)}, bf16[64,1024]{1,0:T(8,128)(2,1)S(1)}, u32[]{:S(2)}, u32[]{:S(2)}) collective-permute-start(bf16[64,1024]{1,0:T(8,128)(2,1)S(1)} %get-tuple-element.23), channel_id=1, source_target_pairs={{48,16},{49,20},{50,24},{51,28},{52,17},{53,21},{54,25},{55,29},{5... | collective-permute-start | bytes 393224 | tf_op jit(solution)/shard_map/ppermute | solution.py:290
  57.6 1.3 collective-permute-start.5
  58.9 0.7 collective-permute-start.4
  59.6 1.3 collective-permute-start.3
  60.9 9.0 %collective-permute-done.6.refs_3_ = bf16[64,1024]{1,0:T(8,128)(2,1)S(1)} collective-permute-done((bf16[64,1024]{1,0:T(8,128)(2,1)S(1)}, bf16[64,1024]{1,0:T(8,128)(2,1)S(1)}, u32[]{:S(2)}, u32[]{:S(2)}) %collective-permute-start.6) | collective-permute-done | bytes 131104 | tf_op jit(solution)/shard_map/ppermute | solution.py:290
  70.0 2.7 %all-to-all-done.1.got_ref = bf16[4,592,128]{2,1,0:T(8,128)(2,1)S(1)} async-done(((bf16[4,592,128]{2,1,0:T(8,128)(2,1)}), bf16[4,592,128]{2,1,0:T(8,128)(2,1)S(1)}, u32[]{:S(2)}, u32[]{:S(2)}) %all-to-all-start.1) | async-done | bytes 606240 | tf_op jit(solution)/shard_map/all_to_all | solution.py:302
  72.7 1.9 %damp.1 = bf16[8,592,128]{2,1,0:T(8,128)(2,1)} custom-call(s32[2]{0:T(128)S(1)} %pad_add_fusion.1.where_ref, bf16[4,592,128]{2,1,0:T(8,128)(2,1)S(1)} %all-to-all-done.1.got_ref, bf16[64,1024]{1,0:T(8,128)(2,1)S(1)} %collective-permute-done.3.refs_0_, bf16[64,1024]{1,0:T(8,128)(2,1)S(1)} %collective-permute-done.4.refs_1_, ...), custom_call_target="tpu_custom_call" | custom-call | bytes 4194304 | tf_op jit(solution)/shard_map/damp/pallas_call | solution.py:39
  74.6 11.1 %all-to-all-start.2 = ((bf16[8,592,128]{2,1,0:T(8,128)(2,1)}), bf16[8,592,128]{2,1,0:T(8,128)(2,1)S(1)}, u32[]{:S(2)}, u32[]{:S(2)}) async-start(bf16[8,592,128]{2,1,0:T(8,128)(2,1)} %damp.1), calls=%async_computation.2 | async-start | bytes 2424832 | tf_op jit(solution)/shard_map/all_to_all | solution.py:310
  85.6 0.1 pad_add_fusion.where_ref
  85.7 15.9 %all-to-all-done.2.packed_ref = bf16[8,592,128]{2,1,0:T(8,128)(2,1)S(1)} async-done(((bf16[8,592,128]{2,1,0:T(8,128)(2,1)}), bf16[8,592,128]{2,1,0:T(8,128)(2,1)S(1)}, u32[]{:S(2)}, u32[]{:S(2)}) %all-to-all-start.2) | async-done | bytes 1212448 | tf_op jit(solution)/shard_map/all_to_all | solution.py:310
  101.7 15.2 %root.1 = (bf16[1024,1024]{1,0:T(8,128)(2,1)S(1)}, bf16[256,128]{1,0:T(8,128)(2,1)S(1)}, bf16[256,128]{1,0:T(8,128)(2,1)S(1)}, bf16[256,128]{1,0:T(8,128)(2,1)S(1)}, bf16[256,128]{1,0:T(8,128)(2,1)S(1)}) custom-call(s32[2]{0:T(128)S(1)} %pad_add_fusion.where_ref, bf16[8,592,128]{2,1,0:T(8,128)(2,1)S(1)} %all-to-all-done.2.packed_ref, ...), custom_call_target="tpu_custom_call" | custom-call | flops 12884901888 | bytes 4194304 | tf_op jit(solution)/shard_map/root/pallas_call | solution.py:39
  116.8 1.3 collective-permute-start.7
  118.1 1.6 %collective-permute-start.8 = (bf16[256,128]{1,0:T(8,128)(2,1)S(1)}, bf16[256,128]{1,0:T(8,128)(2,1)S(1)}, u32[]{:S(2)}, u32[]{:S(2)}) collective-permute-start(bf16[256,128]{1,0:T(8,128)(2,1)S(1)} %get-tuple-element.26), channel_id=1, source_target_pairs={{16,64},{20,65},{24,66},{28,67},{17,68},{21,69},{25,70},{29,71},{1... | collective-permute-start | bytes 196616 | tf_op jit(solution)/shard_map/ppermute | solution.py:327
  119.8 4.1 %collective-permute-start.9 = (bf16[256,128]{1,0:T(8,128)(2,1)S(1)}, bf16[256,128]{1,0:T(8,128)(2,1)S(1)}, u32[]{:S(2)}, u32[]{:S(2)}) collective-permute-start(bf16[256,128]{1,0:T(8,128)(2,1)S(1)} %get-tuple-element.27), channel_id=1, source_target_pairs={{16,128},{20,129},{24,130},{28,131},{17,132},{21,133},{25,134},{29... | collective-permute-start | bytes 196616 | tf_op jit(solution)/shard_map/ppermute | solution.py:327
  123.9 1.3 collective-permute-start.10
  125.2 1.9 %collective-permute-done.9.refs_2_ = bf16[256,128]{1,0:T(8,128)(2,1)S(1)} collective-permute-done((bf16[256,128]{1,0:T(8,128)(2,1)S(1)}, bf16[256,128]{1,0:T(8,128)(2,1)S(1)}, u32[]{:S(2)}, u32[]{:S(2)}) %collective-permute-start.9) | collective-permute-done | bytes 65568 | tf_op jit(solution)/shard_map/ppermute | solution.py:327
  127.2 4.1 %collective-permute-done.10.refs_3_ = bf16[256,128]{1,0:T(8,128)(2,1)S(1)} collective-permute-done((bf16[256,128]{1,0:T(8,128)(2,1)S(1)}, bf16[256,128]{1,0:T(8,128)(2,1)S(1)}, u32[]{:S(2)}, u32[]{:S(2)}) %collective-permute-start.10) | collective-permute-done | bytes 65568 | tf_op jit(solution)/shard_map/ppermute | solution.py:327
  131.2 1.3 left.1
  132.5 23.5 %all_to_all.20 = bf16[64,16,128]{2,1,0:T(8,128)(2,1)S(1)} all-to-all(bf16[64,16,128]{2,1,0:T(8,128)(2,1)S(1)} %bitcast.11), channel_id=1, replica_groups=mesh['zh'=4,'zl'=2,'xl'=2,'y'=4,'xh'=2,'c'=2] {'zh','zl','xl','y'}, dimensions={0} | all-to-all | bytes 524288 | tf_op jit(solution)/shard_map/all_to_all | solution.py:349
  156.0 0.1 copy.7
  156.1 0.7 reshape.11
  (15 shorter events, 0.0 us)
Async XLA Ops:
  5.4 7.5 %copy-start.3 = (bf16[16,1024]{1,0:T(8,128)(2,1)S(1)}, bf16[16,1024]{1,0:T(8,128)(2,1)}, u32[]{:S(2)}) copy-start(bf16[16,1024]{1,0:T(8,128)(2,1)} %get-tuple-element.19) | copy-start | bytes 98308
  5.4 9.0 %copy-start.2 = (bf16[16,1024]{1,0:T(8,128)(2,1)S(1)}, bf16[16,1024]{1,0:T(8,128)(2,1)}, u32[]{:S(2)}) copy-start(bf16[16,1024]{1,0:T(8,128)(2,1)} %get-tuple-element.20) | copy-start | bytes 98308
  5.4 11.7 %copy-start.1 = (bf16[16,1024]{1,0:T(8,128)(2,1)S(1)}, bf16[16,1024]{1,0:T(8,128)(2,1)}, u32[]{:S(2)}) copy-start(bf16[16,1024]{1,0:T(8,128)(2,1)} %get-tuple-element.21) | copy-start | bytes 98308
  5.4 37.9 %copy-start = (bf16[16,1024]{1,0:T(8,128)(2,1)S(1)}, bf16[16,1024]{1,0:T(8,128)(2,1)}, u32[]{:S(2)}) copy-start(bf16[16,1024]{1,0:T(8,128)(2,1)} %get-tuple-element.18.refs_0_) | copy-start | bytes 98308
  5.4 37.9 %all-to-all-start = ((bf16[16,592,128]{2,1,0:T(8,128)(2,1)}), bf16[16,592,128]{2,1,0:T(8,128)(2,1)S(1)}, u32[]{:S(2)}, u32[]{:S(2)}) async-start(bf16[16,592,128]{2,1,0:T(8,128)(2,1)} %get-tuple-element.17), calls=%async_computation | async-start | bytes 4849664 | tf_op jit(solution)/shard_map/all_to_all | solution.py:276
  12.9 30.4 %collective-permute-start = (bf16[16,1024]{1,0:T(8,128)(2,1)S(1)}, bf16[16,1024]{1,0:T(8,128)(2,1)S(1)}, u32[]{:S(2)}, u32[]{:S(2)}) collective-permute-start(bf16[16,1024]{1,0:T(8,128)(2,1)S(1)} %copy-done.3), channel_id=1, source_target_pairs={{0,4},{4,8},{8,12},{12,0},{1,5},{5,9},{9,13},{13,1},{2,6},{6,10},{... | collective-permute-start | bytes 98312 | tf_op jit(solution)/shard_map/ppermute | solution.py:249
  14.5 28.8 %collective-permute-start.1 = (bf16[16,1024]{1,0:T(8,128)(2,1)S(1)}, bf16[16,1024]{1,0:T(8,128)(2,1)S(1)}, u32[]{:S(2)}, u32[]{:S(2)}) collective-permute-start(bf16[16,1024]{1,0:T(8,128)(2,1)S(1)} %copy-done.2), channel_id=1, source_target_pairs={{0,8},{4,12},{8,0},{12,4},{1,9},{5,13},{9,1},{13,5},{2,10},{6,14},... | collective-permute-start | bytes 98312 | tf_op jit(solution)/shard_map/ppermute | solution.py:249
  17.1 26.2 %collective-permute-start.2 = (bf16[16,1024]{1,0:T(8,128)(2,1)S(1)}, bf16[16,1024]{1,0:T(8,128)(2,1)S(1)}, u32[]{:S(2)}, u32[]{:S(2)}) collective-permute-start(bf16[16,1024]{1,0:T(8,128)(2,1)S(1)} %copy-done.1), channel_id=1, source_target_pairs={{0,12},{4,0},{8,4},{12,8},{1,13},{5,1},{9,5},{13,9},{2,14},{6,2},{... | collective-permute-start | bytes 98312 | tf_op jit(solution)/shard_map/ppermute | solution.py:249
  45.2 27.5 %all-to-all-start.1 = ((bf16[4,592,128]{2,1,0:T(8,128)(2,1)}), bf16[4,592,128]{2,1,0:T(8,128)(2,1)S(1)}, u32[]{:S(2)}, u32[]{:S(2)}) async-start(bf16[4,592,128]{2,1,0:T(8,128)(2,1)} %get-tuple-element.22), calls=%async_computation.1 | async-start | bytes 1212416 | tf_op jit(solution)/shard_map/all_to_all | solution.py:302
  52.7 17.2 %collective-permute-start.6 = (bf16[64,1024]{1,0:T(8,128)(2,1)S(1)}, bf16[64,1024]{1,0:T(8,128)(2,1)S(1)}, u32[]{:S(2)}, u32[]{:S(2)}) collective-permute-start(bf16[64,1024]{1,0:T(8,128)(2,1)S(1)} %get-tuple-element.23), channel_id=1, source_target_pairs={{48,16},{49,20},{50,24},{51,28},{52,17},{53,21},{54,25},{55,29},{5... | collective-permute-start | bytes 393224 | tf_op jit(solution)/shard_map/ppermute | solution.py:290
  57.6 12.3 %collective-permute-start.5 = (bf16[64,1024]{1,0:T(8,128)(2,1)S(1)}, bf16[64,1024]{1,0:T(8,128)(2,1)S(1)}, u32[]{:S(2)}, u32[]{:S(2)}) collective-permute-start(bf16[64,1024]{1,0:T(8,128)(2,1)S(1)} %get-tuple-element.23), channel_id=1, source_target_pairs={{32,16},{33,20},{34,24},{35,28},{36,17},{37,21},{38,25},{39,29},{4... | collective-permute-start | bytes 393224 | tf_op jit(solution)/shard_map/ppermute | solution.py:290
  58.9 11.0 %collective-permute-start.4 = (bf16[64,1024]{1,0:T(8,128)(2,1)S(1)}, bf16[64,1024]{1,0:T(8,128)(2,1)S(1)}, u32[]{:S(2)}, u32[]{:S(2)}) collective-permute-start(bf16[64,1024]{1,0:T(8,128)(2,1)S(1)} %get-tuple-element.23), channel_id=1, source_target_pairs={{16,16},{17,20},{18,24},{19,28},{20,17},{21,21},{22,25},{23,29},{2... | collective-permute-start | bytes 393224 | tf_op jit(solution)/shard_map/ppermute | solution.py:290
  59.6 10.3 %collective-permute-start.3 = (bf16[64,1024]{1,0:T(8,128)(2,1)S(1)}, bf16[64,1024]{1,0:T(8,128)(2,1)S(1)}, u32[]{:S(2)}, u32[]{:S(2)}) collective-permute-start(bf16[64,1024]{1,0:T(8,128)(2,1)S(1)} %get-tuple-element.23), channel_id=1, source_target_pairs={{0,16},{1,20},{2,24},{3,28},{4,17},{5,21},{6,25},{7,29},{8,18},{9,... | collective-permute-start | bytes 393224 | tf_op jit(solution)/shard_map/ppermute | solution.py:290
  74.6 27.1 %all-to-all-start.2 = ((bf16[8,592,128]{2,1,0:T(8,128)(2,1)}), bf16[8,592,128]{2,1,0:T(8,128)(2,1)S(1)}, u32[]{:S(2)}, u32[]{:S(2)}) async-start(bf16[8,592,128]{2,1,0:T(8,128)(2,1)} %damp.1), calls=%async_computation.2 | async-start | bytes 2424832 | tf_op jit(solution)/shard_map/all_to_all | solution.py:310
  116.8 8.4 %collective-permute-start.7 = (bf16[256,128]{1,0:T(8,128)(2,1)S(1)}, bf16[256,128]{1,0:T(8,128)(2,1)S(1)}, u32[]{:S(2)}, u32[]{:S(2)}) collective-permute-start(bf16[256,128]{1,0:T(8,128)(2,1)S(1)} %get-tuple-element.25), channel_id=1, source_target_pairs={{16,0},{20,1},{24,2},{28,3},{17,4},{21,5},{25,6},{29,7},{18,8},{22... | collective-permute-start | bytes 196616 | tf_op jit(solution)/shard_map/ppermute | solution.py:327
  118.1 7.1 %collective-permute-start.8 = (bf16[256,128]{1,0:T(8,128)(2,1)S(1)}, bf16[256,128]{1,0:T(8,128)(2,1)S(1)}, u32[]{:S(2)}, u32[]{:S(2)}) collective-permute-start(bf16[256,128]{1,0:T(8,128)(2,1)S(1)} %get-tuple-element.26), channel_id=1, source_target_pairs={{16,64},{20,65},{24,66},{28,67},{17,68},{21,69},{25,70},{29,71},{1... | collective-permute-start | bytes 196616 | tf_op jit(solution)/shard_map/ppermute | solution.py:327
  119.8 7.4 %collective-permute-start.9 = (bf16[256,128]{1,0:T(8,128)(2,1)S(1)}, bf16[256,128]{1,0:T(8,128)(2,1)S(1)}, u32[]{:S(2)}, u32[]{:S(2)}) collective-permute-start(bf16[256,128]{1,0:T(8,128)(2,1)S(1)} %get-tuple-element.27), channel_id=1, source_target_pairs={{16,128},{20,129},{24,130},{28,131},{17,132},{21,133},{25,134},{29... | collective-permute-start | bytes 196616 | tf_op jit(solution)/shard_map/ppermute | solution.py:327
  123.9 7.3 %collective-permute-start.10 = (bf16[256,128]{1,0:T(8,128)(2,1)S(1)}, bf16[256,128]{1,0:T(8,128)(2,1)S(1)}, u32[]{:S(2)}, u32[]{:S(2)}) collective-permute-start(bf16[256,128]{1,0:T(8,128)(2,1)S(1)} %get-tuple-element.28), channel_id=1, source_target_pairs={{16,192},{20,193},{24,194},{28,195},{17,196},{21,197},{25,198},{29... | collective-permute-start | bytes 196616 | tf_op jit(solution)/shard_map/ppermute | solution.py:327

commit v5 on v4

--- a/solution.py
+++ b/solution.py
@@ -150,8 +150,10 @@
     put_halves(where_ref[0], out_ref, sum_halves(where_ref[0], got_ref))
 
 
-def damp_kernel(all_tokens, where_ref, got_ref, *refs):
-    out_ref = refs[-1]
+def damp_kernel(all_tokens, where_ref, got_ref, slab_ref, other_ref, out_ref, slabs_ref):
+    zl, rows = where_ref[2], NY * ROWS
+    slabs_ref[pl.ds(pl.multiple_of(zl * rows, rows), rows), :] = slab_ref[...]
+    slabs_ref[pl.ds(pl.multiple_of((1 - zl) * rows, rows), rows), :] = other_ref[...]
     piece = where_ref[0]
     halves = []
     squares = jnp.zeros((HALF, TILE), F32)
@@ -171,10 +173,7 @@
     put_halves(piece, out_ref, halves, terms)
 
 
-def root_kernel(where_ref, packed_ref, *refs):
-    slab_refs, refs = refs[:NZL * NXL], refs[NZL * NXL:]
-    root_ref, right_refs, refs = refs[0], refs[1:1 + NZH], refs[1 + NZH:]
-    scaled, iterate, iterate_b, square_b, cubic_b, right = refs
+def root_kernel(packed_ref, root_ref, scaled, iterate, iterate_b, square_b, cubic_b):
     terms = sum([packed_ref[n, PIECE:].astype(F32) for n in range(NZL * NY)])[HALVES:HALVES + TERMS]
     frob = jnp.sqrt(jnp.sum(terms, axis=0, keepdims=True)[:, 0:1])
     over_frob = 1.0 / frob
@@ -220,14 +219,15 @@
         if sweep < SWEEPS - 1:
             for s in tiles:
                 iterate_b[:, s] = iterate[:, s].astype(BF16)
-    zh, zl = where_ref[0], where_ref[1]
+
+def right_kernel(where_ref, root_ref, *refs):
+    slab_refs, right_refs, right = refs[:NXL], refs[NXL:NXL + NZH], refs[-1]
+    zh, zl, rows = where_ref[0], where_ref[1], NY * ROWS
     cols = root_ref[:, pl.ds(pl.multiple_of(zl * (NZH * TILE), NZH * TILE), NZH * TILE)]
-    for turn, ref in enumerate(slab_refs):
-        from_zl = lax.rem(zl + turn // NXL, NZL)
-        at = (from_zl * NXL + turn % NXL) * (NY * ROWS)
-        right[pl.ds(pl.multiple_of(at, NY * ROWS), NY * ROWS), :] = jnp.dot(
-            ref[...], cols, preferred_element_type=F32
-        ).astype(BF16)
+    for xl, ref in enumerate(slab_refs):
+        done = jnp.dot(ref[...], cols, preferred_element_type=F32).astype(BF16)
+        for n in range(NZL):
+            right[(n * NXL + xl) * rows:(n * NXL + xl + 1) * rows] = done[n * rows:(n + 1) * rows]
     for shift, ref in enumerate(right_refs):
         at = lax.rem(zh + shift, NZH) * TILE
         ref[...] = right[:, pl.ds(pl.multiple_of(at, TILE), TILE)]
@@ -241,8 +241,8 @@
     out_ref[...] = jnp.dot(root_ref[...], right[...], preferred_element_type=F32).astype(BF16)
 
 
-def place(zl, xl, y, block):
-    return ((zl * NXL + xl) * NY + y) * NBLOCK + block
+def place(xl, y, block):
+    return (xl * NY + y) * NBLOCK + block
 
 
 def turned(x, axes, size, shift):
@@ -252,7 +252,7 @@
 def local(acts, grads_out, gradient):
     all_tokens = acts.shape[0] * NZ * NXL * NY
     y = lax.axis_index("y")
-    where = jnp.stack((lax.axis_index(("zl", "y")), y))
+    where = jnp.stack((lax.axis_index(("zl", "y")), y, lax.axis_index("zl")))
 
     packed, *turns = call(
         gram_kernel,
@@ -284,53 +284,58 @@
         (where, got, *turns),
         specs=[SMEM] + [VMEM] * (1 + NY),
     )
+    other = turned(slab, "zl", NZL, 1)
+    got = lax.all_to_all(pieces, "zh", 0, 0, tiled=True)
+    pieces, slabs = call(
+        functools.partial(damp_kernel, float(all_tokens)),
+        "damp",
+        [
+            jax.ShapeDtypeStruct((NZL * NY, PIECE + REST, TILE), BF16),
+            jax.ShapeDtypeStruct((NZL * NY * ROWS, ORDER), BF16),
+        ],
+        (where, got, slab, other),
+        specs=[SMEM, VMEM, VMEM, VMEM],
+    )
     cells = [(k, i) for k in range(NBLOCK) for i in range(NBLOCK)]
-    count = NZL * NXL * NY * NBLOCK
     slabs = [
         lax.ppermute(
-            slab,
-            ("zl", "xl", "y", "xh", "c"),
-            [
-                (place((zl + turn) % NZL, xl, k, i), place(zl, 1, i, k))
-                for zl in range(NZL)
-                for k, i in cells
-            ],
+            slabs,
+            ("xl", "y", "xh", "c"),
+            [(place(xl, k, i), place(1, i, k)) for k, i in cells],
         )
-        for turn in range(NZL)
         for xl in range(NXL)
     ]
-    got = lax.all_to_all(pieces, "zh", 0, 0, tiled=True)
-    pieces = call(
-        functools.partial(damp_kernel, float(all_tokens)),
-        "damp",
-        jax.ShapeDtypeStruct((NZL * NY, PIECE + REST, TILE), BF16),
-        (where, got, *slabs),
-        specs=[SMEM, VMEM] + [pl.BlockSpec(memory_space=pl.ANY)] * len(slabs),
-    )
     packed = lax.all_to_all(pieces, ("zl", "y"), 0, 0, tiled=True)
 
     square_b = pltpu.VMEM((ORDER, ORDER), BF16)
     z_where = jnp.stack((lax.axis_index("zh"), lax.axis_index("zl")))
     right_done = jax.ShapeDtypeStruct((ZROWS, TILE), BF16)
-    root, *right_done = call(
+    root = call(
         root_kernel,
         "root",
-        [jax.ShapeDtypeStruct((ORDER, ORDER), BF16)] + [right_done] * NZH,
-        (z_where, packed, *slabs),
-        specs=[SMEM] + [VMEM] * (1 + len(slabs)),
-        scratch=[square_b, pltpu.VMEM((ORDER, ORDER), F32), square_b, square_b, square_b,
-                 pltpu.VMEM((ZROWS, NZH * TILE), BF16)],
+        jax.ShapeDtypeStruct((ORDER, ORDER), BF16),
+        (packed,),
+        scratch=[square_b, pltpu.VMEM((ORDER, ORDER), F32), square_b, square_b, square_b],
         flops=6 * SWEEPS * ORDER**3,
     )
-
+    right_done = call(
+        right_kernel,
+        "right",
+        [right_done] * NZH,
+        (z_where, root, *slabs),
+        specs=[SMEM] + [VMEM] * (1 + NXL),
+        scratch=[pltpu.VMEM((ZROWS, NZH * TILE), BF16)],
+        flops=2 * ORDER * ZROWS * NZH * TILE,
+    )
+
+    count = NXL * NY * NBLOCK
     right_done = [
         lax.ppermute(
             right_done[shift],
-            ("zh", "zl", "xl", "y", "xh", "c"),
+            ("zh", "xl", "y", "xh", "c"),
             [
-                (zh * count + place(zl, 1, i, k), (zh + shift) % NZH * count + place(zl, 0, k, i))
+                (zh * count + place(1, i, k), (zh + shift) % NZH * count + place(0, k, i))
                 for zh in range(NZH)
-                for zl in range(NZL)
                 for k, i in cells
             ],
         )

time: 157 us -> 154 us (0.981)
  starting transfers between devices: 48.2 us -> 34.6 us
  waiting for transfers between devices: 58.4 us -> 64.3 us
  blocking collectives: 23.5 us -> 28 us
    ppermute x3 -> x4, waiting for transfers between devices: 24.7 us -> 38.9 us  [turned(): return lax.ppermute(x, axes, [(n, (n + shift) % size) for n in range(size)])]
    ppermute x8 -> x6, waiting for transfers between devices: 15 us -> 4.07 us  [the longest x4 4.07 us: local(): lax.ppermute(right_done[shift], ('zh', 'xl', 'y', 'xh', 'c'), [(zh * coun...]
    ppermute x8 -> x6, starting transfers between devices: 16.5 us -> 7.31 us  [the longest x4 5.17 us: local(): lax.ppermute(right_done[shift], ('zh', 'xl', 'y', 'xh', 'c'), [(zh * coun...]
    all_to_all x1, starting transfers between devices: 11.1 us -> 3.62 us  [local(): packed = lax.all_to_all(pieces, ('zl', 'y'), 0, 0, tiled=True)]
    all_to_all x1, blocking collectives: 23.5 us -> 28 us  [local(): returned = lax.all_to_all(result, DP, 0, 0, tiled=True)]
    ppermute x3 -> x4, starting transfers between devices: 5.68 us -> 8.69 us  [turned(): return lax.ppermute(x, axes, [(n, (n + shift) % size) for n in range(size)])]
    all_to_all x1, waiting for transfers between devices: 15.9 us -> 18.6 us  [local(): packed = lax.all_to_all(pieces, ('zl', 'y'), 0, 0, tiled=True)]
    pallas_call x5 -> x6, Pallas kernels: 25.6 us -> 25.2 us  [call(): pl.pallas_call(kernel, out_shape=out_shape, scratch_shapes=list(scratch),...]
  transfers between devices with their start and end apart: 14 -> 13, of which waited for: 7 -> 8; matrix products, arithmetic and copies ran while one was open for 0% -> 0% of each run, Pallas kernels for 0% -> 9%
where the time goes in v5:
time: 154 us; the launch traced here: 153 us
  waiting for transfers between devices  64.3 us (42%)
  starting transfers between devices  34.6 us (22%)
  blocking collectives  28 us (18%)
  Pallas kernels  25.2 us (16%)
    ppermute x4, waiting for transfers between devices, turned(): return lax.ppermute(x, axes, [(n, (n + shift) % size) for n in range(size)])  38.9 us
    all_to_all x1, blocking collectives, local(): returned = lax.all_to_all(result, DP, 0, 0, tiled=True)  28 us
    pallas_call x6, Pallas kernels, call(): pl.pallas_call(kernel, out_shape=out_shape, scratch_shapes=list(scratch),...  25.2 us
    all_to_all x1, waiting for transfers between devices, local(): packed = lax.all_to_all(pieces, ('zl', 'y'), 0, 0, tiled=True)  18.6 us
    ppermute x4, starting transfers between devices, turned(): return lax.ppermute(x, axes, [(n, (n + shift) % size) for n in range(size)])  8.69 us
    all_to_all x1, starting transfers between devices, local(): got = lax.all_to_all(pieces, 'zh', 0, 0, tiled=True)  7.53 us
    all_to_all x1, starting transfers between devices, local(): got = lax.all_to_all(packed, ('zl', 'xl', 'y'), 0, 0, tiled=True)  7.45 us
    ppermute x4, starting transfers between devices, local(): lax.ppermute(right_done[shift], ('zh', 'xl', 'y', 'xh', 'c'), [(zh * coun...  5.17 us
  transfers between devices with their start and end apart: 13, of which 8 were waited for; matrix products, arithmetic and copies ran while one was open for 0% of the time, Pallas kernels for 9%

profile of v5, /device:TPU:2, one launch (start us, length us, event | category | flops | bytes accessed | tf_op | source)
XLA Modules:
  0.0 153.3 jit_solution(13341454051258032703)
XLA Ops:
  0.0 5.4 %gram.1 = (bf16[16,592,128]{2,1,0:T(8,128)(2,1)}, bf16[16,1024]{1,0:T(8,128)(2,1)}, bf16[16,1024]{1,0:T(8,128)(2,1)}, bf16[16,1024]{1,0:T(8,128)(2,1)}, bf16[16,1024]{1,0:T(8,128)(2,1)}) custom-call(s32[1]{0:T(128)} %bitcast.3.y_ref, bf16[768,1024]{1,0:T(8,128)(2,1)} %acts_ref.1, bf16[768,1024]{1,0:T(8,128)(2,1)} %grads_ref.1, f32[1,16,4096]{2,1,0:T(8,128)} %gradient_ref.1), custom_call_target="tpu_custom_call" | custom-call | flops 3221225472 | bytes 4194304 | tf_op jit(solution)/shard_map/gram/pallas_call | solution.py:39
  5.4 7.5 %all-to-all-start = ((bf16[16,592,128]{2,1,0:T(8,128)(2,1)}), bf16[16,592,128]{2,1,0:T(8,128)(2,1)S(1)}, u32[]{:S(2)}, u32[]{:S(2)}) async-start(bf16[16,592,128]{2,1,0:T(8,128)(2,1)} %get-tuple-element.18), calls=%async_computation | async-start | bytes 4849664 | tf_op jit(solution)/shard_map/all_to_all | solution.py:276
  12.9 1.5 %collective-permute-start = (bf16[16,1024]{1,0:T(8,128)(2,1)S(1)}, bf16[16,1024]{1,0:T(8,128)(2,1)S(1)}, u32[]{:S(2)}, u32[]{:S(2)}) collective-permute-start(bf16[16,1024]{1,0:T(8,128)(2,1)S(1)} %copy-done.3), channel_id=1, source_target_pairs={{0,4},{4,8},{8,12},{12,0},{1,5},{5,9},{9,13},{13,1},{2,6},{6,10},{... | collective-permute-start | bytes 98312 | tf_op jit(solution)/shard_map/ppermute | solution.py:249
  14.5 2.7 %collective-permute-start.1 = (bf16[16,1024]{1,0:T(8,128)(2,1)S(1)}, bf16[16,1024]{1,0:T(8,128)(2,1)S(1)}, u32[]{:S(2)}, u32[]{:S(2)}) collective-permute-start(bf16[16,1024]{1,0:T(8,128)(2,1)S(1)} %copy-done.2), channel_id=1, source_target_pairs={{0,8},{4,12},{8,0},{12,4},{1,9},{5,13},{9,1},{13,5},{2,10},{6,14},... | collective-permute-start | bytes 98312 | tf_op jit(solution)/shard_map/ppermute | solution.py:249
  17.1 1.5 collective-permute-start.2
  18.6 0.1 pad_add_fusion.1.where_ref
  18.7 24.6 %collective-permute-done.refs_1_ = bf16[16,1024]{1,0:T(8,128)(2,1)S(1)} collective-permute-done((bf16[16,1024]{1,0:T(8,128)(2,1)S(1)}, bf16[16,1024]{1,0:T(8,128)(2,1)S(1)}, u32[]{:S(2)}, u32[]{:S(2)}) %collective-permute-start) | collective-permute-done | bytes 32800 | tf_op jit(solution)/shard_map/ppermute | solution.py:249
  43.3 0.1 collective-permute-done.2.refs_3_
  43.4 1.8 %sum.1 = (bf16[4,592,128]{2,1,0:T(8,128)(2,1)}, bf16[64,1024]{1,0:T(8,128)(2,1)S(1)}) custom-call(s32[3]{0:T(128)S(1)} %pad_add_fusion.1.where_ref, bf16[16,592,128]{2,1,0:T(8,128)(2,1)S(1)} %all-to-all-done.got_ref, bf16[16,1024]{1,0:T(8,128)(2,1)S(1)} %copy-done, bf16[16,1024]{1,0:T(8,128)(2,1)S(1)} %collective-permute-done.refs_1_, ...), custom_call_target="tpu_custom_call" | custom-call | bytes 4194304 | tf_op jit(solution)/shard_map/sum/pallas_call | solution.py:39
  45.2 7.5 %all-to-all-start.1 = ((bf16[4,592,128]{2,1,0:T(8,128)(2,1)}), bf16[4,592,128]{2,1,0:T(8,128)(2,1)S(1)}, u32[]{:S(2)}, u32[]{:S(2)}) async-start(bf16[4,592,128]{2,1,0:T(8,128)(2,1)} %get-tuple-element.23), calls=%async_computation.1 | async-start | bytes 1212416 | tf_op jit(solution)/shard_map/all_to_all | solution.py:288
  52.7 3.0 %collective-permute-start.3 = (bf16[64,1024]{1,0:T(8,128)(2,1)S(1)}, bf16[64,1024]{1,0:T(8,128)(2,1)S(1)}, u32[]{:S(2)}, u32[]{:S(2)}) collective-permute-start(bf16[64,1024]{1,0:T(8,128)(2,1)S(1)} %get-tuple-element.24.slab_ref), channel_id=1, source_target_pairs={{0,32},{32,0},{1,33},{33,1},{2,34},{34,2},{3,35},{35,3},{4,36},{36... | collective-permute-start | bytes 393224 | tf_op jit(solution)/shard_map/ppermute | solution.py:249
  55.7 14.2 %collective-permute-done.3.other_ref = bf16[64,1024]{1,0:T(8,128)(2,1)S(1)} collective-permute-done((bf16[64,1024]{1,0:T(8,128)(2,1)S(1)}, bf16[64,1024]{1,0:T(8,128)(2,1)S(1)}, u32[]{:S(2)}, u32[]{:S(2)}) %collective-permute-start.3) | collective-permute-done | bytes 131104 | tf_op jit(solution)/shard_map/ppermute | solution.py:249
  69.9 2.7 %all-to-all-done.1.got_ref = bf16[4,592,128]{2,1,0:T(8,128)(2,1)S(1)} async-done(((bf16[4,592,128]{2,1,0:T(8,128)(2,1)}), bf16[4,592,128]{2,1,0:T(8,128)(2,1)S(1)}, u32[]{:S(2)}, u32[]{:S(2)}) %all-to-all-start.1) | async-done | bytes 606240 | tf_op jit(solution)/shard_map/all_to_all | solution.py:288
  72.7 1.9 %damp.1 = (bf16[8,592,128]{2,1,0:T(8,128)(2,1)}, bf16[128,1024]{1,0:T(8,128)(2,1)S(1)}) custom-call(s32[3]{0:T(128)S(1)} %pad_add_fusion.1.where_ref, bf16[4,592,128]{2,1,0:T(8,128)(2,1)S(1)} %all-to-all-done.1.got_ref, bf16[64,1024]{1,0:T(8,128)(2,1)S(1)} %get-tuple-element.24.slab_ref, bf16[64,1024]{1,0:T(8,128)(2,1)S(1)} %collective-permute-done.3.other_ref), custom_call_target="tpu_custom_call" | custom-call | bytes 4194304 | tf_op jit(solution)/shard_map/damp/pallas_call | solution.py:39
  74.6 3.6 %all-to-all-start.2 = ((bf16[8,592,128]{2,1,0:T(8,128)(2,1)}), bf16[8,592,128]{2,1,0:T(8,128)(2,1)S(1)}, u32[]{:S(2)}, u32[]{:S(2)}) async-start(bf16[8,592,128]{2,1,0:T(8,128)(2,1)} %get-tuple-element.25), calls=%async_computation.2 | async-start | bytes 2424832 | tf_op jit(solution)/shard_map/all_to_all | solution.py:308
  78.2 0.1 pad_add_fusion.where_ref
  78.3 0.7 collective-permute-start.5
  78.9 1.5 collective-permute-start.4
  80.4 18.6 %all-to-all-done.2.packed_ref = bf16[8,592,128]{2,1,0:T(8,128)(2,1)S(1)} async-done(((bf16[8,592,128]{2,1,0:T(8,128)(2,1)}), bf16[8,592,128]{2,1,0:T(8,128)(2,1)S(1)}, u32[]{:S(2)}, u32[]{:S(2)}) %all-to-all-start.2) | async-done | bytes 1212448 | tf_op jit(solution)/shard_map/all_to_all | solution.py:308
  99.0 13.8 %root.1.root_ref = bf16[1024,1024]{1,0:T(8,128)(2,1)S(1)} custom-call(bf16[8,592,128]{2,1,0:T(8,128)(2,1)S(1)} %all-to-all-done.2.packed_ref), custom_call_target="tpu_custom_call" | custom-call | flops 12884901888 | bytes 4194304 | tf_op jit(solution)/shard_map/root/pallas_call | solution.py:39
  112.8 1.1 right.1
  113.9 1.3 collective-permute-start.6
  115.2 1.3 collective-permute-start.7
  116.5 1.3 collective-permute-start.8
  117.8 1.3 collective-permute-start.9
  119.1 0.5 collective-permute-done.7.refs_1_
  119.5 1.5 %collective-permute-done.8.refs_2_ = bf16[256,128]{1,0:T(8,128)(2,1)S(1)} collective-permute-done((bf16[256,128]{1,0:T(8,128)(2,1)S(1)}, bf16[256,128]{1,0:T(8,128)(2,1)S(1)}, u32[]{:S(2)}, u32[]{:S(2)}) %collective-permute-start.8) | collective-permute-done | bytes 65568 | tf_op jit(solution)/shard_map/ppermute | solution.py:333
  121.1 2.1 %collective-permute-done.9.refs_3_ = bf16[256,128]{1,0:T(8,128)(2,1)S(1)} collective-permute-done((bf16[256,128]{1,0:T(8,128)(2,1)S(1)}, bf16[256,128]{1,0:T(8,128)(2,1)S(1)}, u32[]{:S(2)}, u32[]{:S(2)}) %collective-permute-start.9) | collective-permute-done | bytes 65568 | tf_op jit(solution)/shard_map/ppermute | solution.py:333
  123.2 1.3 left.1
  124.4 28.0 %all_to_all.20 = bf16[64,16,128]{2,1,0:T(8,128)(2,1)S(1)} all-to-all(bf16[64,16,128]{2,1,0:T(8,128)(2,1)S(1)} %bitcast.11), channel_id=1, replica_groups=mesh['zh'=4,'zl'=2,'xl'=2,'y'=4,'xh'=2,'c'=2] {'zh','zl','xl','y'}, dimensions={0} | all-to-all | bytes 524288 | tf_op jit(solution)/shard_map/all_to_all | solution.py:354
  152.5 0.1 copy.7
  152.6 0.7 reshape.11
  (14 shorter events, 0.0 us)
Async XLA Ops:
  5.4 7.5 %copy-start.3 = (bf16[16,1024]{1,0:T(8,128)(2,1)S(1)}, bf16[16,1024]{1,0:T(8,128)(2,1)}, u32[]{:S(2)}) copy-start(bf16[16,1024]{1,0:T(8,128)(2,1)} %get-tuple-element.20) | copy-start | bytes 98308
  5.4 9.0 %copy-start.2 = (bf16[16,1024]{1,0:T(8,128)(2,1)S(1)}, bf16[16,1024]{1,0:T(8,128)(2,1)}, u32[]{:S(2)}) copy-start(bf16[16,1024]{1,0:T(8,128)(2,1)} %get-tuple-element.21) | copy-start | bytes 98308
  5.4 11.7 %copy-start.1 = (bf16[16,1024]{1,0:T(8,128)(2,1)S(1)}, bf16[16,1024]{1,0:T(8,128)(2,1)}, u32[]{:S(2)}) copy-start(bf16[16,1024]{1,0:T(8,128)(2,1)} %get-tuple-element.22) | copy-start | bytes 98308
  5.4 37.9 %copy-start = (bf16[16,1024]{1,0:T(8,128)(2,1)S(1)}, bf16[16,1024]{1,0:T(8,128)(2,1)}, u32[]{:S(2)}) copy-start(bf16[16,1024]{1,0:T(8,128)(2,1)} %get-tuple-element.19.refs_0_) | copy-start | bytes 98308
  5.4 37.9 %all-to-all-start = ((bf16[16,592,128]{2,1,0:T(8,128)(2,1)}), bf16[16,592,128]{2,1,0:T(8,128)(2,1)S(1)}, u32[]{:S(2)}, u32[]{:S(2)}) async-start(bf16[16,592,128]{2,1,0:T(8,128)(2,1)} %get-tuple-element.18), calls=%async_computation | async-start | bytes 4849664 | tf_op jit(solution)/shard_map/all_to_all | solution.py:276
  12.9 30.4 %collective-permute-start = (bf16[16,1024]{1,0:T(8,128)(2,1)S(1)}, bf16[16,1024]{1,0:T(8,128)(2,1)S(1)}, u32[]{:S(2)}, u32[]{:S(2)}) collective-permute-start(bf16[16,1024]{1,0:T(8,128)(2,1)S(1)} %copy-done.3), channel_id=1, source_target_pairs={{0,4},{4,8},{8,12},{12,0},{1,5},{5,9},{9,13},{13,1},{2,6},{6,10},{... | collective-permute-start | bytes 98312 | tf_op jit(solution)/shard_map/ppermute | solution.py:249
  14.5 28.8 %collective-permute-start.1 = (bf16[16,1024]{1,0:T(8,128)(2,1)S(1)}, bf16[16,1024]{1,0:T(8,128)(2,1)S(1)}, u32[]{:S(2)}, u32[]{:S(2)}) collective-permute-start(bf16[16,1024]{1,0:T(8,128)(2,1)S(1)} %copy-done.2), channel_id=1, source_target_pairs={{0,8},{4,12},{8,0},{12,4},{1,9},{5,13},{9,1},{13,5},{2,10},{6,14},... | collective-permute-start | bytes 98312 | tf_op jit(solution)/shard_map/ppermute | solution.py:249
  17.1 26.2 %collective-permute-start.2 = (bf16[16,1024]{1,0:T(8,128)(2,1)S(1)}, bf16[16,1024]{1,0:T(8,128)(2,1)S(1)}, u32[]{:S(2)}, u32[]{:S(2)}) collective-permute-start(bf16[16,1024]{1,0:T(8,128)(2,1)S(1)} %copy-done.1), channel_id=1, source_target_pairs={{0,12},{4,0},{8,4},{12,8},{1,13},{5,1},{9,5},{13,9},{2,14},{6,2},{... | collective-permute-start | bytes 98312 | tf_op jit(solution)/shard_map/ppermute | solution.py:249
  45.2 27.5 %all-to-all-start.1 = ((bf16[4,592,128]{2,1,0:T(8,128)(2,1)}), bf16[4,592,128]{2,1,0:T(8,128)(2,1)S(1)}, u32[]{:S(2)}, u32[]{:S(2)}) async-start(bf16[4,592,128]{2,1,0:T(8,128)(2,1)} %get-tuple-element.23), calls=%async_computation.1 | async-start | bytes 1212416 | tf_op jit(solution)/shard_map/all_to_all | solution.py:288
  52.7 17.2 %collective-permute-start.3 = (bf16[64,1024]{1,0:T(8,128)(2,1)S(1)}, bf16[64,1024]{1,0:T(8,128)(2,1)S(1)}, u32[]{:S(2)}, u32[]{:S(2)}) collective-permute-start(bf16[64,1024]{1,0:T(8,128)(2,1)S(1)} %get-tuple-element.24.slab_ref), channel_id=1, source_target_pairs={{0,32},{32,0},{1,33},{33,1},{2,34},{34,2},{3,35},{35,3},{4,36},{36... | collective-permute-start | bytes 393224 | tf_op jit(solution)/shard_map/ppermute | solution.py:249
  74.6 24.4 %all-to-all-start.2 = ((bf16[8,592,128]{2,1,0:T(8,128)(2,1)}), bf16[8,592,128]{2,1,0:T(8,128)(2,1)S(1)}, u32[]{:S(2)}, u32[]{:S(2)}) async-start(bf16[8,592,128]{2,1,0:T(8,128)(2,1)} %get-tuple-element.25), calls=%async_computation.2 | async-start | bytes 2424832 | tf_op jit(solution)/shard_map/all_to_all | solution.py:308
  78.3 34.5 %collective-permute-start.5 = (bf16[128,1024]{1,0:T(8,128)(2,1)S(1)}, bf16[128,1024]{1,0:T(8,128)(2,1)S(1)}, u32[]{:S(2)}, u32[]{:S(2)}) collective-permute-start(bf16[128,1024]{1,0:T(8,128)(2,1)S(1)} %get-tuple-element.26), channel_id=1, source_target_pairs={{16,16},{17,20},{18,24},{19,28},{20,17},{21,21},{22,25},{23,29},{2... | collective-permute-start | bytes 786440 | tf_op jit(solution)/shard_map/ppermute | solution.py:301
  78.9 33.8 %collective-permute-start.4 = (bf16[128,1024]{1,0:T(8,128)(2,1)S(1)}, bf16[128,1024]{1,0:T(8,128)(2,1)S(1)}, u32[]{:S(2)}, u32[]{:S(2)}) collective-permute-start(bf16[128,1024]{1,0:T(8,128)(2,1)S(1)} %get-tuple-element.26), channel_id=1, source_target_pairs={{0,16},{1,20},{2,24},{3,28},{4,17},{5,21},{6,25},{7,29},{8,18},{9,... | collective-permute-start | bytes 786440 | tf_op jit(solution)/shard_map/ppermute | solution.py:301
  113.9 5.2 %collective-permute-start.6 = (bf16[256,128]{1,0:T(8,128)(2,1)S(1)}, bf16[256,128]{1,0:T(8,128)(2,1)S(1)}, u32[]{:S(2)}, u32[]{:S(2)}) collective-permute-start(bf16[256,128]{1,0:T(8,128)(2,1)S(1)} %get-tuple-element.27), channel_id=1, source_target_pairs={{16,0},{20,1},{24,2},{28,3},{17,4},{21,5},{25,6},{29,7},{18,8},{22... | collective-permute-start | bytes 196616 | tf_op jit(solution)/shard_map/ppermute | solution.py:333
  115.2 4.4 %collective-permute-start.7 = (bf16[256,128]{1,0:T(8,128)(2,1)S(1)}, bf16[256,128]{1,0:T(8,128)(2,1)S(1)}, u32[]{:S(2)}, u32[]{:S(2)}) collective-permute-start(bf16[256,128]{1,0:T(8,128)(2,1)S(1)} %get-tuple-element.28), channel_id=1, source_target_pairs={{16,64},{20,65},{24,66},{28,67},{17,68},{21,69},{25,70},{29,71},{1... | collective-permute-start | bytes 196616 | tf_op jit(solution)/shard_map/ppermute | solution.py:333
  116.5 4.6 %collective-permute-start.8 = (bf16[256,128]{1,0:T(8,128)(2,1)S(1)}, bf16[256,128]{1,0:T(8,128)(2,1)S(1)}, u32[]{:S(2)}, u32[]{:S(2)}) collective-permute-start(bf16[256,128]{1,0:T(8,128)(2,1)S(1)} %get-tuple-element.29), channel_id=1, source_target_pairs={{16,128},{20,129},{24,130},{28,131},{17,132},{21,133},{25,134},{29... | collective-permute-start | bytes 196616 | tf_op jit(solution)/shard_map/ppermute | solution.py:333
  117.8 5.4 %collective-permute-start.9 = (bf16[256,128]{1,0:T(8,128)(2,1)S(1)}, bf16[256,128]{1,0:T(8,128)(2,1)S(1)}, u32[]{:S(2)}, u32[]{:S(2)}) collective-permute-start(bf16[256,128]{1,0:T(8,128)(2,1)S(1)} %get-tuple-element.30), channel_id=1, source_target_pairs={{16,192},{20,193},{24,194},{28,195},{17,196},{21,197},{25,198},{29... | collective-permute-start | bytes 196616 | tf_op jit(solution)/shard_map/ppermute | solution.py:333

commit v6 on v5

--- a/solution.py
+++ b/solution.py
@@ -150,10 +150,7 @@
     put_halves(where_ref[0], out_ref, sum_halves(where_ref[0], got_ref))
 
 
-def damp_kernel(all_tokens, where_ref, got_ref, slab_ref, other_ref, out_ref, slabs_ref):
-    zl, rows = where_ref[2], NY * ROWS
-    slabs_ref[pl.ds(pl.multiple_of(zl * rows, rows), rows), :] = slab_ref[...]
-    slabs_ref[pl.ds(pl.multiple_of((1 - zl) * rows, rows), rows), :] = other_ref[...]
+def damp_kernel(all_tokens, where_ref, got_ref, other_ref, out_ref):
     piece = where_ref[0]
     halves = []
     squares = jnp.zeros((HALF, TILE), F32)
@@ -173,11 +170,14 @@
     put_halves(piece, out_ref, halves, terms)
 
 
-def root_kernel(packed_ref, root_ref, scaled, iterate, iterate_b, square_b, cubic_b):
+def scale_kernel(where_ref, packed_ref, slab_ref, other_ref, scaled, over_ref, slabs_ref):
+    zl, rows = where_ref[2], NY * ROWS
+    slabs_ref[pl.ds(pl.multiple_of(zl * rows, rows), rows), :] = slab_ref[...]
+    slabs_ref[pl.ds(pl.multiple_of((1 - zl) * rows, rows), rows), :] = other_ref[...]
     terms = sum([packed_ref[n, PIECE:].astype(F32) for n in range(NZL * NY)])[HALVES:HALVES + TERMS]
     frob = jnp.sqrt(jnp.sum(terms, axis=0, keepdims=True)[:, 0:1])
     over_frob = 1.0 / frob
-    over_root = 1.0 / jnp.sqrt(frob)
+    over_ref[...] = jnp.broadcast_to(1.0 / jnp.sqrt(frob), over_ref.shape)
     for r, c in PAIRS:
         parts = []
         for half in range(2):
@@ -191,6 +191,10 @@
         scaled[r * TILE:(r + 1) * TILE, c * TILE:(c + 1) * TILE] = block
         if r != c:
             scaled[c * TILE:(c + 1) * TILE, r * TILE:(r + 1) * TILE] = block.T
+
+
+def root_kernel(scaled, over_ref, root_ref, iterate, iterate_b, square_b, cubic_b):
+    over_root = over_ref[0:1, 0:1]
     width = 2 * TILE
     tiles = [slice(n, n + width) for n in range(0, ORDER, width)]
     for s in tiles:
@@ -286,14 +290,24 @@
     )
     other = turned(slab, "zl", NZL, 1)
     got = lax.all_to_all(pieces, "zh", 0, 0, tiled=True)
-    pieces, slabs = call(
+    pieces = call(
         functools.partial(damp_kernel, float(all_tokens)),
         "damp",
+        jax.ShapeDtypeStruct((NZL * NY, PIECE + REST, TILE), BF16),
+        (where, got, other),
+        specs=[SMEM, VMEM, pl.BlockSpec(memory_space=pl.ANY)],
+    )
+    packed = lax.all_to_all(pieces, ("zl", "y"), 0, 0, tiled=True)
+
+    scaled, over_root, slabs = call(
+        scale_kernel,
+        "scale",
         [
-            jax.ShapeDtypeStruct((NZL * NY, PIECE + REST, TILE), BF16),
+            jax.ShapeDtypeStruct((ORDER, ORDER), BF16),
+            jax.ShapeDtypeStruct((8, TILE), F32),
             jax.ShapeDtypeStruct((NZL * NY * ROWS, ORDER), BF16),
         ],
-        (where, got, slab, other),
+        (where, packed, slab, other),
         specs=[SMEM, VMEM, VMEM, VMEM],
     )
     cells = [(k, i) for k in range(NBLOCK) for i in range(NBLOCK)]
@@ -305,7 +319,6 @@
         )
         for xl in range(NXL)
     ]
-    packed = lax.all_to_all(pieces, ("zl", "y"), 0, 0, tiled=True)
 
     square_b = pltpu.VMEM((ORDER, ORDER), BF16)
     z_where = jnp.stack((lax.axis_index("zh"), lax.axis_index("zl")))
@@ -314,8 +327,8 @@
         root_kernel,
         "root",
         jax.ShapeDtypeStruct((ORDER, ORDER), BF16),
-        (packed,),
-        scratch=[square_b, pltpu.VMEM((ORDER, ORDER), F32), square_b, square_b, square_b],
+        (scaled, over_root),
+        scratch=[pltpu.VMEM((ORDER, ORDER), F32), square_b, square_b, square_b],
         flops=6 * SWEEPS * ORDER**3,
     )
     right_done = call(

time: 154 us -> 158 us (1.026)
  starting transfers between devices: 34.6 us -> 43 us
  waiting for transfers between devices: 64.3 us -> 59.1 us
    ppermute x4, starting transfers between devices: 5.17 us -> 13.6 us  [local(): lax.ppermute(right_done[shift], ('zh', 'xl', 'y', 'xh', 'c'), [(zh * coun...]
    all_to_all x1, waiting for transfers between devices: 18.6 us -> 11.4 us  [local(): packed = lax.all_to_all(pieces, ('zl', 'y'), 0, 0, tiled=True)]
    ppermute x4, waiting for transfers between devices: 4.07 us -> 6.03 us  [local(): lax.ppermute(right_done[shift], ('zh', 'xl', 'y', 'xh', 'c'), [(zh * coun...]
    pallas_call x6 -> x7, Pallas kernels: 25.2 us -> 25.9 us  [call(): pl.pallas_call(kernel, out_shape=out_shape, scratch_shapes=list(scratch),...]
  transfers between devices with their start and end apart: 13 -> 13, of which waited for: 8 -> 7; matrix products, arithmetic and copies ran while one was open for 0% -> 0% of each run, Pallas kernels for 9% -> 8%
where the time goes in v6:
time: 158 us
  waiting for transfers between devices  59.1 us (37%)
  starting transfers between devices  43 us (27%)
  blocking collectives  28.7 us (18%)
  Pallas kernels  25.9 us (16%)
    ppermute x4, waiting for transfers between devices, turned(): return lax.ppermute(x, axes, [(n, (n + shift) % size) for n in range(size)])  38.9 us
    all_to_all x1, blocking collectives, local(): returned = lax.all_to_all(result, DP, 0, 0, tiled=True)  28.7 us
    pallas_call x7, Pallas kernels, call(): pl.pallas_call(kernel, out_shape=out_shape, scratch_shapes=list(scratch),...  25.9 us
    ppermute x4, starting transfers between devices, local(): lax.ppermute(right_done[shift], ('zh', 'xl', 'y', 'xh', 'c'), [(zh * coun...  13.6 us
    all_to_all x1, waiting for transfers between devices, local(): packed = lax.all_to_all(pieces, ('zl', 'y'), 0, 0, tiled=True)  11.4 us
    ppermute x4, starting transfers between devices, turned(): return lax.ppermute(x, axes, [(n, (n + shift) % size) for n in range(size)])  8.69 us
    all_to_all x1, starting transfers between devices, local(): got = lax.all_to_all(pieces, 'zh', 0, 0, tiled=True)  7.53 us
    all_to_all x1, starting transfers between devices, local(): got = lax.all_to_all(packed, ('zl', 'xl', 'y'), 0, 0, tiled=True)  7.45 us
  transfers between devices with their start and end apart: 13, of which 7 were waited for; matrix products, arithmetic and copies ran while one was open for 0% of the time, Pallas kernels for 8%

profile of v6, /device:TPU:2, one launch (start us, length us, event | category | flops | bytes accessed | tf_op | source)
XLA Modules:
  0.0 157.9 jit_solution(6798078385311684850)
XLA Ops:
  0.0 5.4 %gram.1 = (bf16[16,592,128]{2,1,0:T(8,128)(2,1)}, bf16[16,1024]{1,0:T(8,128)(2,1)}, bf16[16,1024]{1,0:T(8,128)(2,1)}, bf16[16,1024]{1,0:T(8,128)(2,1)}, bf16[16,1024]{1,0:T(8,128)(2,1)}) custom-call(s32[1]{0:T(128)} %bitcast.3.y_ref, bf16[768,1024]{1,0:T(8,128)(2,1)} %acts_ref.1, bf16[768,1024]{1,0:T(8,128)(2,1)} %grads_ref.1, f32[1,16,4096]{2,1,0:T(8,128)} %gradient_ref.1), custom_call_target="tpu_custom_call" | custom-call | flops 3221225472 | bytes 4194304 | tf_op jit(solution)/shard_map/gram/pallas_call | solution.py:39
  5.4 7.5 %all-to-all-start = ((bf16[16,592,128]{2,1,0:T(8,128)(2,1)}), bf16[16,592,128]{2,1,0:T(8,128)(2,1)S(1)}, u32[]{:S(2)}, u32[]{:S(2)}) async-start(bf16[16,592,128]{2,1,0:T(8,128)(2,1)} %get-tuple-element.19), calls=%async_computation | async-start | bytes 4849664 | tf_op jit(solution)/shard_map/all_to_all | solution.py:280
  12.9 1.5 collective-permute-start
  14.5 2.7 %collective-permute-start.1 = (bf16[16,1024]{1,0:T(8,128)(2,1)S(1)}, bf16[16,1024]{1,0:T(8,128)(2,1)S(1)}, u32[]{:S(2)}, u32[]{:S(2)}) collective-permute-start(bf16[16,1024]{1,0:T(8,128)(2,1)S(1)} %copy-done.2), channel_id=1, source_target_pairs={{0,8},{4,12},{8,0},{12,4},{1,9},{5,13},{9,1},{13,5},{2,10},{6,14},... | collective-permute-start | bytes 98312 | tf_op jit(solution)/shard_map/ppermute | solution.py:253
  17.1 1.5 collective-permute-start.2
  18.6 0.1 pad_add_fusion.1.where_ref
  18.7 24.6 %collective-permute-done.refs_1_ = bf16[16,1024]{1,0:T(8,128)(2,1)S(1)} collective-permute-done((bf16[16,1024]{1,0:T(8,128)(2,1)S(1)}, bf16[16,1024]{1,0:T(8,128)(2,1)S(1)}, u32[]{:S(2)}, u32[]{:S(2)}) %collective-permute-start) | collective-permute-done | bytes 32800 | tf_op jit(solution)/shard_map/ppermute | solution.py:253
  43.3 0.1 collective-permute-done.2.refs_3_
  43.4 1.8 %sum.1 = (bf16[4,592,128]{2,1,0:T(8,128)(2,1)}, bf16[64,1024]{1,0:T(8,128)(2,1)S(1)}) custom-call(s32[3]{0:T(128)S(1)} %pad_add_fusion.1.where_ref, bf16[16,592,128]{2,1,0:T(8,128)(2,1)S(1)} %all-to-all-done.got_ref, bf16[16,1024]{1,0:T(8,128)(2,1)S(1)} %copy-done, bf16[16,1024]{1,0:T(8,128)(2,1)S(1)} %collective-permute-done.refs_1_, ...), custom_call_target="tpu_custom_call" | custom-call | bytes 4194304 | tf_op jit(solution)/shard_map/sum/pallas_call | solution.py:39
  45.2 7.5 %all-to-all-start.1 = ((bf16[4,592,128]{2,1,0:T(8,128)(2,1)}), bf16[4,592,128]{2,1,0:T(8,128)(2,1)S(1)}, u32[]{:S(2)}, u32[]{:S(2)}) async-start(bf16[4,592,128]{2,1,0:T(8,128)(2,1)} %get-tuple-element.24), calls=%async_computation.1 | async-start | bytes 1212416 | tf_op jit(solution)/shard_map/all_to_all | solution.py:292
  52.7 3.0 %collective-permute-start.3 = (bf16[64,1024]{1,0:T(8,128)(2,1)S(1)}, bf16[64,1024]{1,0:T(8,128)(2,1)S(1)}, u32[]{:S(2)}, u32[]{:S(2)}) collective-permute-start(bf16[64,1024]{1,0:T(8,128)(2,1)S(1)} %get-tuple-element.25.slab_ref), channel_id=1, source_target_pairs={{0,32},{32,0},{1,33},{33,1},{2,34},{34,2},{3,35},{35,3},{4,36},{36... | collective-permute-start | bytes 393224 | tf_op jit(solution)/shard_map/ppermute | solution.py:253
  55.7 14.2 %collective-permute-done.3.other_ref = bf16[64,1024]{1,0:T(8,128)(2,1)S(1)} collective-permute-done((bf16[64,1024]{1,0:T(8,128)(2,1)S(1)}, bf16[64,1024]{1,0:T(8,128)(2,1)S(1)}, u32[]{:S(2)}, u32[]{:S(2)}) %collective-permute-start.3) | collective-permute-done | bytes 131104 | tf_op jit(solution)/shard_map/ppermute | solution.py:253
  69.9 2.7 %all-to-all-done.1.got_ref = bf16[4,592,128]{2,1,0:T(8,128)(2,1)S(1)} async-done(((bf16[4,592,128]{2,1,0:T(8,128)(2,1)}), bf16[4,592,128]{2,1,0:T(8,128)(2,1)S(1)}, u32[]{:S(2)}, u32[]{:S(2)}) %all-to-all-start.1) | async-done | bytes 606240 | tf_op jit(solution)/shard_map/all_to_all | solution.py:292
  72.7 1.9 %damp.1 = bf16[8,592,128]{2,1,0:T(8,128)(2,1)} custom-call(s32[3]{0:T(128)S(1)} %pad_add_fusion.1.where_ref, bf16[4,592,128]{2,1,0:T(8,128)(2,1)S(1)} %all-to-all-done.1.got_ref, bf16[64,1024]{1,0:T(8,128)(2,1)S(1)} %collective-permute-done.3.other_ref), custom_call_target="tpu_custom_call" | custom-call | bytes 4194304 | tf_op jit(solution)/shard_map/damp/pallas_call | solution.py:39
  74.6 3.6 %all-to-all-start.2 = ((bf16[8,592,128]{2,1,0:T(8,128)(2,1)}), bf16[8,592,128]{2,1,0:T(8,128)(2,1)S(1)}, u32[]{:S(2)}, u32[]{:S(2)}) async-start(bf16[8,592,128]{2,1,0:T(8,128)(2,1)} %damp.1), calls=%async_computation.2 | async-start | bytes 2424832 | tf_op jit(solution)/shard_map/all_to_all | solution.py:300
  78.2 0.1 pad_add_fusion.where_ref
  78.3 11.4 %all-to-all-done.2.packed_ref = bf16[8,592,128]{2,1,0:T(8,128)(2,1)S(1)} async-done(((bf16[8,592,128]{2,1,0:T(8,128)(2,1)}), bf16[8,592,128]{2,1,0:T(8,128)(2,1)S(1)}, u32[]{:S(2)}, u32[]{:S(2)}) %all-to-all-start.2) | async-done | bytes 1212448 | tf_op jit(solution)/shard_map/all_to_all | solution.py:300
  89.7 1.0 scale.1
  90.7 0.7 collective-permute-start.5
  91.4 1.5 collective-permute-start.4
  92.9 13.4 %root.1.root_ref = bf16[1024,1024]{1,0:T(8,128)(2,1)S(1)} custom-call(bf16[1024,1024]{1,0:T(8,128)(2,1)S(1)} %get-tuple-element.26.scaled, f32[8,128]{1,0:T(8,128)S(1)} %get-tuple-element.27.over_ref), custom_call_target="tpu_custom_call" | custom-call | flops 12884901888 | bytes 4194304 | tf_op jit(solution)/shard_map/root/pallas_call | solution.py:39
  106.3 1.1 right.1
  107.4 6.2 %collective-permute-start.6 = (bf16[256,128]{1,0:T(8,128)(2,1)S(1)}, bf16[256,128]{1,0:T(8,128)(2,1)S(1)}, u32[]{:S(2)}, u32[]{:S(2)}) collective-permute-start(bf16[256,128]{1,0:T(8,128)(2,1)S(1)} %get-tuple-element.29), channel_id=1, source_target_pairs={{16,0},{20,1},{24,2},{28,3},{17,4},{21,5},{25,6},{29,7},{18,8},{22... | collective-permute-start | bytes 196616 | tf_op jit(solution)/shard_map/ppermute | solution.py:346
  113.6 4.2 %collective-permute-start.7 = (bf16[256,128]{1,0:T(8,128)(2,1)S(1)}, bf16[256,128]{1,0:T(8,128)(2,1)S(1)}, u32[]{:S(2)}, u32[]{:S(2)}) collective-permute-start(bf16[256,128]{1,0:T(8,128)(2,1)S(1)} %get-tuple-element.30), channel_id=1, source_target_pairs={{16,64},{20,65},{24,66},{28,67},{17,68},{21,69},{25,70},{29,71},{1... | collective-permute-start | bytes 196616 | tf_op jit(solution)/shard_map/ppermute | solution.py:346
  117.8 1.9 %collective-permute-start.8 = (bf16[256,128]{1,0:T(8,128)(2,1)S(1)}, bf16[256,128]{1,0:T(8,128)(2,1)S(1)}, u32[]{:S(2)}, u32[]{:S(2)}) collective-permute-start(bf16[256,128]{1,0:T(8,128)(2,1)S(1)} %get-tuple-element.31), channel_id=1, source_target_pairs={{16,128},{20,129},{24,130},{28,131},{17,132},{21,133},{25,134},{29... | collective-permute-start | bytes 196616 | tf_op jit(solution)/shard_map/ppermute | solution.py:346
  119.7 1.3 collective-permute-start.9
  121.0 1.9 %collective-permute-done.8.refs_2_ = bf16[256,128]{1,0:T(8,128)(2,1)S(1)} collective-permute-done((bf16[256,128]{1,0:T(8,128)(2,1)S(1)}, bf16[256,128]{1,0:T(8,128)(2,1)S(1)}, u32[]{:S(2)}, u32[]{:S(2)}) %collective-permute-start.8) | collective-permute-done | bytes 65568 | tf_op jit(solution)/shard_map/ppermute | solution.py:346
  122.9 4.2 %collective-permute-done.9.refs_3_ = bf16[256,128]{1,0:T(8,128)(2,1)S(1)} collective-permute-done((bf16[256,128]{1,0:T(8,128)(2,1)S(1)}, bf16[256,128]{1,0:T(8,128)(2,1)S(1)}, u32[]{:S(2)}, u32[]{:S(2)}) %collective-permute-start.9) | collective-permute-done | bytes 65568 | tf_op jit(solution)/shard_map/ppermute | solution.py:346
  127.1 1.3 left.1
  128.3 28.7 %all_to_all.20 = bf16[64,16,128]{2,1,0:T(8,128)(2,1)S(1)} all-to-all(bf16[64,16,128]{2,1,0:T(8,128)(2,1)S(1)} %bitcast.11), channel_id=1, replica_groups=mesh['zh'=4,'zl'=2,'xl'=2,'y'=4,'xh'=2,'c'=2] {'zh','zl','xl','y'}, dimensions={0} | all-to-all | bytes 524288 | tf_op jit(solution)/shard_map/all_to_all | solution.py:367
  157.1 0.1 copy.7
  157.2 0.7 reshape.11
  (15 shorter events, 0.0 us)
Async XLA Ops:
  5.4 7.5 %copy-start.3 = (bf16[16,1024]{1,0:T(8,128)(2,1)S(1)}, bf16[16,1024]{1,0:T(8,128)(2,1)}, u32[]{:S(2)}) copy-start(bf16[16,1024]{1,0:T(8,128)(2,1)} %get-tuple-element.21) | copy-start | bytes 98308
  5.4 9.0 %copy-start.2 = (bf16[16,1024]{1,0:T(8,128)(2,1)S(1)}, bf16[16,1024]{1,0:T(8,128)(2,1)}, u32[]{:S(2)}) copy-start(bf16[16,1024]{1,0:T(8,128)(2,1)} %get-tuple-element.22) | copy-start | bytes 98308
  5.4 11.7 %copy-start.1 = (bf16[16,1024]{1,0:T(8,128)(2,1)S(1)}, bf16[16,1024]{1,0:T(8,128)(2,1)}, u32[]{:S(2)}) copy-start(bf16[16,1024]{1,0:T(8,128)(2,1)} %get-tuple-element.23) | copy-start | bytes 98308
  5.4 37.9 %copy-start = (bf16[16,1024]{1,0:T(8,128)(2,1)S(1)}, bf16[16,1024]{1,0:T(8,128)(2,1)}, u32[]{:S(2)}) copy-start(bf16[16,1024]{1,0:T(8,128)(2,1)} %get-tuple-element.20.refs_0_) | copy-start | bytes 98308
  5.4 37.9 %all-to-all-start = ((bf16[16,592,128]{2,1,0:T(8,128)(2,1)}), bf16[16,592,128]{2,1,0:T(8,128)(2,1)S(1)}, u32[]{:S(2)}, u32[]{:S(2)}) async-start(bf16[16,592,128]{2,1,0:T(8,128)(2,1)} %get-tuple-element.19), calls=%async_computation | async-start | bytes 4849664 | tf_op jit(solution)/shard_map/all_to_all | solution.py:280
  12.9 30.4 %collective-permute-start = (bf16[16,1024]{1,0:T(8,128)(2,1)S(1)}, bf16[16,1024]{1,0:T(8,128)(2,1)S(1)}, u32[]{:S(2)}, u32[]{:S(2)}) collective-permute-start(bf16[16,1024]{1,0:T(8,128)(2,1)S(1)} %copy-done.3), channel_id=1, source_target_pairs={{0,4},{4,8},{8,12},{12,0},{1,5},{5,9},{9,13},{13,1},{2,6},{6,10},{... | collective-permute-start | bytes 98312 | tf_op jit(solution)/shard_map/ppermute | solution.py:253
  14.5 28.8 %collective-permute-start.1 = (bf16[16,1024]{1,0:T(8,128)(2,1)S(1)}, bf16[16,1024]{1,0:T(8,128)(2,1)S(1)}, u32[]{:S(2)}, u32[]{:S(2)}) collective-permute-start(bf16[16,1024]{1,0:T(8,128)(2,1)S(1)} %copy-done.2), channel_id=1, source_target_pairs={{0,8},{4,12},{8,0},{12,4},{1,9},{5,13},{9,1},{13,5},{2,10},{6,14},... | collective-permute-start | bytes 98312 | tf_op jit(solution)/shard_map/ppermute | solution.py:253
  17.1 26.2 %collective-permute-start.2 = (bf16[16,1024]{1,0:T(8,128)(2,1)S(1)}, bf16[16,1024]{1,0:T(8,128)(2,1)S(1)}, u32[]{:S(2)}, u32[]{:S(2)}) collective-permute-start(bf16[16,1024]{1,0:T(8,128)(2,1)S(1)} %copy-done.1), channel_id=1, source_target_pairs={{0,12},{4,0},{8,4},{12,8},{1,13},{5,1},{9,5},{13,9},{2,14},{6,2},{... | collective-permute-start | bytes 98312 | tf_op jit(solution)/shard_map/ppermute | solution.py:253
  45.2 27.5 %all-to-all-start.1 = ((bf16[4,592,128]{2,1,0:T(8,128)(2,1)}), bf16[4,592,128]{2,1,0:T(8,128)(2,1)S(1)}, u32[]{:S(2)}, u32[]{:S(2)}) async-start(bf16[4,592,128]{2,1,0:T(8,128)(2,1)} %get-tuple-element.24), calls=%async_computation.1 | async-start | bytes 1212416 | tf_op jit(solution)/shard_map/all_to_all | solution.py:292
  52.7 17.2 %collective-permute-start.3 = (bf16[64,1024]{1,0:T(8,128)(2,1)S(1)}, bf16[64,1024]{1,0:T(8,128)(2,1)S(1)}, u32[]{:S(2)}, u32[]{:S(2)}) collective-permute-start(bf16[64,1024]{1,0:T(8,128)(2,1)S(1)} %get-tuple-element.25.slab_ref), channel_id=1, source_target_pairs={{0,32},{32,0},{1,33},{33,1},{2,34},{34,2},{3,35},{35,3},{4,36},{36... | collective-permute-start | bytes 393224 | tf_op jit(solution)/shard_map/ppermute | solution.py:253
  74.6 15.1 %all-to-all-start.2 = ((bf16[8,592,128]{2,1,0:T(8,128)(2,1)}), bf16[8,592,128]{2,1,0:T(8,128)(2,1)S(1)}, u32[]{:S(2)}, u32[]{:S(2)}) async-start(bf16[8,592,128]{2,1,0:T(8,128)(2,1)} %damp.1), calls=%async_computation.2 | async-start | bytes 2424832 | tf_op jit(solution)/shard_map/all_to_all | solution.py:300
  90.7 15.6 %collective-permute-start.5 = (bf16[128,1024]{1,0:T(8,128)(2,1)S(1)}, bf16[128,1024]{1,0:T(8,128)(2,1)S(1)}, u32[]{:S(2)}, u32[]{:S(2)}) collective-permute-start(bf16[128,1024]{1,0:T(8,128)(2,1)S(1)} %get-tuple-element.28), channel_id=1, source_target_pairs={{16,16},{17,20},{18,24},{19,28},{20,17},{21,21},{22,25},{23,29},{2... | collective-permute-start | bytes 786440 | tf_op jit(solution)/shard_map/ppermute | solution.py:315
  91.4 14.9 %collective-permute-start.4 = (bf16[128,1024]{1,0:T(8,128)(2,1)S(1)}, bf16[128,1024]{1,0:T(8,128)(2,1)S(1)}, u32[]{:S(2)}, u32[]{:S(2)}) collective-permute-start(bf16[128,1024]{1,0:T(8,128)(2,1)S(1)} %get-tuple-element.28), channel_id=1, source_target_pairs={{0,16},{1,20},{2,24},{3,28},{4,17},{5,21},{6,25},{7,29},{8,18},{9,... | collective-permute-start | bytes 786440 | tf_op jit(solution)/shard_map/ppermute | solution.py:315
  107.4 13.6 %collective-permute-start.6 = (bf16[256,128]{1,0:T(8,128)(2,1)S(1)}, bf16[256,128]{1,0:T(8,128)(2,1)S(1)}, u32[]{:S(2)}, u32[]{:S(2)}) collective-permute-start(bf16[256,128]{1,0:T(8,128)(2,1)S(1)} %get-tuple-element.29), channel_id=1, source_target_pairs={{16,0},{20,1},{24,2},{28,3},{17,4},{21,5},{25,6},{29,7},{18,8},{22... | collective-permute-start | bytes 196616 | tf_op jit(solution)/shard_map/ppermute | solution.py:346
  113.6 7.4 %collective-permute-start.7 = (bf16[256,128]{1,0:T(8,128)(2,1)S(1)}, bf16[256,128]{1,0:T(8,128)(2,1)S(1)}, u32[]{:S(2)}, u32[]{:S(2)}) collective-permute-start(bf16[256,128]{1,0:T(8,128)(2,1)S(1)} %get-tuple-element.30), channel_id=1, source_target_pairs={{16,64},{20,65},{24,66},{28,67},{17,68},{21,69},{25,70},{29,71},{1... | collective-permute-start | bytes 196616 | tf_op jit(solution)/shard_map/ppermute | solution.py:346
  117.8 5.1 %collective-permute-start.8 = (bf16[256,128]{1,0:T(8,128)(2,1)S(1)}, bf16[256,128]{1,0:T(8,128)(2,1)S(1)}, u32[]{:S(2)}, u32[]{:S(2)}) collective-permute-start(bf16[256,128]{1,0:T(8,128)(2,1)S(1)} %get-tuple-element.31), channel_id=1, source_target_pairs={{16,128},{20,129},{24,130},{28,131},{17,132},{21,133},{25,134},{29... | collective-permute-start | bytes 196616 | tf_op jit(solution)/shard_map/ppermute | solution.py:346
  119.7 7.3 %collective-permute-start.9 = (bf16[256,128]{1,0:T(8,128)(2,1)S(1)}, bf16[256,128]{1,0:T(8,128)(2,1)S(1)}, u32[]{:S(2)}, u32[]{:S(2)}) collective-permute-start(bf16[256,128]{1,0:T(8,128)(2,1)S(1)} %get-tuple-element.32), channel_id=1, source_target_pairs={{16,192},{20,193},{24,194},{28,195},{17,196},{21,197},{25,198},{29... | collective-permute-start | bytes 196616 | tf_op jit(solution)/shard_map/ppermute | solution.py:346

commit v7 on v5

--- a/solution.py
+++ b/solution.py
@@ -49,6 +49,18 @@
 
 SMEM = pl.BlockSpec(memory_space=pltpu.SMEM)
 VMEM = pl.BlockSpec(memory_space=pltpu.VMEM)
+
+
+def flip(block):
+    return block // NC + block % NC * NXH
+
+
+def partner(block, y):
+    return flip(block) ^ y
+
+
+def flip_scalar(block):
+    return lax.div(block, NC) + lax.rem(block, NC) * NXH
 
 
 def gram_kernel(y_ref, acts_ref, grads_ref, gradient_ref, out_ref, *refs):
@@ -98,7 +110,8 @@
             put_rest(out_ref.at[target_of(which, piece)], lines)
     gradient_load.wait()
     for shift, ref in enumerate(turn_refs):
-        start = pl.multiple_of(lax.rem(y_ref[0] + shift, NY) * ORDER, ORDER)
+        block = flip_scalar(jnp.bitwise_xor(y_ref[1], lax.rem(y_ref[0] + shift, NY)))
+        start = pl.multiple_of(block * ORDER, ORDER)
         ref[...] = gradient[0, :, pl.ds(start, ORDER)].astype(BF16)
 
 
@@ -241,6 +254,14 @@
     out_ref[...] = jnp.dot(root_ref[...], right[...], preferred_element_type=F32).astype(BF16)
 
 
+def place_kernel(block_ref, got_ref, out_ref):
+    for k in range(NBLOCK):
+        y = jnp.bitwise_xor(block_ref[0], flip(k))
+        for z in range(NZ):
+            at = k * ORDER + z % NZL * (NZH * TILE) + z // NZL * TILE
+            out_ref[0, :, at:at + TILE] = got_ref[z * NXL * NY + y]
+
+
 def place(xl, y, block):
     return (xl * NY + y) * NBLOCK + block
 
@@ -252,6 +273,7 @@
 def local(acts, grads_out, gradient):
     all_tokens = acts.shape[0] * NZ * NXL * NY
     y = lax.axis_index("y")
+    block = lax.axis_index(("xh", "c"))
     where = jnp.stack((lax.axis_index(("zl", "y")), y, lax.axis_index("zl")))
 
     packed, *turns = call(
@@ -259,7 +281,7 @@
         "gram",
         [jax.ShapeDtypeStruct((NZL * NXL * NY, PIECE + REST, TILE), BF16)]
         + [jax.ShapeDtypeStruct((ROWS, ORDER), BF16)] * NY,
-        (y[None], acts, grads_out, gradient),
+        (jnp.stack((y, block)), acts, grads_out, gradient),
         specs=[SMEM] + [pl.BlockSpec(memory_space=pltpu.HBM)] * 3,
         scratch=[
             pltpu.VMEM(acts.shape, BF16),
@@ -296,12 +318,12 @@
         (where, got, slab, other),
         specs=[SMEM, VMEM, VMEM, VMEM],
     )
-    cells = [(k, i) for k in range(NBLOCK) for i in range(NBLOCK)]
+    cells = [(partner(k, y), k, y) for k in range(NBLOCK) for y in range(NY)]
     slabs = [
         lax.ppermute(
             slabs,
             ("xl", "y", "xh", "c"),
-            [(place(xl, k, i), place(1, i, k)) for k, i in cells],
+            [(place(xl, y, i), place(1, y, k)) for i, k, y in cells],
         )
         for xl in range(NXL)
     ]
@@ -334,9 +356,9 @@
             right_done[shift],
             ("zh", "xl", "y", "xh", "c"),
             [
-                (zh * count + place(1, i, k), (zh + shift) % NZH * count + place(0, k, i))
+                (zh * count + place(1, y, k), (zh + shift) % NZH * count + place(0, y, i))
                 for zh in range(NZH)
-                for k, i in cells
+                for i, k, y in cells
             ],
         )
         for shift in range(NZH)
@@ -352,8 +374,13 @@
     )
     result = result.reshape(NZ * NXL * NY, ROWS, TILE)
     returned = lax.all_to_all(result, DP, 0, 0, tiled=True)
-    returned = returned.reshape(NZH, NZL, NXL, NY, ROWS, TILE)[:, :, 0]
-    return returned.transpose(3, 2, 1, 0, 4).reshape(1, ROWS, NY * NZ * TILE)
+    return call(
+        place_kernel,
+        "place",
+        jax.ShapeDtypeStruct((1, ROWS, NBLOCK * ORDER), BF16),
+        (block[None], returned),
+        specs=[SMEM, VMEM],
+    )
 
 
 def solution(mesh):

time: 154 us -> 150 us (0.974)
  waiting for transfers between devices: 64.3 us -> 55.7 us
  starting transfers between devices: 34.6 us -> 43 us
  blocking collectives: 28 us -> 23.1 us
    all_to_all x1, waiting for transfers between devices: 18.6 us -> 9.25 us  [local(): packed = lax.all_to_all(pieces, ('zl', 'y'), 0, 0, tiled=True)]
    ppermute x4, starting transfers between devices: 5.17 us -> 13.6 us  [local(): lax.ppermute(right_done[shift], ('zh', 'xl', 'y', 'xh', 'c'), [(zh * coun...]
    all_to_all x1, blocking collectives: 28 us -> 23.1 us  [local(): returned = lax.all_to_all(result, DP, 0, 0, tiled=True)]
    pallas_call x6 -> x7, Pallas kernels: 25.2 us -> 26.6 us  [call(): pl.pallas_call(kernel, out_shape=out_shape, scratch_shapes=list(scratch),...]
  transfers between devices with their start and end apart: 13 -> 13, of which waited for: 8 -> 7; matrix products, arithmetic and copies ran while one was open for 0% -> 0% of each run, Pallas kernels for 9% -> 9%
where the time goes in v7:
time: 150 us; the launch traced here: 149 us
  waiting for transfers between devices  55.7 us (37%)
  starting transfers between devices  43 us (29%)
  Pallas kernels  26.6 us (18%)
  blocking collectives  23.1 us (15%)
    ppermute x4, waiting for transfers between devices, turned(): return lax.ppermute(x, axes, [(n, (n + shift) % size) for n in range(size)])  38.9 us
    pallas_call x7, Pallas kernels, call(): pl.pallas_call(kernel, out_shape=out_shape, scratch_shapes=list(scratch),...  26.6 us
    all_to_all x1, blocking collectives, local(): returned = lax.all_to_all(result, DP, 0, 0, tiled=True)  23.1 us
    ppermute x4, starting transfers between devices, local(): lax.ppermute(right_done[shift], ('zh', 'xl', 'y', 'xh', 'c'), [(zh * coun...  13.6 us
    all_to_all x1, waiting for transfers between devices, local(): packed = lax.all_to_all(pieces, ('zl', 'y'), 0, 0, tiled=True)  9.25 us
    ppermute x4, starting transfers between devices, turned(): return lax.ppermute(x, axes, [(n, (n + shift) % size) for n in range(size)])  8.69 us
    all_to_all x1, starting transfers between devices, local(): got = lax.all_to_all(pieces, 'zh', 0, 0, tiled=True)  7.53 us
    all_to_all x1, starting transfers between devices, local(): got = lax.all_to_all(packed, ('zl', 'xl', 'y'), 0, 0, tiled=True)  7.45 us
  transfers between devices with their start and end apart: 13, of which 7 were waited for; matrix products, arithmetic and copies ran while one was open for 0% of the time, Pallas kernels for 9%

profile of v7, /device:TPU:2, one launch (start us, length us, event | category | flops | bytes accessed | tf_op | source)
XLA Modules:
  0.0 149.4 jit_solution(2473991883935981997)
XLA Ops:
  0.0 0.6 pad_add_fusion.2.y_ref
  0.6 6.1 %gram.1 = (bf16[16,592,128]{2,1,0:T(8,128)(2,1)}, bf16[16,1024]{1,0:T(8,128)(2,1)}, bf16[16,1024]{1,0:T(8,128)(2,1)}, bf16[16,1024]{1,0:T(8,128)(2,1)}, bf16[16,1024]{1,0:T(8,128)(2,1)}) custom-call(s32[2]{0:T(128)} %pad_add_fusion.2.y_ref, bf16[768,1024]{1,0:T(8,128)(2,1)} %acts_ref.1, bf16[768,1024]{1,0:T(8,128)(2,1)} %grads_ref.1, f32[1,16,4096]{2,1,0:T(8,128)} %gradient_ref.1), custom_call_target="tpu_custom_call" | custom-call | flops 3221225472 | bytes 4194304 | tf_op jit(solution)/shard_map/gram/pallas_call | solution.py:39
  6.7 0.0 copy-start
  6.7 7.5 %all-to-all-start = ((bf16[16,592,128]{2,1,0:T(8,128)(2,1)}), bf16[16,592,128]{2,1,0:T(8,128)(2,1)S(1)}, u32[]{:S(2)}, u32[]{:S(2)}) async-start(bf16[16,592,128]{2,1,0:T(8,128)(2,1)} %get-tuple-element.18), calls=%async_computation | async-start | bytes 4849664 | tf_op jit(solution)/shard_map/all_to_all | solution.py:298
  14.2 1.5 %collective-permute-start = (bf16[16,1024]{1,0:T(8,128)(2,1)S(1)}, bf16[16,1024]{1,0:T(8,128)(2,1)S(1)}, u32[]{:S(2)}, u32[]{:S(2)}) collective-permute-start(bf16[16,1024]{1,0:T(8,128)(2,1)S(1)} %copy-done.3), channel_id=1, source_target_pairs={{0,4},{4,8},{8,12},{12,0},{1,5},{5,9},{9,13},{13,1},{2,6},{6,10},{... | collective-permute-start | bytes 98312 | tf_op jit(solution)/shard_map/ppermute | solution.py:270
  15.7 2.7 %collective-permute-start.1 = (bf16[16,1024]{1,0:T(8,128)(2,1)S(1)}, bf16[16,1024]{1,0:T(8,128)(2,1)S(1)}, u32[]{:S(2)}, u32[]{:S(2)}) collective-permute-start(bf16[16,1024]{1,0:T(8,128)(2,1)S(1)} %copy-done.2), channel_id=1, source_target_pairs={{0,8},{4,12},{8,0},{12,4},{1,9},{5,13},{9,1},{13,5},{2,10},{6,14},... | collective-permute-start | bytes 98312 | tf_op jit(solution)/shard_map/ppermute | solution.py:270
  18.4 1.5 collective-permute-start.2
  19.8 0.1 pad_add_fusion.1.where_ref
  19.9 24.6 %collective-permute-done.refs_1_ = bf16[16,1024]{1,0:T(8,128)(2,1)S(1)} collective-permute-done((bf16[16,1024]{1,0:T(8,128)(2,1)S(1)}, bf16[16,1024]{1,0:T(8,128)(2,1)S(1)}, u32[]{:S(2)}, u32[]{:S(2)}) %collective-permute-start) | collective-permute-done | bytes 32800 | tf_op jit(solution)/shard_map/ppermute | solution.py:270
  44.5 0.1 collective-permute-done.2.refs_3_
  44.6 1.8 %sum.1 = (bf16[4,592,128]{2,1,0:T(8,128)(2,1)}, bf16[64,1024]{1,0:T(8,128)(2,1)S(1)}) custom-call(s32[3]{0:T(128)S(1)} %pad_add_fusion.1.where_ref, bf16[16,592,128]{2,1,0:T(8,128)(2,1)S(1)} %all-to-all-done.got_ref, bf16[16,1024]{1,0:T(8,128)(2,1)S(1)} %copy-done, bf16[16,1024]{1,0:T(8,128)(2,1)S(1)} %collective-permute-done.refs_1_, ...), custom_call_target="tpu_custom_call" | custom-call | bytes 4194304 | tf_op jit(solution)/shard_map/sum/pallas_call | solution.py:39
  46.4 7.5 %all-to-all-start.1 = ((bf16[4,592,128]{2,1,0:T(8,128)(2,1)}), bf16[4,592,128]{2,1,0:T(8,128)(2,1)S(1)}, u32[]{:S(2)}, u32[]{:S(2)}) async-start(bf16[4,592,128]{2,1,0:T(8,128)(2,1)} %get-tuple-element.23), calls=%async_computation.1 | async-start | bytes 1212416 | tf_op jit(solution)/shard_map/all_to_all | solution.py:310
  54.0 3.0 %collective-permute-start.3 = (bf16[64,1024]{1,0:T(8,128)(2,1)S(1)}, bf16[64,1024]{1,0:T(8,128)(2,1)S(1)}, u32[]{:S(2)}, u32[]{:S(2)}) collective-permute-start(bf16[64,1024]{1,0:T(8,128)(2,1)S(1)} %get-tuple-element.24.slab_ref), channel_id=1, source_target_pairs={{0,32},{32,0},{1,33},{33,1},{2,34},{34,2},{3,35},{35,3},{4,36},{36... | collective-permute-start | bytes 393224 | tf_op jit(solution)/shard_map/ppermute | solution.py:270
  57.0 14.2 %collective-permute-done.3.other_ref = bf16[64,1024]{1,0:T(8,128)(2,1)S(1)} collective-permute-done((bf16[64,1024]{1,0:T(8,128)(2,1)S(1)}, bf16[64,1024]{1,0:T(8,128)(2,1)S(1)}, u32[]{:S(2)}, u32[]{:S(2)}) %collective-permute-start.3) | collective-permute-done | bytes 131104 | tf_op jit(solution)/shard_map/ppermute | solution.py:270
  71.2 2.7 %all-to-all-done.1.got_ref = bf16[4,592,128]{2,1,0:T(8,128)(2,1)S(1)} async-done(((bf16[4,592,128]{2,1,0:T(8,128)(2,1)}), bf16[4,592,128]{2,1,0:T(8,128)(2,1)S(1)}, u32[]{:S(2)}, u32[]{:S(2)}) %all-to-all-start.1) | async-done | bytes 606240 | tf_op jit(solution)/shard_map/all_to_all | solution.py:310
  73.9 1.9 %damp.1 = (bf16[8,592,128]{2,1,0:T(8,128)(2,1)}, bf16[128,1024]{1,0:T(8,128)(2,1)S(1)}) custom-call(s32[3]{0:T(128)S(1)} %pad_add_fusion.1.where_ref, bf16[4,592,128]{2,1,0:T(8,128)(2,1)S(1)} %all-to-all-done.1.got_ref, bf16[64,1024]{1,0:T(8,128)(2,1)S(1)} %get-tuple-element.24.slab_ref, bf16[64,1024]{1,0:T(8,128)(2,1)S(1)} %collective-permute-done.3.other_ref), custom_call_target="tpu_custom_call" | custom-call | bytes 4194304 | tf_op jit(solution)/shard_map/damp/pallas_call | solution.py:39
  75.8 3.6 %all-to-all-start.2 = ((bf16[8,592,128]{2,1,0:T(8,128)(2,1)}), bf16[8,592,128]{2,1,0:T(8,128)(2,1)S(1)}, u32[]{:S(2)}, u32[]{:S(2)}) async-start(bf16[8,592,128]{2,1,0:T(8,128)(2,1)} %get-tuple-element.25), calls=%async_computation.2 | async-start | bytes 2424832 | tf_op jit(solution)/shard_map/all_to_all | solution.py:330
  79.4 0.1 pad_add_fusion.where_ref
  79.5 0.7 collective-permute-start.5
  80.2 1.5 collective-permute-start.4
  81.7 9.2 %all-to-all-done.2.packed_ref = bf16[8,592,128]{2,1,0:T(8,128)(2,1)S(1)} async-done(((bf16[8,592,128]{2,1,0:T(8,128)(2,1)}), bf16[8,592,128]{2,1,0:T(8,128)(2,1)S(1)}, u32[]{:S(2)}, u32[]{:S(2)}) %all-to-all-start.2) | async-done | bytes 1212448 | tf_op jit(solution)/shard_map/all_to_all | solution.py:330
  90.9 13.8 %root.1.root_ref = bf16[1024,1024]{1,0:T(8,128)(2,1)S(1)} custom-call(bf16[8,592,128]{2,1,0:T(8,128)(2,1)S(1)} %all-to-all-done.2.packed_ref), custom_call_target="tpu_custom_call" | custom-call | flops 12884901888 | bytes 4194304 | tf_op jit(solution)/shard_map/root/pallas_call | solution.py:39
  104.7 1.1 right.1
  105.8 6.2 %collective-permute-start.6 = (bf16[256,128]{1,0:T(8,128)(2,1)S(1)}, bf16[256,128]{1,0:T(8,128)(2,1)S(1)}, u32[]{:S(2)}, u32[]{:S(2)}) collective-permute-start(bf16[256,128]{1,0:T(8,128)(2,1)S(1)} %get-tuple-element.27), channel_id=1, source_target_pairs={{16,0},{20,5},{24,10},{28,15},{17,2},{21,7},{25,8},{29,13},{18,1},... | collective-permute-start | bytes 196616 | tf_op jit(solution)/shard_map/ppermute | solution.py:355
  112.0 4.2 %collective-permute-start.7 = (bf16[256,128]{1,0:T(8,128)(2,1)S(1)}, bf16[256,128]{1,0:T(8,128)(2,1)S(1)}, u32[]{:S(2)}, u32[]{:S(2)}) collective-permute-start(bf16[256,128]{1,0:T(8,128)(2,1)S(1)} %get-tuple-element.28), channel_id=1, source_target_pairs={{16,64},{20,69},{24,74},{28,79},{17,66},{21,71},{25,72},{29,77},{1... | collective-permute-start | bytes 196616 | tf_op jit(solution)/shard_map/ppermute | solution.py:355
  116.2 1.9 %collective-permute-start.8 = (bf16[256,128]{1,0:T(8,128)(2,1)S(1)}, bf16[256,128]{1,0:T(8,128)(2,1)S(1)}, u32[]{:S(2)}, u32[]{:S(2)}) collective-permute-start(bf16[256,128]{1,0:T(8,128)(2,1)S(1)} %get-tuple-element.29), channel_id=1, source_target_pairs={{16,128},{20,133},{24,138},{28,143},{17,130},{21,135},{25,136},{29... | collective-permute-start | bytes 196616 | tf_op jit(solution)/shard_map/ppermute | solution.py:355
  118.1 1.3 collective-permute-start.9
  119.4 2.1 %collective-permute-done.8.refs_2_ = bf16[256,128]{1,0:T(8,128)(2,1)S(1)} collective-permute-done((bf16[256,128]{1,0:T(8,128)(2,1)S(1)}, bf16[256,128]{1,0:T(8,128)(2,1)S(1)}, u32[]{:S(2)}, u32[]{:S(2)}) %collective-permute-start.8) | collective-permute-done | bytes 65568 | tf_op jit(solution)/shard_map/ppermute | solution.py:355
  121.6 2.7 %collective-permute-done.9.refs_3_ = bf16[256,128]{1,0:T(8,128)(2,1)S(1)} collective-permute-done((bf16[256,128]{1,0:T(8,128)(2,1)S(1)}, bf16[256,128]{1,0:T(8,128)(2,1)S(1)}, u32[]{:S(2)}, u32[]{:S(2)}) %collective-permute-start.9) | collective-permute-done | bytes 65568 | tf_op jit(solution)/shard_map/ppermute | solution.py:355
  124.3 1.3 left.1
  125.5 23.1 %all_to_all.20.got_ref = bf16[64,16,128]{2,1,0:T(8,128)(2,1)S(1)} all-to-all(bf16[64,16,128]{2,1,0:T(8,128)(2,1)S(1)} %bitcast.6), channel_id=1, replica_groups=mesh['zh'=4,'zl'=2,'xl'=2,'y'=4,'xh'=2,'c'=2] {'zh','zl','xl','y'}, dimensions={0} | all-to-all | bytes 524288 | tf_op jit(solution)/shard_map/all_to_all | solution.py:376
  148.7 0.7 place.1
  (13 shorter events, 0.0 us)
Async XLA Ops:
  6.7 7.5 %copy-start.3 = (bf16[16,1024]{1,0:T(8,128)(2,1)S(1)}, bf16[16,1024]{1,0:T(8,128)(2,1)}, u32[]{:S(2)}) copy-start(bf16[16,1024]{1,0:T(8,128)(2,1)} %get-tuple-element.20) | copy-start | bytes 98308
  6.7 9.0 %copy-start.2 = (bf16[16,1024]{1,0:T(8,128)(2,1)S(1)}, bf16[16,1024]{1,0:T(8,128)(2,1)}, u32[]{:S(2)}) copy-start(bf16[16,1024]{1,0:T(8,128)(2,1)} %get-tuple-element.21) | copy-start | bytes 98308
  6.7 11.7 %copy-start.1 = (bf16[16,1024]{1,0:T(8,128)(2,1)S(1)}, bf16[16,1024]{1,0:T(8,128)(2,1)}, u32[]{:S(2)}) copy-start(bf16[16,1024]{1,0:T(8,128)(2,1)} %get-tuple-element.22) | copy-start | bytes 98308
  6.7 37.9 %copy-start = (bf16[16,1024]{1,0:T(8,128)(2,1)S(1)}, bf16[16,1024]{1,0:T(8,128)(2,1)}, u32[]{:S(2)}) copy-start(bf16[16,1024]{1,0:T(8,128)(2,1)} %get-tuple-element.19.refs_0_) | copy-start | bytes 98308
  6.7 37.9 %all-to-all-start = ((bf16[16,592,128]{2,1,0:T(8,128)(2,1)}), bf16[16,592,128]{2,1,0:T(8,128)(2,1)S(1)}, u32[]{:S(2)}, u32[]{:S(2)}) async-start(bf16[16,592,128]{2,1,0:T(8,128)(2,1)} %get-tuple-element.18), calls=%async_computation | async-start | bytes 4849664 | tf_op jit(solution)/shard_map/all_to_all | solution.py:298
  14.2 30.4 %collective-permute-start = (bf16[16,1024]{1,0:T(8,128)(2,1)S(1)}, bf16[16,1024]{1,0:T(8,128)(2,1)S(1)}, u32[]{:S(2)}, u32[]{:S(2)}) collective-permute-start(bf16[16,1024]{1,0:T(8,128)(2,1)S(1)} %copy-done.3), channel_id=1, source_target_pairs={{0,4},{4,8},{8,12},{12,0},{1,5},{5,9},{9,13},{13,1},{2,6},{6,10},{... | collective-permute-start | bytes 98312 | tf_op jit(solution)/shard_map/ppermute | solution.py:270
  15.7 28.8 %collective-permute-start.1 = (bf16[16,1024]{1,0:T(8,128)(2,1)S(1)}, bf16[16,1024]{1,0:T(8,128)(2,1)S(1)}, u32[]{:S(2)}, u32[]{:S(2)}) collective-permute-start(bf16[16,1024]{1,0:T(8,128)(2,1)S(1)} %copy-done.2), channel_id=1, source_target_pairs={{0,8},{4,12},{8,0},{12,4},{1,9},{5,13},{9,1},{13,5},{2,10},{6,14},... | collective-permute-start | bytes 98312 | tf_op jit(solution)/shard_map/ppermute | solution.py:270
  18.4 26.2 %collective-permute-start.2 = (bf16[16,1024]{1,0:T(8,128)(2,1)S(1)}, bf16[16,1024]{1,0:T(8,128)(2,1)S(1)}, u32[]{:S(2)}, u32[]{:S(2)}) collective-permute-start(bf16[16,1024]{1,0:T(8,128)(2,1)S(1)} %copy-done.1), channel_id=1, source_target_pairs={{0,12},{4,0},{8,4},{12,8},{1,13},{5,1},{9,5},{13,9},{2,14},{6,2},{... | collective-permute-start | bytes 98312 | tf_op jit(solution)/shard_map/ppermute | solution.py:270
  46.4 27.5 %all-to-all-start.1 = ((bf16[4,592,128]{2,1,0:T(8,128)(2,1)}), bf16[4,592,128]{2,1,0:T(8,128)(2,1)S(1)}, u32[]{:S(2)}, u32[]{:S(2)}) async-start(bf16[4,592,128]{2,1,0:T(8,128)(2,1)} %get-tuple-element.23), calls=%async_computation.1 | async-start | bytes 1212416 | tf_op jit(solution)/shard_map/all_to_all | solution.py:310
  54.0 17.2 %collective-permute-start.3 = (bf16[64,1024]{1,0:T(8,128)(2,1)S(1)}, bf16[64,1024]{1,0:T(8,128)(2,1)S(1)}, u32[]{:S(2)}, u32[]{:S(2)}) collective-permute-start(bf16[64,1024]{1,0:T(8,128)(2,1)S(1)} %get-tuple-element.24.slab_ref), channel_id=1, source_target_pairs={{0,32},{32,0},{1,33},{33,1},{2,34},{34,2},{3,35},{35,3},{4,36},{36... | collective-permute-start | bytes 393224 | tf_op jit(solution)/shard_map/ppermute | solution.py:270
  75.8 15.1 %all-to-all-start.2 = ((bf16[8,592,128]{2,1,0:T(8,128)(2,1)}), bf16[8,592,128]{2,1,0:T(8,128)(2,1)S(1)}, u32[]{:S(2)}, u32[]{:S(2)}) async-start(bf16[8,592,128]{2,1,0:T(8,128)(2,1)} %get-tuple-element.25), calls=%async_computation.2 | async-start | bytes 2424832 | tf_op jit(solution)/shard_map/all_to_all | solution.py:330
  79.5 25.2 %collective-permute-start.5 = (bf16[128,1024]{1,0:T(8,128)(2,1)S(1)}, bf16[128,1024]{1,0:T(8,128)(2,1)S(1)}, u32[]{:S(2)}, u32[]{:S(2)}) collective-permute-start(bf16[128,1024]{1,0:T(8,128)(2,1)S(1)} %get-tuple-element.26), channel_id=1, source_target_pairs={{16,16},{21,20},{26,24},{31,28},{18,17},{23,21},{24,25},{29,29},{1... | collective-permute-start | bytes 786440 | tf_op jit(solution)/shard_map/ppermute | solution.py:323
  80.2 24.5 %collective-permute-start.4 = (bf16[128,1024]{1,0:T(8,128)(2,1)S(1)}, bf16[128,1024]{1,0:T(8,128)(2,1)S(1)}, u32[]{:S(2)}, u32[]{:S(2)}) collective-permute-start(bf16[128,1024]{1,0:T(8,128)(2,1)S(1)} %get-tuple-element.26), channel_id=1, source_target_pairs={{0,16},{5,20},{10,24},{15,28},{2,17},{7,21},{8,25},{13,29},{1,18},... | collective-permute-start | bytes 786440 | tf_op jit(solution)/shard_map/ppermute | solution.py:323
  105.8 13.6 %collective-permute-start.6 = (bf16[256,128]{1,0:T(8,128)(2,1)S(1)}, bf16[256,128]{1,0:T(8,128)(2,1)S(1)}, u32[]{:S(2)}, u32[]{:S(2)}) collective-permute-start(bf16[256,128]{1,0:T(8,128)(2,1)S(1)} %get-tuple-element.27), channel_id=1, source_target_pairs={{16,0},{20,5},{24,10},{28,15},{17,2},{21,7},{25,8},{29,13},{18,1},... | collective-permute-start | bytes 196616 | tf_op jit(solution)/shard_map/ppermute | solution.py:355
  112.0 7.4 %collective-permute-start.7 = (bf16[256,128]{1,0:T(8,128)(2,1)S(1)}, bf16[256,128]{1,0:T(8,128)(2,1)S(1)}, u32[]{:S(2)}, u32[]{:S(2)}) collective-permute-start(bf16[256,128]{1,0:T(8,128)(2,1)S(1)} %get-tuple-element.28), channel_id=1, source_target_pairs={{16,64},{20,69},{24,74},{28,79},{17,66},{21,71},{25,72},{29,77},{1... | collective-permute-start | bytes 196616 | tf_op jit(solution)/shard_map/ppermute | solution.py:355
  116.2 5.4 %collective-permute-start.8 = (bf16[256,128]{1,0:T(8,128)(2,1)S(1)}, bf16[256,128]{1,0:T(8,128)(2,1)S(1)}, u32[]{:S(2)}, u32[]{:S(2)}) collective-permute-start(bf16[256,128]{1,0:T(8,128)(2,1)S(1)} %get-tuple-element.29), channel_id=1, source_target_pairs={{16,128},{20,133},{24,138},{28,143},{17,130},{21,135},{25,136},{29... | collective-permute-start | bytes 196616 | tf_op jit(solution)/shard_map/ppermute | solution.py:355
  118.1 6.2 %collective-permute-start.9 = (bf16[256,128]{1,0:T(8,128)(2,1)S(1)}, bf16[256,128]{1,0:T(8,128)(2,1)S(1)}, u32[]{:S(2)}, u32[]{:S(2)}) collective-permute-start(bf16[256,128]{1,0:T(8,128)(2,1)S(1)} %get-tuple-element.30), channel_id=1, source_target_pairs={{16,192},{20,197},{24,202},{28,207},{17,194},{21,199},{25,200},{29... | collective-permute-start | bytes 196616 | tf_op jit(solution)/shard_map/ppermute | solution.py:355

commit v8 on v7

--- a/solution.py
+++ b/solution.py
@@ -30,12 +30,17 @@
 REST = 16
 ROWS = 16
 TERMS = 3
+SHIFTS = (2, 1, 3, 0)
 LOADS = 4
 ZROWS = NZL * NXL * NY * ROWS
 
 
-def call(kernel, name, out_shape, args, specs=None, scratch=(), flops=0, vmem=VMEM_BYTES):
+def call(
+    kernel, name, out_shape, args, specs=None, out_specs=None, scratch=(), flops=0, vmem=VMEM_BYTES
+):
     extra = {} if specs is None else {"in_specs": specs}
+    if out_specs is not None:
+        extra["out_specs"] = out_specs
     return pl.pallas_call(
         kernel,
         out_shape=out_shape,
@@ -47,7 +52,7 @@
     )(*args)
 
 
-SMEM = pl.BlockSpec(memory_space=pltpu.SMEM)
+HBM = pl.BlockSpec(memory_space=pltpu.HBM)
 VMEM = pl.BlockSpec(memory_space=pltpu.VMEM)
 
 
@@ -63,8 +68,16 @@
     return lax.div(block, NC) + lax.rem(block, NC) * NXH
 
 
-def gram_kernel(y_ref, acts_ref, grads_ref, gradient_ref, out_ref, *refs):
-    turn_refs, (acts, grads, gradient, sems, gradient_sem) = refs[:NY], refs[NY:]
+def block_here():
+    return lax.axis_index("xh") * NC + lax.axis_index("c")
+
+
+def piece_here():
+    return lax.axis_index("zl") * NY + lax.axis_index("y")
+
+
+def gram_kernel(acts_ref, grads_ref, gradient_ref, out_ref, *refs):
+    turn_refs, (acts, grads, gradient, packed, sems, gradient_sem, out_sems) = refs[:NY], refs[NY:]
     rows = acts.shape[0] // LOADS
     loads = []
     for which, (far, near) in enumerate(((acts_ref, acts), (grads_ref, grads))):
@@ -78,6 +91,7 @@
     eye = lax.broadcasted_iota(jnp.int32, (TILE, TILE), 0) == lax.broadcasted_iota(
         jnp.int32, (TILE, TILE), 1
     )
+    stores = []
     for which, ref in enumerate((acts, grads)):
         for load in loads[which * LOADS:(which + 1) * LOADS]:
             load.wait()
@@ -98,7 +112,7 @@
                     block_b = block.astype(BF16)
                     for half in range(2):
                         piece, at = divmod(2 * WHERE[(r, c)] + half, HALVES)
-                        out_ref[target_of(which, piece), at * HALF:(at + 1) * HALF] = block_b[
+                        packed[target_of(which, piece), at * HALF:(at + 1) * HALF] = block_b[
                             half * HALF:(half + 1) * HALF
                         ]
                         if r == c:
@@ -107,12 +121,21 @@
                             )
         for piece in range(NZL * NY):
             lines = [rest.get((piece, at), jnp.zeros((1, TILE), F32)) for at in range(HALVES)]
-            put_rest(out_ref.at[target_of(which, piece)], lines)
+            put_rest(packed.at[target_of(which, piece)], lines)
+        for zl in range(NZL):
+            part = pl.ds(target_of(which, zl * NY), NY)
+            stores.append(
+                pltpu.make_async_copy(packed.at[part], out_ref.at[part], out_sems.at[which, zl])
+            )
+            stores[-1].start()
     gradient_load.wait()
+    y, own = lax.axis_index("y"), block_here()
     for shift, ref in enumerate(turn_refs):
-        block = flip_scalar(jnp.bitwise_xor(y_ref[1], lax.rem(y_ref[0] + shift, NY)))
+        block = flip_scalar(jnp.bitwise_xor(own, lax.rem(y + shift, NY)))
         start = pl.multiple_of(block * ORDER, ORDER)
         ref[...] = gradient[0, :, pl.ds(start, ORDER)].astype(BF16)
+    for store in stores:
+        store.wait()
 
 
 def target_of(which, piece):
@@ -131,13 +154,14 @@
     )
 
 
-def sum_halves(piece, got_ref):
-    count = got_ref.shape[0]
-    rest = sum([got_ref[n, PIECE:].astype(F32) for n in range(1, count)], got_ref[0, PIECE:].astype(F32))
+def sum_halves(piece, parts):
+    def added(rows):
+        return sum([part[rows].astype(F32) for part in parts[1:]], parts[0][rows].astype(F32))
+
+    rest = added(slice(PIECE, PIECE + REST))
     halves = []
     for at in range(HALVES):
-        s = slice(at * HALF, (at + 1) * HALF)
-        total = sum([got_ref[n, s].astype(F32) for n in range(1, count)], got_ref[0, s].astype(F32))
+        total = added(slice(at * HALF, (at + 1) * HALF))
         halves.append(total + jnp.where(eye_of(piece, at), rest[at:at + 1], 0.0))
     return halves
 
@@ -149,28 +173,25 @@
         lines.append(
             jnp.sum(jnp.where(eye_of(piece, at), half - half_b.astype(F32), 0.0), axis=0, keepdims=True)
         )
-        for n in range(out_ref.shape[0]):
-            out_ref[n, at * HALF:(at + 1) * HALF] = half_b
-    for n in range(out_ref.shape[0]):
-        put_rest(out_ref.at[n], lines + list(more))
-
-
-def sum_kernel(where_ref, got_ref, *refs):
+        out_ref[at * HALF:(at + 1) * HALF] = half_b
+    put_rest(out_ref, lines + list(more))
+
+
+def sum_kernel(got_ref, *refs):
     turn_refs, (out_ref, slab_ref) = refs[:NY], refs[NY:]
     for turn, ref in enumerate(turn_refs):
-        at = lax.rem(where_ref[1] + NY - turn, NY) * ROWS
+        at = lax.rem(lax.axis_index("y") + NY - turn, NY) * ROWS
         slab_ref[pl.ds(pl.multiple_of(at, ROWS), ROWS), :] = ref[...]
-    put_halves(where_ref[0], out_ref, sum_halves(where_ref[0], got_ref))
-
-
-def damp_kernel(all_tokens, where_ref, got_ref, slab_ref, other_ref, out_ref, slabs_ref):
-    zl, rows = where_ref[2], NY * ROWS
-    slabs_ref[pl.ds(pl.multiple_of(zl * rows, rows), rows), :] = slab_ref[...]
-    slabs_ref[pl.ds(pl.multiple_of((1 - zl) * rows, rows), rows), :] = other_ref[...]
-    piece = where_ref[0]
+    piece = piece_here()
+    put_halves(piece, out_ref, sum_halves(piece, [got_ref.at[n] for n in range(got_ref.shape[0])]))
+
+
+def damp_kernel(all_tokens, *refs):
+    parts, (slab_ref, other_ref, out_ref, slabs_ref, damped, sems) = refs[:NZH], refs[NZH:]
+    piece = piece_here()
     halves = []
     squares = jnp.zeros((HALF, TILE), F32)
-    for at, half in enumerate(sum_halves(piece, got_ref)):
+    for at, half in enumerate(sum_halves(piece, parts)):
         block = lax.div(piece * HALVES + at, 2)
         on_diag = functools.reduce(jnp.logical_or, [block == WHERE[(r, r)] for r in range(GRID)])
         damping = jnp.where(on_diag, DAMPING, 0.0)
@@ -183,7 +204,17 @@
     for _ in range(TERMS):
         terms.append(left.astype(BF16).astype(F32))
         left = left - terms[-1]
-    put_halves(piece, out_ref, halves, terms)
+    put_halves(piece, damped, halves, terms)
+    stores = [
+        pltpu.make_async_copy(damped, out_ref.at[n], sems.at[n]) for n in range(out_ref.shape[0])
+    ]
+    for store in stores:
+        store.start()
+    zl, rows = lax.axis_index("zl"), NY * ROWS
+    slabs_ref[pl.ds(pl.multiple_of(zl * rows, rows), rows), :] = slab_ref[...]
+    slabs_ref[pl.ds(pl.multiple_of((1 - zl) * rows, rows), rows), :] = other_ref[...]
+    for store in stores:
+        store.wait()
 
 
 def root_kernel(packed_ref, root_ref, scaled, iterate, iterate_b, square_b, cubic_b):
@@ -233,30 +264,31 @@
             for s in tiles:
                 iterate_b[:, s] = iterate[:, s].astype(BF16)
 
-def right_kernel(where_ref, root_ref, *refs):
+def right_kernel(root_ref, *refs):
     slab_refs, right_refs, right = refs[:NXL], refs[NXL:NXL + NZH], refs[-1]
-    zh, zl, rows = where_ref[0], where_ref[1], NY * ROWS
+    zh, zl, rows = lax.axis_index("zh"), lax.axis_index("zl"), NY * ROWS
     cols = root_ref[:, pl.ds(pl.multiple_of(zl * (NZH * TILE), NZH * TILE), NZH * TILE)]
     for xl, ref in enumerate(slab_refs):
         done = jnp.dot(ref[...], cols, preferred_element_type=F32).astype(BF16)
         for n in range(NZL):
             right[(n * NXL + xl) * rows:(n * NXL + xl + 1) * rows] = done[n * rows:(n + 1) * rows]
-    for shift, ref in enumerate(right_refs):
+    for shift, ref in zip(SHIFTS, right_refs):
         at = lax.rem(zh + shift, NZH) * TILE
         ref[...] = right[:, pl.ds(pl.multiple_of(at, TILE), TILE)]
 
 
-def left_kernel(where_ref, root_ref, *refs):
+def left_kernel(root_ref, *refs):
     right_refs, (out_ref, right) = refs[:NZH], refs[NZH:]
-    for shift, ref in enumerate(right_refs):
-        at = lax.rem(where_ref[0] + NZH - shift, NZH) * ZROWS
+    for shift, ref in zip(SHIFTS, right_refs):
+        at = lax.rem(lax.axis_index("zh") + NZH - shift, NZH) * ZROWS
         right[pl.ds(pl.multiple_of(at, ZROWS), ZROWS), :] = ref[...]
     out_ref[...] = jnp.dot(root_ref[...], right[...], preferred_element_type=F32).astype(BF16)
 
 
-def place_kernel(block_ref, got_ref, out_ref):
+def place_kernel(got_ref, out_ref):
+    own = block_here()
     for k in range(NBLOCK):
-        y = jnp.bitwise_xor(block_ref[0], flip(k))
+        y = jnp.bitwise_xor(own, flip(k))
         for z in range(NZ):
             at = k * ORDER + z % NZL * (NZH * TILE) + z // NZL * TILE
             out_ref[0, :, at:at + TILE] = got_ref[z * NXL * NY + y]
@@ -272,23 +304,22 @@
 
 def local(acts, grads_out, gradient):
     all_tokens = acts.shape[0] * NZ * NXL * NY
-    y = lax.axis_index("y")
-    block = lax.axis_index(("xh", "c"))
-    where = jnp.stack((lax.axis_index(("zl", "y")), y, lax.axis_index("zl")))
-
     packed, *turns = call(
         gram_kernel,
         "gram",
         [jax.ShapeDtypeStruct((NZL * NXL * NY, PIECE + REST, TILE), BF16)]
         + [jax.ShapeDtypeStruct((ROWS, ORDER), BF16)] * NY,
-        (jnp.stack((y, block)), acts, grads_out, gradient),
-        specs=[SMEM] + [pl.BlockSpec(memory_space=pltpu.HBM)] * 3,
+        (acts, grads_out, gradient),
+        specs=[HBM] * 3,
+        out_specs=[HBM] + [VMEM] * NY,
         scratch=[
             pltpu.VMEM(acts.shape, BF16),
             pltpu.VMEM(acts.shape, BF16),
             pltpu.VMEM(gradient.shape, F32),
+            pltpu.VMEM((NZL * NXL * NY, PIECE + REST, TILE), BF16),
             pltpu.SemaphoreType.DMA((2, LOADS)),
             pltpu.SemaphoreType.DMA(()),
+            pltpu.SemaphoreType.DMA((2, NZL)),
         ],
         flops=4 * acts.shape[0] * ORDER * ORDER,
         vmem=60 << 20,
@@ -296,18 +327,17 @@
     turns = [turns[0]] + [turned(turns[shift], "y", NY, shift) for shift in range(1, NY)]
 
     got = lax.all_to_all(packed, ("zl", "xl", "y"), 0, 0, tiled=True)
-    pieces, slab = call(
+    part, slab = call(
         sum_kernel,
         "sum",
         [
-            jax.ShapeDtypeStruct((NZH, PIECE + REST, TILE), BF16),
+            jax.ShapeDtypeStruct((PIECE + REST, TILE), BF16),
             jax.ShapeDtypeStruct((NY * ROWS, ORDER), BF16),
         ],
-        (where, got, *turns),
-        specs=[SMEM] + [VMEM] * (1 + NY),
+        (got, *turns),
     )
     other = turned(slab, "zl", NZL, 1)
-    got = lax.all_to_all(pieces, "zh", 0, 0, tiled=True)
+    parts = [part] + [turned(part, "zh", NZH, shift) for shift in SHIFTS[2::-1]]
     pieces, slabs = call(
         functools.partial(damp_kernel, float(all_tokens)),
         "damp",
@@ -315,8 +345,12 @@
             jax.ShapeDtypeStruct((NZL * NY, PIECE + REST, TILE), BF16),
             jax.ShapeDtypeStruct((NZL * NY * ROWS, ORDER), BF16),
         ],
-        (where, got, slab, other),
-        specs=[SMEM, VMEM, VMEM, VMEM],
+        (*parts, slab, other),
+        out_specs=[HBM, VMEM],
+        scratch=[
+            pltpu.VMEM((PIECE + REST, TILE), BF16),
+            pltpu.SemaphoreType.DMA((NZL * NY,)),
+        ],
     )
     cells = [(partner(k, y), k, y) for k in range(NBLOCK) for y in range(NY)]
     slabs = [
@@ -330,7 +364,6 @@
     packed = lax.all_to_all(pieces, ("zl", "y"), 0, 0, tiled=True)
 
     square_b = pltpu.VMEM((ORDER, ORDER), BF16)
-    z_where = jnp.stack((lax.axis_index("zh"), lax.axis_index("zl")))
     right_done = jax.ShapeDtypeStruct((ZROWS, TILE), BF16)
     root = call(
         root_kernel,
@@ -344,8 +377,7 @@
         right_kernel,
         "right",
         [right_done] * NZH,
-        (z_where, root, *slabs),
-        specs=[SMEM] + [VMEM] * (1 + NXL),
+        (root, *slabs),
         scratch=[pltpu.VMEM((ZROWS, NZH * TILE), BF16)],
         flops=2 * ORDER * ZROWS * NZH * TILE,
     )
@@ -353,7 +385,7 @@
     count = NXL * NY * NBLOCK
     right_done = [
         lax.ppermute(
-            right_done[shift],
+            right_done[n],
             ("zh", "xl", "y", "xh", "c"),
             [
                 (zh * count + place(1, y, k), (zh + shift) % NZH * count + place(0, y, i))
@@ -361,14 +393,13 @@
                 for i, k, y in cells
             ],
         )
-        for shift in range(NZH)
+        for n, shift in enumerate(SHIFTS)
     ]
     result = call(
         left_kernel,
         "left",
         jax.ShapeDtypeStruct((ORDER, TILE), BF16),
-        (z_where, root, *right_done),
-        specs=[SMEM] + [VMEM] * (1 + NZH),
+        (root, *right_done),
         scratch=[pltpu.VMEM((ORDER, TILE), BF16)],
         flops=2 * ORDER * ORDER * TILE,
     )
@@ -378,8 +409,7 @@
         place_kernel,
         "place",
         jax.ShapeDtypeStruct((1, ROWS, NBLOCK * ORDER), BF16),
-        (block[None], returned),
-        specs=[SMEM, VMEM],
+        (returned,),
     )
 
 

time: 150 us -> 139 us (0.927)
  waiting for transfers between devices: 55.7 us -> 50.9 us
  Pallas kernels: 26.6 us -> 23.2 us
    ppermute x4 -> x7, starting transfers between devices: 8.69 us -> 19.2 us  [turned(): return lax.ppermute(x, axes, [(n, (n + shift) % size) for n in range(size)])]
    all_to_all x1 -> x0, starting transfers between devices: 7.53 us -> none  [local(): got = lax.all_to_all(pieces, 'zh', 0, 0, tiled=True)]
    ppermute x4 -> x7, waiting for transfers between devices: 38.9 us -> 34.6 us  [turned(): return lax.ppermute(x, axes, [(n, (n + shift) % size) for n in range(size)])]
    ppermute x4, starting transfers between devices: 13.6 us -> 10.1 us  [local(): lax.ppermute(right_done[n], ('zh', 'xl', 'y', 'xh', 'c'), [(zh * count +...]
    pallas_call x7, Pallas kernels: 26.6 us -> 23.2 us  [call(): pl.pallas_call(kernel, out_shape=out_shape, scratch_shapes=list(scratch),...]
    all_to_all x1, waiting for transfers between devices: 9.25 us -> 12.5 us  [local(): packed = lax.all_to_all(pieces, ('zl', 'y'), 0, 0, tiled=True)]
    all_to_all x1 -> x0, waiting for transfers between devices: 2.74 us -> none  [local(): got = lax.all_to_all(pieces, 'zh', 0, 0, tiled=True)]
  transfers between devices with their start and end apart: 13 -> 15, of which waited for: 7 -> 5; matrix products, arithmetic and copies ran while one was open for 0% -> 0% of each run, Pallas kernels for 9% -> 10%
where the time goes in v8:
time: 139 us
  waiting for transfers between devices  50.9 us (37%)
  starting transfers between devices  43.1 us (31%)
  Pallas kernels  23.2 us (17%)
  blocking collectives  21.7 us (16%)
    ppermute x7, waiting for transfers between devices, turned(): return lax.ppermute(x, axes, [(n, (n + shift) % size) for n in range(size)])  34.6 us
    pallas_call x7, Pallas kernels, call(): pl.pallas_call(kernel, out_shape=out_shape, scratch_shapes=list(scratch),...  23.2 us
    all_to_all x1, blocking collectives, local(): returned = lax.all_to_all(result, DP, 0, 0, tiled=True)  21.7 us
    ppermute x7, starting transfers between devices, turned(): return lax.ppermute(x, axes, [(n, (n + shift) % size) for n in range(size)])  19.2 us
    all_to_all x1, waiting for transfers between devices, local(): packed = lax.all_to_all(pieces, ('zl', 'y'), 0, 0, tiled=True)  12.5 us
    ppermute x4, starting transfers between devices, local(): lax.ppermute(right_done[n], ('zh', 'xl', 'y', 'xh', 'c'), [(zh * count +...  10.1 us
    all_to_all x1, starting transfers between devices, local(): got = lax.all_to_all(packed, ('zl', 'xl', 'y'), 0, 0, tiled=True)  7.45 us
    all_to_all x1, starting transfers between devices, local(): packed = lax.all_to_all(pieces, ('zl', 'y'), 0, 0, tiled=True)  4.19 us
  transfers between devices with their start and end apart: 15, of which 5 were waited for; matrix products, arithmetic and copies ran while one was open for 0% of the time, Pallas kernels for 10%

profile of v8, /device:TPU:2, one launch (start us, length us, event | category | flops | bytes accessed | tf_op | source)
XLA Modules:
  0.0 139.1 jit_solution(12370064116440949438)
XLA Ops:
  0.0 5.6 %gram.1 = (bf16[16,592,128]{2,1,0:T(8,128)(2,1)}, bf16[16,1024]{1,0:T(8,128)(2,1)}, bf16[16,1024]{1,0:T(8,128)(2,1)}, bf16[16,1024]{1,0:T(8,128)(2,1)}, bf16[16,1024]{1,0:T(8,128)(2,1)}) custom-call(bf16[768,1024]{1,0:T(8,128)(2,1)} %acts_ref.1, bf16[768,1024]{1,0:T(8,128)(2,1)} %grads_ref.1, f32[1,16,4096]{2,1,0:T(8,128)} %gradient_ref.1), custom_call_target="tpu_custom_call" | custom-call | flops 3221225472 | bytes 4194304 | tf_op jit(solution)/shard_map/gram/pallas_call | solution.py:44
  5.7 0.0 copy-start
  5.7 7.5 %all-to-all-start = ((bf16[16,592,128]{2,1,0:T(8,128)(2,1)}), bf16[16,592,128]{2,1,0:T(8,128)(2,1)S(1)}, u32[]{:S(2)}, u32[]{:S(2)}) async-start(bf16[16,592,128]{2,1,0:T(8,128)(2,1)} %get-tuple-element.18), calls=%async_computation | async-start | bytes 4849664 | tf_op jit(solution)/shard_map/all_to_all | solution.py:329
  13.1 1.5 %collective-permute-start = (bf16[16,1024]{1,0:T(8,128)(2,1)S(1)}, bf16[16,1024]{1,0:T(8,128)(2,1)S(1)}, u32[]{:S(2)}, u32[]{:S(2)}) collective-permute-start(bf16[16,1024]{1,0:T(8,128)(2,1)S(1)} %copy-done.3), channel_id=1, source_target_pairs={{0,4},{4,8},{8,12},{12,0},{1,5},{5,9},{9,13},{13,1},{2,6},{6,10},{... | collective-permute-start | bytes 98312 | tf_op jit(solution)/shard_map/ppermute | solution.py:302
  14.7 2.7 %collective-permute-start.1 = (bf16[16,1024]{1,0:T(8,128)(2,1)S(1)}, bf16[16,1024]{1,0:T(8,128)(2,1)S(1)}, u32[]{:S(2)}, u32[]{:S(2)}) collective-permute-start(bf16[16,1024]{1,0:T(8,128)(2,1)S(1)} %copy-done.2), channel_id=1, source_target_pairs={{0,8},{4,12},{8,0},{12,4},{1,9},{5,13},{9,1},{13,5},{2,10},{6,14},... | collective-permute-start | bytes 98312 | tf_op jit(solution)/shard_map/ppermute | solution.py:302
  17.4 1.5 %collective-permute-start.2 = (bf16[16,1024]{1,0:T(8,128)(2,1)S(1)}, bf16[16,1024]{1,0:T(8,128)(2,1)S(1)}, u32[]{:S(2)}, u32[]{:S(2)}) collective-permute-start(bf16[16,1024]{1,0:T(8,128)(2,1)S(1)} %copy-done.1), channel_id=1, source_target_pairs={{0,12},{4,0},{8,4},{12,8},{1,13},{5,1},{9,5},{13,9},{2,14},{6,2},{... | collective-permute-start | bytes 98312 | tf_op jit(solution)/shard_map/ppermute | solution.py:302
  18.8 24.7 %collective-permute-done.refs_1_ = bf16[16,1024]{1,0:T(8,128)(2,1)S(1)} collective-permute-done((bf16[16,1024]{1,0:T(8,128)(2,1)S(1)}, bf16[16,1024]{1,0:T(8,128)(2,1)S(1)}, u32[]{:S(2)}, u32[]{:S(2)}) %collective-permute-start) | collective-permute-done | bytes 32800 | tf_op jit(solution)/shard_map/ppermute | solution.py:302
  43.5 0.0 collective-permute-done.1.refs_2_
  43.5 0.1 collective-permute-done.2.refs_3_
  43.6 0.0 all-to-all-done.got_ref
  43.6 0.4 sum.1
  44.0 6.3 %collective-permute-start.5 = (bf16[592,128]{1,0:T(8,128)(2,1)S(1)}, bf16[592,128]{1,0:T(8,128)(2,1)S(1)}, u32[]{:S(2)}, u32[]{:S(2)}) collective-permute-start(bf16[592,128]{1,0:T(8,128)(2,1)S(1)} %get-tuple-element.23.refs_0_), channel_id=1, source_target_pairs={{0,128},{64,192},{128,0},{192,64},{1,129},{65,193},{129,1},{193,65... | collective-permute-start | bytes 454664 | tf_op jit(solution)/shard_map/ppermute | solution.py:302
  50.4 1.5 %collective-permute-start.4 = (bf16[592,128]{1,0:T(8,128)(2,1)S(1)}, bf16[592,128]{1,0:T(8,128)(2,1)S(1)}, u32[]{:S(2)}, u32[]{:S(2)}) collective-permute-start(bf16[592,128]{1,0:T(8,128)(2,1)S(1)} %get-tuple-element.23.refs_0_), channel_id=1, source_target_pairs={{0,64},{64,128},{128,192},{192,0},{1,65},{65,129},{129,193},{193,1... | collective-permute-start | bytes 454664 | tf_op jit(solution)/shard_map/ppermute | solution.py:302
  51.8 2.7 %collective-permute-start.3 = (bf16[592,128]{1,0:T(8,128)(2,1)S(1)}, bf16[592,128]{1,0:T(8,128)(2,1)S(1)}, u32[]{:S(2)}, u32[]{:S(2)}) collective-permute-start(bf16[592,128]{1,0:T(8,128)(2,1)S(1)} %get-tuple-element.23.refs_0_), channel_id=1, source_target_pairs={{0,192},{64,0},{128,64},{192,128},{1,193},{65,1},{129,65},{193,129... | collective-permute-start | bytes 454664 | tf_op jit(solution)/shard_map/ppermute | solution.py:302
  54.5 3.0 %collective-permute-start.6 = (bf16[64,1024]{1,0:T(8,128)(2,1)S(1)}, bf16[64,1024]{1,0:T(8,128)(2,1)S(1)}, u32[]{:S(2)}, u32[]{:S(2)}) collective-permute-start(bf16[64,1024]{1,0:T(8,128)(2,1)S(1)} %get-tuple-element.24.refs_4_), channel_id=1, source_target_pairs={{0,32},{32,0},{1,33},{33,1},{2,34},{34,2},{3,35},{35,3},{4,36},{36... | collective-permute-start | bytes 393224 | tf_op jit(solution)/shard_map/ppermute | solution.py:302
  57.5 9.8 %collective-permute-done.6.refs_5_ = bf16[64,1024]{1,0:T(8,128)(2,1)S(1)} collective-permute-done((bf16[64,1024]{1,0:T(8,128)(2,1)S(1)}, bf16[64,1024]{1,0:T(8,128)(2,1)S(1)}, u32[]{:S(2)}, u32[]{:S(2)}) %collective-permute-start.6) | collective-permute-done | bytes 131104 | tf_op jit(solution)/shard_map/ppermute | solution.py:302
  67.4 0.0 collective-permute-done.5.refs_3_
  67.4 1.4 %damp.1 = (bf16[8,592,128]{2,1,0:T(8,128)(2,1)}, bf16[128,1024]{1,0:T(8,128)(2,1)S(1)}) custom-call(bf16[592,128]{1,0:T(8,128)(2,1)S(1)} %get-tuple-element.23.refs_0_, bf16[592,128]{1,0:T(8,128)(2,1)S(1)} %collective-permute-done.3.refs_1_, bf16[592,128]{1,0:T(8,128)(2,1)S(1)} %collective-permute-done.4.refs_2_, ...), custom_call_target="tpu_custom_call" | custom-call | bytes 4194304 | tf_op jit(solution)/shard_map/damp/pallas_call | solution.py:44
  68.8 4.2 %all-to-all-start.1 = ((bf16[8,592,128]{2,1,0:T(8,128)(2,1)}), bf16[8,592,128]{2,1,0:T(8,128)(2,1)S(1)}, u32[]{:S(2)}, u32[]{:S(2)}) async-start(bf16[8,592,128]{2,1,0:T(8,128)(2,1)} %get-tuple-element.25), calls=%async_computation.1 | async-start | bytes 2424832 | tf_op jit(solution)/shard_map/all_to_all | solution.py:364
  73.0 0.7 collective-permute-start.8
  73.7 1.5 %collective-permute-start.7 = (bf16[128,1024]{1,0:T(8,128)(2,1)S(1)}, bf16[128,1024]{1,0:T(8,128)(2,1)S(1)}, u32[]{:S(2)}, u32[]{:S(2)}) collective-permute-start(bf16[128,1024]{1,0:T(8,128)(2,1)S(1)} %get-tuple-element.26), channel_id=1, source_target_pairs={{0,16},{5,20},{10,24},{15,28},{2,17},{7,21},{8,25},{13,29},{1,18},... | collective-permute-start | bytes 786440 | tf_op jit(solution)/shard_map/ppermute | solution.py:357
  75.1 12.5 %all-to-all-done.1.packed_ref = bf16[8,592,128]{2,1,0:T(8,128)(2,1)S(1)} async-done(((bf16[8,592,128]{2,1,0:T(8,128)(2,1)}), bf16[8,592,128]{2,1,0:T(8,128)(2,1)S(1)}, u32[]{:S(2)}, u32[]{:S(2)}) %all-to-all-start.1) | async-done | bytes 1212448 | tf_op jit(solution)/shard_map/all_to_all | solution.py:364
  87.7 13.8 %root.1.root_ref = bf16[1024,1024]{1,0:T(8,128)(2,1)S(1)} custom-call(bf16[8,592,128]{2,1,0:T(8,128)(2,1)S(1)} %all-to-all-done.1.packed_ref), custom_call_target="tpu_custom_call" | custom-call | flops 12884901888 | bytes 4194304 | tf_op jit(solution)/shard_map/root/pallas_call | solution.py:44
  101.5 0.5 right.1
  102.0 5.3 %collective-permute-start.9 = (bf16[256,128]{1,0:T(8,128)(2,1)S(1)}, bf16[256,128]{1,0:T(8,128)(2,1)S(1)}, u32[]{:S(2)}, u32[]{:S(2)}) collective-permute-start(bf16[256,128]{1,0:T(8,128)(2,1)S(1)} %get-tuple-element.27), channel_id=1, source_target_pairs={{16,128},{20,133},{24,138},{28,143},{17,130},{21,135},{25,136},{29... | collective-permute-start | bytes 196616 | tf_op jit(solution)/shard_map/ppermute | solution.py:387
  107.3 1.8 %collective-permute-start.10 = (bf16[256,128]{1,0:T(8,128)(2,1)S(1)}, bf16[256,128]{1,0:T(8,128)(2,1)S(1)}, u32[]{:S(2)}, u32[]{:S(2)}) collective-permute-start(bf16[256,128]{1,0:T(8,128)(2,1)S(1)} %get-tuple-element.28), channel_id=1, source_target_pairs={{16,64},{20,69},{24,74},{28,79},{17,66},{21,71},{25,72},{29,77},{1... | collective-permute-start | bytes 196616 | tf_op jit(solution)/shard_map/ppermute | solution.py:387
  109.2 1.7 %collective-permute-start.11 = (bf16[256,128]{1,0:T(8,128)(2,1)S(1)}, bf16[256,128]{1,0:T(8,128)(2,1)S(1)}, u32[]{:S(2)}, u32[]{:S(2)}) collective-permute-start(bf16[256,128]{1,0:T(8,128)(2,1)S(1)} %get-tuple-element.29), channel_id=1, source_target_pairs={{16,192},{20,197},{24,202},{28,207},{17,194},{21,199},{25,200},{29... | collective-permute-start | bytes 196616 | tf_op jit(solution)/shard_map/ppermute | solution.py:387
  110.9 1.3 collective-permute-start.12
  112.2 3.7 %collective-permute-done.11.refs_2_ = bf16[256,128]{1,0:T(8,128)(2,1)S(1)} collective-permute-done((bf16[256,128]{1,0:T(8,128)(2,1)S(1)}, bf16[256,128]{1,0:T(8,128)(2,1)S(1)}, u32[]{:S(2)}, u32[]{:S(2)}) %collective-permute-start.11) | collective-permute-done | bytes 65568 | tf_op jit(solution)/shard_map/ppermute | solution.py:387
  115.9 0.7 left.1
  116.7 21.7 %all_to_all.15.got_ref = bf16[64,16,128]{2,1,0:T(8,128)(2,1)S(1)} all-to-all(bf16[64,16,128]{2,1,0:T(8,128)(2,1)S(1)} %bitcast.1), channel_id=1, replica_groups=mesh['zh'=4,'zl'=2,'xl'=2,'y'=4,'xh'=2,'c'=2] {'zh','zl','xl','y'}, dimensions={0} | all-to-all | bytes 524288 | tf_op jit(solution)/shard_map/all_to_all | solution.py:407
  138.4 0.7 place.1
  (14 shorter events, 0.0 us)
Async XLA Ops:
  5.6 7.5 %copy-start.3 = (bf16[16,1024]{1,0:T(8,128)(2,1)S(1)}, bf16[16,1024]{1,0:T(8,128)(2,1)}, u32[]{:S(2)}) copy-start(bf16[16,1024]{1,0:T(8,128)(2,1)} %get-tuple-element.20) | copy-start | bytes 98308
  5.7 9.0 %copy-start.2 = (bf16[16,1024]{1,0:T(8,128)(2,1)S(1)}, bf16[16,1024]{1,0:T(8,128)(2,1)}, u32[]{:S(2)}) copy-start(bf16[16,1024]{1,0:T(8,128)(2,1)} %get-tuple-element.21) | copy-start | bytes 98308
  5.7 11.7 %copy-start.1 = (bf16[16,1024]{1,0:T(8,128)(2,1)S(1)}, bf16[16,1024]{1,0:T(8,128)(2,1)}, u32[]{:S(2)}) copy-start(bf16[16,1024]{1,0:T(8,128)(2,1)} %get-tuple-element.22) | copy-start | bytes 98308
  5.7 37.9 %copy-start = (bf16[16,1024]{1,0:T(8,128)(2,1)S(1)}, bf16[16,1024]{1,0:T(8,128)(2,1)}, u32[]{:S(2)}) copy-start(bf16[16,1024]{1,0:T(8,128)(2,1)} %get-tuple-element.19.refs_0_) | copy-start | bytes 98308
  5.7 37.9 %all-to-all-start = ((bf16[16,592,128]{2,1,0:T(8,128)(2,1)}), bf16[16,592,128]{2,1,0:T(8,128)(2,1)S(1)}, u32[]{:S(2)}, u32[]{:S(2)}) async-start(bf16[16,592,128]{2,1,0:T(8,128)(2,1)} %get-tuple-element.18), calls=%async_computation | async-start | bytes 4849664 | tf_op jit(solution)/shard_map/all_to_all | solution.py:329
  13.1 30.4 %collective-permute-start = (bf16[16,1024]{1,0:T(8,128)(2,1)S(1)}, bf16[16,1024]{1,0:T(8,128)(2,1)S(1)}, u32[]{:S(2)}, u32[]{:S(2)}) collective-permute-start(bf16[16,1024]{1,0:T(8,128)(2,1)S(1)} %copy-done.3), channel_id=1, source_target_pairs={{0,4},{4,8},{8,12},{12,0},{1,5},{5,9},{9,13},{13,1},{2,6},{6,10},{... | collective-permute-start | bytes 98312 | tf_op jit(solution)/shard_map/ppermute | solution.py:302
  14.7 28.8 %collective-permute-start.1 = (bf16[16,1024]{1,0:T(8,128)(2,1)S(1)}, bf16[16,1024]{1,0:T(8,128)(2,1)S(1)}, u32[]{:S(2)}, u32[]{:S(2)}) collective-permute-start(bf16[16,1024]{1,0:T(8,128)(2,1)S(1)} %copy-done.2), channel_id=1, source_target_pairs={{0,8},{4,12},{8,0},{12,4},{1,9},{5,13},{9,1},{13,5},{2,10},{6,14},... | collective-permute-start | bytes 98312 | tf_op jit(solution)/shard_map/ppermute | solution.py:302
  17.4 26.2 %collective-permute-start.2 = (bf16[16,1024]{1,0:T(8,128)(2,1)S(1)}, bf16[16,1024]{1,0:T(8,128)(2,1)S(1)}, u32[]{:S(2)}, u32[]{:S(2)}) collective-permute-start(bf16[16,1024]{1,0:T(8,128)(2,1)S(1)} %copy-done.1), channel_id=1, source_target_pairs={{0,12},{4,0},{8,4},{12,8},{1,13},{5,1},{9,5},{13,9},{2,14},{6,2},{... | collective-permute-start | bytes 98312 | tf_op jit(solution)/shard_map/ppermute | solution.py:302
  44.0 23.3 %collective-permute-start.5 = (bf16[592,128]{1,0:T(8,128)(2,1)S(1)}, bf16[592,128]{1,0:T(8,128)(2,1)S(1)}, u32[]{:S(2)}, u32[]{:S(2)}) collective-permute-start(bf16[592,128]{1,0:T(8,128)(2,1)S(1)} %get-tuple-element.23.refs_0_), channel_id=1, source_target_pairs={{0,128},{64,192},{128,0},{192,64},{1,129},{65,193},{129,1},{193,65... | collective-permute-start | bytes 454664 | tf_op jit(solution)/shard_map/ppermute | solution.py:302
  50.4 17.0 %collective-permute-start.4 = (bf16[592,128]{1,0:T(8,128)(2,1)S(1)}, bf16[592,128]{1,0:T(8,128)(2,1)S(1)}, u32[]{:S(2)}, u32[]{:S(2)}) collective-permute-start(bf16[592,128]{1,0:T(8,128)(2,1)S(1)} %get-tuple-element.23.refs_0_), channel_id=1, source_target_pairs={{0,64},{64,128},{128,192},{192,0},{1,65},{65,129},{129,193},{193,1... | collective-permute-start | bytes 454664 | tf_op jit(solution)/shard_map/ppermute | solution.py:302
  51.8 15.5 %collective-permute-start.3 = (bf16[592,128]{1,0:T(8,128)(2,1)S(1)}, bf16[592,128]{1,0:T(8,128)(2,1)S(1)}, u32[]{:S(2)}, u32[]{:S(2)}) collective-permute-start(bf16[592,128]{1,0:T(8,128)(2,1)S(1)} %get-tuple-element.23.refs_0_), channel_id=1, source_target_pairs={{0,192},{64,0},{128,64},{192,128},{1,193},{65,1},{129,65},{193,129... | collective-permute-start | bytes 454664 | tf_op jit(solution)/shard_map/ppermute | solution.py:302
  54.5 12.8 %collective-permute-start.6 = (bf16[64,1024]{1,0:T(8,128)(2,1)S(1)}, bf16[64,1024]{1,0:T(8,128)(2,1)S(1)}, u32[]{:S(2)}, u32[]{:S(2)}) collective-permute-start(bf16[64,1024]{1,0:T(8,128)(2,1)S(1)} %get-tuple-element.24.refs_4_), channel_id=1, source_target_pairs={{0,32},{32,0},{1,33},{33,1},{2,34},{34,2},{3,35},{35,3},{4,36},{36... | collective-permute-start | bytes 393224 | tf_op jit(solution)/shard_map/ppermute | solution.py:302
  68.8 18.9 %all-to-all-start.1 = ((bf16[8,592,128]{2,1,0:T(8,128)(2,1)}), bf16[8,592,128]{2,1,0:T(8,128)(2,1)S(1)}, u32[]{:S(2)}, u32[]{:S(2)}) async-start(bf16[8,592,128]{2,1,0:T(8,128)(2,1)} %get-tuple-element.25), calls=%async_computation.1 | async-start | bytes 2424832 | tf_op jit(solution)/shard_map/all_to_all | solution.py:364
  73.0 28.5 %collective-permute-start.8 = (bf16[128,1024]{1,0:T(8,128)(2,1)S(1)}, bf16[128,1024]{1,0:T(8,128)(2,1)S(1)}, u32[]{:S(2)}, u32[]{:S(2)}) collective-permute-start(bf16[128,1024]{1,0:T(8,128)(2,1)S(1)} %get-tuple-element.26), channel_id=1, source_target_pairs={{16,16},{21,20},{26,24},{31,28},{18,17},{23,21},{24,25},{29,29},{1... | collective-permute-start | bytes 786440 | tf_op jit(solution)/shard_map/ppermute | solution.py:357
  73.7 27.8 %collective-permute-start.7 = (bf16[128,1024]{1,0:T(8,128)(2,1)S(1)}, bf16[128,1024]{1,0:T(8,128)(2,1)S(1)}, u32[]{:S(2)}, u32[]{:S(2)}) collective-permute-start(bf16[128,1024]{1,0:T(8,128)(2,1)S(1)} %get-tuple-element.26), channel_id=1, source_target_pairs={{0,16},{5,20},{10,24},{15,28},{2,17},{7,21},{8,25},{13,29},{1,18},... | collective-permute-start | bytes 786440 | tf_op jit(solution)/shard_map/ppermute | solution.py:357
  102.0 10.1 %collective-permute-start.9 = (bf16[256,128]{1,0:T(8,128)(2,1)S(1)}, bf16[256,128]{1,0:T(8,128)(2,1)S(1)}, u32[]{:S(2)}, u32[]{:S(2)}) collective-permute-start(bf16[256,128]{1,0:T(8,128)(2,1)S(1)} %get-tuple-element.27), channel_id=1, source_target_pairs={{16,128},{20,133},{24,138},{28,143},{17,130},{21,135},{25,136},{29... | collective-permute-start | bytes 196616 | tf_op jit(solution)/shard_map/ppermute | solution.py:387
  107.3 4.9 %collective-permute-start.10 = (bf16[256,128]{1,0:T(8,128)(2,1)S(1)}, bf16[256,128]{1,0:T(8,128)(2,1)S(1)}, u32[]{:S(2)}, u32[]{:S(2)}) collective-permute-start(bf16[256,128]{1,0:T(8,128)(2,1)S(1)} %get-tuple-element.28), channel_id=1, source_target_pairs={{16,64},{20,69},{24,74},{28,79},{17,66},{21,71},{25,72},{29,77},{1... | collective-permute-start | bytes 196616 | tf_op jit(solution)/shard_map/ppermute | solution.py:387
  109.2 6.8 %collective-permute-start.11 = (bf16[256,128]{1,0:T(8,128)(2,1)S(1)}, bf16[256,128]{1,0:T(8,128)(2,1)S(1)}, u32[]{:S(2)}, u32[]{:S(2)}) collective-permute-start(bf16[256,128]{1,0:T(8,128)(2,1)S(1)} %get-tuple-element.29), channel_id=1, source_target_pairs={{16,192},{20,197},{24,202},{28,207},{17,194},{21,199},{25,200},{29... | collective-permute-start | bytes 196616 | tf_op jit(solution)/shard_map/ppermute | solution.py:387
  110.9 5.1 %collective-permute-start.12 = (bf16[256,128]{1,0:T(8,128)(2,1)S(1)}, bf16[256,128]{1,0:T(8,128)(2,1)S(1)}, u32[]{:S(2)}, u32[]{:S(2)}) collective-permute-start(bf16[256,128]{1,0:T(8,128)(2,1)S(1)} %get-tuple-element.30), channel_id=1, source_target_pairs={{16,0},{20,5},{24,10},{28,15},{17,2},{21,7},{25,8},{29,13},{18,1},... | collective-permute-start | bytes 196616 | tf_op jit(solution)/shard_map/ppermute | solution.py:387

commit v9 on v8

--- a/solution.py
+++ b/solution.py
@@ -76,8 +76,7 @@
     return lax.axis_index("zl") * NY + lax.axis_index("y")
 
 
-def gram_kernel(acts_ref, grads_ref, gradient_ref, out_ref, *refs):
-    turn_refs, (acts, grads, gradient, packed, sems, gradient_sem, out_sems) = refs[:NY], refs[NY:]
+def gram_kernel(acts_ref, grads_ref, out_ref, acts, grads, packed, sems, out_sems):
     rows = acts.shape[0] // LOADS
     loads = []
     for which, (far, near) in enumerate(((acts_ref, acts), (grads_ref, grads))):
@@ -85,8 +84,6 @@
             part = pl.ds(n * rows, rows)
             loads.append(pltpu.make_async_copy(far.at[part], near.at[part], sems.at[which, n]))
             loads[-1].start()
-    gradient_load = pltpu.make_async_copy(gradient_ref, gradient, gradient_sem)
-    gradient_load.start()
     width = 2 * TILE
     eye = lax.broadcasted_iota(jnp.int32, (TILE, TILE), 0) == lax.broadcasted_iota(
         jnp.int32, (TILE, TILE), 1
@@ -128,12 +125,6 @@
                 pltpu.make_async_copy(packed.at[part], out_ref.at[part], out_sems.at[which, zl])
             )
             stores[-1].start()
-    gradient_load.wait()
-    y, own = lax.axis_index("y"), block_here()
-    for shift, ref in enumerate(turn_refs):
-        block = flip_scalar(jnp.bitwise_xor(own, lax.rem(y + shift, NY)))
-        start = pl.multiple_of(block * ORDER, ORDER)
-        ref[...] = gradient[0, :, pl.ds(start, ORDER)].astype(BF16)
     for store in stores:
         store.wait()
 
@@ -177,17 +168,19 @@
     put_rest(out_ref, lines + list(more))
 
 
-def sum_kernel(got_ref, *refs):
-    turn_refs, (out_ref, slab_ref) = refs[:NY], refs[NY:]
-    for turn, ref in enumerate(turn_refs):
-        at = lax.rem(lax.axis_index("y") + NY - turn, NY) * ROWS
-        slab_ref[pl.ds(pl.multiple_of(at, ROWS), ROWS), :] = ref[...]
+def sum_kernel(got_ref, gradient_ref, out_ref, *turn_refs):
+    y, own = lax.axis_index("y"), block_here()
+    for shift, ref in enumerate(turn_refs):
+        block = flip_scalar(jnp.bitwise_xor(own, lax.rem(y + shift, NY)))
+        start = pl.multiple_of(block * ORDER, ORDER)
+        ref[...] = gradient_ref[0, :, pl.ds(start, ORDER)].astype(BF16)
     piece = piece_here()
     put_halves(piece, out_ref, sum_halves(piece, [got_ref.at[n] for n in range(got_ref.shape[0])]))
 
 
 def damp_kernel(all_tokens, *refs):
-    parts, (slab_ref, other_ref, out_ref, slabs_ref, damped, sems) = refs[:NZH], refs[NZH:]
+    parts, turn_refs = refs[:NZH], refs[NZH:NZH + NY]
+    out_ref, slab_ref, damped, sems = refs[NZH + NY:]
     piece = piece_here()
     halves = []
     squares = jnp.zeros((HALF, TILE), F32)
@@ -210,9 +203,9 @@
     ]
     for store in stores:
         store.start()
-    zl, rows = lax.axis_index("zl"), NY * ROWS
-    slabs_ref[pl.ds(pl.multiple_of(zl * rows, rows), rows), :] = slab_ref[...]
-    slabs_ref[pl.ds(pl.multiple_of((1 - zl) * rows, rows), rows), :] = other_ref[...]
+    for turn, ref in enumerate(turn_refs):
+        at = lax.rem(lax.axis_index("y") + NY - turn, NY) * ROWS
+        slab_ref[pl.ds(pl.multiple_of(at, ROWS), ROWS), :] = ref[...]
     for store in stores:
         store.wait()
 
@@ -265,13 +258,14 @@
                 iterate_b[:, s] = iterate[:, s].astype(BF16)
 
 def right_kernel(root_ref, *refs):
-    slab_refs, right_refs, right = refs[:NXL], refs[NXL:NXL + NZH], refs[-1]
+    slab_refs, right_refs, right = refs[:NZL * NXL], refs[NZL * NXL:NZL * NXL + NZH], refs[-1]
     zh, zl, rows = lax.axis_index("zh"), lax.axis_index("zl"), NY * ROWS
     cols = root_ref[:, pl.ds(pl.multiple_of(zl * (NZH * TILE), NZH * TILE), NZH * TILE)]
-    for xl, ref in enumerate(slab_refs):
-        done = jnp.dot(ref[...], cols, preferred_element_type=F32).astype(BF16)
-        for n in range(NZL):
-            right[(n * NXL + xl) * rows:(n * NXL + xl + 1) * rows] = done[n * rows:(n + 1) * rows]
+    for turn, ref in enumerate(slab_refs):
+        at = (lax.rem(zl + turn // NXL, NZL) * NXL + turn % NXL) * rows
+        right[pl.ds(pl.multiple_of(at, rows), rows), :] = jnp.dot(
+            ref[...], cols, preferred_element_type=F32
+        ).astype(BF16)
     for shift, ref in zip(SHIFTS, right_refs):
         at = lax.rem(zh + shift, NZH) * TILE
         ref[...] = right[:, pl.ds(pl.multiple_of(at, TILE), TILE)]
@@ -304,61 +298,61 @@
 
 def local(acts, grads_out, gradient):
     all_tokens = acts.shape[0] * NZ * NXL * NY
-    packed, *turns = call(
+    packed = call(
         gram_kernel,
         "gram",
-        [jax.ShapeDtypeStruct((NZL * NXL * NY, PIECE + REST, TILE), BF16)]
-        + [jax.ShapeDtypeStruct((ROWS, ORDER), BF16)] * NY,
-        (acts, grads_out, gradient),
-        specs=[HBM] * 3,
-        out_specs=[HBM] + [VMEM] * NY,
+        jax.ShapeDtypeStruct((NZL * NXL * NY, PIECE + REST, TILE), BF16),
+        (acts, grads_out),
+        specs=[HBM] * 2,
+        out_specs=HBM,
         scratch=[
             pltpu.VMEM(acts.shape, BF16),
             pltpu.VMEM(acts.shape, BF16),
-            pltpu.VMEM(gradient.shape, F32),
             pltpu.VMEM((NZL * NXL * NY, PIECE + REST, TILE), BF16),
             pltpu.SemaphoreType.DMA((2, LOADS)),
-            pltpu.SemaphoreType.DMA(()),
             pltpu.SemaphoreType.DMA((2, NZL)),
         ],
         flops=4 * acts.shape[0] * ORDER * ORDER,
         vmem=60 << 20,
     )
-    turns = [turns[0]] + [turned(turns[shift], "y", NY, shift) for shift in range(1, NY)]
 
     got = lax.all_to_all(packed, ("zl", "xl", "y"), 0, 0, tiled=True)
-    part, slab = call(
+    part, *turns = call(
         sum_kernel,
         "sum",
-        [
-            jax.ShapeDtypeStruct((PIECE + REST, TILE), BF16),
-            jax.ShapeDtypeStruct((NY * ROWS, ORDER), BF16),
-        ],
-        (got, *turns),
-    )
-    other = turned(slab, "zl", NZL, 1)
+        [jax.ShapeDtypeStruct((PIECE + REST, TILE), BF16)]
+        + [jax.ShapeDtypeStruct((ROWS, ORDER), BF16)] * NY,
+        (got, gradient),
+    )
+    turns = [turns[0]] + [turned(turns[shift], "y", NY, shift) for shift in range(1, NY)]
     parts = [part] + [turned(part, "zh", NZH, shift) for shift in SHIFTS[2::-1]]
-    pieces, slabs = call(
+    pieces, slab = call(
         functools.partial(damp_kernel, float(all_tokens)),
         "damp",
         [
             jax.ShapeDtypeStruct((NZL * NY, PIECE + REST, TILE), BF16),
-            jax.ShapeDtypeStruct((NZL * NY * ROWS, ORDER), BF16),
+            jax.ShapeDtypeStruct((NY * ROWS, ORDER), BF16),
         ],
-        (*parts, slab, other),
+        (*parts, *turns),
         out_specs=[HBM, VMEM],
         scratch=[
             pltpu.VMEM((PIECE + REST, TILE), BF16),
             pltpu.SemaphoreType.DMA((NZL * NY,)),
         ],
     )
+    count = NXL * NY * NBLOCK
     cells = [(partner(k, y), k, y) for k in range(NBLOCK) for y in range(NY)]
     slabs = [
         lax.ppermute(
-            slabs,
-            ("xl", "y", "xh", "c"),
-            [(place(xl, y, i), place(1, y, k)) for i, k, y in cells],
+            slab,
+            ("zl", "xl", "y", "xh", "c"),
+            [
+                ((zl + turn) % NZL * count + place(xl, y, i), zl * count + place(1, y, k))
+                for zl in range(NZL)
+                for i, k, y in cells
+            ],
         )
+        for turn in range(NZL)
         for xl in range(NXL)
     ]
     packed = lax.all_to_all(pieces, ("zl", "y"), 0, 0, tiled=True)
@@ -382,7 +376,6 @@
         flops=2 * ORDER * ZROWS * NZH * TILE,
     )
 
-    count = NXL * NY * NBLOCK
     right_done = [
         lax.ppermute(
             right_done[n],

time: 139 us -> 137 us (0.986)
  blocking collectives: 21.7 us -> 60.7 us
  waiting for transfers between devices: 50.9 us -> 17.3 us
  starting transfers between devices: 43.1 us -> 35.9 us
    all_to_all x0 -> x1, blocking collectives: none -> 37.5 us  [local(): got = lax.all_to_all(packed, ('zl', 'xl', 'y'), 0, 0, tiled=True)]
    ppermute x7 -> x6, waiting for transfers between devices: 34.6 us -> 6.01 us  [turned(): return lax.ppermute(x, axes, [(n, (n + shift) % size) for n in range(size)])]
    all_to_all x1 -> x0, starting transfers between devices: 7.45 us -> none  [local(): got = lax.all_to_all(packed, ('zl', 'xl', 'y'), 0, 0, tiled=True)]
    ppermute x7 -> x6, starting transfers between devices: 19.2 us -> 13.5 us  [turned(): return lax.ppermute(x, axes, [(n, (n + shift) % size) for n in range(size)])]
    ppermute x2 -> x4, starting transfers between devices: 2.14 us -> 7.35 us  [local(): lax.ppermute(slab, ('zl', 'xl', 'y', 'xh', 'c'), [((zl + turn) % NZL * co...]
    all_to_all x1, waiting for transfers between devices: 12.5 us -> 8.67 us  [local(): packed = lax.all_to_all(pieces, ('zl', 'y'), 0, 0, tiled=True)]
    all_to_all x1, blocking collectives: 21.7 us -> 23.2 us  [local(): returned = lax.all_to_all(result, DP, 0, 0, tiled=True)]
where the time goes in v9:
time: 137 us
  blocking collectives  60.7 us (44%)
  starting transfers between devices  35.9 us (26%)
  Pallas kernels  22.9 us (17%)
  waiting for transfers between devices  17.3 us (13%)
    all_to_all x1, blocking collectives, local(): got = lax.all_to_all(packed, ('zl', 'xl', 'y'), 0, 0, tiled=True)  37.5 us
    all_to_all x1, blocking collectives, local(): returned = lax.all_to_all(result, DP, 0, 0, tiled=True)  23.2 us
    pallas_call x7, Pallas kernels, call(): pl.pallas_call(kernel, out_shape=out_shape, scratch_shapes=list(scratch),...  22.9 us
    ppermute x6, starting transfers between devices, turned(): return lax.ppermute(x, axes, [(n, (n + shift) % size) for n in range(size)])  13.5 us
    ppermute x4, starting transfers between devices, local(): lax.ppermute(right_done[n], ('zh', 'xl', 'y', 'xh', 'c'), [(zh * count +...  11.3 us
    all_to_all x1, waiting for transfers between devices, local(): packed = lax.all_to_all(pieces, ('zl', 'y'), 0, 0, tiled=True)  8.67 us
    ppermute x4, starting transfers between devices, local(): lax.ppermute(slab, ('zl', 'xl', 'y', 'xh', 'c'), [((zl + turn) % NZL * co...  7.35 us
    ppermute x6, waiting for transfers between devices, turned(): return lax.ppermute(x, axes, [(n, (n + shift) % size) for n in range(size)])  6.01 us
  transfers between devices with their start and end apart: 15, of which 5 were waited for; matrix products, arithmetic and copies ran while one was open for 0% of the time, Pallas kernels for 10%

profile of v9, /device:TPU:2, one launch (start us, length us, event | category | flops | bytes accessed | tf_op | source)
XLA Modules:
  0.0 137.0 jit_solution(9060211174331722968)
XLA Ops:
  0.0 5.0 %gram.1 = bf16[16,592,128]{2,1,0:T(8,128)(2,1)} custom-call(bf16[768,1024]{1,0:T(8,128)(2,1)} %acts_ref.1, bf16[768,1024]{1,0:T(8,128)(2,1)} %grads_ref.1), custom_call_target="tpu_custom_call" | custom-call | flops 3221225472 | bytes 4194304 | tf_op jit(solution)/shard_map/gram/pallas_call | solution.py:44
  5.0 0.0 copy-start
  5.0 37.5 %all_to_all.15.got_ref = bf16[16,592,128]{2,1,0:T(8,128)(2,1)S(1)} all-to-all(bf16[16,592,128]{2,1,0:T(8,128)(2,1)} %gram.1), channel_id=1, replica_groups=mesh['zh'=4,'zl'=2,'xl'=2,'y'=4,'xh'=2,'c'=2] {'zl','xl','y'}, dimensions={0} | all-to-all | bytes 4849664 | tf_op jit(solution)/shard_map/all_to_all | solution.py:319
  42.5 0.4 sum.1
  42.9 6.4 %collective-permute-start.2 = (bf16[592,128]{1,0:T(8,128)(2,1)S(1)}, bf16[592,128]{1,0:T(8,128)(2,1)S(1)}, u32[]{:S(2)}, u32[]{:S(2)}) collective-permute-start(bf16[592,128]{1,0:T(8,128)(2,1)S(1)} %get-tuple-element.16.refs_0_), channel_id=1, source_target_pairs={{0,128},{64,192},{128,0},{192,64},{1,129},{65,193},{129,1},{193,65... | collective-permute-start | bytes 454664 | tf_op jit(solution)/shard_map/ppermute | solution.py:296
  49.3 1.5 %collective-permute-start.1 = (bf16[592,128]{1,0:T(8,128)(2,1)S(1)}, bf16[592,128]{1,0:T(8,128)(2,1)S(1)}, u32[]{:S(2)}, u32[]{:S(2)}) collective-permute-start(bf16[592,128]{1,0:T(8,128)(2,1)S(1)} %get-tuple-element.16.refs_0_), channel_id=1, source_target_pairs={{0,64},{64,128},{128,192},{192,0},{1,65},{65,129},{129,193},{193,1... | collective-permute-start | bytes 454664 | tf_op jit(solution)/shard_map/ppermute | solution.py:296
  50.8 2.7 %collective-permute-start = (bf16[592,128]{1,0:T(8,128)(2,1)S(1)}, bf16[592,128]{1,0:T(8,128)(2,1)S(1)}, u32[]{:S(2)}, u32[]{:S(2)}) collective-permute-start(bf16[592,128]{1,0:T(8,128)(2,1)S(1)} %get-tuple-element.16.refs_0_), channel_id=1, source_target_pairs={{0,192},{64,0},{128,64},{192,128},{1,193},{65,1},{129,65},{193,129... | collective-permute-start | bytes 454664 | tf_op jit(solution)/shard_map/ppermute | solution.py:296
  53.4 0.4 collective-permute-start.3
  53.8 2.4 %collective-permute-start.4 = (bf16[16,1024]{1,0:T(8,128)(2,1)S(1)}, bf16[16,1024]{1,0:T(8,128)(2,1)S(1)}, u32[]{:S(2)}, u32[]{:S(2)}) collective-permute-start(bf16[16,1024]{1,0:T(8,128)(2,1)S(1)} %get-tuple-element.19), channel_id=1, source_target_pairs={{0,8},{4,12},{8,0},{12,4},{1,9},{5,13},{9,1},{13,5},{2,10},{6,14},... | collective-permute-start | bytes 98312 | tf_op jit(solution)/shard_map/ppermute | solution.py:296
  56.3 2.3 %collective-permute-done.3.refs_5_ = bf16[16,1024]{1,0:T(8,128)(2,1)S(1)} collective-permute-done((bf16[16,1024]{1,0:T(8,128)(2,1)S(1)}, bf16[16,1024]{1,0:T(8,128)(2,1)S(1)}, u32[]{:S(2)}, u32[]{:S(2)}) %collective-permute-start.3) | collective-permute-done | bytes 32800 | tf_op jit(solution)/shard_map/ppermute | solution.py:296
  58.6 0.2 collective-permute-start.5
  58.7 0.5 collective-permute-done.4.refs_6_
  59.3 3.2 %collective-permute-done.5.refs_7_ = bf16[16,1024]{1,0:T(8,128)(2,1)S(1)} collective-permute-done((bf16[16,1024]{1,0:T(8,128)(2,1)S(1)}, bf16[16,1024]{1,0:T(8,128)(2,1)S(1)}, u32[]{:S(2)}, u32[]{:S(2)}) %collective-permute-start.5) | collective-permute-done | bytes 32800 | tf_op jit(solution)/shard_map/ppermute | solution.py:296
  62.5 1.4 %damp.1 = (bf16[8,592,128]{2,1,0:T(8,128)(2,1)}, bf16[64,1024]{1,0:T(8,128)(2,1)S(1)}) custom-call(bf16[592,128]{1,0:T(8,128)(2,1)S(1)} %get-tuple-element.16.refs_0_, bf16[592,128]{1,0:T(8,128)(2,1)S(1)} %collective-permute-done.refs_1_, bf16[592,128]{1,0:T(8,128)(2,1)S(1)} %collective-permute-done.1.refs_2_, ...), custom_call_target="tpu_custom_call" | custom-call | bytes 4194304 | tf_op jit(solution)/shard_map/damp/pallas_call | solution.py:44
  63.9 3.7 %all-to-all-start.1 = ((bf16[8,592,128]{2,1,0:T(8,128)(2,1)}), bf16[8,592,128]{2,1,0:T(8,128)(2,1)S(1)}, u32[]{:S(2)}, u32[]{:S(2)}) async-start(bf16[8,592,128]{2,1,0:T(8,128)(2,1)} %get-tuple-element.21), calls=%async_computation.1 | async-start | bytes 2424832 | tf_op jit(solution)/shard_map/all_to_all | solution.py:358
  67.6 3.9 %collective-permute-start.9 = (bf16[64,1024]{1,0:T(8,128)(2,1)S(1)}, bf16[64,1024]{1,0:T(8,128)(2,1)S(1)}, u32[]{:S(2)}, u32[]{:S(2)}) collective-permute-start(bf16[64,1024]{1,0:T(8,128)(2,1)S(1)} %get-tuple-element.22), channel_id=1, source_target_pairs={{48,16},{53,20},{58,24},{63,28},{50,17},{55,21},{56,25},{61,29},{4... | collective-permute-start | bytes 393224 | tf_op jit(solution)/shard_map/ppermute | solution.py:346
  71.5 1.3 collective-permute-start.8
  72.8 0.7 collective-permute-start.7
  73.5 1.5 %collective-permute-start.6 = (bf16[64,1024]{1,0:T(8,128)(2,1)S(1)}, bf16[64,1024]{1,0:T(8,128)(2,1)S(1)}, u32[]{:S(2)}, u32[]{:S(2)}) collective-permute-start(bf16[64,1024]{1,0:T(8,128)(2,1)S(1)} %get-tuple-element.22), channel_id=1, source_target_pairs={{0,16},{5,20},{10,24},{15,28},{2,17},{7,21},{8,25},{13,29},{1,18},... | collective-permute-start | bytes 393224 | tf_op jit(solution)/shard_map/ppermute | solution.py:346
  74.9 8.7 %all-to-all-done.1.packed_ref = bf16[8,592,128]{2,1,0:T(8,128)(2,1)S(1)} async-done(((bf16[8,592,128]{2,1,0:T(8,128)(2,1)}), bf16[8,592,128]{2,1,0:T(8,128)(2,1)S(1)}, u32[]{:S(2)}, u32[]{:S(2)}) %all-to-all-start.1) | async-done | bytes 1212448 | tf_op jit(solution)/shard_map/all_to_all | solution.py:358
  83.6 13.8 %root.1.root_ref = bf16[1024,1024]{1,0:T(8,128)(2,1)S(1)} custom-call(bf16[8,592,128]{2,1,0:T(8,128)(2,1)S(1)} %all-to-all-done.1.packed_ref), custom_call_target="tpu_custom_call" | custom-call | flops 12884901888 | bytes 4194304 | tf_op jit(solution)/shard_map/root/pallas_call | solution.py:44
  97.4 0.0 collective-permute-done.9.refs_3_
  97.4 0.0 collective-permute-done.7.refs_1_
  97.4 0.9 right.1
  98.3 6.7 %collective-permute-start.10 = (bf16[256,128]{1,0:T(8,128)(2,1)S(1)}, bf16[256,128]{1,0:T(8,128)(2,1)S(1)}, u32[]{:S(2)}, u32[]{:S(2)}) collective-permute-start(bf16[256,128]{1,0:T(8,128)(2,1)S(1)} %get-tuple-element.23), channel_id=1, source_target_pairs={{16,128},{20,133},{24,138},{28,143},{17,130},{21,135},{25,136},{29... | collective-permute-start | bytes 196616 | tf_op jit(solution)/shard_map/ppermute | solution.py:380
  105.1 1.3 collective-permute-start.11
  106.4 2.0 %collective-permute-start.12 = (bf16[256,128]{1,0:T(8,128)(2,1)S(1)}, bf16[256,128]{1,0:T(8,128)(2,1)S(1)}, u32[]{:S(2)}, u32[]{:S(2)}) collective-permute-start(bf16[256,128]{1,0:T(8,128)(2,1)S(1)} %get-tuple-element.25), channel_id=1, source_target_pairs={{16,192},{20,197},{24,202},{28,207},{17,194},{21,199},{25,200},{29... | collective-permute-start | bytes 196616 | tf_op jit(solution)/shard_map/ppermute | solution.py:380
  108.4 1.3 collective-permute-start.13
  109.7 2.6 %collective-permute-done.12.refs_2_ = bf16[256,128]{1,0:T(8,128)(2,1)S(1)} collective-permute-done((bf16[256,128]{1,0:T(8,128)(2,1)S(1)}, bf16[256,128]{1,0:T(8,128)(2,1)S(1)}, u32[]{:S(2)}, u32[]{:S(2)}) %collective-permute-start.12) | collective-permute-done | bytes 65568 | tf_op jit(solution)/shard_map/ppermute | solution.py:380
  112.3 0.7 left.1
  113.1 23.2 %all_to_all.16.got_ref = bf16[64,16,128]{2,1,0:T(8,128)(2,1)S(1)} all-to-all(bf16[64,16,128]{2,1,0:T(8,128)(2,1)S(1)} %bitcast.1), channel_id=1, replica_groups=mesh['zh'=4,'zl'=2,'xl'=2,'y'=4,'xh'=2,'c'=2] {'zh','zl','xl','y'}, dimensions={0} | all-to-all | bytes 524288 | tf_op jit(solution)/shard_map/all_to_all | solution.py:400
  136.3 0.7 place.1
  (9 shorter events, 0.0 us)
Async XLA Ops:
  5.0 37.5 %copy-start = (f32[1,16,4096]{2,1,0:T(8,128)S(1)}, f32[1,16,4096]{2,1,0:T(8,128)}, u32[]{:S(2)}) copy-start(f32[1,16,4096]{2,1,0:T(8,128)} %gradient_ref.1) | copy-start | bytes 786436
  42.9 19.6 %collective-permute-start.2 = (bf16[592,128]{1,0:T(8,128)(2,1)S(1)}, bf16[592,128]{1,0:T(8,128)(2,1)S(1)}, u32[]{:S(2)}, u32[]{:S(2)}) collective-permute-start(bf16[592,128]{1,0:T(8,128)(2,1)S(1)} %get-tuple-element.16.refs_0_), channel_id=1, source_target_pairs={{0,128},{64,192},{128,0},{192,64},{1,129},{65,193},{129,1},{193,65... | collective-permute-start | bytes 454664 | tf_op jit(solution)/shard_map/ppermute | solution.py:296
  49.3 13.2 %collective-permute-start.1 = (bf16[592,128]{1,0:T(8,128)(2,1)S(1)}, bf16[592,128]{1,0:T(8,128)(2,1)S(1)}, u32[]{:S(2)}, u32[]{:S(2)}) collective-permute-start(bf16[592,128]{1,0:T(8,128)(2,1)S(1)} %get-tuple-element.16.refs_0_), channel_id=1, source_target_pairs={{0,64},{64,128},{128,192},{192,0},{1,65},{65,129},{129,193},{193,1... | collective-permute-start | bytes 454664 | tf_op jit(solution)/shard_map/ppermute | solution.py:296
  50.8 11.7 %collective-permute-start = (bf16[592,128]{1,0:T(8,128)(2,1)S(1)}, bf16[592,128]{1,0:T(8,128)(2,1)S(1)}, u32[]{:S(2)}, u32[]{:S(2)}) collective-permute-start(bf16[592,128]{1,0:T(8,128)(2,1)S(1)} %get-tuple-element.16.refs_0_), channel_id=1, source_target_pairs={{0,192},{64,0},{128,64},{192,128},{1,193},{65,1},{129,65},{193,129... | collective-permute-start | bytes 454664 | tf_op jit(solution)/shard_map/ppermute | solution.py:296
  53.4 5.1 %collective-permute-start.3 = (bf16[16,1024]{1,0:T(8,128)(2,1)S(1)}, bf16[16,1024]{1,0:T(8,128)(2,1)S(1)}, u32[]{:S(2)}, u32[]{:S(2)}) collective-permute-start(bf16[16,1024]{1,0:T(8,128)(2,1)S(1)} %get-tuple-element.18), channel_id=1, source_target_pairs={{0,4},{4,8},{8,12},{12,0},{1,5},{5,9},{9,13},{13,1},{2,6},{6,10},{... | collective-permute-start | bytes 98312 | tf_op jit(solution)/shard_map/ppermute | solution.py:296
  53.8 5.4 %collective-permute-start.4 = (bf16[16,1024]{1,0:T(8,128)(2,1)S(1)}, bf16[16,1024]{1,0:T(8,128)(2,1)S(1)}, u32[]{:S(2)}, u32[]{:S(2)}) collective-permute-start(bf16[16,1024]{1,0:T(8,128)(2,1)S(1)} %get-tuple-element.19), channel_id=1, source_target_pairs={{0,8},{4,12},{8,0},{12,4},{1,9},{5,13},{9,1},{13,5},{2,10},{6,14},... | collective-permute-start | bytes 98312 | tf_op jit(solution)/shard_map/ppermute | solution.py:296
  58.6 3.9 %collective-permute-start.5 = (bf16[16,1024]{1,0:T(8,128)(2,1)S(1)}, bf16[16,1024]{1,0:T(8,128)(2,1)S(1)}, u32[]{:S(2)}, u32[]{:S(2)}) collective-permute-start(bf16[16,1024]{1,0:T(8,128)(2,1)S(1)} %get-tuple-element.20), channel_id=1, source_target_pairs={{0,12},{4,0},{8,4},{12,8},{1,13},{5,1},{9,5},{13,9},{2,14},{6,2},{... | collective-permute-start | bytes 98312 | tf_op jit(solution)/shard_map/ppermute | solution.py:296
  63.9 19.7 %all-to-all-start.1 = ((bf16[8,592,128]{2,1,0:T(8,128)(2,1)}), bf16[8,592,128]{2,1,0:T(8,128)(2,1)S(1)}, u32[]{:S(2)}, u32[]{:S(2)}) async-start(bf16[8,592,128]{2,1,0:T(8,128)(2,1)} %get-tuple-element.21), calls=%async_computation.1 | async-start | bytes 2424832 | tf_op jit(solution)/shard_map/all_to_all | solution.py:358
  67.6 29.8 %collective-permute-start.9 = (bf16[64,1024]{1,0:T(8,128)(2,1)S(1)}, bf16[64,1024]{1,0:T(8,128)(2,1)S(1)}, u32[]{:S(2)}, u32[]{:S(2)}) collective-permute-start(bf16[64,1024]{1,0:T(8,128)(2,1)S(1)} %get-tuple-element.22), channel_id=1, source_target_pairs={{48,16},{53,20},{58,24},{63,28},{50,17},{55,21},{56,25},{61,29},{4... | collective-permute-start | bytes 393224 | tf_op jit(solution)/shard_map/ppermute | solution.py:346
  71.5 25.9 %collective-permute-start.8 = (bf16[64,1024]{1,0:T(8,128)(2,1)S(1)}, bf16[64,1024]{1,0:T(8,128)(2,1)S(1)}, u32[]{:S(2)}, u32[]{:S(2)}) collective-permute-start(bf16[64,1024]{1,0:T(8,128)(2,1)S(1)} %get-tuple-element.22), channel_id=1, source_target_pairs={{32,16},{37,20},{42,24},{47,28},{34,17},{39,21},{40,25},{45,29},{3... | collective-permute-start | bytes 393224 | tf_op jit(solution)/shard_map/ppermute | solution.py:346
  72.8 24.6 %collective-permute-start.7 = (bf16[64,1024]{1,0:T(8,128)(2,1)S(1)}, bf16[64,1024]{1,0:T(8,128)(2,1)S(1)}, u32[]{:S(2)}, u32[]{:S(2)}) collective-permute-start(bf16[64,1024]{1,0:T(8,128)(2,1)S(1)} %get-tuple-element.22), channel_id=1, source_target_pairs={{16,16},{21,20},{26,24},{31,28},{18,17},{23,21},{24,25},{29,29},{1... | collective-permute-start | bytes 393224 | tf_op jit(solution)/shard_map/ppermute | solution.py:346
  73.5 24.0 %collective-permute-start.6 = (bf16[64,1024]{1,0:T(8,128)(2,1)S(1)}, bf16[64,1024]{1,0:T(8,128)(2,1)S(1)}, u32[]{:S(2)}, u32[]{:S(2)}) collective-permute-start(bf16[64,1024]{1,0:T(8,128)(2,1)S(1)} %get-tuple-element.22), channel_id=1, source_target_pairs={{0,16},{5,20},{10,24},{15,28},{2,17},{7,21},{8,25},{13,29},{1,18},... | collective-permute-start | bytes 393224 | tf_op jit(solution)/shard_map/ppermute | solution.py:346
  98.3 11.4 %collective-permute-start.10 = (bf16[256,128]{1,0:T(8,128)(2,1)S(1)}, bf16[256,128]{1,0:T(8,128)(2,1)S(1)}, u32[]{:S(2)}, u32[]{:S(2)}) collective-permute-start(bf16[256,128]{1,0:T(8,128)(2,1)S(1)} %get-tuple-element.23), channel_id=1, source_target_pairs={{16,128},{20,133},{24,138},{28,143},{17,130},{21,135},{25,136},{29... | collective-permute-start | bytes 196616 | tf_op jit(solution)/shard_map/ppermute | solution.py:380
  105.1 4.6 %collective-permute-start.11 = (bf16[256,128]{1,0:T(8,128)(2,1)S(1)}, bf16[256,128]{1,0:T(8,128)(2,1)S(1)}, u32[]{:S(2)}, u32[]{:S(2)}) collective-permute-start(bf16[256,128]{1,0:T(8,128)(2,1)S(1)} %get-tuple-element.24), channel_id=1, source_target_pairs={{16,64},{20,69},{24,74},{28,79},{17,66},{21,71},{25,72},{29,77},{1... | collective-permute-start | bytes 196616 | tf_op jit(solution)/shard_map/ppermute | solution.py:380
  106.4 5.9 %collective-permute-start.12 = (bf16[256,128]{1,0:T(8,128)(2,1)S(1)}, bf16[256,128]{1,0:T(8,128)(2,1)S(1)}, u32[]{:S(2)}, u32[]{:S(2)}) collective-permute-start(bf16[256,128]{1,0:T(8,128)(2,1)S(1)} %get-tuple-element.25), channel_id=1, source_target_pairs={{16,192},{20,197},{24,202},{28,207},{17,194},{21,199},{25,200},{29... | collective-permute-start | bytes 196616 | tf_op jit(solution)/shard_map/ppermute | solution.py:380
  108.4 3.9 %collective-permute-start.13 = (bf16[256,128]{1,0:T(8,128)(2,1)S(1)}, bf16[256,128]{1,0:T(8,128)(2,1)S(1)}, u32[]{:S(2)}, u32[]{:S(2)}) collective-permute-start(bf16[256,128]{1,0:T(8,128)(2,1)S(1)} %get-tuple-element.26), channel_id=1, source_target_pairs={{16,0},{20,5},{24,10},{28,15},{17,2},{21,7},{25,8},{29,13},{18,1},... | collective-permute-start | bytes 196616 | tf_op jit(solution)/shard_map/ppermute | solution.py:380

commit v10 on v9

--- a/solution.py
+++ b/solution.py
@@ -11,7 +11,7 @@
 SWEEPS = 2
 DAMPING = 0.05
 TILE = 128
-VMEM_BYTES = 48 << 20
+VMEM_BYTES = 28 << 20
 
 AXES = ("zh", "zl", "xl", "y", "xh", "c")
 SIZES = (4, 2, 2, 4, 2, 2)
@@ -210,11 +210,11 @@
         store.wait()
 
 
-def root_kernel(packed_ref, root_ref, scaled, iterate, iterate_b, square_b, cubic_b):
+def root_kernel(packed_ref, over_ref, iterate, iterate_b, cubic_b, scaled, square_b):
     terms = sum([packed_ref[n, PIECE:].astype(F32) for n in range(NZL * NY)])[HALVES:HALVES + TERMS]
     frob = jnp.sqrt(jnp.sum(terms, axis=0, keepdims=True)[:, 0:1])
     over_frob = 1.0 / frob
-    over_root = 1.0 / jnp.sqrt(frob)
+    over_ref[...] = jnp.broadcast_to(1.0 / jnp.sqrt(frob), over_ref.shape)
     for r, c in PAIRS:
         parts = []
         for half in range(2):
@@ -238,29 +238,40 @@
         iterate_b[:, s] = first.astype(BF16)
     for sweep in range(SWEEPS):
         for s in tiles:
-            square_b[:, s] = jnp.dot(
-                iterate_b[...], iterate_b[:, s], preferred_element_type=F32
+            upper = jnp.dot(
+                iterate_b[:s.stop], iterate_b[:, s], preferred_element_type=F32
             ).astype(BF16)
+            square_b[:s.stop, s] = upper
+            for t in tiles[:s.start // width]:
+                square_b[s, t] = upper[t].T
         for s in tiles:
             cubic_b[:, s] = jnp.dot(
                 square_b[...], scaled[:, s], preferred_element_type=F32
             ).astype(BF16)
-        for s in tiles:
-            new = 1.5 * iterate[:, s] - 0.5 * jnp.dot(
-                cubic_b[...], iterate_b[:, s], preferred_element_type=F32
-            )
-            if sweep < SWEEPS - 1:
-                iterate[:, s] = new
-            else:
-                root_ref[:, s] = (new * over_root).astype(BF16)
         if sweep < SWEEPS - 1:
             for s in tiles:
+                iterate[:, s] = last_product(iterate[:, s], cubic_b, iterate_b[:, s])
+            for s in tiles:
                 iterate_b[:, s] = iterate[:, s].astype(BF16)
 
-def right_kernel(root_ref, *refs):
+
+def last_product(iterate, cubic_b, iterate_b):
+    return 1.5 * iterate - 0.5 * jnp.dot(cubic_b[...], iterate_b, preferred_element_type=F32)
+
+
+def rest_kernel(over_ref, iterate, iterate_b, cubic_b, root_ref):
+    width = 2 * TILE
+    for s in [slice(n, n + width) for n in range(0, ORDER, width)]:
+        new = last_product(iterate[:, s], cubic_b, iterate_b[:, s])
+        root_ref[:, s] = (new * over_ref[0:1, 0:1]).astype(BF16)
+
+
+def right_kernel(over_ref, iterate, iterate_b, cubic_b, *refs):
     slab_refs, right_refs, right = refs[:NZL * NXL], refs[NZL * NXL:NZL * NXL + NZH], refs[-1]
     zh, zl, rows = lax.axis_index("zh"), lax.axis_index("zl"), NY * ROWS
-    cols = root_ref[:, pl.ds(pl.multiple_of(zl * (NZH * TILE), NZH * TILE), NZH * TILE)]
+    here = pl.ds(pl.multiple_of(zl * (NZH * TILE), NZH * TILE), NZH * TILE)
+    cols = last_product(iterate[:, here], cubic_b, iterate_b[:, here])
+    cols = (cols * over_ref[0:1, 0:1]).astype(BF16)
     for turn, ref in enumerate(slab_refs):
         at = (lax.rem(zl + turn // NXL, NZL) * NXL + turn % NXL) * rows
         right[pl.ds(pl.multiple_of(at, rows), rows), :] = jnp.dot(
@@ -359,22 +370,29 @@
 
     square_b = pltpu.VMEM((ORDER, ORDER), BF16)
     right_done = jax.ShapeDtypeStruct((ZROWS, TILE), BF16)
-    root = call(
+    square = jax.ShapeDtypeStruct((ORDER, ORDER), BF16)
+    factors = call(
         root_kernel,
         "root",
-        jax.ShapeDtypeStruct((ORDER, ORDER), BF16),
+        [
+            jax.ShapeDtypeStruct((8, TILE), F32),
+            jax.ShapeDtypeStruct((ORDER, ORDER), F32),
+            square,
+            square,
+        ],
         (packed,),
-        scratch=[square_b, pltpu.VMEM((ORDER, ORDER), F32), square_b, square_b, square_b],
-        flops=6 * SWEEPS * ORDER**3,
+        scratch=[square_b, square_b],
+        flops=10 * ORDER**3,
     )
     right_done = call(
         right_kernel,
         "right",
         [right_done] * NZH,
-        (root, *slabs),
+        (*factors, *slabs),
         scratch=[pltpu.VMEM((ZROWS, NZH * TILE), BF16)],
-        flops=2 * ORDER * ZROWS * NZH * TILE,
-    )
+        flops=2 * ORDER * (ZROWS + ORDER) * NZH * TILE,
+    )
+    root = call(rest_kernel, "rest", square, factors, flops=2 * ORDER**3)
 
     right_done = [
         lax.ppermute(

time: 137 us -> 134 us (0.978)
  starting transfers between devices: 35.9 us -> 33.5 us
    ppermute x4, waiting for transfers between devices: 2.6 us -> 0.48 us  [local(): lax.ppermute(right_done[n], ('zh', 'xl', 'y', 'xh', 'c'), [(zh * count +...]
    ppermute x4, starting transfers between devices: 11.3 us -> 9.72 us  [local(): lax.ppermute(right_done[n], ('zh', 'xl', 'y', 'xh', 'c'), [(zh * count +...]
    ppermute x6, waiting for transfers between devices: 6.01 us -> 7.61 us  [turned(): return lax.ppermute(x, axes, [(n, (n + shift) % size) for n in range(size)])]
    pallas_call x7 -> x8, Pallas kernels: 22.9 us -> 24.1 us  [call(): pl.pallas_call(kernel, out_shape=out_shape, scratch_shapes=list(scratch),...]
  transfers between devices with their start and end apart: 15 -> 15, of which waited for: 5 -> 6; matrix products, arithmetic and copies ran while one was open for 0% -> 0% of each run, Pallas kernels for 10% -> 10%
where the time goes in v10:
time: 134 us
  blocking collectives  60 us (45%)
  starting transfers between devices  33.5 us (25%)
  Pallas kernels  24.1 us (18%)
  waiting for transfers between devices  16.1 us (12%)
    all_to_all x1, blocking collectives, local(): got = lax.all_to_all(packed, ('zl', 'xl', 'y'), 0, 0, tiled=True)  37.5 us
    pallas_call x8, Pallas kernels, call(): pl.pallas_call(kernel, out_shape=out_shape, scratch_shapes=list(scratch),...  24.1 us
    all_to_all x1, blocking collectives, local(): returned = lax.all_to_all(result, DP, 0, 0, tiled=True)  22.5 us
    ppermute x6, starting transfers between devices, turned(): return lax.ppermute(x, axes, [(n, (n + shift) % size) for n in range(size)])  12.3 us
    ppermute x4, starting transfers between devices, local(): lax.ppermute(right_done[n], ('zh', 'xl', 'y', 'xh', 'c'), [(zh * count +...  9.72 us
    all_to_all x1, waiting for transfers between devices, local(): packed = lax.all_to_all(pieces, ('zl', 'y'), 0, 0, tiled=True)  8 us
    ppermute x6, waiting for transfers between devices, turned(): return lax.ppermute(x, axes, [(n, (n + shift) % size) for n in range(size)])  7.61 us
    ppermute x4, starting transfers between devices, local(): lax.ppermute(slab, ('zl', 'xl', 'y', 'xh', 'c'), [((zl + turn) % NZL * co...  7.35 us
  transfers between devices with their start and end apart: 15, of which 6 were waited for; matrix products, arithmetic and copies ran while one was open for 0% of the time, Pallas kernels for 10%

profile of v10, /device:TPU:2, one launch (start us, length us, event | category | flops | bytes accessed | tf_op | source)
XLA Modules:
  0.0 133.8 jit_solution(1412597936027779479)
XLA Ops:
  0.0 5.0 %gram.1 = bf16[16,592,128]{2,1,0:T(8,128)(2,1)} custom-call(bf16[768,1024]{1,0:T(8,128)(2,1)} %acts_ref.1, bf16[768,1024]{1,0:T(8,128)(2,1)} %grads_ref.1), custom_call_target="tpu_custom_call" | custom-call | flops 3221225472 | bytes 4194304 | tf_op jit(solution)/shard_map/gram/pallas_call | solution.py:44
  5.0 0.0 copy-start
  5.0 37.5 %all_to_all.15.got_ref = bf16[16,592,128]{2,1,0:T(8,128)(2,1)S(1)} all-to-all(bf16[16,592,128]{2,1,0:T(8,128)(2,1)} %gram.1), channel_id=1, replica_groups=mesh['zh'=4,'zl'=2,'xl'=2,'y'=4,'xh'=2,'c'=2] {'zl','xl','y'}, dimensions={0} | all-to-all | bytes 4849664 | tf_op jit(solution)/shard_map/all_to_all | solution.py:330
  42.5 0.4 sum.1
  42.9 5.5 %collective-permute-start = (bf16[592,128]{1,0:T(8,128)(2,1)S(1)}, bf16[592,128]{1,0:T(8,128)(2,1)S(1)}, u32[]{:S(2)}, u32[]{:S(2)}) collective-permute-start(bf16[592,128]{1,0:T(8,128)(2,1)S(1)} %get-tuple-element.20.refs_0_), channel_id=1, source_target_pairs={{0,192},{64,0},{128,64},{192,128},{1,193},{65,1},{129,65},{193,129... | collective-permute-start | bytes 454664 | tf_op jit(solution)/shard_map/ppermute | solution.py:307
  48.4 3.8 %collective-permute-start.2 = (bf16[592,128]{1,0:T(8,128)(2,1)S(1)}, bf16[592,128]{1,0:T(8,128)(2,1)S(1)}, u32[]{:S(2)}, u32[]{:S(2)}) collective-permute-start(bf16[592,128]{1,0:T(8,128)(2,1)S(1)} %get-tuple-element.20.refs_0_), channel_id=1, source_target_pairs={{0,128},{64,192},{128,0},{192,64},{1,129},{65,193},{129,1},{193,65... | collective-permute-start | bytes 454664 | tf_op jit(solution)/shard_map/ppermute | solution.py:307
  52.2 0.4 collective-permute-start.3
  52.6 2.4 %collective-permute-start.4 = (bf16[16,1024]{1,0:T(8,128)(2,1)S(1)}, bf16[16,1024]{1,0:T(8,128)(2,1)S(1)}, u32[]{:S(2)}, u32[]{:S(2)}) collective-permute-start(bf16[16,1024]{1,0:T(8,128)(2,1)S(1)} %get-tuple-element.23), channel_id=1, source_target_pairs={{0,8},{4,12},{8,0},{12,4},{1,9},{5,13},{9,1},{13,5},{2,10},{6,14},... | collective-permute-start | bytes 98312 | tf_op jit(solution)/shard_map/ppermute | solution.py:307
  55.1 2.3 %collective-permute-done.3.refs_5_ = bf16[16,1024]{1,0:T(8,128)(2,1)S(1)} collective-permute-done((bf16[16,1024]{1,0:T(8,128)(2,1)S(1)}, bf16[16,1024]{1,0:T(8,128)(2,1)S(1)}, u32[]{:S(2)}, u32[]{:S(2)}) %collective-permute-start.3) | collective-permute-done | bytes 32800 | tf_op jit(solution)/shard_map/ppermute | solution.py:307
  57.3 0.2 collective-permute-start.5
  57.5 0.5 collective-permute-done.4.refs_6_
  58.0 3.2 %collective-permute-done.5.refs_7_ = bf16[16,1024]{1,0:T(8,128)(2,1)S(1)} collective-permute-done((bf16[16,1024]{1,0:T(8,128)(2,1)S(1)}, bf16[16,1024]{1,0:T(8,128)(2,1)S(1)}, u32[]{:S(2)}, u32[]{:S(2)}) %collective-permute-start.5) | collective-permute-done | bytes 32800 | tf_op jit(solution)/shard_map/ppermute | solution.py:307
  61.2 0.0 collective-permute-done.refs_1_
  61.2 1.6 %collective-permute-done.2.refs_3_ = bf16[592,128]{1,0:T(8,128)(2,1)S(1)} collective-permute-done((bf16[592,128]{1,0:T(8,128)(2,1)S(1)}, bf16[592,128]{1,0:T(8,128)(2,1)S(1)}, u32[]{:S(2)}, u32[]{:S(2)}) %collective-permute-start.2) | collective-permute-done | bytes 151584 | tf_op jit(solution)/shard_map/ppermute | solution.py:307
  62.8 1.4 %damp.1 = (bf16[8,592,128]{2,1,0:T(8,128)(2,1)}, bf16[64,1024]{1,0:T(8,128)(2,1)S(1)}) custom-call(bf16[592,128]{1,0:T(8,128)(2,1)S(1)} %get-tuple-element.20.refs_0_, bf16[592,128]{1,0:T(8,128)(2,1)S(1)} %collective-permute-done.refs_1_, bf16[592,128]{1,0:T(8,128)(2,1)S(1)} %collective-permute-done.1.refs_2_, ...), custom_call_target="tpu_custom_call" | custom-call | bytes 4194304 | tf_op jit(solution)/shard_map/damp/pallas_call | solution.py:44
  64.3 4.1 %all-to-all-start.1 = ((bf16[8,592,128]{2,1,0:T(8,128)(2,1)}), bf16[8,592,128]{2,1,0:T(8,128)(2,1)S(1)}, u32[]{:S(2)}, u32[]{:S(2)}) async-start(bf16[8,592,128]{2,1,0:T(8,128)(2,1)} %get-tuple-element.25), calls=%async_computation.1 | async-start | bytes 2424832 | tf_op jit(solution)/shard_map/all_to_all | solution.py:369
  68.4 1.3 collective-permute-start.6
  69.6 0.7 collective-permute-start.7
  70.3 1.3 collective-permute-start.8
  71.6 4.1 %collective-permute-start.9 = (bf16[64,1024]{1,0:T(8,128)(2,1)S(1)}, bf16[64,1024]{1,0:T(8,128)(2,1)S(1)}, u32[]{:S(2)}, u32[]{:S(2)}) collective-permute-start(bf16[64,1024]{1,0:T(8,128)(2,1)S(1)} %get-tuple-element.30), channel_id=1, source_target_pairs={{48,16},{53,20},{58,24},{63,28},{50,17},{55,21},{56,25},{61,29},{4... | collective-permute-start | bytes 393224 | tf_op jit(solution)/shard_map/ppermute | solution.py:357
  75.7 8.0 %all-to-all-done.1.packed_ref = bf16[8,592,128]{2,1,0:T(8,128)(2,1)S(1)} async-done(((bf16[8,592,128]{2,1,0:T(8,128)(2,1)}), bf16[8,592,128]{2,1,0:T(8,128)(2,1)S(1)}, u32[]{:S(2)}, u32[]{:S(2)}) %all-to-all-start.1) | async-done | bytes 1212448 | tf_op jit(solution)/shard_map/all_to_all | solution.py:369
  83.7 11.3 %root.1 = (f32[8,128]{1,0:T(8,128)S(1)}, f32[1024,1024]{1,0:T(8,128)S(1)}, bf16[1024,1024]{1,0:T(8,128)(2,1)S(1)}, bf16[1024,1024]{1,0:T(8,128)(2,1)S(1)}) custom-call(bf16[8,592,128]{2,1,0:T(8,128)(2,1)S(1)} %all-to-all-done.1.packed_ref), custom_call_target="tpu_custom_call" | custom-call | flops 10737418240 | bytes 4194304 | tf_op jit(solution)/shard_map/root/pallas_call | solution.py:44
  95.1 2.1 %right.1 = (bf16[256,128]{1,0:T(8,128)(2,1)S(1)}, bf16[256,128]{1,0:T(8,128)(2,1)S(1)}, bf16[256,128]{1,0:T(8,128)(2,1)S(1)}, bf16[256,128]{1,0:T(8,128)(2,1)S(1)}) custom-call(f32[8,128]{1,0:T(8,128)S(1)} %get-tuple-element.26.over_ref, f32[1024,1024]{1,0:T(8,128)S(1)} %get-tuple-element.27.iterate, bf16[1024,1024]{1,0:T(8,128)(2,1)S(1)} %get-tuple-element.28.iterate_b, ...), custom_call_target="tpu_custom_call" | custom-call | flops 1342177280 | bytes 4194304 | tf_op jit(solution)/shard_map/right/pallas_call | solution.py:44
  97.2 5.5 %collective-permute-start.10 = (bf16[256,128]{1,0:T(8,128)(2,1)S(1)}, bf16[256,128]{1,0:T(8,128)(2,1)S(1)}, u32[]{:S(2)}, u32[]{:S(2)}) collective-permute-start(bf16[256,128]{1,0:T(8,128)(2,1)S(1)} %get-tuple-element.31), channel_id=1, source_target_pairs={{16,128},{20,133},{24,138},{28,143},{17,130},{21,135},{25,136},{29... | collective-permute-start | bytes 196616 | tf_op jit(solution)/shard_map/ppermute | solution.py:398
  102.7 1.3 collective-permute-start.11
  104.0 1.4 %collective-permute-start.12 = (bf16[256,128]{1,0:T(8,128)(2,1)S(1)}, bf16[256,128]{1,0:T(8,128)(2,1)S(1)}, u32[]{:S(2)}, u32[]{:S(2)}) collective-permute-start(bf16[256,128]{1,0:T(8,128)(2,1)S(1)} %get-tuple-element.33), channel_id=1, source_target_pairs={{16,192},{20,197},{24,202},{28,207},{17,194},{21,199},{25,200},{29... | collective-permute-start | bytes 196616 | tf_op jit(solution)/shard_map/ppermute | solution.py:398
  105.4 1.5 %collective-permute-start.13 = (bf16[256,128]{1,0:T(8,128)(2,1)S(1)}, bf16[256,128]{1,0:T(8,128)(2,1)S(1)}, u32[]{:S(2)}, u32[]{:S(2)}) collective-permute-start(bf16[256,128]{1,0:T(8,128)(2,1)S(1)} %get-tuple-element.34), channel_id=1, source_target_pairs={{16,0},{20,5},{24,10},{28,15},{17,2},{21,7},{25,8},{29,13},{18,1},... | collective-permute-start | bytes 196616 | tf_op jit(solution)/shard_map/ppermute | solution.py:398
  106.9 2.5 %rest.1.root_ref = bf16[1024,1024]{1,0:T(8,128)(2,1)S(1)} custom-call(f32[8,128]{1,0:T(8,128)S(1)} %get-tuple-element.26.over_ref, f32[1024,1024]{1,0:T(8,128)S(1)} %get-tuple-element.27.iterate, bf16[1024,1024]{1,0:T(8,128)(2,1)S(1)} %get-tuple-element.28.iterate_b, bf16[1024,1024]{1,0:T(8,128)(2,1)S(1)} %get-tuple-element.29.cubic_b), custom_call_target="tpu_custom_call" | custom-call | flops 2147483648 | bytes 4194304 | tf_op jit(solution)/shard_map/rest/pallas_call | solution.py:44
  109.4 0.5 collective-permute-done.12.refs_2_
  109.9 0.7 left.1
  110.6 22.5 %all_to_all.16.got_ref = bf16[64,16,128]{2,1,0:T(8,128)(2,1)S(1)} all-to-all(bf16[64,16,128]{2,1,0:T(8,128)(2,1)S(1)} %bitcast.1), channel_id=1, replica_groups=mesh['zh'=4,'zl'=2,'xl'=2,'y'=4,'xh'=2,'c'=2] {'zh','zl','xl','y'}, dimensions={0} | all-to-all | bytes 524288 | tf_op jit(solution)/shard_map/all_to_all | solution.py:418
  133.1 0.7 place.1
  (10 shorter events, 0.0 us)
Async XLA Ops:
  5.0 37.5 %copy-start = (f32[1,16,4096]{2,1,0:T(8,128)S(1)}, f32[1,16,4096]{2,1,0:T(8,128)}, u32[]{:S(2)}) copy-start(f32[1,16,4096]{2,1,0:T(8,128)} %gradient_ref.1) | copy-start | bytes 786436
  42.9 18.3 %collective-permute-start = (bf16[592,128]{1,0:T(8,128)(2,1)S(1)}, bf16[592,128]{1,0:T(8,128)(2,1)S(1)}, u32[]{:S(2)}, u32[]{:S(2)}) collective-permute-start(bf16[592,128]{1,0:T(8,128)(2,1)S(1)} %get-tuple-element.20.refs_0_), channel_id=1, source_target_pairs={{0,192},{64,0},{128,64},{192,128},{1,193},{65,1},{129,65},{193,129... | collective-permute-start | bytes 454664 | tf_op jit(solution)/shard_map/ppermute | solution.py:307
  48.4 12.9 %collective-permute-start.1 = (bf16[592,128]{1,0:T(8,128)(2,1)S(1)}, bf16[592,128]{1,0:T(8,128)(2,1)S(1)}, u32[]{:S(2)}, u32[]{:S(2)}) collective-permute-start(bf16[592,128]{1,0:T(8,128)(2,1)S(1)} %get-tuple-element.20.refs_0_), channel_id=1, source_target_pairs={{0,64},{64,128},{128,192},{192,0},{1,65},{65,129},{129,193},{193,1... | collective-permute-start | bytes 454664 | tf_op jit(solution)/shard_map/ppermute | solution.py:307
  48.4 14.5 %collective-permute-start.2 = (bf16[592,128]{1,0:T(8,128)(2,1)S(1)}, bf16[592,128]{1,0:T(8,128)(2,1)S(1)}, u32[]{:S(2)}, u32[]{:S(2)}) collective-permute-start(bf16[592,128]{1,0:T(8,128)(2,1)S(1)} %get-tuple-element.20.refs_0_), channel_id=1, source_target_pairs={{0,128},{64,192},{128,0},{192,64},{1,129},{65,193},{129,1},{193,65... | collective-permute-start | bytes 454664 | tf_op jit(solution)/shard_map/ppermute | solution.py:307
  52.2 5.1 %collective-permute-start.3 = (bf16[16,1024]{1,0:T(8,128)(2,1)S(1)}, bf16[16,1024]{1,0:T(8,128)(2,1)S(1)}, u32[]{:S(2)}, u32[]{:S(2)}) collective-permute-start(bf16[16,1024]{1,0:T(8,128)(2,1)S(1)} %get-tuple-element.22), channel_id=1, source_target_pairs={{0,4},{4,8},{8,12},{12,0},{1,5},{5,9},{9,13},{13,1},{2,6},{6,10},{... | collective-permute-start | bytes 98312 | tf_op jit(solution)/shard_map/ppermute | solution.py:307
  52.6 5.4 %collective-permute-start.4 = (bf16[16,1024]{1,0:T(8,128)(2,1)S(1)}, bf16[16,1024]{1,0:T(8,128)(2,1)S(1)}, u32[]{:S(2)}, u32[]{:S(2)}) collective-permute-start(bf16[16,1024]{1,0:T(8,128)(2,1)S(1)} %get-tuple-element.23), channel_id=1, source_target_pairs={{0,8},{4,12},{8,0},{12,4},{1,9},{5,13},{9,1},{13,5},{2,10},{6,14},... | collective-permute-start | bytes 98312 | tf_op jit(solution)/shard_map/ppermute | solution.py:307
  57.3 3.9 %collective-permute-start.5 = (bf16[16,1024]{1,0:T(8,128)(2,1)S(1)}, bf16[16,1024]{1,0:T(8,128)(2,1)S(1)}, u32[]{:S(2)}, u32[]{:S(2)}) collective-permute-start(bf16[16,1024]{1,0:T(8,128)(2,1)S(1)} %get-tuple-element.24), channel_id=1, source_target_pairs={{0,12},{4,0},{8,4},{12,8},{1,13},{5,1},{9,5},{13,9},{2,14},{6,2},{... | collective-permute-start | bytes 98312 | tf_op jit(solution)/shard_map/ppermute | solution.py:307
  64.3 19.5 %all-to-all-start.1 = ((bf16[8,592,128]{2,1,0:T(8,128)(2,1)}), bf16[8,592,128]{2,1,0:T(8,128)(2,1)S(1)}, u32[]{:S(2)}, u32[]{:S(2)}) async-start(bf16[8,592,128]{2,1,0:T(8,128)(2,1)} %get-tuple-element.25), calls=%async_computation.1 | async-start | bytes 2424832 | tf_op jit(solution)/shard_map/all_to_all | solution.py:369
  68.4 26.7 %collective-permute-start.6 = (bf16[64,1024]{1,0:T(8,128)(2,1)S(1)}, bf16[64,1024]{1,0:T(8,128)(2,1)S(1)}, u32[]{:S(2)}, u32[]{:S(2)}) collective-permute-start(bf16[64,1024]{1,0:T(8,128)(2,1)S(1)} %get-tuple-element.30), channel_id=1, source_target_pairs={{0,16},{5,20},{10,24},{15,28},{2,17},{7,21},{8,25},{13,29},{1,18},... | collective-permute-start | bytes 393224 | tf_op jit(solution)/shard_map/ppermute | solution.py:357
  69.6 25.4 %collective-permute-start.7 = (bf16[64,1024]{1,0:T(8,128)(2,1)S(1)}, bf16[64,1024]{1,0:T(8,128)(2,1)S(1)}, u32[]{:S(2)}, u32[]{:S(2)}) collective-permute-start(bf16[64,1024]{1,0:T(8,128)(2,1)S(1)} %get-tuple-element.30), channel_id=1, source_target_pairs={{16,16},{21,20},{26,24},{31,28},{18,17},{23,21},{24,25},{29,29},{1... | collective-permute-start | bytes 393224 | tf_op jit(solution)/shard_map/ppermute | solution.py:357
  70.3 24.8 %collective-permute-start.8 = (bf16[64,1024]{1,0:T(8,128)(2,1)S(1)}, bf16[64,1024]{1,0:T(8,128)(2,1)S(1)}, u32[]{:S(2)}, u32[]{:S(2)}) collective-permute-start(bf16[64,1024]{1,0:T(8,128)(2,1)S(1)} %get-tuple-element.30), channel_id=1, source_target_pairs={{32,16},{37,20},{42,24},{47,28},{34,17},{39,21},{40,25},{45,29},{3... | collective-permute-start | bytes 393224 | tf_op jit(solution)/shard_map/ppermute | solution.py:357
  71.6 23.5 %collective-permute-start.9 = (bf16[64,1024]{1,0:T(8,128)(2,1)S(1)}, bf16[64,1024]{1,0:T(8,128)(2,1)S(1)}, u32[]{:S(2)}, u32[]{:S(2)}) collective-permute-start(bf16[64,1024]{1,0:T(8,128)(2,1)S(1)} %get-tuple-element.30), channel_id=1, source_target_pairs={{48,16},{53,20},{58,24},{63,28},{50,17},{55,21},{56,25},{61,29},{4... | collective-permute-start | bytes 393224 | tf_op jit(solution)/shard_map/ppermute | solution.py:357
  97.2 12.2 %collective-permute-start.10 = (bf16[256,128]{1,0:T(8,128)(2,1)S(1)}, bf16[256,128]{1,0:T(8,128)(2,1)S(1)}, u32[]{:S(2)}, u32[]{:S(2)}) collective-permute-start(bf16[256,128]{1,0:T(8,128)(2,1)S(1)} %get-tuple-element.31), channel_id=1, source_target_pairs={{16,128},{20,133},{24,138},{28,143},{17,130},{21,135},{25,136},{29... | collective-permute-start | bytes 196616 | tf_op jit(solution)/shard_map/ppermute | solution.py:398
  102.7 6.7 %collective-permute-start.11 = (bf16[256,128]{1,0:T(8,128)(2,1)S(1)}, bf16[256,128]{1,0:T(8,128)(2,1)S(1)}, u32[]{:S(2)}, u32[]{:S(2)}) collective-permute-start(bf16[256,128]{1,0:T(8,128)(2,1)S(1)} %get-tuple-element.32), channel_id=1, source_target_pairs={{16,64},{20,69},{24,74},{28,79},{17,66},{21,71},{25,72},{29,77},{1... | collective-permute-start | bytes 196616 | tf_op jit(solution)/shard_map/ppermute | solution.py:398
  104.0 5.9 %collective-permute-start.12 = (bf16[256,128]{1,0:T(8,128)(2,1)S(1)}, bf16[256,128]{1,0:T(8,128)(2,1)S(1)}, u32[]{:S(2)}, u32[]{:S(2)}) collective-permute-start(bf16[256,128]{1,0:T(8,128)(2,1)S(1)} %get-tuple-element.33), channel_id=1, source_target_pairs={{16,192},{20,197},{24,202},{28,207},{17,194},{21,199},{25,200},{29... | collective-permute-start | bytes 196616 | tf_op jit(solution)/shard_map/ppermute | solution.py:398
  105.4 4.5 %collective-permute-start.13 = (bf16[256,128]{1,0:T(8,128)(2,1)S(1)}, bf16[256,128]{1,0:T(8,128)(2,1)S(1)}, u32[]{:S(2)}, u32[]{:S(2)}) collective-permute-start(bf16[256,128]{1,0:T(8,128)(2,1)S(1)} %get-tuple-element.34), channel_id=1, source_target_pairs={{16,0},{20,5},{24,10},{28,15},{17,2},{21,7},{25,8},{29,13},{18,1},... | collective-permute-start | bytes 196616 | tf_op jit(solution)/shard_map/ppermute | solution.py:398

commit v11 on v10

--- a/solution.py
+++ b/solution.py
@@ -116,15 +116,17 @@
                             rest[(piece, at)] = jnp.sum(
                                 jnp.where(eye, block - block_b.astype(F32), 0.0), axis=0, keepdims=True
                             )
-        for piece in range(NZL * NY):
-            lines = [rest.get((piece, at), jnp.zeros((1, TILE), F32)) for at in range(HALVES)]
-            put_rest(packed.at[target_of(which, piece)], lines)
-        for zl in range(NZL):
-            part = pl.ds(target_of(which, zl * NY), NY)
-            stores.append(
-                pltpu.make_async_copy(packed.at[part], out_ref.at[part], out_sems.at[which, zl])
-            )
-            stores[-1].start()
+            last = 2 * WHERE[(first // TILE + 1, GRID - 1)] + 2
+            for piece in range(len(stores) - which * NZL * NY, last // HALVES):
+                lines = [rest.get((piece, at), jnp.zeros((1, TILE), F32)) for at in range(HALVES)]
+                target = target_of(which, piece)
+                put_rest(packed.at[target], lines)
+                stores.append(
+                    pltpu.make_async_copy(
+                        packed.at[target], out_ref.at[target], out_sems.at[which, piece]
+                    )
+                )
+                stores[-1].start()
     for store in stores:
         store.wait()
 
@@ -179,8 +181,7 @@
 
 
 def damp_kernel(all_tokens, *refs):
-    parts, turn_refs = refs[:NZH], refs[NZH:NZH + NY]
-    out_ref, slab_ref, damped, sems = refs[NZH + NY:]
+    parts, (out_ref, done_ref, damped, sems) = refs[:NZH], refs[NZH:]
     piece = piece_here()
     halves = []
     squares = jnp.zeros((HALF, TILE), F32)
@@ -203,11 +204,16 @@
     ]
     for store in stores:
         store.start()
+    done_ref[...] = jnp.zeros(done_ref.shape, F32)
+    for store in stores:
+        store.wait()
+
+
+def join_kernel(done_ref, *refs):
+    turn_refs, slab_ref = refs[:NY], refs[NY]
     for turn, ref in enumerate(turn_refs):
         at = lax.rem(lax.axis_index("y") + NY - turn, NY) * ROWS
         slab_ref[pl.ds(pl.multiple_of(at, ROWS), ROWS), :] = ref[...]
-    for store in stores:
-        store.wait()
 
 
 def root_kernel(packed_ref, over_ref, iterate, iterate_b, cubic_b, scaled, square_b):
@@ -321,7 +327,7 @@
             pltpu.VMEM(acts.shape, BF16),
             pltpu.VMEM((NZL * NXL * NY, PIECE + REST, TILE), BF16),
             pltpu.SemaphoreType.DMA((2, LOADS)),
-            pltpu.SemaphoreType.DMA((2, NZL)),
+            pltpu.SemaphoreType.DMA((2, NZL * NY)),
         ],
         flops=4 * acts.shape[0] * ORDER * ORDER,
         vmem=60 << 20,
@@ -336,20 +342,23 @@
         (got, gradient),
     )
     turns = [turns[0]] + [turned(turns[shift], "y", NY, shift) for shift in range(1, NY)]
-    parts = [part] + [turned(part, "zh", NZH, shift) for shift in SHIFTS[2::-1]]
-    pieces, slab = call(
+    parts = [part] + [turned(part, "zh", NZH, shift) for shift in SHIFTS if shift]
+    pieces, done = call(
         functools.partial(damp_kernel, float(all_tokens)),
         "damp",
         [
             jax.ShapeDtypeStruct((NZL * NY, PIECE + REST, TILE), BF16),
-            jax.ShapeDtypeStruct((NY * ROWS, ORDER), BF16),
+            jax.ShapeDtypeStruct((8, TILE), F32),
         ],
-        (*parts, *turns),
+        tuple(parts),
         out_specs=[HBM, VMEM],
         scratch=[
             pltpu.VMEM((PIECE + REST, TILE), BF16),
             pltpu.SemaphoreType.DMA((NZL * NY,)),
         ],
+    )
+    slab = call(
+        join_kernel, "join", jax.ShapeDtypeStruct((NY * ROWS, ORDER), BF16), (done, *turns)
     )
     count = NXL * NY * NBLOCK
     cells = [(partner(k, y), k, y) for k in range(NBLOCK) for y in range(NY)]

time: 134 us -> 146 us (1.090)
  starting transfers between devices: 33.5 us -> 38.2 us
  waiting for transfers between devices: 16.1 us -> 20.5 us
  blocking collectives: 60 us -> 61.9 us
    ppermute x6, waiting for transfers between devices: 7.61 us -> 19.6 us  [turned(): return lax.ppermute(x, axes, [(n, (n + shift) % size) for n in range(size)])]
    all_to_all x1, waiting for transfers between devices: 8 us -> 0.01 us  [local(): packed = lax.all_to_all(pieces, ('zl', 'y'), 0, 0, tiled=True)]
    ppermute x6, starting transfers between devices: 12.3 us -> 16.7 us  [turned(): return lax.ppermute(x, axes, [(n, (n + shift) % size) for n in range(size)])]
    all_to_all x1, blocking collectives: 22.5 us -> 24.5 us  [local(): returned = lax.all_to_all(result, DP, 0, 0, tiled=True)]
    pallas_call x8 -> x9, Pallas kernels: 24.1 us -> 23.9 us  [call(): pl.pallas_call(kernel, out_shape=out_shape, scratch_shapes=list(scratch),...]
where the time goes in v11:
time: 146 us; the launch traced here: 145 us
  blocking collectives  61.9 us (42%)
  starting transfers between devices  38.2 us (26%)
  Pallas kernels  23.9 us (16%)
  waiting for transfers between devices  20.5 us (14%)
    all_to_all x1, blocking collectives, local(): got = lax.all_to_all(packed, ('zl', 'xl', 'y'), 0, 0, tiled=True)  37.5 us
    all_to_all x1, blocking collectives, local(): returned = lax.all_to_all(result, DP, 0, 0, tiled=True)  24.5 us
    pallas_call x9, Pallas kernels, call(): pl.pallas_call(kernel, out_shape=out_shape, scratch_shapes=list(scratch),...  23.9 us
    ppermute x6, waiting for transfers between devices, turned(): return lax.ppermute(x, axes, [(n, (n + shift) % size) for n in range(size)])  19.6 us
    ppermute x6, starting transfers between devices, turned(): return lax.ppermute(x, axes, [(n, (n + shift) % size) for n in range(size)])  16.7 us
    ppermute x4, starting transfers between devices, local(): lax.ppermute(right_done[n], ('zh', 'xl', 'y', 'xh', 'c'), [(zh * count +...  10.2 us
    ppermute x4, starting transfers between devices, local(): lax.ppermute(slab, ('zl', 'xl', 'y', 'xh', 'c'), [((zl + turn) % NZL * co...  6.83 us
    all_to_all x1, starting transfers between devices, local(): packed = lax.all_to_all(pieces, ('zl', 'y'), 0, 0, tiled=True)  4.46 us
  transfers between devices with their start and end apart: 15, of which 6 were waited for; matrix products, arithmetic and copies ran while one was open for 0% of the time, Pallas kernels for 10%

profile of v11, /device:TPU:2, one launch (start us, length us, event | category | flops | bytes accessed | tf_op | source)
XLA Modules:
  0.0 144.7 jit_solution(14385694598136235409)
XLA Ops:
  0.0 4.8 %gram.1 = bf16[16,592,128]{2,1,0:T(8,128)(2,1)} custom-call(bf16[768,1024]{1,0:T(8,128)(2,1)} %acts_ref.1, bf16[768,1024]{1,0:T(8,128)(2,1)} %grads_ref.1), custom_call_target="tpu_custom_call" | custom-call | flops 3221225472 | bytes 4194304 | tf_op jit(solution)/shard_map/gram/pallas_call | solution.py:44
  4.8 0.0 copy-start
  4.8 37.5 %all_to_all.15.got_ref = bf16[16,592,128]{2,1,0:T(8,128)(2,1)S(1)} all-to-all(bf16[16,592,128]{2,1,0:T(8,128)(2,1)} %gram.1), channel_id=1, replica_groups=mesh['zh'=4,'zl'=2,'xl'=2,'y'=4,'xh'=2,'c'=2] {'zl','xl','y'}, dimensions={0} | all-to-all | bytes 4849664 | tf_op jit(solution)/shard_map/all_to_all | solution.py:336
  42.3 0.4 sum.1
  42.7 6.4 %collective-permute-start = (bf16[592,128]{1,0:T(8,128)(2,1)S(1)}, bf16[592,128]{1,0:T(8,128)(2,1)S(1)}, u32[]{:S(2)}, u32[]{:S(2)}) collective-permute-start(bf16[592,128]{1,0:T(8,128)(2,1)S(1)} %get-tuple-element.20.refs_0_), channel_id=1, source_target_pairs={{0,128},{64,192},{128,0},{192,64},{1,129},{65,193},{129,1},{193,65... | collective-permute-start | bytes 454664 | tf_op jit(solution)/shard_map/ppermute | solution.py:313
  49.1 1.5 %collective-permute-start.1 = (bf16[592,128]{1,0:T(8,128)(2,1)S(1)}, bf16[592,128]{1,0:T(8,128)(2,1)S(1)}, u32[]{:S(2)}, u32[]{:S(2)}) collective-permute-start(bf16[592,128]{1,0:T(8,128)(2,1)S(1)} %get-tuple-element.20.refs_0_), channel_id=1, source_target_pairs={{0,64},{64,128},{128,192},{192,0},{1,65},{65,129},{129,193},{193,1... | collective-permute-start | bytes 454664 | tf_op jit(solution)/shard_map/ppermute | solution.py:313
  50.6 2.7 %collective-permute-start.2 = (bf16[592,128]{1,0:T(8,128)(2,1)S(1)}, bf16[592,128]{1,0:T(8,128)(2,1)S(1)}, u32[]{:S(2)}, u32[]{:S(2)}) collective-permute-start(bf16[592,128]{1,0:T(8,128)(2,1)S(1)} %get-tuple-element.20.refs_0_), channel_id=1, source_target_pairs={{0,192},{64,0},{128,64},{192,128},{1,193},{65,1},{129,65},{193,129... | collective-permute-start | bytes 454664 | tf_op jit(solution)/shard_map/ppermute | solution.py:313
  53.2 4.0 %collective-permute-done.refs_1_ = bf16[592,128]{1,0:T(8,128)(2,1)S(1)} collective-permute-done((bf16[592,128]{1,0:T(8,128)(2,1)S(1)}, bf16[592,128]{1,0:T(8,128)(2,1)S(1)}, u32[]{:S(2)}, u32[]{:S(2)}) %collective-permute-start) | collective-permute-done | bytes 151584 | tf_op jit(solution)/shard_map/ppermute | solution.py:313
  57.3 2.5 %collective-permute-done.1.refs_2_ = bf16[592,128]{1,0:T(8,128)(2,1)S(1)} collective-permute-done((bf16[592,128]{1,0:T(8,128)(2,1)S(1)}, bf16[592,128]{1,0:T(8,128)(2,1)S(1)}, u32[]{:S(2)}, u32[]{:S(2)}) %collective-permute-start.1) | collective-permute-done | bytes 151584 | tf_op jit(solution)/shard_map/ppermute | solution.py:313
  59.7 1.8 %collective-permute-done.2.refs_3_ = bf16[592,128]{1,0:T(8,128)(2,1)S(1)} collective-permute-done((bf16[592,128]{1,0:T(8,128)(2,1)S(1)}, bf16[592,128]{1,0:T(8,128)(2,1)S(1)}, u32[]{:S(2)}, u32[]{:S(2)}) %collective-permute-start.2) | collective-permute-done | bytes 151584 | tf_op jit(solution)/shard_map/ppermute | solution.py:313
  61.5 1.4 damp.1
  62.9 4.5 %all-to-all-start.1 = ((bf16[8,592,128]{2,1,0:T(8,128)(2,1)}), bf16[8,592,128]{2,1,0:T(8,128)(2,1)S(1)}, u32[]{:S(2)}, u32[]{:S(2)}) async-start(bf16[8,592,128]{2,1,0:T(8,128)(2,1)} %get-tuple-element.21), calls=%async_computation.1 | async-start | bytes 2424832 | tf_op jit(solution)/shard_map/all_to_all | solution.py:378
  67.3 2.0 %collective-permute-start.3 = (bf16[16,1024]{1,0:T(8,128)(2,1)S(1)}, bf16[16,1024]{1,0:T(8,128)(2,1)S(1)}, u32[]{:S(2)}, u32[]{:S(2)}) collective-permute-start(bf16[16,1024]{1,0:T(8,128)(2,1)S(1)} %get-tuple-element.28), channel_id=1, source_target_pairs={{0,4},{4,8},{8,12},{12,0},{1,5},{5,9},{9,13},{13,1},{2,6},{6,10},{... | collective-permute-start | bytes 98312 | tf_op jit(solution)/shard_map/ppermute | solution.py:313
  69.4 2.7 %collective-permute-start.4 = (bf16[16,1024]{1,0:T(8,128)(2,1)S(1)}, bf16[16,1024]{1,0:T(8,128)(2,1)S(1)}, u32[]{:S(2)}, u32[]{:S(2)}) collective-permute-start(bf16[16,1024]{1,0:T(8,128)(2,1)S(1)} %get-tuple-element.29), channel_id=1, source_target_pairs={{0,8},{4,12},{8,0},{12,4},{1,9},{5,13},{9,1},{13,5},{2,10},{6,14},... | collective-permute-start | bytes 98312 | tf_op jit(solution)/shard_map/ppermute | solution.py:313
  72.0 1.5 %collective-permute-start.5 = (bf16[16,1024]{1,0:T(8,128)(2,1)S(1)}, bf16[16,1024]{1,0:T(8,128)(2,1)S(1)}, u32[]{:S(2)}, u32[]{:S(2)}) collective-permute-start(bf16[16,1024]{1,0:T(8,128)(2,1)S(1)} %get-tuple-element.30), channel_id=1, source_target_pairs={{0,12},{4,0},{8,4},{12,8},{1,13},{5,1},{9,5},{13,9},{2,14},{6,2},{... | collective-permute-start | bytes 98312 | tf_op jit(solution)/shard_map/ppermute | solution.py:313
  73.5 10.7 %collective-permute-done.3.refs_1_ = bf16[16,1024]{1,0:T(8,128)(2,1)S(1)} collective-permute-done((bf16[16,1024]{1,0:T(8,128)(2,1)S(1)}, bf16[16,1024]{1,0:T(8,128)(2,1)S(1)}, u32[]{:S(2)}, u32[]{:S(2)}) %collective-permute-start.3) | collective-permute-done | bytes 32800 | tf_op jit(solution)/shard_map/ppermute | solution.py:313
  84.2 0.7 collective-permute-done.4.refs_2_
  84.9 1.3 collective-permute-start.6
  86.2 0.7 collective-permute-start.7
  86.9 1.3 collective-permute-start.8
  88.2 3.6 %collective-permute-start.9 = (bf16[64,1024]{1,0:T(8,128)(2,1)S(1)}, bf16[64,1024]{1,0:T(8,128)(2,1)S(1)}, u32[]{:S(2)}, u32[]{:S(2)}) collective-permute-start(bf16[64,1024]{1,0:T(8,128)(2,1)S(1)} %join.1), channel_id=1, source_target_pairs={{48,16},{53,20},{58,24},{63,28},{50,17},{55,21},{56,25},{61,29},{4... | collective-permute-start | bytes 393224 | tf_op jit(solution)/shard_map/ppermute | solution.py:366
  91.8 11.3 %root.1 = (f32[8,128]{1,0:T(8,128)S(1)}, f32[1024,1024]{1,0:T(8,128)S(1)}, bf16[1024,1024]{1,0:T(8,128)(2,1)S(1)}, bf16[1024,1024]{1,0:T(8,128)(2,1)S(1)}) custom-call(bf16[8,592,128]{2,1,0:T(8,128)(2,1)S(1)} %all-to-all-done.1.packed_ref), custom_call_target="tpu_custom_call" | custom-call | flops 10737418240 | bytes 4194304 | tf_op jit(solution)/shard_map/root/pallas_call | solution.py:44
  103.2 2.1 %right.1 = (bf16[256,128]{1,0:T(8,128)(2,1)S(1)}, bf16[256,128]{1,0:T(8,128)(2,1)S(1)}, bf16[256,128]{1,0:T(8,128)(2,1)S(1)}, bf16[256,128]{1,0:T(8,128)(2,1)S(1)}) custom-call(f32[8,128]{1,0:T(8,128)S(1)} %get-tuple-element.22.over_ref, f32[1024,1024]{1,0:T(8,128)S(1)} %get-tuple-element.23.iterate, bf16[1024,1024]{1,0:T(8,128)(2,1)S(1)} %get-tuple-element.24.iterate_b, ...), custom_call_target="tpu_custom_call" | custom-call | flops 1342177280 | bytes 4194304 | tf_op jit(solution)/shard_map/right/pallas_call | solution.py:44
  105.2 6.0 %collective-permute-start.10 = (bf16[256,128]{1,0:T(8,128)(2,1)S(1)}, bf16[256,128]{1,0:T(8,128)(2,1)S(1)}, u32[]{:S(2)}, u32[]{:S(2)}) collective-permute-start(bf16[256,128]{1,0:T(8,128)(2,1)S(1)} %get-tuple-element.31), channel_id=1, source_target_pairs={{16,128},{20,133},{24,138},{28,143},{17,130},{21,135},{25,136},{29... | collective-permute-start | bytes 196616 | tf_op jit(solution)/shard_map/ppermute | solution.py:407
  111.3 1.3 collective-permute-start.11
  112.6 1.4 collective-permute-start.12
  113.9 1.5 %collective-permute-start.13 = (bf16[256,128]{1,0:T(8,128)(2,1)S(1)}, bf16[256,128]{1,0:T(8,128)(2,1)S(1)}, u32[]{:S(2)}, u32[]{:S(2)}) collective-permute-start(bf16[256,128]{1,0:T(8,128)(2,1)S(1)} %get-tuple-element.34), channel_id=1, source_target_pairs={{16,0},{20,5},{24,10},{28,15},{17,2},{21,7},{25,8},{29,13},{18,1},... | collective-permute-start | bytes 196616 | tf_op jit(solution)/shard_map/ppermute | solution.py:407
  115.4 2.5 %rest.1.root_ref = bf16[1024,1024]{1,0:T(8,128)(2,1)S(1)} custom-call(f32[8,128]{1,0:T(8,128)S(1)} %get-tuple-element.22.over_ref, f32[1024,1024]{1,0:T(8,128)S(1)} %get-tuple-element.23.iterate, bf16[1024,1024]{1,0:T(8,128)(2,1)S(1)} %get-tuple-element.24.iterate_b, bf16[1024,1024]{1,0:T(8,128)(2,1)S(1)} %get-tuple-element.25.cubic_b), custom_call_target="tpu_custom_call" | custom-call | flops 2147483648 | bytes 4194304 | tf_op jit(solution)/shard_map/rest/pallas_call | solution.py:44
  117.9 0.9 collective-permute-done.12.refs_2_
  118.8 0.7 left.1
  119.6 24.5 %all_to_all.16.got_ref = bf16[64,16,128]{2,1,0:T(8,128)(2,1)S(1)} all-to-all(bf16[64,16,128]{2,1,0:T(8,128)(2,1)S(1)} %bitcast.1), channel_id=1, replica_groups=mesh['zh'=4,'zl'=2,'xl'=2,'y'=4,'xh'=2,'c'=2] {'zh','zl','xl','y'}, dimensions={0} | all-to-all | bytes 524288 | tf_op jit(solution)/shard_map/all_to_all | solution.py:427
  144.0 0.7 place.1
  (11 shorter events, 0.0 us)
Async XLA Ops:
  4.8 37.5 %copy-start = (f32[1,16,4096]{2,1,0:T(8,128)S(1)}, f32[1,16,4096]{2,1,0:T(8,128)}, u32[]{:S(2)}) copy-start(f32[1,16,4096]{2,1,0:T(8,128)} %gradient_ref.1) | copy-start | bytes 786436
  42.7 14.6 %collective-permute-start = (bf16[592,128]{1,0:T(8,128)(2,1)S(1)}, bf16[592,128]{1,0:T(8,128)(2,1)S(1)}, u32[]{:S(2)}, u32[]{:S(2)}) collective-permute-start(bf16[592,128]{1,0:T(8,128)(2,1)S(1)} %get-tuple-element.20.refs_0_), channel_id=1, source_target_pairs={{0,128},{64,192},{128,0},{192,64},{1,129},{65,193},{129,1},{193,65... | collective-permute-start | bytes 454664 | tf_op jit(solution)/shard_map/ppermute | solution.py:313
  49.1 10.6 %collective-permute-start.1 = (bf16[592,128]{1,0:T(8,128)(2,1)S(1)}, bf16[592,128]{1,0:T(8,128)(2,1)S(1)}, u32[]{:S(2)}, u32[]{:S(2)}) collective-permute-start(bf16[592,128]{1,0:T(8,128)(2,1)S(1)} %get-tuple-element.20.refs_0_), channel_id=1, source_target_pairs={{0,64},{64,128},{128,192},{192,0},{1,65},{65,129},{129,193},{193,1... | collective-permute-start | bytes 454664 | tf_op jit(solution)/shard_map/ppermute | solution.py:313
  50.6 10.9 %collective-permute-start.2 = (bf16[592,128]{1,0:T(8,128)(2,1)S(1)}, bf16[592,128]{1,0:T(8,128)(2,1)S(1)}, u32[]{:S(2)}, u32[]{:S(2)}) collective-permute-start(bf16[592,128]{1,0:T(8,128)(2,1)S(1)} %get-tuple-element.20.refs_0_), channel_id=1, source_target_pairs={{0,192},{64,0},{128,64},{192,128},{1,193},{65,1},{129,65},{193,129... | collective-permute-start | bytes 454664 | tf_op jit(solution)/shard_map/ppermute | solution.py:313
  62.9 28.9 %all-to-all-start.1 = ((bf16[8,592,128]{2,1,0:T(8,128)(2,1)}), bf16[8,592,128]{2,1,0:T(8,128)(2,1)S(1)}, u32[]{:S(2)}, u32[]{:S(2)}) async-start(bf16[8,592,128]{2,1,0:T(8,128)(2,1)} %get-tuple-element.21), calls=%async_computation.1 | async-start | bytes 2424832 | tf_op jit(solution)/shard_map/all_to_all | solution.py:378
  67.3 16.9 %collective-permute-start.3 = (bf16[16,1024]{1,0:T(8,128)(2,1)S(1)}, bf16[16,1024]{1,0:T(8,128)(2,1)S(1)}, u32[]{:S(2)}, u32[]{:S(2)}) collective-permute-start(bf16[16,1024]{1,0:T(8,128)(2,1)S(1)} %get-tuple-element.28), channel_id=1, source_target_pairs={{0,4},{4,8},{8,12},{12,0},{1,5},{5,9},{9,13},{13,1},{2,6},{6,10},{... | collective-permute-start | bytes 98312 | tf_op jit(solution)/shard_map/ppermute | solution.py:313
  69.4 15.5 %collective-permute-start.4 = (bf16[16,1024]{1,0:T(8,128)(2,1)S(1)}, bf16[16,1024]{1,0:T(8,128)(2,1)S(1)}, u32[]{:S(2)}, u32[]{:S(2)}) collective-permute-start(bf16[16,1024]{1,0:T(8,128)(2,1)S(1)} %get-tuple-element.29), channel_id=1, source_target_pairs={{0,8},{4,12},{8,0},{12,4},{1,9},{5,13},{9,1},{13,5},{2,10},{6,14},... | collective-permute-start | bytes 98312 | tf_op jit(solution)/shard_map/ppermute | solution.py:313
  72.0 12.9 %collective-permute-start.5 = (bf16[16,1024]{1,0:T(8,128)(2,1)S(1)}, bf16[16,1024]{1,0:T(8,128)(2,1)S(1)}, u32[]{:S(2)}, u32[]{:S(2)}) collective-permute-start(bf16[16,1024]{1,0:T(8,128)(2,1)S(1)} %get-tuple-element.30), channel_id=1, source_target_pairs={{0,12},{4,0},{8,4},{12,8},{1,13},{5,1},{9,5},{13,9},{2,14},{6,2},{... | collective-permute-start | bytes 98312 | tf_op jit(solution)/shard_map/ppermute | solution.py:313
  84.9 18.2 %collective-permute-start.6 = (bf16[64,1024]{1,0:T(8,128)(2,1)S(1)}, bf16[64,1024]{1,0:T(8,128)(2,1)S(1)}, u32[]{:S(2)}, u32[]{:S(2)}) collective-permute-start(bf16[64,1024]{1,0:T(8,128)(2,1)S(1)} %join.1), channel_id=1, source_target_pairs={{0,16},{5,20},{10,24},{15,28},{2,17},{7,21},{8,25},{13,29},{1,18},... | collective-permute-start | bytes 393224 | tf_op jit(solution)/shard_map/ppermute | solution.py:366
  86.2 16.9 %collective-permute-start.7 = (bf16[64,1024]{1,0:T(8,128)(2,1)S(1)}, bf16[64,1024]{1,0:T(8,128)(2,1)S(1)}, u32[]{:S(2)}, u32[]{:S(2)}) collective-permute-start(bf16[64,1024]{1,0:T(8,128)(2,1)S(1)} %join.1), channel_id=1, source_target_pairs={{16,16},{21,20},{26,24},{31,28},{18,17},{23,21},{24,25},{29,29},{1... | collective-permute-start | bytes 393224 | tf_op jit(solution)/shard_map/ppermute | solution.py:366
  86.9 16.2 %collective-permute-start.8 = (bf16[64,1024]{1,0:T(8,128)(2,1)S(1)}, bf16[64,1024]{1,0:T(8,128)(2,1)S(1)}, u32[]{:S(2)}, u32[]{:S(2)}) collective-permute-start(bf16[64,1024]{1,0:T(8,128)(2,1)S(1)} %join.1), channel_id=1, source_target_pairs={{32,16},{37,20},{42,24},{47,28},{34,17},{39,21},{40,25},{45,29},{3... | collective-permute-start | bytes 393224 | tf_op jit(solution)/shard_map/ppermute | solution.py:366
  88.2 14.9 %collective-permute-start.9 = (bf16[64,1024]{1,0:T(8,128)(2,1)S(1)}, bf16[64,1024]{1,0:T(8,128)(2,1)S(1)}, u32[]{:S(2)}, u32[]{:S(2)}) collective-permute-start(bf16[64,1024]{1,0:T(8,128)(2,1)S(1)} %join.1), channel_id=1, source_target_pairs={{48,16},{53,20},{58,24},{63,28},{50,17},{55,21},{56,25},{61,29},{4... | collective-permute-start | bytes 393224 | tf_op jit(solution)/shard_map/ppermute | solution.py:366
  105.2 12.7 %collective-permute-start.10 = (bf16[256,128]{1,0:T(8,128)(2,1)S(1)}, bf16[256,128]{1,0:T(8,128)(2,1)S(1)}, u32[]{:S(2)}, u32[]{:S(2)}) collective-permute-start(bf16[256,128]{1,0:T(8,128)(2,1)S(1)} %get-tuple-element.31), channel_id=1, source_target_pairs={{16,128},{20,133},{24,138},{28,143},{17,130},{21,135},{25,136},{29... | collective-permute-start | bytes 196616 | tf_op jit(solution)/shard_map/ppermute | solution.py:407
  111.3 6.7 %collective-permute-start.11 = (bf16[256,128]{1,0:T(8,128)(2,1)S(1)}, bf16[256,128]{1,0:T(8,128)(2,1)S(1)}, u32[]{:S(2)}, u32[]{:S(2)}) collective-permute-start(bf16[256,128]{1,0:T(8,128)(2,1)S(1)} %get-tuple-element.32), channel_id=1, source_target_pairs={{16,64},{20,69},{24,74},{28,79},{17,66},{21,71},{25,72},{29,77},{1... | collective-permute-start | bytes 196616 | tf_op jit(solution)/shard_map/ppermute | solution.py:407
  112.6 6.3 %collective-permute-start.12 = (bf16[256,128]{1,0:T(8,128)(2,1)S(1)}, bf16[256,128]{1,0:T(8,128)(2,1)S(1)}, u32[]{:S(2)}, u32[]{:S(2)}) collective-permute-start(bf16[256,128]{1,0:T(8,128)(2,1)S(1)} %get-tuple-element.33), channel_id=1, source_target_pairs={{16,192},{20,197},{24,202},{28,207},{17,194},{21,199},{25,200},{29... | collective-permute-start | bytes 196616 | tf_op jit(solution)/shard_map/ppermute | solution.py:407
  113.9 4.9 %collective-permute-start.13 = (bf16[256,128]{1,0:T(8,128)(2,1)S(1)}, bf16[256,128]{1,0:T(8,128)(2,1)S(1)}, u32[]{:S(2)}, u32[]{:S(2)}) collective-permute-start(bf16[256,128]{1,0:T(8,128)(2,1)S(1)} %get-tuple-element.34), channel_id=1, source_target_pairs={{16,0},{20,5},{24,10},{28,15},{17,2},{21,7},{25,8},{29,13},{18,1},... | collective-permute-start | bytes 196616 | tf_op jit(solution)/shard_map/ppermute | solution.py:407

commit v12 on v10

--- a/solution.py
+++ b/solution.py
@@ -237,17 +237,14 @@
         iterate[:, s] = first
         iterate_b[:, s] = first.astype(BF16)
     for sweep in range(SWEEPS):
-        for s in tiles:
-            upper = jnp.dot(
-                iterate_b[:s.stop], iterate_b[:, s], preferred_element_type=F32
-            ).astype(BF16)
-            square_b[:s.stop, s] = upper
-            for t in tiles[:s.start // width]:
-                square_b[s, t] = upper[t].T
-        for s in tiles:
-            cubic_b[:, s] = jnp.dot(
-                square_b[...], scaled[:, s], preferred_element_type=F32
-            ).astype(BF16)
+        for left, other, out in ((iterate_b, iterate_b, square_b), (square_b, scaled, cubic_b)):
+            for s in tiles:
+                upper = jnp.dot(
+                    left[:s.stop], other[:, s], preferred_element_type=F32
+                ).astype(BF16)
+                out[:s.stop, s] = upper
+                for t in tiles[:s.start // width]:
+                    out[s, t] = upper[t].T
         if sweep < SWEEPS - 1:
             for s in tiles:
                 iterate[:, s] = last_product(iterate[:, s], cubic_b, iterate_b[:, s])
@@ -399,9 +396,13 @@
             right_done[n],
             ("zh", "xl", "y", "xh", "c"),
             [
-                (zh * count + place(1, y, k), (zh + shift) % NZH * count + place(0, y, i))
+                (zh * count + source, (zh + shift) % NZH * count + target)
                 for zh in range(NZH)
                 for i, k, y in cells
+                for source, target in (
+                    (place(1, y, k), place(0, y, i)),
+                    (place(0, y, i), place(1, y, k)),
+                )
             ],
         )
         for n, shift in enumerate(SHIFTS)

time: 134 us -> 133 us (level)
  Pallas kernels: 24.1 us -> 22.4 us
  waiting for transfers between devices: 16.1 us -> 17.7 us
    pallas_call x8, Pallas kernels: 24.1 us -> 22.4 us  [call(): pl.pallas_call(kernel, out_shape=out_shape, scratch_shapes=list(scratch),...]
    ppermute x4, waiting for transfers between devices: 0.48 us -> 2.07 us  [local(): lax.ppermute(right_done[n], ('zh', 'xl', 'y', 'xh', 'c'), [(zh * count +...]
  transfers between devices with their start and end apart: 15 -> 15, of which waited for: 6 -> 8; matrix products, arithmetic and copies ran while one was open for 0% -> 0% of each run, Pallas kernels for 10% -> 9%
where the time goes in v12:
time: 133 us; the launch traced here: 132 us
  blocking collectives  58.8 us (44%)
  starting transfers between devices  32.5 us (24%)
  Pallas kernels  22.4 us (17%)
  waiting for transfers between devices  17.7 us (13%)
    all_to_all x1, blocking collectives, local(): got = lax.all_to_all(packed, ('zl', 'xl', 'y'), 0, 0, tiled=True)  37.5 us
    pallas_call x8, Pallas kernels, call(): pl.pallas_call(kernel, out_shape=out_shape, scratch_shapes=list(scratch),...  22.4 us
    all_to_all x1, blocking collectives, local(): returned = lax.all_to_all(result, DP, 0, 0, tiled=True)  21.3 us
    ppermute x6, starting transfers between devices, turned(): return lax.ppermute(x, axes, [(n, (n + shift) % size) for n in range(size)])  12.3 us
    ppermute x4, starting transfers between devices, local(): lax.ppermute(right_done[n], ('zh', 'xl', 'y', 'xh', 'c'), [(zh * count +...  8.72 us
    all_to_all x1, waiting for transfers between devices, local(): packed = lax.all_to_all(pieces, ('zl', 'y'), 0, 0, tiled=True)  8 us
    ppermute x6, waiting for transfers between devices, turned(): return lax.ppermute(x, axes, [(n, (n + shift) % size) for n in range(size)])  7.61 us
    ppermute x4, starting transfers between devices, local(): lax.ppermute(slab, ('zl', 'xl', 'y', 'xh', 'c'), [((zl + turn) % NZL * co...  7.35 us
  transfers between devices with their start and end apart: 15, of which 8 were waited for; matrix products, arithmetic and copies ran while one was open for 0% of the time, Pallas kernels for 9%

profile of v12, /device:TPU:2, one launch (start us, length us, event | category | flops | bytes accessed | tf_op | source)
XLA Modules:
  0.0 131.5 jit_solution(6957120186363933218)
XLA Ops:
  0.0 5.0 %gram.1 = bf16[16,592,128]{2,1,0:T(8,128)(2,1)} custom-call(bf16[768,1024]{1,0:T(8,128)(2,1)} %acts_ref.1, bf16[768,1024]{1,0:T(8,128)(2,1)} %grads_ref.1), custom_call_target="tpu_custom_call" | custom-call | flops 3221225472 | bytes 4194304 | tf_op jit(solution)/shard_map/gram/pallas_call | solution.py:44
  5.0 0.0 copy-start
  5.0 37.5 %all_to_all.15.got_ref = bf16[16,592,128]{2,1,0:T(8,128)(2,1)S(1)} all-to-all(bf16[16,592,128]{2,1,0:T(8,128)(2,1)} %gram.1), channel_id=1, replica_groups=mesh['zh'=4,'zl'=2,'xl'=2,'y'=4,'xh'=2,'c'=2] {'zl','xl','y'}, dimensions={0} | all-to-all | bytes 4849664 | tf_op jit(solution)/shard_map/all_to_all | solution.py:327
  42.5 0.4 sum.1
  42.9 5.5 %collective-permute-start = (bf16[592,128]{1,0:T(8,128)(2,1)S(1)}, bf16[592,128]{1,0:T(8,128)(2,1)S(1)}, u32[]{:S(2)}, u32[]{:S(2)}) collective-permute-start(bf16[592,128]{1,0:T(8,128)(2,1)S(1)} %get-tuple-element.20.refs_0_), channel_id=1, source_target_pairs={{0,192},{64,0},{128,64},{192,128},{1,193},{65,1},{129,65},{193,129... | collective-permute-start | bytes 454664 | tf_op jit(solution)/shard_map/ppermute | solution.py:304
  48.4 3.8 %collective-permute-start.2 = (bf16[592,128]{1,0:T(8,128)(2,1)S(1)}, bf16[592,128]{1,0:T(8,128)(2,1)S(1)}, u32[]{:S(2)}, u32[]{:S(2)}) collective-permute-start(bf16[592,128]{1,0:T(8,128)(2,1)S(1)} %get-tuple-element.20.refs_0_), channel_id=1, source_target_pairs={{0,128},{64,192},{128,0},{192,64},{1,129},{65,193},{129,1},{193,65... | collective-permute-start | bytes 454664 | tf_op jit(solution)/shard_map/ppermute | solution.py:304
  52.2 0.4 collective-permute-start.3
  52.6 2.4 %collective-permute-start.4 = (bf16[16,1024]{1,0:T(8,128)(2,1)S(1)}, bf16[16,1024]{1,0:T(8,128)(2,1)S(1)}, u32[]{:S(2)}, u32[]{:S(2)}) collective-permute-start(bf16[16,1024]{1,0:T(8,128)(2,1)S(1)} %get-tuple-element.23), channel_id=1, source_target_pairs={{0,8},{4,12},{8,0},{12,4},{1,9},{5,13},{9,1},{13,5},{2,10},{6,14},... | collective-permute-start | bytes 98312 | tf_op jit(solution)/shard_map/ppermute | solution.py:304
  55.1 2.3 %collective-permute-done.3.refs_5_ = bf16[16,1024]{1,0:T(8,128)(2,1)S(1)} collective-permute-done((bf16[16,1024]{1,0:T(8,128)(2,1)S(1)}, bf16[16,1024]{1,0:T(8,128)(2,1)S(1)}, u32[]{:S(2)}, u32[]{:S(2)}) %collective-permute-start.3) | collective-permute-done | bytes 32800 | tf_op jit(solution)/shard_map/ppermute | solution.py:304
  57.3 0.2 collective-permute-start.5
  57.5 0.5 collective-permute-done.4.refs_6_
  58.0 3.2 %collective-permute-done.5.refs_7_ = bf16[16,1024]{1,0:T(8,128)(2,1)S(1)} collective-permute-done((bf16[16,1024]{1,0:T(8,128)(2,1)S(1)}, bf16[16,1024]{1,0:T(8,128)(2,1)S(1)}, u32[]{:S(2)}, u32[]{:S(2)}) %collective-permute-start.5) | collective-permute-done | bytes 32800 | tf_op jit(solution)/shard_map/ppermute | solution.py:304
  61.2 1.6 %collective-permute-done.2.refs_3_ = bf16[592,128]{1,0:T(8,128)(2,1)S(1)} collective-permute-done((bf16[592,128]{1,0:T(8,128)(2,1)S(1)}, bf16[592,128]{1,0:T(8,128)(2,1)S(1)}, u32[]{:S(2)}, u32[]{:S(2)}) %collective-permute-start.2) | collective-permute-done | bytes 151584 | tf_op jit(solution)/shard_map/ppermute | solution.py:304
  62.8 1.4 %damp.1 = (bf16[8,592,128]{2,1,0:T(8,128)(2,1)}, bf16[64,1024]{1,0:T(8,128)(2,1)S(1)}) custom-call(bf16[592,128]{1,0:T(8,128)(2,1)S(1)} %get-tuple-element.20.refs_0_, bf16[592,128]{1,0:T(8,128)(2,1)S(1)} %collective-permute-done.refs_1_, bf16[592,128]{1,0:T(8,128)(2,1)S(1)} %collective-permute-done.1.refs_2_, ...), custom_call_target="tpu_custom_call" | custom-call | bytes 4194304 | tf_op jit(solution)/shard_map/damp/pallas_call | solution.py:44
  64.3 4.1 %all-to-all-start.1 = ((bf16[8,592,128]{2,1,0:T(8,128)(2,1)}), bf16[8,592,128]{2,1,0:T(8,128)(2,1)S(1)}, u32[]{:S(2)}, u32[]{:S(2)}) async-start(bf16[8,592,128]{2,1,0:T(8,128)(2,1)} %get-tuple-element.25), calls=%async_computation.1 | async-start | bytes 2424832 | tf_op jit(solution)/shard_map/all_to_all | solution.py:366
  68.4 1.3 collective-permute-start.6
  69.6 0.7 collective-permute-start.7
  70.3 1.3 collective-permute-start.8
  71.6 4.1 %collective-permute-start.9 = (bf16[64,1024]{1,0:T(8,128)(2,1)S(1)}, bf16[64,1024]{1,0:T(8,128)(2,1)S(1)}, u32[]{:S(2)}, u32[]{:S(2)}) collective-permute-start(bf16[64,1024]{1,0:T(8,128)(2,1)S(1)} %get-tuple-element.30), channel_id=1, source_target_pairs={{48,16},{53,20},{58,24},{63,28},{50,17},{55,21},{56,25},{61,29},{4... | collective-permute-start | bytes 393224 | tf_op jit(solution)/shard_map/ppermute | solution.py:354
  75.7 8.0 %all-to-all-done.1.packed_ref = bf16[8,592,128]{2,1,0:T(8,128)(2,1)S(1)} async-done(((bf16[8,592,128]{2,1,0:T(8,128)(2,1)}), bf16[8,592,128]{2,1,0:T(8,128)(2,1)S(1)}, u32[]{:S(2)}, u32[]{:S(2)}) %all-to-all-start.1) | async-done | bytes 1212448 | tf_op jit(solution)/shard_map/all_to_all | solution.py:366
  83.7 9.7 %root.1 = (f32[8,128]{1,0:T(8,128)S(1)}, f32[1024,1024]{1,0:T(8,128)S(1)}, bf16[1024,1024]{1,0:T(8,128)(2,1)S(1)}, bf16[1024,1024]{1,0:T(8,128)(2,1)S(1)}) custom-call(bf16[8,592,128]{2,1,0:T(8,128)(2,1)S(1)} %all-to-all-done.1.packed_ref), custom_call_target="tpu_custom_call" | custom-call | flops 10737418240 | bytes 4194304 | tf_op jit(solution)/shard_map/root/pallas_call | solution.py:44
  93.5 2.1 %right.1 = (bf16[256,128]{1,0:T(8,128)(2,1)S(1)}, bf16[256,128]{1,0:T(8,128)(2,1)S(1)}, bf16[256,128]{1,0:T(8,128)(2,1)S(1)}, bf16[256,128]{1,0:T(8,128)(2,1)S(1)}) custom-call(f32[8,128]{1,0:T(8,128)S(1)} %get-tuple-element.26.over_ref, f32[1024,1024]{1,0:T(8,128)S(1)} %get-tuple-element.27.iterate, bf16[1024,1024]{1,0:T(8,128)(2,1)S(1)} %get-tuple-element.28.iterate_b, ...), custom_call_target="tpu_custom_call" | custom-call | flops 1342177280 | bytes 4194304 | tf_op jit(solution)/shard_map/right/pallas_call | solution.py:44
  95.5 3.7 %collective-permute-start.10 = (bf16[256,128]{1,0:T(8,128)(2,1)S(1)}, bf16[256,128]{1,0:T(8,128)(2,1)S(1)}, u32[]{:S(2)}, u32[]{:S(2)}) collective-permute-start(bf16[256,128]{1,0:T(8,128)(2,1)S(1)} %get-tuple-element.31), channel_id=1, source_target_pairs={{16,128},{0,144},{20,133},{5,148},{24,138},{10,152},{28,143},{15,1... | collective-permute-start | bytes 196616 | tf_op jit(solution)/shard_map/ppermute | solution.py:395
  99.2 1.9 %collective-permute-start.11 = (bf16[256,128]{1,0:T(8,128)(2,1)S(1)}, bf16[256,128]{1,0:T(8,128)(2,1)S(1)}, u32[]{:S(2)}, u32[]{:S(2)}) collective-permute-start(bf16[256,128]{1,0:T(8,128)(2,1)S(1)} %get-tuple-element.32), channel_id=1, source_target_pairs={{16,64},{0,80},{20,69},{5,84},{24,74},{10,88},{28,79},{15,92},{17,... | collective-permute-start | bytes 196616 | tf_op jit(solution)/shard_map/ppermute | solution.py:395
  101.1 3.1 %collective-permute-start.12 = (bf16[256,128]{1,0:T(8,128)(2,1)S(1)}, bf16[256,128]{1,0:T(8,128)(2,1)S(1)}, u32[]{:S(2)}, u32[]{:S(2)}) collective-permute-start(bf16[256,128]{1,0:T(8,128)(2,1)S(1)} %get-tuple-element.33), channel_id=1, source_target_pairs={{16,192},{0,208},{20,197},{5,212},{24,202},{10,216},{28,207},{15,2... | collective-permute-start | bytes 196616 | tf_op jit(solution)/shard_map/ppermute | solution.py:395
  104.2 2.5 %rest.1.root_ref = bf16[1024,1024]{1,0:T(8,128)(2,1)S(1)} custom-call(f32[8,128]{1,0:T(8,128)S(1)} %get-tuple-element.26.over_ref, f32[1024,1024]{1,0:T(8,128)S(1)} %get-tuple-element.27.iterate, bf16[1024,1024]{1,0:T(8,128)(2,1)S(1)} %get-tuple-element.28.iterate_b, bf16[1024,1024]{1,0:T(8,128)(2,1)S(1)} %get-tuple-element.29.cubic_b), custom_call_target="tpu_custom_call" | custom-call | flops 2147483648 | bytes 4194304 | tf_op jit(solution)/shard_map/rest/pallas_call | solution.py:44
  106.7 1.2 collective-permute-done.11.refs_1_
  108.0 0.2 collective-permute-done.12.refs_2_
  108.1 0.7 collective-permute-done.13.refs_3_
  108.8 0.7 left.1
  109.5 21.3 %all_to_all.16.got_ref = bf16[64,16,128]{2,1,0:T(8,128)(2,1)S(1)} all-to-all(bf16[64,16,128]{2,1,0:T(8,128)(2,1)S(1)} %bitcast.1), channel_id=1, replica_groups=mesh['zh'=4,'zl'=2,'xl'=2,'y'=4,'xh'=2,'c'=2] {'zh','zl','xl','y'}, dimensions={0} | all-to-all | bytes 524288 | tf_op jit(solution)/shard_map/all_to_all | solution.py:419
  130.9 0.7 place.1
  (10 shorter events, 0.0 us)
Async XLA Ops:
  5.0 37.5 %copy-start = (f32[1,16,4096]{2,1,0:T(8,128)S(1)}, f32[1,16,4096]{2,1,0:T(8,128)}, u32[]{:S(2)}) copy-start(f32[1,16,4096]{2,1,0:T(8,128)} %gradient_ref.1) | copy-start | bytes 786436
  42.9 18.3 %collective-permute-start = (bf16[592,128]{1,0:T(8,128)(2,1)S(1)}, bf16[592,128]{1,0:T(8,128)(2,1)S(1)}, u32[]{:S(2)}, u32[]{:S(2)}) collective-permute-start(bf16[592,128]{1,0:T(8,128)(2,1)S(1)} %get-tuple-element.20.refs_0_), channel_id=1, source_target_pairs={{0,192},{64,0},{128,64},{192,128},{1,193},{65,1},{129,65},{193,129... | collective-permute-start | bytes 454664 | tf_op jit(solution)/shard_map/ppermute | solution.py:304
  48.4 12.9 %collective-permute-start.1 = (bf16[592,128]{1,0:T(8,128)(2,1)S(1)}, bf16[592,128]{1,0:T(8,128)(2,1)S(1)}, u32[]{:S(2)}, u32[]{:S(2)}) collective-permute-start(bf16[592,128]{1,0:T(8,128)(2,1)S(1)} %get-tuple-element.20.refs_0_), channel_id=1, source_target_pairs={{0,64},{64,128},{128,192},{192,0},{1,65},{65,129},{129,193},{193,1... | collective-permute-start | bytes 454664 | tf_op jit(solution)/shard_map/ppermute | solution.py:304
  48.4 14.5 %collective-permute-start.2 = (bf16[592,128]{1,0:T(8,128)(2,1)S(1)}, bf16[592,128]{1,0:T(8,128)(2,1)S(1)}, u32[]{:S(2)}, u32[]{:S(2)}) collective-permute-start(bf16[592,128]{1,0:T(8,128)(2,1)S(1)} %get-tuple-element.20.refs_0_), channel_id=1, source_target_pairs={{0,128},{64,192},{128,0},{192,64},{1,129},{65,193},{129,1},{193,65... | collective-permute-start | bytes 454664 | tf_op jit(solution)/shard_map/ppermute | solution.py:304
  52.2 5.1 %collective-permute-start.3 = (bf16[16,1024]{1,0:T(8,128)(2,1)S(1)}, bf16[16,1024]{1,0:T(8,128)(2,1)S(1)}, u32[]{:S(2)}, u32[]{:S(2)}) collective-permute-start(bf16[16,1024]{1,0:T(8,128)(2,1)S(1)} %get-tuple-element.22), channel_id=1, source_target_pairs={{0,4},{4,8},{8,12},{12,0},{1,5},{5,9},{9,13},{13,1},{2,6},{6,10},{... | collective-permute-start | bytes 98312 | tf_op jit(solution)/shard_map/ppermute | solution.py:304
  52.6 5.4 %collective-permute-start.4 = (bf16[16,1024]{1,0:T(8,128)(2,1)S(1)}, bf16[16,1024]{1,0:T(8,128)(2,1)S(1)}, u32[]{:S(2)}, u32[]{:S(2)}) collective-permute-start(bf16[16,1024]{1,0:T(8,128)(2,1)S(1)} %get-tuple-element.23), channel_id=1, source_target_pairs={{0,8},{4,12},{8,0},{12,4},{1,9},{5,13},{9,1},{13,5},{2,10},{6,14},... | collective-permute-start | bytes 98312 | tf_op jit(solution)/shard_map/ppermute | solution.py:304
  57.3 3.9 %collective-permute-start.5 = (bf16[16,1024]{1,0:T(8,128)(2,1)S(1)}, bf16[16,1024]{1,0:T(8,128)(2,1)S(1)}, u32[]{:S(2)}, u32[]{:S(2)}) collective-permute-start(bf16[16,1024]{1,0:T(8,128)(2,1)S(1)} %get-tuple-element.24), channel_id=1, source_target_pairs={{0,12},{4,0},{8,4},{12,8},{1,13},{5,1},{9,5},{13,9},{2,14},{6,2},{... | collective-permute-start | bytes 98312 | tf_op jit(solution)/shard_map/ppermute | solution.py:304
  64.3 19.5 %all-to-all-start.1 = ((bf16[8,592,128]{2,1,0:T(8,128)(2,1)}), bf16[8,592,128]{2,1,0:T(8,128)(2,1)S(1)}, u32[]{:S(2)}, u32[]{:S(2)}) async-start(bf16[8,592,128]{2,1,0:T(8,128)(2,1)} %get-tuple-element.25), calls=%async_computation.1 | async-start | bytes 2424832 | tf_op jit(solution)/shard_map/all_to_all | solution.py:366
  68.4 25.1 %collective-permute-start.6 = (bf16[64,1024]{1,0:T(8,128)(2,1)S(1)}, bf16[64,1024]{1,0:T(8,128)(2,1)S(1)}, u32[]{:S(2)}, u32[]{:S(2)}) collective-permute-start(bf16[64,1024]{1,0:T(8,128)(2,1)S(1)} %get-tuple-element.30), channel_id=1, source_target_pairs={{0,16},{5,20},{10,24},{15,28},{2,17},{7,21},{8,25},{13,29},{1,18},... | collective-permute-start | bytes 393224 | tf_op jit(solution)/shard_map/ppermute | solution.py:354
  69.6 23.8 %collective-permute-start.7 = (bf16[64,1024]{1,0:T(8,128)(2,1)S(1)}, bf16[64,1024]{1,0:T(8,128)(2,1)S(1)}, u32[]{:S(2)}, u32[]{:S(2)}) collective-permute-start(bf16[64,1024]{1,0:T(8,128)(2,1)S(1)} %get-tuple-element.30), channel_id=1, source_target_pairs={{16,16},{21,20},{26,24},{31,28},{18,17},{23,21},{24,25},{29,29},{1... | collective-permute-start | bytes 393224 | tf_op jit(solution)/shard_map/ppermute | solution.py:354
  70.3 23.1 %collective-permute-start.8 = (bf16[64,1024]{1,0:T(8,128)(2,1)S(1)}, bf16[64,1024]{1,0:T(8,128)(2,1)S(1)}, u32[]{:S(2)}, u32[]{:S(2)}) collective-permute-start(bf16[64,1024]{1,0:T(8,128)(2,1)S(1)} %get-tuple-element.30), channel_id=1, source_target_pairs={{32,16},{37,20},{42,24},{47,28},{34,17},{39,21},{40,25},{45,29},{3... | collective-permute-start | bytes 393224 | tf_op jit(solution)/shard_map/ppermute | solution.py:354
  71.6 21.8 %collective-permute-start.9 = (bf16[64,1024]{1,0:T(8,128)(2,1)S(1)}, bf16[64,1024]{1,0:T(8,128)(2,1)S(1)}, u32[]{:S(2)}, u32[]{:S(2)}) collective-permute-start(bf16[64,1024]{1,0:T(8,128)(2,1)S(1)} %get-tuple-element.30), channel_id=1, source_target_pairs={{48,16},{53,20},{58,24},{63,28},{50,17},{55,21},{56,25},{61,29},{4... | collective-permute-start | bytes 393224 | tf_op jit(solution)/shard_map/ppermute | solution.py:354
  95.5 11.2 %collective-permute-start.10 = (bf16[256,128]{1,0:T(8,128)(2,1)S(1)}, bf16[256,128]{1,0:T(8,128)(2,1)S(1)}, u32[]{:S(2)}, u32[]{:S(2)}) collective-permute-start(bf16[256,128]{1,0:T(8,128)(2,1)S(1)} %get-tuple-element.31), channel_id=1, source_target_pairs={{16,128},{0,144},{20,133},{5,148},{24,138},{10,152},{28,143},{15,1... | collective-permute-start | bytes 196616 | tf_op jit(solution)/shard_map/ppermute | solution.py:395
  99.2 8.7 %collective-permute-start.11 = (bf16[256,128]{1,0:T(8,128)(2,1)S(1)}, bf16[256,128]{1,0:T(8,128)(2,1)S(1)}, u32[]{:S(2)}, u32[]{:S(2)}) collective-permute-start(bf16[256,128]{1,0:T(8,128)(2,1)S(1)} %get-tuple-element.32), channel_id=1, source_target_pairs={{16,64},{0,80},{20,69},{5,84},{24,74},{10,88},{28,79},{15,92},{17,... | collective-permute-start | bytes 196616 | tf_op jit(solution)/shard_map/ppermute | solution.py:395
  101.1 7.0 %collective-permute-start.12 = (bf16[256,128]{1,0:T(8,128)(2,1)S(1)}, bf16[256,128]{1,0:T(8,128)(2,1)S(1)}, u32[]{:S(2)}, u32[]{:S(2)}) collective-permute-start(bf16[256,128]{1,0:T(8,128)(2,1)S(1)} %get-tuple-element.33), channel_id=1, source_target_pairs={{16,192},{0,208},{20,197},{5,212},{24,202},{10,216},{28,207},{15,2... | collective-permute-start | bytes 196616 | tf_op jit(solution)/shard_map/ppermute | solution.py:395
  104.2 4.6 %collective-permute-start.13 = (bf16[256,128]{1,0:T(8,128)(2,1)S(1)}, bf16[256,128]{1,0:T(8,128)(2,1)S(1)}, u32[]{:S(2)}, u32[]{:S(2)}) collective-permute-start(bf16[256,128]{1,0:T(8,128)(2,1)S(1)} %get-tuple-element.34), channel_id=1, source_target_pairs={{16,0},{0,16},{20,5},{5,20},{24,10},{10,24},{28,15},{15,28},{17,2}... | collective-permute-start | bytes 196616 | tf_op jit(solution)/shard_map/ppermute | solution.py:395
